TPU v7x, 32 devices: a whole 2x2x4 slice. The times are simulated.
32 devices in a mesh: row: 4 (over x, core), col: 8 (over z, y).
Axes of the slice: x: 2, y: 2, z: 4, core: 2. Of those that a mesh axis runs over, the one named last changes fastest.
Arguments:
- factor: float32 [6, 4, 8, 512, 512], P(None, 'row', 'col'), may hold values from -0.1875 to 0.1875
- rhs: float32 [6, 4, 8, 128, 128], P(None, 'row', 'col'), may hold values from -6 to 6
- inverses: float32 [4, 512, 512], replicated, may hold values from -0.5 to 2, as said below
Outputs:
- solved: float32 [4, 512, 128], P(None, 'col')
- remaining: float32 [6, 4, 8, 128, 128], P(None, 'row', 'col')
Inputs may be any that keep to these rules, and one draw needn't show every extreme that they name: `inverses`: each block is lower triangular with its diagonal between 0.5 and 2 and entries below it of magnitude at most 4 / sqrt(512).
All inputs are finite; a program needn't handle non-finite values.
Results may differ from a plain program's by a relative error of at most 0.00011.
Values sent between devices are 32-bit elements; how exact they have to be, the bound alone decides.
No kernel may reach another device: no remote copies, remote signals or barrier semaphores. Data moves between devices by JAX's collectives and lax.ppermute only.
A program may use at most 64 MiB of HBM per device.

v0:
```python
import jax
import jax.numpy as jnp
from jax import lax
from jax.sharding import PartitionSpec as P


def shifted(block, axis, distance):
    devices = range(lax.axis_size(axis))
    route = [((i - distance) % len(devices), i) for i in devices]
    return lax.ppermute(block, axis, route)


def broadcast(x, axis, root):
    mine = lax.axis_index(axis) == root
    return lax.psum(jnp.where(mine, x, jnp.zeros_like(x)), axis)


def group_reduce(update, member, steps, groups):
    blocks = update.shape[0]
    nrhs = update.shape[2]
    split = update.reshape(blocks, steps, update.shape[1] // steps, nrhs)
    total = lax.dynamic_index_in_dim(split, member, 1, keepdims=False)
    for offset in range(1, steps):
        piece = lax.dynamic_index_in_dim(split, (member + offset) % steps, 1, keepdims=False)
        total = total + shifted(piece, "col", offset * groups)
    return total


def on_device(factor, rhs, inverses):
    steps = inverses.shape[0]
    blocks = factor.shape[0]
    width = factor.shape[3]
    quarter = rhs.shape[3]
    nrhs = rhs.shape[4]
    row_count = lax.axis_size("row")
    col_count = lax.axis_size("col")
    groups = col_count // steps
    row_pos = lax.axis_index("row")
    col_pos = lax.axis_index("col")
    member = col_pos // groups
    group = col_pos % groups
    block_ids = (jnp.arange(blocks, dtype=jnp.int32) * row_count + row_pos) * groups + group
    panel = factor[:, 0, 0]
    current = rhs[:, 0, 0]
    solved_list = []
    for k in range(steps):
        owner_row = k // groups
        owner_group = k % groups
        placed = lax.dynamic_update_slice(
            jnp.zeros((width, nrhs), jnp.float32),
            current[0],
            (member * quarter, jnp.zeros((), jnp.int32)),
        )
        contrib = placed
        is_owner = jnp.logical_and(row_pos == owner_row, group == owner_group)
        contrib = jnp.where(is_owner, contrib, jnp.zeros_like(contrib))
        complete = lax.psum(contrib, "col")
        solved_block = jnp.dot(inverses[k], complete, precision=lax.Precision.HIGHEST)
        solved_block = broadcast(solved_block, "row", owner_row)
        solved_list.append(solved_block)
        keep = (block_ids > k).astype(jnp.float32)[:, None, None]

        def column_update(solved_now=solved_block, keep_now=keep):
            return (
                jnp.einsum("rji,jh->rih", panel, solved_now, precision=lax.Precision.HIGHEST)
                * keep_now
            )

        def no_update():
            return jnp.zeros((blocks, width, nrhs), jnp.float32)

        update = lax.cond(member == k, column_update, no_update)
        current = current - group_reduce(update, member, steps, groups)
    stacked = jnp.stack(solved_list)
    share = width // col_count
    solved_rows = lax.dynamic_slice_in_dim(stacked, col_pos * share, share, 1)
    return (solved_rows, current[:, None, None])


def solution(mesh):
    in_specs = (P(None, "row", "col", None, None), P(None, "row", "col", None, None), P())
    out_specs = (P(None, "col", None), P(None, "row", "col", None, None))
    return jax.shard_map(
        on_device, mesh=mesh, in_specs=in_specs, out_specs=out_specs, check_vma=False
    )
```

profile of v0, /device:TPU:0, one launch (start us, length us, event | category | flops | bytes accessed | tf_op | source)
XLA Modules:
  0.0 615.0 jit_solution(8668786151128359799)
XLA Ops:
  7.2 0.0 all-reduce.9.cloned.1.call-start
  7.3 0.9 bitcast_dynamic-update-slice_fusion
  8.1 0.7 copy-done.5
  8.9 0.0 all-reduce.11.cloned.1.call-start
  9.0 6.6 %copy.5 = f32[6,1,1,512,512]{3,4,0,2,1:T(8,128)} copy(f32[6,1,1,512,512]{4,3,2,1,0:T(8,128)} %param.11) | data formatting | bytes 12582912 | tf_op args[0]
  15.6 69.6 %all-reduce.9.cloned.1.call-done = f32[512,128]{1,0:T(8,128)} async-done(((f32[512,128]{1,0:T(8,128)}), f32[512,128]{1,0:T(8,128)}) %all-reduce.9.cloned.1.call-update) | async-done | bytes 262160 | tf_op jit(solution)/shard_map/psum | solution.py:57
  85.2 3.3 fusion.7
  88.4 0.0 all-reduce.11.cloned.1.call-update
  88.5 0.0 all-reduce.13.cloned.1.call-start
  88.5 31.3 %all-reduce.11.cloned.1.call-done = f32[512,128]{0,1:T(8,128)} async-done(((f32[512,128]{0,1:T(8,128)}), f32[512,128]{0,1:T(8,128)}) %all-reduce.11.cloned.1.call-update) | async-done | bytes 262160 | tf_op jit(solution)/shard_map/psum | solution.py:15
  119.9 7.2 %conditional.4 = (f32[6,4,128,128]{3,2,1,0:T(8,128)S(1)}) conditional(s32[]{:T(128)} %convert_element_type.52, () %tuple.40, (f32[6,512,512]{1,2,0:T(8,128)}, f32[512,128]{0,1:T(8,128)}, f32[6,1,1]{0,2,1:T(1,128)S(1)}) %tuple.89), branch_computations={%region_2.3_spmd, %region_3.4_spmd} | conditional | flops 2416312320 | bytes 8126496 | solution.py:72
  119.9 7.2 %convolution_multiply_fusion = f32[6,512,128]{2,1,0:T(8,128)S(1)} fusion(f32[6,512,512]{1,2,0:T(8,128)} %get-tuple-element.40, f32[6]{0:T(128)S(1)} %bitcast.144, f32[512,128]{0,1:T(8,128)} %get-tuple-element.55), kind=kOutput, calls=%fused_computation | convolution fusion | flops 2416312320 | bytes 8126488 | tf_op jit(solution)/shard_map/cond/branch_1_fun/rji,jh->rih/dot_general | solution.py:65
  127.0 0.9 dynamic-slice_bitcast_fusion.11
  127.9 3.8 collective-permute-start.2
  131.7 10.3 %collective-permute-done = f32[6,128,128]{2,1,0:T(8,128)S(1)} collective-permute-done((f32[6,128,128]{2,1,0:T(8,128)}, f32[6,128,128]{2,1,0:T(8,128)S(1)}, u32[]{:S(2)}, u32[]{:S(2)}) %collective-permute-start) | collective-permute-done | bytes 393248 | tf_op jit(solution)/shard_map/ppermute | solution.py:10
  142.0 14.3 %collective-permute-done.1 = f32[6,128,128]{2,1,0:T(8,128)S(1)} collective-permute-done((f32[6,128,128]{2,1,0:T(8,128)S(1)}, f32[6,128,128]{2,1,0:T(8,128)S(1)}, u32[]{:S(2)}, u32[]{:S(2)}) %collective-permute-start.1) | collective-permute-done | bytes 393248 | tf_op jit(solution)/shard_map/ppermute | solution.py:10
  156.3 1.1 fusion.28
  157.5 0.7 copy-done.6
  158.2 0.0 all-reduce.13.cloned.1.call-update
  158.2 0.0 all-reduce.15.cloned.1.call-start
  158.3 75.8 %all-reduce.13.cloned.1.call-done = f32[512,128]{1,0:T(8,128)} async-done(((f32[512,128]{1,0:T(8,128)}), f32[512,128]{1,0:T(8,128)}) %all-reduce.13.cloned.1.call-update) | async-done | bytes 262160 | tf_op jit(solution)/shard_map/psum | solution.py:57
  234.1 3.3 fusion.6
  237.3 0.0 all-reduce.17.cloned.1.call-start
  237.4 31.4 %all-reduce.15.cloned.1.call-done = f32[512,128]{0,1:T(8,128)} async-done(((f32[512,128]{0,1:T(8,128)}), f32[512,128]{0,1:T(8,128)}) %all-reduce.15.cloned.1.call-update) | async-done | bytes 262160 | tf_op jit(solution)/shard_map/psum | solution.py:15
  268.7 0.2 conditional.5
  268.7 0.2 reshape.83
  268.9 0.9 dynamic-slice_bitcast_fusion.8
  269.8 8.5 %collective-permute-start.3 = (f32[6,128,128]{2,1,0:T(8,128)}, f32[6,128,128]{2,1,0:T(8,128)S(1)}, u32[]{:S(2)}, u32[]{:S(2)}) collective-permute-start(f32[6,128,128]{2,1,0:T(8,128)} %get-tuple-element.76), channel_id=1, source_target_pairs={{6,0},{7,1},{0,2},{1,3},{2,4},{3,5},{4,6},{5,7},{14,8},{15,9},{8,1... | collective-permute-start | bytes 1179656 | tf_op jit(solution)/shard_map/ppermute | solution.py:10
  278.3 2.4 collective-permute-start.5
  280.6 7.5 %collective-permute-done.3 = f32[6,128,128]{2,1,0:T(8,128)S(1)} collective-permute-done((f32[6,128,128]{2,1,0:T(8,128)}, f32[6,128,128]{2,1,0:T(8,128)S(1)}, u32[]{:S(2)}, u32[]{:S(2)}) %collective-permute-start.3) | collective-permute-done | bytes 393248 | tf_op jit(solution)/shard_map/ppermute | solution.py:10
  288.1 10.1 %collective-permute-done.4 = f32[6,128,128]{2,1,0:T(8,128)S(1)} collective-permute-done((f32[6,128,128]{2,1,0:T(8,128)S(1)}, f32[6,128,128]{2,1,0:T(8,128)S(1)}, u32[]{:S(2)}, u32[]{:S(2)}) %collective-permute-start.4) | collective-permute-done | bytes 393248 | tf_op jit(solution)/shard_map/ppermute | solution.py:10
  298.2 4.4 collective-permute-done.5
  302.6 1.1 fusion.25
  303.8 0.7 copy-done.7
  304.5 0.0 all-reduce.19.cloned.1.call-start
  304.5 79.1 %all-reduce.17.cloned.1.call-done = f32[512,128]{1,0:T(8,128)} async-done(((f32[512,128]{1,0:T(8,128)}), f32[512,128]{1,0:T(8,128)}) %all-reduce.17.cloned.1.call-update) | async-done | bytes 262160 | tf_op jit(solution)/shard_map/psum | solution.py:57
  383.7 3.3 fusion.5
  387.0 0.0 all-reduce.21.cloned.1.call-start
  387.0 31.4 %all-reduce.19.cloned.1.call-done = f32[512,128]{0,1:T(8,128)} async-done(((f32[512,128]{0,1:T(8,128)}), f32[512,128]{0,1:T(8,128)}) %all-reduce.19.cloned.1.call-update) | async-done | bytes 262160 | tf_op jit(solution)/shard_map/psum | solution.py:15
  418.4 0.3 conditional.6
  418.4 0.2 reshape.85
  418.7 0.9 dynamic-slice_bitcast_fusion.5
  419.6 1.5 collective-permute-start.6
  421.1 7.7 %collective-permute-start.7 = (f32[6,128,128]{2,1,0:T(8,128)S(1)}, f32[6,128,128]{2,1,0:T(8,128)S(1)}, u32[]{:S(2)}, u32[]{:S(2)}) collective-permute-start(f32[6,128,128]{2,1,0:T(8,128)S(1)} %get-tuple-element.75), channel_id=1, source_target_pairs={{4,0},{5,1},{6,2},{7,3},{0,4},{1,5},{2,6},{3,7},{12,8},{13,9},{14,... | collective-permute-start | bytes 1179656 | tf_op jit(solution)/shard_map/ppermute | solution.py:10
  428.8 2.9 collective-permute-start.8
  431.7 16.3 %collective-permute-done.7 = f32[6,128,128]{2,1,0:T(8,128)S(1)} collective-permute-done((f32[6,128,128]{2,1,0:T(8,128)S(1)}, f32[6,128,128]{2,1,0:T(8,128)S(1)}, u32[]{:S(2)}, u32[]{:S(2)}) %collective-permute-start.7) | collective-permute-done | bytes 393248 | tf_op jit(solution)/shard_map/ppermute | solution.py:10
  448.1 1.1 fusion.22
  449.2 0.7 copy-done.4
  449.9 0.0 all-reduce.23.cloned.1.call-start
  450.0 84.5 %all-reduce.21.cloned.1.call-done = f32[512,128]{1,0:T(8,128)} async-done(((f32[512,128]{1,0:T(8,128)}), f32[512,128]{1,0:T(8,128)}) %all-reduce.21.cloned.1.call-update) | async-done | bytes 262160 | tf_op jit(solution)/shard_map/psum | solution.py:57
  534.5 3.3 fusion.4
  537.8 31.4 %all-reduce.23.cloned.1.call-done = f32[512,128]{0,1:T(8,128)} async-done(((f32[512,128]{0,1:T(8,128)}), f32[512,128]{0,1:T(8,128)}) %all-reduce.23.cloned.1.call-update) | async-done | bytes 262160 | tf_op jit(solution)/shard_map/psum | solution.py:15
  569.2 0.2 conditional.7
  569.2 0.2 reshape.87
  569.4 1.1 dynamic-slice_bitcast_fusion.2
  570.4 2.4 collective-permute-start.10
  572.8 7.9 %collective-permute-start.11 = (f32[6,128,128]{2,1,0:T(8,128)}, f32[6,128,128]{2,1,0:T(8,128)}, u32[]{:S(2)}, u32[]{:S(2)}) collective-permute-start(f32[6,128,128]{2,1,0:T(8,128)} %get-tuple-element.71), channel_id=1, source_target_pairs={{2,0},{3,1},{4,2},{5,3},{6,4},{7,5},{0,6},{1,7},{10,8},{11,9},{12,... | collective-permute-start | bytes 1179656 | tf_op jit(solution)/shard_map/ppermute | solution.py:10
  580.8 0.6 collective-permute-start.9
  581.3 0.1 fusion.31
  581.5 0.8 copy.10
  582.3 6.5 %collective-permute-done.10 = f32[6,128,128]{2,1,0:T(8,128)} collective-permute-done((f32[6,128,128]{2,1,0:T(8,128)}, f32[6,128,128]{2,1,0:T(8,128)}, u32[]{:S(2)}, u32[]{:S(2)}) %collective-permute-start.10) | collective-permute-done | bytes 393248 | tf_op jit(solution)/shard_map/ppermute | solution.py:10
  588.7 2.0 collective-permute-done.11
  590.7 15.4 %collective-permute-done.9 = f32[6,128,128]{2,1,0:T(8,128)} collective-permute-done((f32[6,128,128]{2,1,0:T(8,128)}, f32[6,128,128]{2,1,0:T(8,128)}, u32[]{:S(2)}, u32[]{:S(2)}) %collective-permute-start.9) | collective-permute-done | bytes 393248 | tf_op jit(solution)/shard_map/ppermute | solution.py:10
  606.1 2.1 fusion.19
  (35 shorter events, 0.3 us)
Async XLA Ops:
  7.2 78.0 %all-reduce.9.cloned.1.call-start = ((), (), s32[]{:S(2)}) async-start(), calls=%async_computation | async-start | bytes 524288 | tf_op jit(solution)/shard_map/psum | solution.py:57
  8.1 0.7 copy-start.5
  8.9 111.0 %all-reduce.11.cloned.1.call-start = ((), (), s32[]{:S(2)}) async-start(), calls=%async_computation.1 | async-start | bytes 524288 | tf_op jit(solution)/shard_map/psum | solution.py:15
  88.5 145.6 %all-reduce.13.cloned.1.call-start = ((), (), s32[]{:S(2)}) async-start(), calls=%async_computation.2 | async-start | bytes 524288 | tf_op jit(solution)/shard_map/psum | solution.py:57
  127.0 29.3 %copy-start.8 = (f32[6,1,1,128,128]{4,3,2,1,0:T(8,128)S(1)}, f32[6,1,1,128,128]{4,3,2,1,0:T(8,128)}, u32[]{:S(2)}) copy-start(f32[6,1,1,128,128]{4,3,2,1,0:T(8,128)} %param.12) | copy-start | bytes 1179652
  127.9 14.1 %collective-permute-start = (f32[6,128,128]{2,1,0:T(8,128)}, f32[6,128,128]{2,1,0:T(8,128)S(1)}, u32[]{:S(2)}, u32[]{:S(2)}) collective-permute-start(f32[6,128,128]{2,1,0:T(8,128)} %get-tuple-element.79), channel_id=1, source_target_pairs={{6,0},{7,1},{0,2},{1,3},{2,4},{3,5},{4,6},{5,7},{14,8},{15,9},{8,1... | collective-permute-start | bytes 1179656 | tf_op jit(solution)/shard_map/ppermute | solution.py:10
  127.9 28.4 %collective-permute-start.1 = (f32[6,128,128]{2,1,0:T(8,128)S(1)}, f32[6,128,128]{2,1,0:T(8,128)S(1)}, u32[]{:S(2)}, u32[]{:S(2)}) collective-permute-start(f32[6,128,128]{2,1,0:T(8,128)S(1)} %get-tuple-element.81), channel_id=1, source_target_pairs={{4,0},{5,1},{6,2},{7,3},{0,4},{1,5},{2,6},{3,7},{12,8},{13,9},{14,... | collective-permute-start | bytes 1179656 | tf_op jit(solution)/shard_map/ppermute | solution.py:10
  127.9 28.4 %collective-permute-start.2 = (f32[6,128,128]{2,1,0:T(8,128)S(1)}, f32[6,128,128]{2,1,0:T(8,128)}, u32[]{:S(2)}, u32[]{:S(2)}) collective-permute-start(f32[6,128,128]{2,1,0:T(8,128)S(1)} %get-tuple-element.80), channel_id=1, source_target_pairs={{2,0},{3,1},{4,2},{5,3},{6,4},{7,5},{0,6},{1,7},{10,8},{11,9},{12,... | collective-permute-start | bytes 1179656 | tf_op jit(solution)/shard_map/ppermute | solution.py:10
  157.5 0.7 copy-start.6
  158.2 110.5 %all-reduce.15.cloned.1.call-start = ((), (), s32[]{:S(2)}) async-start(), calls=%async_computation.3 | async-start | bytes 524288 | tf_op jit(solution)/shard_map/psum | solution.py:15
  237.3 146.3 %all-reduce.17.cloned.1.call-start = ((), (), s32[]{:S(2)}) async-start(), calls=%async_computation.4 | async-start | bytes 524288 | tf_op jit(solution)/shard_map/psum | solution.py:57
  269.8 18.4 %collective-permute-start.3 = (f32[6,128,128]{2,1,0:T(8,128)}, f32[6,128,128]{2,1,0:T(8,128)S(1)}, u32[]{:S(2)}, u32[]{:S(2)}) collective-permute-start(f32[6,128,128]{2,1,0:T(8,128)} %get-tuple-element.76), channel_id=1, source_target_pairs={{6,0},{7,1},{0,2},{1,3},{2,4},{3,5},{4,6},{5,7},{14,8},{15,9},{8,1... | collective-permute-start | bytes 1179656 | tf_op jit(solution)/shard_map/ppermute | solution.py:10
  278.3 20.0 %collective-permute-start.4 = (f32[6,128,128]{2,1,0:T(8,128)S(1)}, f32[6,128,128]{2,1,0:T(8,128)S(1)}, u32[]{:S(2)}, u32[]{:S(2)}) collective-permute-start(f32[6,128,128]{2,1,0:T(8,128)S(1)} %get-tuple-element.78), channel_id=1, source_target_pairs={{4,0},{5,1},{6,2},{7,3},{0,4},{1,5},{2,6},{3,7},{12,8},{13,9},{14,... | collective-permute-start | bytes 1179656 | tf_op jit(solution)/shard_map/ppermute | solution.py:10
  278.3 24.4 %collective-permute-start.5 = (f32[6,128,128]{2,1,0:T(8,128)S(1)}, f32[6,128,128]{2,1,0:T(8,128)}, u32[]{:S(2)}, u32[]{:S(2)}) collective-permute-start(f32[6,128,128]{2,1,0:T(8,128)S(1)} %get-tuple-element.77), channel_id=1, source_target_pairs={{2,0},{3,1},{4,2},{5,3},{6,4},{7,5},{0,6},{1,7},{10,8},{11,9},{12,... | collective-permute-start | bytes 1179656 | tf_op jit(solution)/shard_map/ppermute | solution.py:10
  303.8 0.7 copy-start.7
  304.5 113.9 %all-reduce.19.cloned.1.call-start = ((), (), s32[]{:S(2)}) async-start(), calls=%async_computation.5 | async-start | bytes 524288 | tf_op jit(solution)/shard_map/psum | solution.py:15
  387.0 147.5 %all-reduce.21.cloned.1.call-start = ((), (), s32[]{:S(2)}) async-start(), calls=%async_computation.6 | async-start | bytes 524288 | tf_op jit(solution)/shard_map/psum | solution.py:57
  419.6 12.2 %collective-permute-start.6 = (f32[6,128,128]{2,1,0:T(8,128)}, f32[6,128,128]{2,1,0:T(8,128)S(1)}, u32[]{:S(2)}, u32[]{:S(2)}) collective-permute-start(f32[6,128,128]{2,1,0:T(8,128)} %get-tuple-element.73), channel_id=1, source_target_pairs={{6,0},{7,1},{0,2},{1,3},{2,4},{3,5},{4,6},{5,7},{14,8},{15,9},{8,1... | collective-permute-start | bytes 1179656 | tf_op jit(solution)/shard_map/ppermute | solution.py:10
  421.1 27.0 %collective-permute-start.7 = (f32[6,128,128]{2,1,0:T(8,128)S(1)}, f32[6,128,128]{2,1,0:T(8,128)S(1)}, u32[]{:S(2)}, u32[]{:S(2)}) collective-permute-start(f32[6,128,128]{2,1,0:T(8,128)S(1)} %get-tuple-element.75), channel_id=1, source_target_pairs={{4,0},{5,1},{6,2},{7,3},{0,4},{1,5},{2,6},{3,7},{12,8},{13,9},{14,... | collective-permute-start | bytes 1179656 | tf_op jit(solution)/shard_map/ppermute | solution.py:10
  428.8 19.2 %collective-permute-start.8 = (f32[6,128,128]{2,1,0:T(8,128)S(1)}, f32[6,128,128]{2,1,0:T(8,128)}, u32[]{:S(2)}, u32[]{:S(2)}) collective-permute-start(f32[6,128,128]{2,1,0:T(8,128)S(1)} %get-tuple-element.74), channel_id=1, source_target_pairs={{2,0},{3,1},{4,2},{5,3},{6,4},{7,5},{0,6},{1,7},{10,8},{11,9},{12,... | collective-permute-start | bytes 1179656 | tf_op jit(solution)/shard_map/ppermute | solution.py:10
  449.2 0.7 copy-start.4
  449.9 119.2 %all-reduce.23.cloned.1.call-start = ((), (), s32[]{:S(2)}) async-start(), calls=%async_computation.7 | async-start | bytes 524288 | tf_op jit(solution)/shard_map/psum | solution.py:15
  569.3 12.0 %copy-start = (f32[512,128]{0,1:T(8,128)S(1)}, f32[512,128]{0,1:T(8,128)}, u32[]{:S(2)}) copy-start(f32[512,128]{0,1:T(8,128)} %all-reduce.11.cloned.1.call-done) | copy-start | bytes 786436
  569.3 12.0 %copy-start.1 = (f32[512,128]{0,1:T(8,128)S(1)}, f32[512,128]{0,1:T(8,128)}, u32[]{:S(2)}) copy-start(f32[512,128]{0,1:T(8,128)} %all-reduce.15.cloned.1.call-done) | copy-start | bytes 786436
  569.4 12.0 %copy-start.2 = (f32[512,128]{0,1:T(8,128)S(1)}, f32[512,128]{0,1:T(8,128)}, u32[]{:S(2)}) copy-start(f32[512,128]{0,1:T(8,128)} %all-reduce.19.cloned.1.call-done) | copy-start | bytes 786436
  569.4 12.0 %copy-start.3 = (f32[512,128]{0,1:T(8,128)S(1)}, f32[512,128]{0,1:T(8,128)}, u32[]{:S(2)}) copy-start(f32[512,128]{0,1:T(8,128)} %all-reduce.23.cloned.1.call-done) | copy-start | bytes 786436
  570.4 18.3 %collective-permute-start.10 = (f32[6,128,128]{2,1,0:T(8,128)}, f32[6,128,128]{2,1,0:T(8,128)}, u32[]{:S(2)}, u32[]{:S(2)}) collective-permute-start(f32[6,128,128]{2,1,0:T(8,128)} %get-tuple-element.72), channel_id=1, source_target_pairs={{4,0},{5,1},{6,2},{7,3},{0,4},{1,5},{2,6},{3,7},{12,8},{13,9},{14,... | collective-permute-start | bytes 1179656 | tf_op jit(solution)/shard_map/ppermute | solution.py:10
  572.8 17.9 %collective-permute-start.11 = (f32[6,128,128]{2,1,0:T(8,128)}, f32[6,128,128]{2,1,0:T(8,128)}, u32[]{:S(2)}, u32[]{:S(2)}) collective-permute-start(f32[6,128,128]{2,1,0:T(8,128)} %get-tuple-element.71), channel_id=1, source_target_pairs={{2,0},{3,1},{4,2},{5,3},{6,4},{7,5},{0,6},{1,7},{10,8},{11,9},{12,... | collective-permute-start | bytes 1179656 | tf_op jit(solution)/shard_map/ppermute | solution.py:10
  580.8 25.3 %collective-permute-start.9 = (f32[6,128,128]{2,1,0:T(8,128)}, f32[6,128,128]{2,1,0:T(8,128)}, u32[]{:S(2)}, u32[]{:S(2)}) collective-permute-start(f32[6,128,128]{2,1,0:T(8,128)} %get-tuple-element.70), channel_id=1, source_target_pairs={{6,0},{7,1},{0,2},{1,3},{2,4},{3,5},{4,6},{5,7},{14,8},{15,9},{8,1... | collective-permute-start | bytes 1179656 | tf_op jit(solution)/shard_map/ppermute | solution.py:10
Sparse Core Ops, SparseCore 0:
  11.9 73.2 all-reduce.8
  88.6 31.2 all-reduce.10
  158.3 75.6 all-reduce.12
  237.5 31.2 all-reduce.14
  304.6 79.0 all-reduce.16
  387.1 31.2 all-reduce.18
  450.1 84.3 all-reduce.20
  537.9 31.2 all-reduce.22
where the time goes:
time: 615 us
  waiting for transfers between devices  521 us (85%)
  starting transfers between devices  38 us (6%)
  matrix products  20.2 us (3%)
  between operations  14.4 us (2%)
  local copies, waits for them, and re-layouts  14.3 us (2%)
  other arithmetic  6.4 us (1%)
    psum x4, waiting for transfers between devices, on_device(): complete = lax.psum(contrib, 'col')  309 us
    psum x4, waiting for transfers between devices, broadcast(): return lax.psum(jnp.where(mine, x, jnp.zeros_like(x)), axis)  125 us
    ppermute x12, waiting for transfers between devices, shifted(): return lax.ppermute(block, axis, route)  86.7 us
    ppermute x12, starting transfers between devices, shifted(): return lax.ppermute(block, axis, route)  37.7 us
    dot_general x4, matrix products, on_device(): jnp.dot(inverses[k], complete, precision=lax.Precision.HIGHEST)  13.1 us
  transfers between devices with their start and end apart: 20, of which 17 were waited for; matrix products, arithmetic and copies ran while one was open for 1% of the time, Pallas kernels for 0%

commit v1 on v0

v1 whole, which is shorter than its diff:
```python
import jax
import jax.numpy as jnp
from jax import lax
from jax.sharding import PartitionSpec as P

HIGH = lax.Precision.HIGH
AXES = ("row", "col")


def times(block, x):
    return lax.dot_general(block, x, (((0,), (0,)), ((), ())), precision=HIGH)


def on_device(factor, rhs, inverses):
    steps = inverses.shape[0]
    blocks = factor.shape[0]
    width = factor.shape[3]
    quarter = rhs.shape[3]
    nrhs = rhs.shape[4]
    row_count = lax.axis_size("row")
    col_count = lax.axis_size("col")
    groups = col_count // steps
    row_pos = lax.axis_index("row")
    col_pos = lax.axis_index("col")
    member = col_pos // groups
    group = col_pos % groups
    share = width // col_count

    def dev(row, mem, grp):
        return row * col_count + mem * groups + grp

    def line(g, mem):
        return dev(g // groups, mem, g % groups)

    def home(k):
        return line(k, k)

    def send(x, pairs):
        return lax.ppermute(x, AXES, pairs)

    def spread(x, planes):
        todo = {}
        have = {}
        for k in planes:
            row, grp = k // groups, k % groups
            twin = row ^ 1
            have[k] = [(row, grp)]
            rows = [r for r in range(row_count) if r % 2 == row % 2]
            todo[k] = [(r, g) for r in rows for g in range(groups) if (r, g) != (row, grp)]
        while any(todo.values()):
            rounds = [[] for _ in range(3)]
            for k in planes:
                fresh = []
                for src in have[k]:
                    for slot in range(3):
                        if todo[k]:
                            dst = todo[k].pop(0)
                            fresh.append(dst)
                            rounds[slot].append((dev(src[0], k, src[1]), dev(dst[0], k, dst[1])))
                have[k] += fresh
            got = x
            for pairs in rounds:
                if pairs:
                    me = row_pos * col_count + col_pos
                    here = jnp.zeros((), bool)
                    for _, d in pairs:
                        here = here | (me == d)
                    got = jnp.where(here, send(x, pairs), got)
            x = got
        pairs = [(dev(r, k, g), dev(r ^ 1, k, g)) for k in planes for r, g in have[k]]
        other = send(x, pairs)
        me = row_pos * col_count + col_pos
        here = jnp.zeros((), bool)
        for _, d in pairs:
            here = here | (me == d)
        return jnp.where(here, other, x)

    panel = factor[:, 0, 0]
    mine = rhs[0, 0, 0]
    low = member < 2

    lx = send(panel[0], [(line(2, 0), home(0)), (line(2, 1), home(1))])
    ly = send(panel[0], [(line(3, 0), home(0)), (line(3, 1), home(1))])
    la = send(panel[0], [(line(1, 0), home(1)), (line(3, 2), home(3))])

    whole = jnp.zeros((steps, quarter, nrhs), jnp.float32)
    whole = lax.dynamic_update_index_in_dim(whole, mine, member, 0)
    needs = {0: (0, 1), 1: (1,), 2: (2, 3), 3: (3,)}
    for offset in range(1, steps):
        pairs = [
            (line(g, (m - offset) % steps), line(g, m)) for g in needs for m in needs[g]
        ]
        piece = send(mine, pairs)
        whole = lax.dynamic_update_index_in_dim(whole, piece, (member - offset) % steps, 0)
    own = whole.reshape(width, nrhs)
    lent = send(own, [(line(0, 1), home(1)), (line(2, 3), home(3))])
    first = jnp.where(member % 2 == 1, lent, own)

    s_a = jnp.dot(inverses[0], first, precision=HIGH)
    s_b = jnp.dot(inverses[1], own - times(la, s_a), precision=HIGH)
    s_low = jnp.where(member == 0, s_a, s_b)
    w = jnp.stack([times(lx, s_low), times(ly, s_low)])
    w_a = send(w, [(home(0), home(3)), (home(1), home(2))])
    w_b = send(w, [(home(1), home(3)), (home(0), home(2))])

    w_sum = w_a + w_b
    s_c = jnp.dot(inverses[2], first - w_sum[0], precision=HIGH)
    s_d = jnp.dot(inverses[3], own - w_sum[1] - times(la, s_c), precision=HIGH)
    s_high = jnp.where(member == 2, s_c, s_d)

    block_ids = (jnp.arange(blocks, dtype=jnp.int32) * row_count + row_pos) * groups + group
    keep = (block_ids > member).astype(jnp.float32)[:, None, None]

    def update(s):
        full = jnp.einsum("rji,jh->rih", panel, s, precision=HIGH) * keep
        return full.reshape(blocks, steps, quarter, nrhs)

    def part_of(s, full, to):
        piece = lax.dynamic_index_in_dim(full, to, 1, keepdims=False)
        rows = lax.dynamic_slice_in_dim(s, (to * groups + group) * share, share, 0)
        return jnp.concatenate([piece.reshape(blocks * quarter, nrhs), rows])

    def exchange(s, full, sources):
        out = []
        for offset in range(1, steps):
            part = part_of(s, full, (member + offset) % steps)
            pairs = [
                (dev(r, m, g), dev(r, (m + offset) % steps, g))
                for m in sources for r in range(row_count) for g in range(groups)
            ]
            out.append(send(part, pairs))
        return out

    s_low = spread(s_low, (0, 1))
    full_low = update(s_low)
    got_low = exchange(s_low, full_low, (0, 1))
    s_high = spread(s_high, (2, 3))
    full_high = update(s_high)
    got_high = exchange(s_high, full_high, (2, 3))

    here = jnp.where(low, part_of(s_low, full_low, member), part_of(s_high, full_high, member))
    total = here[: blocks * quarter]
    solved = jnp.zeros((steps, share, nrhs), jnp.float32)
    solved = lax.dynamic_update_index_in_dim(solved, here[blocks * quarter:], member, 0)
    for offset in range(1, steps):
        source = (member - offset) % steps
        got = jnp.where(source < 2, got_low[offset - 1], got_high[offset - 1])
        total = total + got[: blocks * quarter]
        solved = lax.dynamic_update_index_in_dim(solved, got[blocks * quarter:], source, 0)
    remaining = rhs[:, 0, 0] - total.reshape(blocks, quarter, nrhs)
    return solved, remaining[:, None, None]


def solution(mesh):
    in_specs = (P(None, "row", "col", None, None), P(None, "row", "col", None, None), P())
    out_specs = (P(None, "col", None), P(None, "row", "col", None, None))
    return jax.shard_map(
        on_device, mesh=mesh, in_specs=in_specs, out_specs=out_specs, check_vma=False
    )
```

time: 615 us -> 154 us (0.25)
  the two profiles are of different devices: /device:TPU:0 before, /device:TPU:15 now
where the time goes in v1:
time: 154 us; the launch traced here: 153 us
  waiting for transfers between devices  55.2 us (36%)
  starting transfers between devices  39.7 us (26%)
  local copies, waits for them, and re-layouts  27.2 us (18%)
  matrix products  19.7 us (13%)
  other arithmetic  9.72 us (6%)
  between operations  1.61 us (1%)
    ppermute x23, waiting for transfers between devices, send(): return lax.ppermute(x, AXES, pairs)  55.2 us
    ppermute x23, starting transfers between devices, send(): return lax.ppermute(x, AXES, pairs)  39.7 us
    dynamic_slice x10, local copies, waits for them, and re-layouts, part_of(): piece = lax.dynamic_index_in_dim(full, to, 1, keepdims=False)  9.49 us
    dot_general x2, matrix products, update(): full = jnp.einsum('rji,jh->rih', panel, s, precision=HIGH) * keep  9.31 us
    dynamic_slice x9, local copies, waits for them, and re-layouts, part_of(): rows = lax.dynamic_slice_in_dim(s, (to * groups + group) * share, share, 0)  6.41 us
    dynamic_update_slice x3, local copies, waits for them, and re-layouts, on_device(): lax.dynamic_update_index_in_dim(whole, piece, (member - offset) % steps, 0)  4.44 us
    concatenate x6, other arithmetic, part_of(): return jnp.concatenate([piece.reshape(blocks * quarter, nrhs), rows])  4.02 us
  transfers between devices with their start and end apart: 23, of which 5 were waited for; matrix products, arithmetic and copies ran while one was open for 25% of the time, Pallas kernels for 0%

profile of v1, /device:TPU:15, one launch (start us, length us, event | category | flops | bytes accessed | tf_op | source)
XLA Modules:
  0.0 153.2 jit_solution(13493053364718922275)
XLA Ops:
  0.6 2.3 %slice_bitcast_fusion = f32[512,512]{1,0:T(8,128)} fusion(f32[6,1,1,512,512]{4,3,2,1,0:T(8,128)} %param.3), kind=kLoop, calls=%fused_computation.23 | loop fusion | bytes 2097152 | tf_op jit(solution)/shard_map/squeeze | solution.py:84
  2.9 0.7 collective-permute-start.4
  3.6 0.9 slice_bitcast_fusion.3
  4.5 0.7 collective-permute-start.2
  5.2 0.7 collective-permute-start.1
  5.8 0.7 collective-permute-start
  6.7 1.5 dynamic_update_slice.26
  8.6 1.5 dynamic_update_slice.27
  10.0 1.5 dynamic_update_slice.28
  11.5 1.5 dynamic_update_slice.29
  13.0 0.7 collective-permute-start.3
  13.7 1.6 %collective-permute-start.10 = (f32[512,512]{1,0:T(8,128)}, f32[512,512]{1,0:T(8,128)}, u32[]{:S(2)}, u32[]{:S(2)}) collective-permute-start(f32[512,512]{1,0:T(8,128)} %slice_bitcast_fusion), channel_id=1, source_target_pairs={{9,0},{11,3}} | collective-permute-start | bytes 3145736 | tf_op jit(solution)/shard_map/ppermute | solution.py:39
  15.4 0.7 collective-permute-start.9
  16.1 1.9 %fusion.14 = f32[128,512]{1,0:T(8,128)S(1)} fusion(f32[4,512,512]{2,1,0:T(8,128)} %param.5, f32[512,128]{0,1:T(8,128)S(1)} %collective-permute-done.3, pred[]{:T(512)S(6)} %eq.119, f32[16,8,4,128]{3,2,1,0:T(4,128)S(1)} %bitcast.126), kind=kOutput, calls=%fused_computation.18 | convolution fusion | flops 201392128 | bytes 1835009 | tf_op jit(solution)/shard_map/dot_general | solution.py:99
  18.4 1.9 %convolution_select_fusion.1 = f32[128,512]{1,0:T(8,128)S(1)} fusion(f32[128,512]{1,0:T(8,128)S(1)} %fusion.14, f32[512,128]{0,1:T(8,128)S(1)} %fusion.8, f32[4,512,512]{2,1,0:T(8,128)} %param.5, pred[]{:T(512)S(6)} %eq.118), kind=kOutput, calls=%fused_computation.13 | convolution fusion | flops 201392128 | bytes 1835009 | tf_op jit(solution)/shard_map/dot_general | solution.py:100
  20.4 1.6 %convolution_bitcast_fusion.1 = f32[1,512,128]{1,2,0:T(8,128)S(1)} fusion(f32[128,512]{1,0:T(8,128)S(1)} %convolution_select_fusion.1, f32[512,512]{1,0:T(8,128)} %collective-permute-done.10), kind=kOutput, calls=%fused_computation.7 | convolution fusion | flops 201326592 | bytes 1572864 | tf_op jit(solution)/shard_map/dot_general | solution.py:11
  22.4 0.8 pad_maximum_fusion
  23.3 0.7 collective-permute-start.12
  24.0 0.7 collective-permute-start.11
  24.7 0.7 collective-permute-start.7
  25.4 0.7 collective-permute-start.6
  26.0 1.4 collective-permute-start.5
  27.4 0.7 copy-done.3
  28.2 1.3 collective-permute-start.8
  29.6 1.9 %fusion.11 = f32[128,512]{1,0:T(8,128)S(1)} fusion(f32[4,512,512]{2,1,0:T(8,128)} %param.5, f32[2,512,128]{1,2,0:T(8,128)S(1)} %add.170, f32[512,128]{0,1:T(8,128)S(1)} %collective-permute-done.3, pred[]{:T(512)S(6)} %eq.119, f32[16,8,4,128]{3,2,1,0:T(4,128)S(1)} %bitcast.128), kind=kOutput, calls=%fused_computation.15 | convolution fusion | flops 201457664 | bytes 2097153 | tf_op jit(solution)/shard_map/dot_general | solution.py:107
  32.0 1.9 %fusion.9 = f32[512,128]{0,1:T(8,128)S(1)} fusion(f32[128,512]{1,0:T(8,128)S(1)} %fusion.11, f32[4,512,512]{2,1,0:T(8,128)} %param.5, f32[512,128]{0,1:T(8,128)S(1)} %convolution_bitcast_fusion, f32[2,512,128]{1,2,0:T(8,128)S(1)} %add.170, pred[]{:T(512)S(6)} %eq.134, f32[16,8,4,128]{3,2,1,0:T(4,128)S(1)} %bitcast.129), kind=kOutput, calls=%fused_computation.12 | convolution fusion | flops 201523200 | bytes 2359297 | tf_op jit(solution)/shard_map/dot_general | solution.py:108
  33.9 0.7 collective-permute-start.15
  34.5 0.7 collective-permute-start.14
  35.2 0.7 collective-permute-start.13
  36.1 27.5 %collective-permute-done.8 = f32[512,128]{0,1:T(8,128)S(1)} collective-permute-done((f32[512,128]{0,1:T(8,128)S(1)}, f32[512,128]{0,1:T(8,128)S(1)}, u32[]{:S(2)}, u32[]{:S(2)}) %collective-permute-start.8) | collective-permute-done | bytes 262176 | tf_op jit(solution)/shard_map/ppermute | solution.py:39
  63.7 0.8 select_select_fusion
  64.5 1.4 collective-permute-start.16
  65.8 4.7 %multiply_bitcast_fusion.1 = f32[6,512,128]{1,2,0:T(8,128)S(1)} fusion(f32[6,1,1,512,512]{4,3,2,1,0:T(8,128)} %param.3, f32[6]{0:T(128)S(1)} %compare_convert_fusion, f32[512,128]{0,1:T(8,128)S(1)} %broadcast_select_fusion.5), kind=kOutput, calls=%fused_computation.5 | convolution fusion | flops 1208352768 | bytes 8126488 | tf_op jit(solution)/shard_map/rji,jh->rih/dot_general | solution.py:115
  70.5 0.5 reshape.62
  71.1 1.7 %constant_dynamic-slice_fusion.3 = (f32[6,1,128,128]{2,1,3,0:T(1,128)S(1)}, f32[6,1,128,128]{2,1,3,0:T(1,128)S(1)}, f32[6,1,128,128]{2,1,3,0:T(1,128)S(1)}, f32[6,1,128,128]{2,1,3,0:T(1,128)S(1)}) fusion(f32[6,4,128,128]{2,1,3,0:T(4,128)S(1)} %reshape.62, s32[]{:T(128)S(6)} %select_n.249, s32[]{:T(128)S(6)} %select_n.244, s32[]{:T(128)S(6)} %select_n.239, ...), kind=kLoop, calls=%fused_computation.65 | loop fusion | bytes 3145744 | tf_op jit(solution)/shard_map/jit(dynamic_index_in_dim)/dynamic_slice | solution.py:119
  73.8 1.0 copy.9
  74.8 1.0 broadcast_select_fusion.3
  75.8 4.7 %multiply_bitcast_fusion = f32[6,512,128]{1,2,0:T(8,128)S(1)} fusion(f32[6,1,1,512,512]{4,3,2,1,0:T(8,128)} %param.3, f32[6]{0:T(128)S(1)} %compare_convert_fusion, f32[512,128]{0,1:T(8,128)S(1)} %broadcast_select_fusion.3), kind=kOutput, calls=%fused_computation.4 | convolution fusion | flops 1208352768 | bytes 8126488 | tf_op jit(solution)/shard_map/rji,jh->rih/dot_general | solution.py:115
  80.5 0.9 constant_dynamic-slice_fusion
  81.4 1.5 copy.20
  82.9 1.5 copy.16
  84.4 1.5 copy.12
  85.9 0.7 copy.10
  86.8 0.8 pad_maximum_fusion.1
  87.6 16.0 %collective-permute-start.17 = (f32[832,128]{1,0:T(8,128)}, f32[832,128]{1,0:T(8,128)}, u32[]{:S(2)}, u32[]{:S(2)}) collective-permute-start(f32[832,128]{1,0:T(8,128)} %pad_maximum_fusion.1), channel_id=1, source_target_pairs={{0,2},{1,3},{8,10},{9,11},{16,18},{17,19},{24,26},{25,27},{2,4},{3... | collective-permute-start | bytes 1277960 | tf_op jit(solution)/shard_map/ppermute | solution.py:39
  103.6 0.8 pad_maximum_fusion.3
  104.5 2.0 %collective-permute-start.19 = (f32[832,128]{1,0:T(8,128)}, f32[832,128]{1,0:T(8,128)}, u32[]{:S(2)}, u32[]{:S(2)}) collective-permute-start(f32[832,128]{1,0:T(8,128)} %pad_maximum_fusion.3), channel_id=1, source_target_pairs={{0,4},{1,5},{8,12},{9,13},{16,20},{17,21},{24,28},{25,29},{2,6},{3... | collective-permute-start | bytes 1277960 | tf_op jit(solution)/shard_map/ppermute | solution.py:39
  106.5 0.8 pad_maximum_fusion.5
  107.3 3.9 %collective-permute-start.21 = (f32[832,128]{1,0:T(8,128)}, f32[832,128]{1,0:T(8,128)}, u32[]{:S(2)}, u32[]{:S(2)}) collective-permute-start(f32[832,128]{1,0:T(8,128)} %pad_maximum_fusion.5), channel_id=1, source_target_pairs={{0,6},{1,7},{8,14},{9,15},{16,22},{17,23},{24,30},{25,31},{2,0},{3... | collective-permute-start | bytes 1277960 | tf_op jit(solution)/shard_map/ppermute | solution.py:39
  111.7 2.6 %constant_dynamic-slice_fusion.1 = (f32[6,1,128,128]{2,1,3,0:T(1,128)S(1)}, f32[6,1,128,128]{2,1,3,0:T(1,128)}, f32[6,1,128,128]{2,1,3,0:T(1,128)S(1)}, f32[6,1,128,128]{2,1,3,0:T(1,128)}) fusion(f32[6,4,128,128]{2,1,3,0:T(4,128)S(1)} %reshape.64, s32[]{:T(128)S(6)} %select_n.249, s32[]{:T(128)S(6)} %select_n.244, s32[]{:T(128)S(6)} %select_n.239, ...), kind=kLoop, calls=%fused_computation.63 | loop fusion | bytes 3145744 | tf_op jit(solution)/shard_map/jit(dynamic_index_in_dim)/dynamic_slice | solution.py:119
  114.3 1.2 copy.19
  115.9 1.2 copy.11
  117.1 0.8 pad_maximum_fusion.2
  117.9 0.7 collective-permute-start.18
  118.6 0.8 pad_maximum_fusion.4
  119.4 1.3 collective-permute-start.20
  120.7 0.8 maximum_select_fusion
  122.1 7.0 %collective-permute-done.17 = f32[832,128]{1,0:T(8,128)} collective-permute-done((f32[832,128]{1,0:T(8,128)}, f32[832,128]{1,0:T(8,128)}, u32[]{:S(2)}, u32[]{:S(2)}) %collective-permute-start.17) | collective-permute-done | bytes 426016 | tf_op jit(solution)/shard_map/ppermute | solution.py:39
  129.1 1.3 collective-permute-start.22
  130.4 1.1 broadcast_select_fusion.2
  131.4 2.2 %collective-permute-done.19 = f32[832,128]{1,0:T(8,128)} collective-permute-done((f32[832,128]{1,0:T(8,128)}, f32[832,128]{1,0:T(8,128)}, u32[]{:S(2)}, u32[]{:S(2)}) %collective-permute-start.19) | collective-permute-done | bytes 426016 | tf_op jit(solution)/shard_map/ppermute | solution.py:39
  133.6 4.7 %collective-permute-done.20 = f32[832,128]{1,0:T(8,128)S(1)} collective-permute-done((f32[832,128]{1,0:T(8,128)S(1)}, f32[832,128]{1,0:T(8,128)S(1)}, u32[]{:S(2)}, u32[]{:S(2)}) %collective-permute-start.20) | collective-permute-done | bytes 426016 | tf_op jit(solution)/shard_map/ppermute | solution.py:39
  138.4 13.7 %collective-permute-done.22 = f32[832,128]{1,0:T(8,128)S(1)} collective-permute-done((f32[832,128]{1,0:T(8,128)S(1)}, f32[832,128]{1,0:T(8,128)S(1)}, u32[]{:S(2)}, u32[]{:S(2)}) %collective-permute-start.22) | collective-permute-done | bytes 426016 | tf_op jit(solution)/shard_map/ppermute | solution.py:39
  152.4 0.8 sub.40
  (59 shorter events, 4.7 us)
Async XLA Ops:
  2.9 15.1 %collective-permute-start.4 = (f32[512,512]{1,0:T(8,128)}, f32[512,512]{1,0:T(8,128)S(1)}, u32[]{:S(2)}, u32[]{:S(2)}) collective-permute-start(f32[512,512]{1,0:T(8,128)} %slice_bitcast_fusion), channel_id=1, source_target_pairs={{1,3},{13,15}} | collective-permute-start | bytes 3145736 | tf_op jit(solution)/shard_map/ppermute | solution.py:39
  4.5 3.7 %collective-permute-start.2 = (f32[128,128]{1,0:T(8,128)S(1)}, f32[128,128]{1,0:T(8,128)S(1)}, u32[]{:S(2)}, u32[]{:S(2)}) collective-permute-start(f32[128,128]{1,0:T(8,128)S(1)} %get-tuple-element.10), channel_id=1, source_target_pairs={{2,0},{4,2},{5,3},{14,12},{8,14},{9,15}} | collective-permute-start | bytes 196616 | tf_op jit(solution)/shard_map/ppermute | solution.py:39
  5.2 3.2 %collective-permute-start.1 = (f32[128,128]{1,0:T(8,128)S(1)}, f32[128,128]{1,0:T(8,128)S(1)}, u32[]{:S(2)}, u32[]{:S(2)}) collective-permute-start(f32[128,128]{1,0:T(8,128)S(1)} %get-tuple-element.10), channel_id=1, source_target_pairs={{4,0},{6,2},{7,3},{8,12},{10,14},{11,15}} | collective-permute-start | bytes 196616 | tf_op jit(solution)/shard_map/ppermute | solution.py:39
  5.8 2.6 %collective-permute-start = (f32[128,128]{1,0:T(8,128)S(1)}, f32[128,128]{1,0:T(8,128)S(1)}, u32[]{:S(2)}, u32[]{:S(2)}) collective-permute-start(f32[128,128]{1,0:T(8,128)S(1)} %get-tuple-element.10), channel_id=1, source_target_pairs={{6,0},{0,2},{1,3},{10,12},{12,14},{13,15}} | collective-permute-start | bytes 196616 | tf_op jit(solution)/shard_map/ppermute | solution.py:39
  13.0 3.1 %collective-permute-start.3 = (f32[512,128]{0,1:T(8,128)S(1)}, f32[512,128]{0,1:T(8,128)S(1)}, u32[]{:S(2)}, u32[]{:S(2)}) collective-permute-start(f32[512,128]{0,1:T(8,128)S(1)} %bitcast.142), channel_id=1, source_target_pairs={{2,3},{14,15}} | collective-permute-start | bytes 786440 | tf_op jit(solution)/shard_map/ppermute | solution.py:39
  13.7 6.6 %collective-permute-start.10 = (f32[512,512]{1,0:T(8,128)}, f32[512,512]{1,0:T(8,128)}, u32[]{:S(2)}, u32[]{:S(2)}) collective-permute-start(f32[512,512]{1,0:T(8,128)} %slice_bitcast_fusion), channel_id=1, source_target_pairs={{9,0},{11,3}} | collective-permute-start | bytes 3145736 | tf_op jit(solution)/shard_map/ppermute | solution.py:39
  15.4 6.6 %collective-permute-start.9 = (f32[512,512]{1,0:T(8,128)}, f32[512,512]{1,0:T(8,128)S(1)}, u32[]{:S(2)}, u32[]{:S(2)}) collective-permute-start(f32[512,512]{1,0:T(8,128)} %slice_bitcast_fusion), channel_id=1, source_target_pairs={{8,0},{10,3}} | collective-permute-start | bytes 3145736 | tf_op jit(solution)/shard_map/ppermute | solution.py:39
  23.3 6.3 %collective-permute-start.12 = (f32[2,512,128]{1,2,0:T(8,128)}, f32[2,512,128]{1,2,0:T(8,128)S(1)}, u32[]{:S(2)}, u32[]{:S(2)}) collective-permute-start(f32[2,512,128]{1,2,0:T(8,128)} %pad_maximum_fusion), channel_id=1, source_target_pairs={{3,15},{0,12}} | collective-permute-start | bytes 1572872 | tf_op jit(solution)/shard_map/ppermute | solution.py:39
  24.0 5.6 %collective-permute-start.11 = (f32[2,512,128]{1,2,0:T(8,128)}, f32[2,512,128]{1,2,0:T(8,128)S(1)}, u32[]{:S(2)}, u32[]{:S(2)}) collective-permute-start(f32[2,512,128]{1,2,0:T(8,128)} %pad_maximum_fusion), channel_id=1, source_target_pairs={{0,15},{3,12}} | collective-permute-start | bytes 1572872 | tf_op jit(solution)/shard_map/ppermute | solution.py:39
  24.7 2.8 %collective-permute-start.7 = (f32[512,128]{0,1:T(8,128)S(1)}, f32[512,128]{0,1:T(8,128)S(1)}, u32[]{:S(2)}, u32[]{:S(2)}) collective-permute-start(f32[512,128]{0,1:T(8,128)S(1)} %bitcast.130), channel_id=1, source_target_pairs={{0,1},{3,2}} | collective-permute-start | bytes 786440 | tf_op jit(solution)/shard_map/ppermute | solution.py:39
  25.4 2.1 %collective-permute-start.6 = (f32[512,128]{0,1:T(8,128)S(1)}, f32[512,128]{0,1:T(8,128)S(1)}, u32[]{:S(2)}, u32[]{:S(2)}) collective-permute-start(f32[512,128]{0,1:T(8,128)S(1)} %bitcast.131), channel_id=1, source_target_pairs={{0,16},{3,18}} | collective-permute-start | bytes 786440 | tf_op jit(solution)/shard_map/ppermute | solution.py:39
  26.0 2.1 %collective-permute-start.5 = (f32[512,128]{0,1:T(8,128)S(1)}, f32[512,128]{0,1:T(8,128)}, u32[]{:S(2)}, u32[]{:S(2)}) collective-permute-start(f32[512,128]{0,1:T(8,128)S(1)} %bitcast.132), channel_id=1, source_target_pairs={{0,17},{3,19}} | collective-permute-start | bytes 786440 | tf_op jit(solution)/shard_map/ppermute | solution.py:39
  27.4 0.7 copy-start.3
  28.2 35.4 %collective-permute-start.8 = (f32[512,128]{0,1:T(8,128)S(1)}, f32[512,128]{0,1:T(8,128)S(1)}, u32[]{:S(2)}, u32[]{:S(2)}) collective-permute-start(f32[512,128]{0,1:T(8,128)S(1)} %select_select_fusion.1), channel_id=1, source_target_pairs={{0,8},{1,9},{16,24},{17,25},{3,11},{2,10},{18,26},{19,27}} | collective-permute-start | bytes 786440 | tf_op jit(solution)/shard_map/ppermute | solution.py:39
  33.9 29.8 %collective-permute-start.15 = (f32[512,128]{0,1:T(8,128)S(1)}, f32[512,128]{0,1:T(8,128)S(1)}, u32[]{:S(2)}, u32[]{:S(2)}) collective-permute-start(f32[512,128]{0,1:T(8,128)S(1)} %fusion.9), channel_id=1, source_target_pairs={{12,13},{15,14}} | collective-permute-start | bytes 786440 | tf_op jit(solution)/shard_map/ppermute | solution.py:39
  34.5 29.1 %collective-permute-start.14 = (f32[512,128]{0,1:T(8,128)S(1)}, f32[512,128]{0,1:T(8,128)S(1)}, u32[]{:S(2)}, u32[]{:S(2)}) collective-permute-start(f32[512,128]{0,1:T(8,128)S(1)} %fusion.9), channel_id=1, source_target_pairs={{12,28},{15,30}} | collective-permute-start | bytes 786440 | tf_op jit(solution)/shard_map/ppermute | solution.py:39
  35.2 28.4 %collective-permute-start.13 = (f32[512,128]{0,1:T(8,128)S(1)}, f32[512,128]{0,1:T(8,128)S(1)}, u32[]{:S(2)}, u32[]{:S(2)}) collective-permute-start(f32[512,128]{0,1:T(8,128)S(1)} %fusion.9), channel_id=1, source_target_pairs={{12,29},{15,31}} | collective-permute-start | bytes 786440 | tf_op jit(solution)/shard_map/ppermute | solution.py:39
  64.5 10.3 %collective-permute-start.16 = (f32[512,128]{0,1:T(8,128)}, f32[512,128]{0,1:T(8,128)}, u32[]{:S(2)}, u32[]{:S(2)}) collective-permute-start(f32[512,128]{0,1:T(8,128)} %select_select_fusion), channel_id=1, source_target_pairs={{12,4},{13,5},{28,20},{29,21},{15,7},{14,6},{30,22},{31,23}} | collective-permute-start | bytes 786440 | tf_op jit(solution)/shard_map/ppermute | solution.py:39
  87.6 41.4 %collective-permute-start.17 = (f32[832,128]{1,0:T(8,128)}, f32[832,128]{1,0:T(8,128)}, u32[]{:S(2)}, u32[]{:S(2)}) collective-permute-start(f32[832,128]{1,0:T(8,128)} %pad_maximum_fusion.1), channel_id=1, source_target_pairs={{0,2},{1,3},{8,10},{9,11},{16,18},{17,19},{24,26},{25,27},{2,4},{3... | collective-permute-start | bytes 1277960 | tf_op jit(solution)/shard_map/ppermute | solution.py:39
  104.5 29.2 %collective-permute-start.19 = (f32[832,128]{1,0:T(8,128)}, f32[832,128]{1,0:T(8,128)}, u32[]{:S(2)}, u32[]{:S(2)}) collective-permute-start(f32[832,128]{1,0:T(8,128)} %pad_maximum_fusion.3), channel_id=1, source_target_pairs={{0,4},{1,5},{8,12},{9,13},{16,20},{17,21},{24,28},{25,29},{2,6},{3... | collective-permute-start | bytes 1277960 | tf_op jit(solution)/shard_map/ppermute | solution.py:39
  107.3 31.1 %collective-permute-start.21 = (f32[832,128]{1,0:T(8,128)}, f32[832,128]{1,0:T(8,128)}, u32[]{:S(2)}, u32[]{:S(2)}) collective-permute-start(f32[832,128]{1,0:T(8,128)} %pad_maximum_fusion.5), channel_id=1, source_target_pairs={{0,6},{1,7},{8,14},{9,15},{16,22},{17,23},{24,30},{25,31},{2,0},{3... | collective-permute-start | bytes 1277960 | tf_op jit(solution)/shard_map/ppermute | solution.py:39
  111.7 9.0 %copy-start = (f32[6,1,128,128]{3,2,0,1:T(8,128)S(1)}, f32[6,1,128,128]{3,2,0,1:T(8,128)}, u32[]{:S(2)}) copy-start(f32[6,1,128,128]{3,2,0,1:T(8,128)} %copy.9) | copy-start | bytes 1179652
  114.3 7.3 %copy-start.2 = (f32[64,128]{0,1:T(8,128)S(1)}, f32[64,128]{0,1:T(8,128)}, u32[]{:S(2)}) copy-start(f32[64,128]{0,1:T(8,128)} %get-tuple-element.12) | copy-start | bytes 98308
  117.9 12.4 %collective-permute-start.18 = (f32[832,128]{1,0:T(8,128)S(1)}, f32[832,128]{1,0:T(8,128)S(1)}, u32[]{:S(2)}, u32[]{:S(2)}) collective-permute-start(f32[832,128]{1,0:T(8,128)S(1)} %pad_maximum_fusion.2), channel_id=1, source_target_pairs={{4,6},{5,7},{12,14},{13,15},{20,22},{21,23},{28,30},{29,31},{6,0},... | collective-permute-start | bytes 1277960 | tf_op jit(solution)/shard_map/ppermute | solution.py:39
  119.4 18.9 %collective-permute-start.20 = (f32[832,128]{1,0:T(8,128)S(1)}, f32[832,128]{1,0:T(8,128)S(1)}, u32[]{:S(2)}, u32[]{:S(2)}) collective-permute-start(f32[832,128]{1,0:T(8,128)S(1)} %pad_maximum_fusion.4), channel_id=1, source_target_pairs={{4,0},{5,1},{12,8},{13,9},{20,16},{21,17},{28,24},{29,25},{6,2},{7... | collective-permute-start | bytes 1277960 | tf_op jit(solution)/shard_map/ppermute | solution.py:39
  121.6 30.8 %copy-start.1 = (f32[6,1,1,128,128]{4,3,2,1,0:T(8,128)S(1)}, f32[6,1,1,128,128]{4,3,2,1,0:T(8,128)}, u32[]{:S(2)}) copy-start(f32[6,1,1,128,128]{4,3,2,1,0:T(8,128)} %param.4) | copy-start | bytes 1179652
  129.1 23.1 %collective-permute-start.22 = (f32[832,128]{1,0:T(8,128)S(1)}, f32[832,128]{1,0:T(8,128)S(1)}, u32[]{:S(2)}, u32[]{:S(2)}) collective-permute-start(f32[832,128]{1,0:T(8,128)S(1)} %pad_maximum_fusion.6), channel_id=1, source_target_pairs={{4,2},{5,3},{12,10},{13,11},{20,18},{21,19},{28,26},{29,27},{6,4},... | collective-permute-start | bytes 1277960 | tf_op jit(solution)/shard_map/ppermute | solution.py:39
  152.3 0.8 copy-start.4

commit v2 on v0

v2 whole, which is shorter than its diff:
```python
import functools

import jax
import jax.numpy as jnp
from jax import lax
from jax.experimental import pallas as pl
from jax.experimental.pallas import tpu as pltpu
from jax.sharding import PartitionSpec as P

AXES = ("row", "col")
F32 = jnp.float32
VMEM = pltpu.VMEM
PARAMS = pltpu.CompilerParams(vmem_limit_bytes=40 * 2**20)
CHEAP = pl.CostEstimate(flops=1000, bytes_accessed=1000, transcendentals=0)


def split(x):
    high = x.astype(jnp.bfloat16)
    return high, (x - high.astype(F32)).astype(jnp.bfloat16)


def product(a, b, transposed=False):
    dims = (((1,), (1 if transposed else 0,)), ((), ()))
    a_high, a_low = split(a)
    b_high, b_low = split(b)
    n = a.shape[0]
    both = lax.dot_general(
        jnp.concatenate([a_high, a_low], 0), b_high, dims, preferred_element_type=F32
    )
    cross = lax.dot_general(a_high, b_low, dims, preferred_element_type=F32)
    return both[:n] + (both[n:] + cross)


def position(col_count):
    return lax.axis_index("row") * col_count + lax.axis_index("col")


def stacked(pieces, which):
    return jnp.concatenate([p[which].T for p in pieces], axis=1)


def low_kernel(homes, col_count, own, g1, g2, g3, near, la, lx, ly, inv, w, s_a, s_b):
    me = position(col_count)

    def work(block):
        pieces = (own, g1, g2, g3)
        first = product(stacked(pieces, 0), inv[0], True)
        s_a[...] = first
        second = product(stacked(pieces, 1) - product(first, block[...]), inv[1], True)
        s_b[...] = second
        w[...] = product(first, lx[...]) + product(second, ly[...])

    @pl.when(me == homes[0])
    def _():
        work(la)

    @pl.when(me == homes[1])
    def _():
        work(near)


def high_kernel(homes, col_count, own, g1, g2, g3, l_even, l_odd, w_1, w_2, inv, after, s_a, s_b):
    del after
    me = position(col_count)

    def work(block, w_even, w_odd):
        pieces = (g3, g2, g1, own)
        first = product(stacked(pieces, 0) - w_even[...], inv[0], True)
        s_a[...] = first
        s_b[...] = product(
            stacked(pieces, 1) - w_odd[...] - product(first, block[...]), inv[1], True
        )

    @pl.when(me == homes[0])
    def _():
        work(l_even, w_1, w_2)

    @pl.when(me == homes[1])
    def _():
        work(l_odd, w_2, w_1)


def update_kernel(cfg, s_twin, s_mine, panel, *rest):
    steps, groups, row_count, share, parity, members = cfg
    outs, full = rest[:steps], rest[steps]
    quarter = full.shape[1] // steps
    step = pl.program_id(0)
    row = lax.axis_index("row")
    col = lax.axis_index("col")
    member = col // groups
    group = col % groups
    block_id = (step * row_count + row) * groups + group
    keep = (block_id > member).astype(F32)

    def work(s):
        full[...] = product(s[...], panel[...]) * keep
        for offset in range(steps):
            to = lax.rem(member + offset, steps)
            columns = pl.ds(pl.multiple_of(to * quarter, quarter), quarter)
            rows = pl.ds(pl.multiple_of(step * quarter, quarter), quarter)
            outs[offset][rows, :] = full[:, columns]

        @pl.when(step == pl.num_programs(0) - 1)
        def _():
            for offset in range(steps):
                to = lax.rem(member + offset, steps)
                columns = pl.ds(pl.multiple_of(to * quarter, quarter), quarter)
                full[:, :quarter] = s[:, columns].T
                rows = pl.ds(pl.multiple_of(group * share, share), share)
                last = outs[offset].shape[0] - share
                outs[offset][last:, :] = full[rows, :quarter]

    here = functools.reduce(jnp.logical_or, [member == m for m in members])

    @pl.when(here & (lax.rem(row, 2) == parity))
    def _():
        work(s_mine)

    @pl.when(here & (lax.rem(row, 2) != parity))
    def _():
        work(s_twin)


def last_kernel(steps, groups, rhs, *refs):
    sources, (solved, out) = refs[: 2 * steps], refs[2 * steps:]
    lows, highs = sources[:steps], sources[steps:]
    blocks, quarter = rhs.shape[0], rhs.shape[1]
    member = lax.axis_index("col") // groups

    def finish(own):
        for r in range(blocks):
            rows = pl.ds(r * quarter, quarter)
            total = own[rows, :]
            for part in lows[1:] + highs[1:]:
                total = total + part[rows, :]
            out[r] = rhs[r] - total.T
        last = blocks * quarter
        solved[member] = own[last:, :]
        for offset in range(1, steps):
            solved[lax.rem(member + steps - offset, steps)] = (
                lows[offset][last:, :] + highs[offset][last:, :]
            )

    @pl.when(member < steps // 2)
    def _():
        finish(lows[0])

    @pl.when(member >= steps // 2)
    def _():
        finish(highs[0])


def on_device(factor, rhs, inverses):
    steps = inverses.shape[0]
    blocks = factor.shape[0]
    width = factor.shape[3]
    quarter = rhs.shape[3]
    nrhs = rhs.shape[4]
    row_count = lax.axis_size("row")
    col_count = lax.axis_size("col")
    groups = col_count // steps
    row_pos = lax.axis_index("row")
    col_pos = lax.axis_index("col")
    member = col_pos // groups
    group = col_pos % groups
    share = width // col_count
    top = steps - 1
    me = row_pos * col_count + col_pos

    def dev(row, mem, grp):
        return row * col_count + mem * groups + grp

    def line(g, mem):
        return dev(g // groups, mem, g % groups)

    low_homes = (line(0, 0), line(1, 0))
    high_homes = (line(2, top), line(3, top))

    def send(x, pairs):
        return lax.ppermute(x, AXES, pairs)

    def chosen(pairs, new, old):
        here = functools.reduce(jnp.logical_or, [me == d for _, d in pairs])
        return jnp.where(here, new, old)

    vmem = pl.BlockSpec(memory_space=VMEM)
    two_inverses = [pl.BlockSpec((2, width, width), lambda i, h=h: (h, 0, 0)) for h in (0, 1)]

    mine = rhs[0, 0, 0]
    other = send(mine, [(line(g ^ 1, m), line(g, m)) for g in range(4) for m in range(steps)])
    even = group % 2 == 0
    both = jnp.stack([jnp.where(even, mine, other), jnp.where(even, other, mine)])
    near = factor[0, 0, 0]
    ly = send(near, [(line(2, 1), low_homes[0]), (line(3, 1), low_homes[1]), (line(3, 2), high_homes[0])])
    la = send(near, [(line(1, 0), low_homes[0]), (line(3, 2), high_homes[1])])
    lx = send(near, [(line(2, 0), low_homes[0]), (line(3, 0), low_homes[1])])
    gathered = [
        send(both, [(line(g, j), line(g, 0)) for g in (0, 1)] + [(line(g, top - j), line(g, top)) for g in (2, 3)])
        for j in range(1, steps)
    ]

    vector = jax.ShapeDtypeStruct((nrhs, width), F32)
    full_piece = pl.BlockSpec((2, quarter, nrhs), lambda i: (0, 0, 0))
    square = pl.BlockSpec((width, width), lambda i: (0, 0))
    vec = pl.BlockSpec((nrhs, width), lambda i: (0, 0))
    w, s_0, s_1 = pl.pallas_call(
        functools.partial(low_kernel, low_homes, col_count),
        grid=(1,),
        in_specs=[full_piece] * 4 + [square] * 4 + [two_inverses[0]],
        out_specs=[vec] * 3,
        out_shape=[vector] * 3,
        compiler_params=PARAMS,
        cost_estimate=CHEAP,
        name="solve_low",
    )(both, *gathered, near, la, lx, ly, inverses)
    w_1 = send(w, [(low_homes[0], high_homes[0]), (low_homes[1], high_homes[1])])
    w_2 = send(w, [(low_homes[0], high_homes[1]), (low_homes[1], high_homes[0])])

    def spread(outer, inner, at, away, lines):
        moved = send(inner, [(line(g, at), line(g, away)) for g in lines])
        s = jnp.where(member == at, outer, moved)
        core = (lines[0] // groups) % 2
        have = [(g // groups, g % groups) for g in lines]
        todo = [
            (r, g) for r in range(row_count) for g in range(groups)
            if r % 2 == core and (r, g) not in have
        ]
        while todo:
            new, todo = todo[: len(have)], todo[len(have):]
            pairs = [
                (dev(a[0], m, a[1]), dev(b[0], m, b[1]))
                for m in (at, away) for a, b in zip(have, new)
            ]
            s = chosen(pairs, send(s, pairs), s)
            have = have + new
        pairs = [(dev(r, m, g), dev(r ^ 1, m, g)) for m in (at, away) for r, g in have]
        return send(s, pairs), s, core

    def update(twin, s, core, members):
        part = jax.ShapeDtypeStruct((blocks * quarter + share, nrhs), F32)
        cfg = (steps, groups, row_count, share, core, members)
        parts = pl.pallas_call(
            functools.partial(update_kernel, cfg),
            grid=(blocks,),
            in_specs=[vec, vec, pl.BlockSpec((None, None, None, width, width), lambda i: (i, 0, 0, 0, 0))],
            out_specs=[pl.BlockSpec(part.shape, lambda i: (0, 0))] * steps,
            out_shape=[part] * steps,
            scratch_shapes=[VMEM((nrhs, width), F32)],
            compiler_params=PARAMS,
            cost_estimate=CHEAP,
            name="update",
        )(twin, s, factor)
        got = [parts[0]]
        for offset in range(1, steps):
            pairs = [
                (dev(r, m, g), dev(r, (m + offset) % steps, g))
                for m in members for r in range(row_count) for g in range(groups)
            ]
            got.append(send(parts[offset], pairs))
        return got

    lows = update(*spread(s_0, s_1, 0, 1, (0, 1)), (0, 1))
    s_2, s_3 = pl.pallas_call(
        functools.partial(high_kernel, high_homes, col_count),
        grid=(1,),
        in_specs=[full_piece] * 4 + [square] * 2 + [vec] * 2 + [two_inverses[1], pl.BlockSpec(memory_space=pl.ANY)],
        out_specs=[vec] * 2,
        out_shape=[vector] * 2,
        compiler_params=PARAMS,
        cost_estimate=CHEAP,
        name="solve_high",
    )(both, *gathered, ly, la, w_1, w_2, inverses, lows[0])
    highs = update(*spread(s_3, s_2, top, top - 1, (2, 3)), (top - 1, top))

    solved, remaining = pl.pallas_call(
        functools.partial(last_kernel, steps, groups),
        in_specs=[vmem] * (1 + 2 * steps),
        out_specs=[vmem] * 2,
        out_shape=[
            jax.ShapeDtypeStruct((steps, share, nrhs), F32),
            jax.ShapeDtypeStruct((blocks, quarter, nrhs), F32),
        ],
        compiler_params=PARAMS,
        cost_estimate=CHEAP,
        name="add_up",
    )(rhs[:, 0, 0], *lows, *highs)
    return solved, remaining[:, None, None]


def solution(mesh):
    in_specs = (P(None, "row", "col", None, None), P(None, "row", "col", None, None), P())
    out_specs = (P(None, "col", None), P(None, "row", "col", None, None))
    return jax.shard_map(
        on_device, mesh=mesh, in_specs=in_specs, out_specs=out_specs, check_vma=False
    )
```

time: 615 us -> 134 us (0.22)
  the two profiles are of different devices: /device:TPU:0 before, /device:TPU:11 now
where the time goes in v2:
time: 134 us; the launch traced here: 133 us
  waiting for transfers between devices  77.6 us (58%)
  starting transfers between devices  34.3 us (26%)
  local copies, waits for them, and re-layouts  12.1 us (9%)
  Pallas kernels  6.68 us (5%)
    ppermute x21, waiting for transfers between devices, send(): return lax.ppermute(x, AXES, pairs)  77.6 us
    ppermute x21, starting transfers between devices, send(): return lax.ppermute(x, AXES, pairs)  34.3 us
    unnamed x26, local copies, waits for them, and re-layouts  9.91 us
    pallas_call x2, Pallas kernels, update(): pl.pallas_call(functools.partial(update_kernel, cfg), grid=(blocks,), in_...  3.04 us
  transfers between devices with their start and end apart: 21, of which 4 were waited for; matrix products, arithmetic and copies ran while one was open for 1% of the time, Pallas kernels for 2%

profile of v2, /device:TPU:11, one launch (start us, length us, event | category | flops | bytes accessed | tf_op | source)
XLA Modules:
  0.0 132.7 jit_solution(3186251509537661598)
XLA Ops:
  0.6 1.3 slice_bitcast_fusion.near
  1.9 0.7 collective-permute-start.6
  2.7 1.6 %collective-permute-start.5 = (f32[512,512]{1,0:T(8,128)S(1)}, f32[512,512]{1,0:T(8,128)}, u32[]{:S(2)}, u32[]{:S(2)}) collective-permute-start(f32[512,512]{1,0:T(8,128)S(1)} %slice_bitcast_fusion.near), channel_id=1, source_target_pairs={{8,0},{9,1}} | collective-permute-start | bytes 3145736 | tf_op jit(solution)/shard_map/ppermute | solution.py:180
  4.3 0.7 collective-permute-start.4
  5.0 0.8 slice_bitcast_fusion.1
  5.9 0.7 collective-permute-start
  6.6 0.0 collective-permute-done
  6.6 0.9 select_bitcast_fusion.1
  7.5 0.7 collective-permute-start.3
  8.1 0.7 collective-permute-start.2
  8.8 0.0 collective-permute-done.3.g3
  8.8 0.7 collective-permute-start.1
  9.5 0.0 collective-permute-done.2.g2
  9.5 0.0 collective-permute-done.1.g1
  9.5 0.0 copy-start.5
  9.5 0.0 collective-permute-done.6.ly.l_even
  9.5 0.0 collective-permute-done.5.lx
  9.6 0.0 collective-permute-done.4.la.l_odd
  9.6 0.0 copy-start.2
  9.6 2.2 %copy-done.2 = f32[4,512,512]{2,1,0:T(8,128)S(1)} copy-done((f32[4,512,512]{2,1,0:T(8,128)S(1)}, f32[4,512,512]{2,1,0:T(8,128)}, u32[]{:S(2)}) %copy-start.2) | copy-done | bytes 4194328
  11.8 1.9 %solve_low.1 = (f32[128,512]{1,0:T(8,128)S(1)}, f32[128,512]{1,0:T(8,128)S(1)}, f32[128,512]{1,0:T(8,128)}) custom-call(f32[2,128,128]{2,1,0:T(8,128)S(1)} %pad_maximum_fusion.own, f32[2,128,128]{2,1,0:T(8,128)S(1)} %collective-permute-done.1.g1, f32[2,128,128]{2,1,0:T(8,128)S(1)} %collective-permute-done.2.g2, ...), custom_call_target="tpu_custom_call" | custom-call | flops 1000 | bytes 1000 | tf_op jit(solution)/shard_map/solve_low/pallas_call | solution.py:206
  13.7 0.0 copy-done.5
  13.7 0.7 copy-done.7
  14.4 0.7 copy-done.12
  15.1 0.8 collective-permute-start.7
  15.9 0.0 collective-permute-done.7
  16.0 1.4 %collective-permute-start.8 = (f32[128,512]{1,0:T(8,128)S(1)}, f32[128,512]{1,0:T(8,128)}, u32[]{:S(2)}, u32[]{:S(2)}) collective-permute-start(f32[128,512]{1,0:T(8,128)S(1)} %broadcast_select_fusion.2), channel_id=1, source_target_pairs={{0,16},{1,17},{2,18},{3,19}} | collective-permute-start | bytes 786440 | tf_op jit(solution)/shard_map/ppermute | solution.py:180
  17.4 0.0 collective-permute-done.8
  17.4 1.3 collective-permute-start.9
  18.7 0.7 collective-permute-start.14
  19.4 0.7 collective-permute-start.13
  20.1 41.8 %collective-permute-done.9.s_twin = f32[128,512]{1,0:T(8,128)S(1)} collective-permute-done((f32[128,512]{1,0:T(8,128)S(1)}, f32[128,512]{1,0:T(8,128)S(1)}, u32[]{:S(2)}, u32[]{:S(2)}) %collective-permute-start.9) | collective-permute-done | bytes 262176 | tf_op jit(solution)/shard_map/ppermute | solution.py:180
  61.9 2.8 %copy-done = f32[6,1,1,512,512]{4,3,2,1,0:T(8,128)S(1)} copy-done((f32[6,1,1,512,512]{4,3,2,1,0:T(8,128)S(1)}, f32[6,1,1,512,512]{4,3,2,1,0:T(8,128)}, u32[]{:S(2)}) %copy-start) | copy-done | bytes 6291480
  64.7 3.0 %update.2 = (f32[832,128]{1,0:T(8,128)S(1)}, f32[832,128]{1,0:T(8,128)S(1)}, f32[832,128]{1,0:T(8,128)S(1)}, f32[832,128]{1,0:T(8,128)S(1)}) custom-call(f32[128,512]{1,0:T(8,128)S(1)} %collective-permute-done.9.s_twin, f32[128,512]{1,0:T(8,128)S(1)} %broadcast_select_fusion.3.s_mine, f32[6,1,1,512,512]{4,3,2,1,0:T(8,128)S(1)} %copy-done), custom_call_target="tpu_custom_call" | custom-call | flops 1000 | bytes 1000 | tf_op jit(solution)/shard_map/update/pallas_call | solution.py:242
  67.7 0.0 copy-start.9
  67.7 0.0 copy-start.10
  67.7 0.0 copy-start.11
  67.7 0.0 collective-permute-done.14.w_2
  67.8 0.0 collective-permute-done.13.w_1
  67.8 0.0 copy-start.4
  67.8 0.7 solve_high.1
  68.5 0.0 copy-done.9
  68.6 0.7 copy-done.8
  69.3 0.7 collective-permute-start.15
  69.9 0.0 collective-permute-done.15
  70.0 0.7 collective-permute-start.16
  70.7 1.9 %collective-permute-start.10 = (f32[832,128]{1,0:T(8,128)}, f32[832,128]{1,0:T(8,128)S(1)}, u32[]{:S(2)}, u32[]{:S(2)}) collective-permute-start(f32[832,128]{1,0:T(8,128)} %copy-done.11), channel_id=1, source_target_pairs={{0,2},{1,3},{8,10},{9,11},{16,18},{17,19},{24,26},{25,27},{2,4},{3... | collective-permute-start | bytes 1277960 | tf_op jit(solution)/shard_map/ppermute | solution.py:180
  72.6 0.0 collective-permute-done.16
  72.7 0.7 collective-permute-start.17
  73.4 13.2 %collective-permute-start.11 = (f32[832,128]{1,0:T(8,128)}, f32[832,128]{1,0:T(8,128)S(1)}, u32[]{:S(2)}, u32[]{:S(2)}) collective-permute-start(f32[832,128]{1,0:T(8,128)} %copy-done.10), channel_id=1, source_target_pairs={{0,4},{1,5},{8,12},{9,13},{16,20},{17,21},{24,28},{25,29},{2,6},{3... | collective-permute-start | bytes 1277960 | tf_op jit(solution)/shard_map/ppermute | solution.py:180
  86.6 3.4 %collective-permute-start.12 = (f32[832,128]{1,0:T(8,128)}, f32[832,128]{1,0:T(8,128)S(1)}, u32[]{:S(2)}, u32[]{:S(2)}) collective-permute-start(f32[832,128]{1,0:T(8,128)} %copy-done.9), channel_id=1, source_target_pairs={{0,6},{1,7},{8,14},{9,15},{16,22},{17,23},{24,30},{25,31},{2,0},{3... | collective-permute-start | bytes 1277960 | tf_op jit(solution)/shard_map/ppermute | solution.py:180
  89.9 0.0 collective-permute-done.17.s_twin
  90.0 0.0 copy-start.1
  90.0 2.8 %copy-done.1 = f32[6,1,1,512,512]{4,3,2,1,0:T(8,128)S(1)} copy-done((f32[6,1,1,512,512]{4,3,2,1,0:T(8,128)S(1)}, f32[6,1,1,512,512]{4,3,2,1,0:T(8,128)}, u32[]{:S(2)}) %copy-start.1) | copy-done | bytes 6291480
  92.7 0.7 collective-permute-start.18
  93.4 1.3 collective-permute-start.19
  94.7 0.0 collective-permute-done.10.refs_1_
  94.7 1.3 collective-permute-start.20
  96.0 13.9 %collective-permute-done.11.refs_2_ = f32[832,128]{1,0:T(8,128)S(1)} collective-permute-done((f32[832,128]{1,0:T(8,128)}, f32[832,128]{1,0:T(8,128)S(1)}, u32[]{:S(2)}, u32[]{:S(2)}) %collective-permute-start.11) | collective-permute-done | bytes 426016 | tf_op jit(solution)/shard_map/ppermute | solution.py:180
  110.0 0.0 collective-permute-done.12.refs_3_
  110.0 0.0 collective-permute-done.18.refs_5_
  110.0 6.1 %collective-permute-done.19.refs_6_ = f32[832,128]{1,0:T(8,128)S(1)} collective-permute-done((f32[832,128]{1,0:T(8,128)S(1)}, f32[832,128]{1,0:T(8,128)S(1)}, u32[]{:S(2)}, u32[]{:S(2)}) %collective-permute-start.19) | collective-permute-done | bytes 426016 | tf_op jit(solution)/shard_map/ppermute | solution.py:180
  116.1 15.7 %collective-permute-done.20.refs_7_ = f32[832,128]{1,0:T(8,128)S(1)} collective-permute-done((f32[832,128]{1,0:T(8,128)S(1)}, f32[832,128]{1,0:T(8,128)S(1)}, u32[]{:S(2)}, u32[]{:S(2)}) %collective-permute-start.20) | collective-permute-done | bytes 426016 | tf_op jit(solution)/shard_map/ppermute | solution.py:180
  131.8 1.0 add_up.1
  (17 shorter events, 0.2 us)
Async XLA Ops:
  1.9 7.6 %collective-permute-start.6 = (f32[512,512]{1,0:T(8,128)S(1)}, f32[512,512]{1,0:T(8,128)S(1)}, u32[]{:S(2)}, u32[]{:S(2)}) collective-permute-start(f32[512,512]{1,0:T(8,128)S(1)} %slice_bitcast_fusion.near), channel_id=1, source_target_pairs={{10,0},{11,1},{13,14}} | collective-permute-start | bytes 3145736 | tf_op jit(solution)/shard_map/ppermute | solution.py:180
  2.7 6.9 %collective-permute-start.5 = (f32[512,512]{1,0:T(8,128)S(1)}, f32[512,512]{1,0:T(8,128)}, u32[]{:S(2)}, u32[]{:S(2)}) collective-permute-start(f32[512,512]{1,0:T(8,128)S(1)} %slice_bitcast_fusion.near), channel_id=1, source_target_pairs={{8,0},{9,1}} | collective-permute-start | bytes 3145736 | tf_op jit(solution)/shard_map/ppermute | solution.py:180
  4.3 5.2 %collective-permute-start.4 = (f32[512,512]{1,0:T(8,128)S(1)}, f32[512,512]{1,0:T(8,128)S(1)}, u32[]{:S(2)}, u32[]{:S(2)}) collective-permute-start(f32[512,512]{1,0:T(8,128)S(1)} %slice_bitcast_fusion.near), channel_id=1, source_target_pairs={{1,0},{13,15}} | collective-permute-start | bytes 3145736 | tf_op jit(solution)/shard_map/ppermute | solution.py:180
  5.9 0.7 collective-permute-start
  7.5 1.4 %collective-permute-start.3 = (f32[2,128,128]{2,1,0:T(8,128)S(1)}, f32[2,128,128]{2,1,0:T(8,128)S(1)}, u32[]{:S(2)}, u32[]{:S(2)}) collective-permute-start(f32[2,128,128]{2,1,0:T(8,128)S(1)} %pad_maximum_fusion.own), channel_id=1, source_target_pairs={{6,0},{7,1},{8,14},{9,15}} | collective-permute-start | bytes 393224 | tf_op jit(solution)/shard_map/ppermute | solution.py:180
  8.1 1.4 %collective-permute-start.2 = (f32[2,128,128]{2,1,0:T(8,128)S(1)}, f32[2,128,128]{2,1,0:T(8,128)S(1)}, u32[]{:S(2)}, u32[]{:S(2)}) collective-permute-start(f32[2,128,128]{2,1,0:T(8,128)S(1)} %pad_maximum_fusion.own), channel_id=1, source_target_pairs={{4,0},{5,1},{10,14},{11,15}} | collective-permute-start | bytes 393224 | tf_op jit(solution)/shard_map/ppermute | solution.py:180
  8.8 0.7 collective-permute-start.1
  9.5 4.2 %copy-start.5 = (f32[2,128,128]{2,1,0:T(8,128)}, f32[2,128,128]{2,1,0:T(8,128)S(1)}, u32[]{:S(2)}) copy-start(f32[2,128,128]{2,1,0:T(8,128)S(1)} %collective-permute-done.1.g1) | copy-start | bytes 393220
  9.6 2.2 %copy-start.2 = (f32[4,512,512]{2,1,0:T(8,128)S(1)}, f32[4,512,512]{2,1,0:T(8,128)}, u32[]{:S(2)}) copy-start(f32[4,512,512]{2,1,0:T(8,128)} %inv.3) | copy-start | bytes 12582916
  13.7 0.7 copy-start.7
  14.4 0.7 copy-start.12
  15.1 52.7 %copy-start.6 = (f32[2,128,128]{2,1,0:T(8,128)S(1)}, f32[2,128,128]{2,1,0:T(8,128)}, u32[]{:S(2)}) copy-start(f32[2,128,128]{2,1,0:T(8,128)} %copy-done.5) | copy-start | bytes 393220
  15.1 0.8 collective-permute-start.7
  16.0 1.4 %collective-permute-start.8 = (f32[128,512]{1,0:T(8,128)S(1)}, f32[128,512]{1,0:T(8,128)}, u32[]{:S(2)}, u32[]{:S(2)}) collective-permute-start(f32[128,512]{1,0:T(8,128)S(1)} %broadcast_select_fusion.2), channel_id=1, source_target_pairs={{0,16},{1,17},{2,18},{3,19}} | collective-permute-start | bytes 786440 | tf_op jit(solution)/shard_map/ppermute | solution.py:180
  17.4 44.5 %collective-permute-start.9 = (f32[128,512]{1,0:T(8,128)S(1)}, f32[128,512]{1,0:T(8,128)S(1)}, u32[]{:S(2)}, u32[]{:S(2)}) collective-permute-start(f32[128,512]{1,0:T(8,128)S(1)} %broadcast_select_fusion.3.s_mine), channel_id=1, source_target_pairs={{0,8},{1,9},{16,24},{17,25},{2,10},{3,11},{18,26},{19,27}} | collective-permute-start | bytes 786440 | tf_op jit(solution)/shard_map/ppermute | solution.py:180
  18.7 49.1 %collective-permute-start.14 = (f32[128,512]{1,0:T(8,128)}, f32[128,512]{1,0:T(8,128)S(1)}, u32[]{:S(2)}, u32[]{:S(2)}) collective-permute-start(f32[128,512]{1,0:T(8,128)} %copy-done.12), channel_id=1, source_target_pairs={{0,15},{1,14}} | collective-permute-start | bytes 786440 | tf_op jit(solution)/shard_map/ppermute | solution.py:180
  19.4 48.4 %collective-permute-start.13 = (f32[128,512]{1,0:T(8,128)}, f32[128,512]{1,0:T(8,128)S(1)}, u32[]{:S(2)}, u32[]{:S(2)}) collective-permute-start(f32[128,512]{1,0:T(8,128)} %copy-done.12), channel_id=1, source_target_pairs={{0,14},{1,15}} | collective-permute-start | bytes 786440 | tf_op jit(solution)/shard_map/ppermute | solution.py:180
  61.9 2.8 %copy-start = (f32[6,1,1,512,512]{4,3,2,1,0:T(8,128)S(1)}, f32[6,1,1,512,512]{4,3,2,1,0:T(8,128)}, u32[]{:S(2)}) copy-start(f32[6,1,1,512,512]{4,3,2,1,0:T(8,128)} %panel.3) | copy-start | bytes 18874372
  64.7 3.1 %copy-start.3 = (f32[4,512,512]{2,1,0:T(8,128)S(1)}, f32[4,512,512]{2,1,0:T(8,128)}, u32[]{:S(2)}) copy-start(f32[4,512,512]{2,1,0:T(8,128)} %inv.3) | copy-start | bytes 12582916
  67.7 0.8 copy-start.9
  67.7 1.5 %copy-start.10 = (f32[832,128]{1,0:T(8,128)}, f32[832,128]{1,0:T(8,128)S(1)}, u32[]{:S(2)}) copy-start(f32[832,128]{1,0:T(8,128)S(1)} %get-tuple-element.21) | copy-start | bytes 1277956
  67.7 1.5 %copy-start.11 = (f32[832,128]{1,0:T(8,128)}, f32[832,128]{1,0:T(8,128)S(1)}, u32[]{:S(2)}) copy-start(f32[832,128]{1,0:T(8,128)S(1)} %get-tuple-element.20) | copy-start | bytes 1277956
  67.8 64.0 %copy-start.4 = (f32[6,1,1,128,128]{4,3,2,1,0:T(8,128)S(1)}, f32[6,1,1,128,128]{4,3,2,1,0:T(8,128)}, u32[]{:S(2)}) copy-start(f32[6,1,1,128,128]{4,3,2,1,0:T(8,128)} %param.4) | copy-start | bytes 1179652
  68.6 0.7 copy-start.8
  69.3 0.7 collective-permute-start.15
  70.0 2.6 %collective-permute-start.16 = (f32[128,512]{1,0:T(8,128)S(1)}, f32[128,512]{1,0:T(8,128)S(1)}, u32[]{:S(2)}, u32[]{:S(2)}) collective-permute-start(f32[128,512]{1,0:T(8,128)S(1)} %broadcast_select_fusion), channel_id=1, source_target_pairs={{14,30},{15,31},{12,28},{13,29}} | collective-permute-start | bytes 786440 | tf_op jit(solution)/shard_map/ppermute | solution.py:180
  70.7 24.0 %collective-permute-start.10 = (f32[832,128]{1,0:T(8,128)}, f32[832,128]{1,0:T(8,128)S(1)}, u32[]{:S(2)}, u32[]{:S(2)}) collective-permute-start(f32[832,128]{1,0:T(8,128)} %copy-done.11), channel_id=1, source_target_pairs={{0,2},{1,3},{8,10},{9,11},{16,18},{17,19},{24,26},{25,27},{2,4},{3... | collective-permute-start | bytes 1277960 | tf_op jit(solution)/shard_map/ppermute | solution.py:180
  72.7 17.3 %collective-permute-start.17 = (f32[128,512]{1,0:T(8,128)S(1)}, f32[128,512]{1,0:T(8,128)S(1)}, u32[]{:S(2)}, u32[]{:S(2)}) collective-permute-start(f32[128,512]{1,0:T(8,128)S(1)} %broadcast_select_fusion.1.s_mine), channel_id=1, source_target_pairs={{14,6},{15,7},{30,22},{31,23},{12,4},{13,5},{28,20},{29,21}} | collective-permute-start | bytes 786440 | tf_op jit(solution)/shard_map/ppermute | solution.py:180
  73.4 36.6 %collective-permute-start.11 = (f32[832,128]{1,0:T(8,128)}, f32[832,128]{1,0:T(8,128)S(1)}, u32[]{:S(2)}, u32[]{:S(2)}) collective-permute-start(f32[832,128]{1,0:T(8,128)} %copy-done.10), channel_id=1, source_target_pairs={{0,4},{1,5},{8,12},{9,13},{16,20},{17,21},{24,28},{25,29},{2,6},{3... | collective-permute-start | bytes 1277960 | tf_op jit(solution)/shard_map/ppermute | solution.py:180
  86.6 23.4 %collective-permute-start.12 = (f32[832,128]{1,0:T(8,128)}, f32[832,128]{1,0:T(8,128)S(1)}, u32[]{:S(2)}, u32[]{:S(2)}) collective-permute-start(f32[832,128]{1,0:T(8,128)} %copy-done.9), channel_id=1, source_target_pairs={{0,6},{1,7},{8,14},{9,15},{16,22},{17,23},{24,30},{25,31},{2,0},{3... | collective-permute-start | bytes 1277960 | tf_op jit(solution)/shard_map/ppermute | solution.py:180
  90.0 2.8 %copy-start.1 = (f32[6,1,1,512,512]{4,3,2,1,0:T(8,128)S(1)}, f32[6,1,1,512,512]{4,3,2,1,0:T(8,128)}, u32[]{:S(2)}) copy-start(f32[6,1,1,512,512]{4,3,2,1,0:T(8,128)} %panel.3) | copy-start | bytes 18874372
  92.7 17.2 %collective-permute-start.18 = (f32[832,128]{1,0:T(8,128)S(1)}, f32[832,128]{1,0:T(8,128)S(1)}, u32[]{:S(2)}, u32[]{:S(2)}) collective-permute-start(f32[832,128]{1,0:T(8,128)S(1)} %get-tuple-element.27), channel_id=1, source_target_pairs={{4,6},{5,7},{12,14},{13,15},{20,22},{21,23},{28,30},{29,31},{6,0},... | collective-permute-start | bytes 1277960 | tf_op jit(solution)/shard_map/ppermute | solution.py:180
  93.4 22.6 %collective-permute-start.19 = (f32[832,128]{1,0:T(8,128)S(1)}, f32[832,128]{1,0:T(8,128)S(1)}, u32[]{:S(2)}, u32[]{:S(2)}) collective-permute-start(f32[832,128]{1,0:T(8,128)S(1)} %get-tuple-element.28), channel_id=1, source_target_pairs={{4,0},{5,1},{12,8},{13,9},{20,16},{21,17},{28,24},{29,25},{6,2},{7... | collective-permute-start | bytes 1277960 | tf_op jit(solution)/shard_map/ppermute | solution.py:180
  94.7 37.0 %collective-permute-start.20 = (f32[832,128]{1,0:T(8,128)S(1)}, f32[832,128]{1,0:T(8,128)S(1)}, u32[]{:S(2)}, u32[]{:S(2)}) collective-permute-start(f32[832,128]{1,0:T(8,128)S(1)} %get-tuple-element.29), channel_id=1, source_target_pairs={{4,2},{5,3},{12,10},{13,11},{20,18},{21,19},{28,26},{29,27},{6,4},... | collective-permute-start | bytes 1277960 | tf_op jit(solution)/shard_map/ppermute | solution.py:180

commit v3 on v2

v3 whole, which is shorter than its diff:
```python
import functools

import jax
import jax.numpy as jnp
from jax import lax
from jax.experimental import pallas as pl
from jax.experimental.pallas import tpu as pltpu
from jax.sharding import PartitionSpec as P

AXES = ("row", "col")
F32 = jnp.float32
VMEM = pltpu.VMEM
PARAMS = pltpu.CompilerParams(vmem_limit_bytes=40 * 2**20)
CHEAP = pl.CostEstimate(flops=1000, bytes_accessed=1000, transcendentals=0)


def split(x):
    high = x.astype(jnp.bfloat16)
    return high, (x - high.astype(F32)).astype(jnp.bfloat16)


def product(a, b, transposed=False):
    dims = (((1,), (1 if transposed else 0,)), ((), ()))
    a_high, a_low = split(a)
    b_high, b_low = split(b)
    n = a.shape[0]
    both = lax.dot_general(
        jnp.concatenate([a_high, a_low], 0), b_high, dims, preferred_element_type=F32
    )
    cross = lax.dot_general(a_high, b_low, dims, preferred_element_type=F32)
    return both[:n] + (both[n:] + cross)


def position(col_count):
    return lax.axis_index("row") * col_count + lax.axis_index("col")


def stacked(pieces, which):
    return jnp.concatenate([p[which].T for p in pieces], axis=1)


def low_kernel(homes, col_count, own, g1, g2, g3, near, la, lx, ly, inverses, w, s_a, s_b, inv, sem):
    me = position(col_count)

    def work(block):
        copies = [pltpu.make_async_copy(inverses.at[i], inv.at[i], sem.at[i]) for i in range(2)]
        for copy in copies:
            copy.start()
        pieces = (own, g1, g2, g3)
        right = stacked(pieces, 0)
        copies[0].wait()
        first = product(right, inv[0], True)
        s_a[...] = first
        right = stacked(pieces, 1) - product(first, block[...])
        copies[1].wait()
        second = product(right, inv[1], True)
        s_b[...] = second
        w[...] = product(first, lx[...]) + product(second, ly[...])

    @pl.when(me == homes[0])
    def _():
        work(la)

    @pl.when(me == homes[1])
    def _():
        work(near)


def high_kernel(homes, col_count, own, g1, g2, g3, l_even, l_odd, w_1, w_2, inverses, s_a, s_b, inv, sem):
    me = position(col_count)

    def work(block, w_even, w_odd):
        copies = [pltpu.make_async_copy(inverses.at[2 + i], inv.at[i], sem.at[i]) for i in range(2)]
        for copy in copies:
            copy.start()
        pieces = (g3, g2, g1, own)
        right = stacked(pieces, 0) - w_even[...]
        copies[0].wait()
        first = product(right, inv[0], True)
        s_a[...] = first
        right = stacked(pieces, 1) - w_odd[...] - product(first, block[...])
        copies[1].wait()
        s_b[...] = product(right, inv[1], True)

    @pl.when(me == homes[0])
    def _():
        work(l_even, w_1, w_2)

    @pl.when(me == homes[1])
    def _():
        work(l_odd, w_2, w_1)


def update_kernel(cfg, *refs):
    steps, groups, row_count, share, have, members, blocks = cfg
    ways, panel = refs[:8], refs[8]
    outs, (tiles, s, full, sems) = refs[9: 9 + steps], refs[9 + steps:]
    quarter = full.shape[2] // steps
    row = lax.axis_index("row")
    col = lax.axis_index("col")
    member = col // groups
    group = col % groups

    def among(spots):
        return functools.reduce(jnp.logical_or, [(row == r) & (group == g) for r, g in spots])

    core = have[0][0] % 2
    first, first_twin = among(have), among([(r ^ 1, g) for r, g in have])
    same = lax.rem(row, 2) == core
    roles = (
        first, same & jnp.logical_not(first), first_twin,
        jnp.logical_not(same) & jnp.logical_not(first_twin),
    )

    @pl.when(functools.reduce(jnp.logical_or, [member == m for m in members]))
    def _():
        copies = [
            pltpu.make_async_copy(panel.at[r, 0, 0], tiles.at[r], sems.at[r]) for r in range(blocks)
        ]
        for copy in copies:
            copy.start()
        for m, plane in enumerate(members):
            for way, role in enumerate(roles):
                @pl.when((member == plane) & role)
                def _(src=ways[4 * m + way]):
                    s[...] = src[...]

        for r in range(blocks):
            copies[r].wait()
            block_id = (r * row_count + row) * groups + group
            keep = (block_id > member).astype(F32)
            full[r] = product(s[...], tiles[r]) * keep
        for offset in range(steps):
            to = lax.rem(member + offset, steps)
            columns = pl.ds(pl.multiple_of(to * quarter, quarter), quarter)
            for r in range(blocks):
                outs[offset][pl.ds(r * quarter, quarter), :] = full[r, :, columns]
            full[blocks, :, :quarter] = s[:, columns].T
            rows = pl.ds(pl.multiple_of(group * share, share), share)
            outs[offset][blocks * quarter:, :] = full[blocks, rows, :quarter]


def last_kernel(steps, groups, rhs, *refs):
    sources, (solved, out) = refs[: 2 * steps], refs[2 * steps:]
    lows, highs = sources[:steps], sources[steps:]
    blocks, quarter = rhs.shape[0], rhs.shape[1]
    member = lax.axis_index("col") // groups

    def finish(own):
        for r in range(blocks):
            rows = pl.ds(r * quarter, quarter)
            total = own[rows, :]
            for part in lows[1:] + highs[1:]:
                total = total + part[rows, :]
            out[r] = rhs[r] - total.T
        last = blocks * quarter
        solved[member] = own[last:, :]
        for offset in range(1, steps):
            solved[lax.rem(member + steps - offset, steps)] = (
                lows[offset][last:, :] + highs[offset][last:, :]
            )

    @pl.when(member < steps // 2)
    def _():
        finish(lows[0])

    @pl.when(member >= steps // 2)
    def _():
        finish(highs[0])


def on_device(factor, rhs, inverses):
    steps = inverses.shape[0]
    blocks = factor.shape[0]
    width = factor.shape[3]
    quarter = rhs.shape[3]
    nrhs = rhs.shape[4]
    row_count = lax.axis_size("row")
    col_count = lax.axis_size("col")
    groups = col_count // steps
    row_pos = lax.axis_index("row")
    col_pos = lax.axis_index("col")
    member = col_pos // groups
    group = col_pos % groups
    share = width // col_count
    top = steps - 1
    me = row_pos * col_count + col_pos

    def dev(row, mem, grp):
        return row * col_count + mem * groups + grp

    def line(g, mem):
        return dev(g // groups, mem, g % groups)

    low_homes = (line(0, 0), line(1, 0))
    high_homes = (line(2, top), line(3, top))

    def send(x, pairs):
        return lax.ppermute(x, AXES, pairs)

    def chosen(pairs, new, old):
        here = functools.reduce(jnp.logical_or, [me == d for _, d in pairs])
        return jnp.where(here, new, old)

    vmem = pl.BlockSpec(memory_space=VMEM)
    hbm = pl.BlockSpec(memory_space=pltpu.HBM)

    held_factor = pltpu.with_memory_space_constraint(factor, pltpu.HBM)
    held_inverses = pltpu.with_memory_space_constraint(inverses, pltpu.HBM)

    mine = rhs[0, 0, 0]
    other = send(mine, [(line(g ^ 1, m), line(g, m)) for g in range(4) for m in range(steps)])
    even = group % 2 == 0
    both = jnp.stack([jnp.where(even, mine, other), jnp.where(even, other, mine)])
    near = factor[0, 0, 0]
    ly = send(near, [(line(2, 1), low_homes[0]), (line(3, 1), low_homes[1]), (line(3, 2), high_homes[0])])
    later = lax.optimization_barrier((near, other))[0]
    la = send(later, [(line(1, 0), low_homes[0]), (line(3, 2), high_homes[1])])
    lx = send(later, [(line(2, 0), low_homes[0]), (line(3, 0), low_homes[1])])
    gathered = [
        send(both, [(line(g, j), line(g, 0)) for g in (0, 1)] + [(line(g, top - j), line(g, top)) for g in (2, 3)])
        for j in range(1, steps)
    ]

    vector = jax.ShapeDtypeStruct((nrhs, width), F32)
    two = [VMEM((2, width, width), F32), pltpu.SemaphoreType.DMA((2,))]
    w, s_0, s_1 = pl.pallas_call(
        functools.partial(low_kernel, low_homes, col_count),
        in_specs=[vmem] * 8 + [hbm],
        out_specs=[vmem] * 3,
        out_shape=[vector] * 3,
        scratch_shapes=two,
        compiler_params=PARAMS,
        cost_estimate=CHEAP,
        name="solve_low",
    )(both, *gathered, near, la, lx, ly, held_inverses)
    w_1 = send(w, [(low_homes[0], high_homes[0]), (low_homes[1], high_homes[1])])
    w_2 = send(w, [(low_homes[0], high_homes[1]), (low_homes[1], high_homes[0])])
    s_2, s_3 = pl.pallas_call(
        functools.partial(high_kernel, high_homes, col_count),
        in_specs=[vmem] * 8 + [hbm],
        out_specs=[vmem] * 2,
        out_shape=[vector] * 2,
        scratch_shapes=two,
        compiler_params=PARAMS,
        cost_estimate=CHEAP,
        name="solve_high",
    )(both, *gathered, ly, la, w_1, w_2, held_inverses)

    def spread(s, plane, lines):
        have = [(g // groups, g % groups) for g in lines]
        todo = [
            (r, g) for r in range(row_count) for g in range(groups)
            if r % 2 == have[0][0] % 2 and (r, g) not in have
        ]
        spots, far = list(have), None
        while todo:
            new, todo = todo[: len(spots)], todo[len(spots):]
            pairs = [(dev(a[0], plane, a[1]), dev(b[0], plane, b[1])) for a, b in zip(spots, new)]
            if far is None:
                far = send(s, pairs)
            else:
                held = chosen([(0, dev(r, plane, g)) for r, g in have], s, far)
                far = chosen(pairs, send(held, pairs), far)
            spots = spots + new
        twins = [(dev(r, plane, g), dev(r ^ 1, plane, g)) for r, g in spots]
        return s, far, send(s, twins[: len(have)]), send(far, twins[len(have):])

    def update(ways, lines, members):
        part = jax.ShapeDtypeStruct((blocks * quarter + share, nrhs), F32)
        have = [(g // groups, g % groups) for g in lines]
        cfg = (steps, groups, row_count, share, have, members, blocks)
        parts = pl.pallas_call(
            functools.partial(update_kernel, cfg),
            in_specs=[vmem] * 8 + [hbm],
            out_specs=[vmem] * steps,
            out_shape=[part] * steps,
            scratch_shapes=[
                VMEM((blocks, width, width), F32),
                VMEM((nrhs, width), F32),
                VMEM((blocks + 1, nrhs, width), F32),
                pltpu.SemaphoreType.DMA((blocks,)),
            ],
            compiler_params=PARAMS,
            cost_estimate=CHEAP,
            name="update",
        )(*ways, held_factor)
        got = [parts[0]]
        for offset in range(1, steps):
            pairs = [
                (dev(r, m, g), dev(r, (m + offset) % steps, g))
                for m in members for r in range(row_count) for g in range(groups)
            ]
            got.append(send(parts[offset], pairs))
        return got

    def both_planes(outer, inner, at, away, lines):
        moved = send(inner, [(line(g, at), line(g, away)) for g in lines])
        return spread(outer, at, lines) + spread(moved, away, lines)

    lows = update(both_planes(s_0, s_1, 0, 1, (0, 1)), (0, 1), (0, 1))
    highs = update(both_planes(s_3, s_2, top, top - 1, (2, 3)), (2, 3), (top, top - 1))

    solved, remaining = pl.pallas_call(
        functools.partial(last_kernel, steps, groups),
        in_specs=[vmem] * (1 + 2 * steps),
        out_specs=[vmem] * 2,
        out_shape=[
            jax.ShapeDtypeStruct((steps, share, nrhs), F32),
            jax.ShapeDtypeStruct((blocks, quarter, nrhs), F32),
        ],
        compiler_params=PARAMS,
        cost_estimate=CHEAP,
        name="add_up",
    )(rhs[:, 0, 0], *lows, *highs)
    return solved, remaining[:, None, None]


def solution(mesh):
    in_specs = (P(None, "row", "col", None, None), P(None, "row", "col", None, None), P())
    out_specs = (P(None, "col", None), P(None, "row", "col", None, None))
    return jax.shard_map(
        on_device, mesh=mesh, in_specs=in_specs, out_specs=out_specs, check_vma=False
    )
```

time: 134 us -> 115 us (0.86)
  the two profiles are of different devices: /device:TPU:11 before, /device:TPU:9 now
where the time goes in v3:
time: 115 us; the launch traced here: 114 us
  waiting for transfers between devices  51.9 us (45%)
  starting transfers between devices  51.8 us (45%)
  Pallas kernels  6.19 us (5%)
  local copies, waits for them, and re-layouts  2.15 us (2%)
    ppermute x29, waiting for transfers between devices, send(): return lax.ppermute(x, AXES, pairs)  51.9 us
    ppermute x29, starting transfers between devices, send(): return lax.ppermute(x, AXES, pairs)  51.8 us
    pallas_call x2, Pallas kernels, update(): pl.pallas_call(functools.partial(update_kernel, cfg), in_specs=[vmem] * 8...  3.92 us
  transfers between devices with their start and end apart: 29, of which 6 were waited for; matrix products, arithmetic and copies ran while one was open for 2% of the time, Pallas kernels for 3%

profile of v3, /device:TPU:9, one launch (start us, length us, event | category | flops | bytes accessed | tf_op | source)
XLA Modules:
  0.0 114.0 jit_solution(2872382538964137578)
XLA Ops:
  0.6 0.8 slice_bitcast_fusion.1
  1.5 3.1 %collective-permute-start = (f32[128,128]{1,0:T(8,128)S(1)}, f32[128,128]{1,0:T(8,128)S(1)}, u32[]{:S(2)}, u32[]{:S(2)}) collective-permute-start(f32[128,128]{1,0:T(8,128)S(1)} %slice_bitcast_fusion.1), channel_id=1, source_target_pairs={{1,0},{3,2},{5,4},{7,6},{0,1},{2,3},{4,5},{6,7},{9,8},{11,10},{13,... | collective-permute-start | bytes 196616 | tf_op jit(solution)/shard_map/ppermute | solution.py:199
  4.6 1.3 %slice_bitcast_fusion.near = f32[512,512]{1,0:T(8,128)S(1)} fusion(f32[6,1,1,512,512]{4,3,2,1,0:T(8,128)} %refs_8_.3), kind=kLoop, calls=%fused_computation | loop fusion | bytes 2097152 | tf_op jit(solution)/shard_map/squeeze | solution.py:215
  5.9 3.0 %collective-permute-start.6 = (f32[512,512]{1,0:T(8,128)S(1)}, f32[512,512]{1,0:T(8,128)S(1)}, u32[]{:S(2)}, u32[]{:S(2)}) collective-permute-start(f32[512,512]{1,0:T(8,128)S(1)} %slice_bitcast_fusion.near), channel_id=1, source_target_pairs={{10,0},{11,1},{13,14}} | collective-permute-start | bytes 3145736 | tf_op jit(solution)/shard_map/ppermute | solution.py:199
  8.9 0.0 collective-permute-done
  8.9 1.7 %collective-permute-start.5 = (f32[512,512]{1,0:T(8,128)S(1)}, f32[512,512]{1,0:T(8,128)}, u32[]{:S(2)}, u32[]{:S(2)}) collective-permute-start(f32[512,512]{1,0:T(8,128)S(1)} %slice_bitcast_fusion.near), channel_id=1, source_target_pairs={{8,0},{9,1}} | collective-permute-start | bytes 3145736 | tf_op jit(solution)/shard_map/ppermute | solution.py:199
  10.6 0.7 collective-permute-start.4
  11.3 0.9 select_bitcast_fusion.1
  12.2 0.7 collective-permute-start.3
  12.9 3.2 %collective-permute-start.2 = (f32[2,128,128]{2,1,0:T(8,128)S(1)}, f32[2,128,128]{2,1,0:T(8,128)S(1)}, u32[]{:S(2)}, u32[]{:S(2)}) collective-permute-start(f32[2,128,128]{2,1,0:T(8,128)S(1)} %pad_maximum_fusion.own), channel_id=1, source_target_pairs={{4,0},{5,1},{10,14},{11,15}} | collective-permute-start | bytes 393224 | tf_op jit(solution)/shard_map/ppermute | solution.py:199
  16.0 0.0 collective-permute-done.3.g3
  16.0 0.7 collective-permute-start.1
  16.7 2.2 %collective-permute-done.2.g2 = f32[2,128,128]{2,1,0:T(8,128)S(1)} collective-permute-done((f32[2,128,128]{2,1,0:T(8,128)S(1)}, f32[2,128,128]{2,1,0:T(8,128)S(1)}, u32[]{:S(2)}, u32[]{:S(2)}) %collective-permute-start.2) | collective-permute-done | bytes 131104 | tf_op jit(solution)/shard_map/ppermute | solution.py:199
  18.9 0.0 collective-permute-done.1.g1
  18.9 4.4 %collective-permute-done.6.ly.l_even = f32[512,512]{1,0:T(8,128)S(1)} collective-permute-done((f32[512,512]{1,0:T(8,128)S(1)}, f32[512,512]{1,0:T(8,128)S(1)}, u32[]{:S(2)}, u32[]{:S(2)}) %collective-permute-start.6) | collective-permute-done | bytes 1048608 | tf_op jit(solution)/shard_map/ppermute | solution.py:199
  23.4 0.0 collective-permute-done.5.lx
  23.4 0.0 collective-permute-done.4.la.l_odd
  23.4 1.2 %solve_low.1 = (f32[128,512]{1,0:T(8,128)S(1)}, f32[128,512]{1,0:T(8,128)S(1)}, f32[128,512]{1,0:T(8,128)S(1)}) custom-call(f32[2,128,128]{2,1,0:T(8,128)S(1)} %pad_maximum_fusion.own, f32[2,128,128]{2,1,0:T(8,128)S(1)} %collective-permute-done.1.g1, f32[2,128,128]{2,1,0:T(8,128)S(1)} %collective-permute-done.2.g2, ...), custom_call_target="tpu_custom_call" | custom-call | flops 1000 | bytes 1000 | tf_op jit(solution)/shard_map/solve_low/pallas_call | solution.py:227
  24.6 0.7 collective-permute-start.10
  25.3 0.7 collective-permute-start.18
  26.0 0.7 collective-permute-start.17
  26.7 0.7 collective-permute-start.7
  27.4 0.0 collective-permute-done.10.refs_4_
  27.4 0.7 collective-permute-start.11
  28.1 0.7 collective-permute-start.8
  28.8 0.0 collective-permute-done.18.w_2
  28.8 0.0 collective-permute-done.17.w_1
  28.8 0.7 collective-permute-start.22
  29.5 1.3 %collective-permute-start.12 = (f32[128,512]{1,0:T(8,128)S(1)}, f32[128,512]{1,0:T(8,128)S(1)}, u32[]{:S(2)}, u32[]{:S(2)}) collective-permute-start(f32[128,512]{1,0:T(8,128)S(1)} %collective-permute-done.10.refs_4_), channel_id=1, source_target_pairs={{2,10},{3,11}} | collective-permute-start | bytes 786440 | tf_op jit(solution)/shard_map/ppermute | solution.py:199
  30.8 0.0 collective-permute-done.7.refs_1_
  30.8 0.7 collective-permute-start.9
  31.5 0.0 collective-permute-done.11.refs_5_
  31.5 0.7 collective-permute-start.13
  32.2 0.0 collective-permute-done.8.refs_2_
  32.2 0.7 collective-permute-start.19
  32.9 0.0 collective-permute-done.22.refs_4_
  32.9 0.7 collective-permute-start.23
  33.6 9.1 %collective-permute-done.12.refs_6_ = f32[128,512]{1,0:T(8,128)S(1)} collective-permute-done((f32[128,512]{1,0:T(8,128)S(1)}, f32[128,512]{1,0:T(8,128)S(1)}, u32[]{:S(2)}, u32[]{:S(2)}) %collective-permute-start.12) | collective-permute-done | bytes 262176 | tf_op jit(solution)/shard_map/ppermute | solution.py:199
  42.7 0.0 collective-permute-done.9.refs_3_
  42.7 0.0 collective-permute-done.13.refs_7_
  42.7 3.8 %update.2 = (f32[832,128]{1,0:T(8,128)S(1)}, f32[832,128]{1,0:T(8,128)S(1)}, f32[832,128]{1,0:T(8,128)S(1)}, f32[832,128]{1,0:T(8,128)S(1)}) custom-call(f32[128,512]{1,0:T(8,128)S(1)} %get-tuple-element.19.refs_0_, f32[128,512]{1,0:T(8,128)S(1)} %collective-permute-done.7.refs_1_, f32[128,512]{1,0:T(8,128)S(1)} %collective-permute-done.8.refs_2_, ...), custom_call_target="tpu_custom_call" | custom-call | flops 1000 | bytes 1000 | tf_op jit(solution)/shard_map/update/pallas_call | solution.py:273
  46.5 0.0 copy-start
  46.6 19.1 %collective-permute-start.14 = (f32[832,128]{1,0:T(8,128)S(1)}, f32[832,128]{1,0:T(8,128)S(1)}, u32[]{:S(2)}, u32[]{:S(2)}) collective-permute-start(f32[832,128]{1,0:T(8,128)S(1)} %get-tuple-element.22), channel_id=1, source_target_pairs={{0,2},{1,3},{8,10},{9,11},{16,18},{17,19},{24,26},{25,27},{2,4},{3... | collective-permute-start | bytes 1277960 | tf_op jit(solution)/shard_map/ppermute | solution.py:199
  65.7 0.7 collective-permute-start.20
  66.3 0.7 collective-permute-start.24
  67.0 0.0 collective-permute-done.19.refs_1_
  67.0 0.7 collective-permute-start.21
  67.7 0.0 collective-permute-done.23.refs_5_
  67.7 0.7 collective-permute-start.25
  68.4 0.0 collective-permute-done.20.refs_2_
  68.4 1.3 %collective-permute-start.15 = (f32[832,128]{1,0:T(8,128)S(1)}, f32[832,128]{1,0:T(8,128)S(1)}, u32[]{:S(2)}, u32[]{:S(2)}) collective-permute-start(f32[832,128]{1,0:T(8,128)S(1)} %get-tuple-element.23), channel_id=1, source_target_pairs={{0,4},{1,5},{8,12},{9,13},{16,20},{17,21},{24,28},{25,29},{2,6},{3... | collective-permute-start | bytes 1277960 | tf_op jit(solution)/shard_map/ppermute | solution.py:199
  69.8 0.0 collective-permute-done.24.refs_6_
  69.8 3.7 %collective-permute-start.16 = (f32[832,128]{1,0:T(8,128)S(1)}, f32[832,128]{1,0:T(8,128)S(1)}, u32[]{:S(2)}, u32[]{:S(2)}) collective-permute-start(f32[832,128]{1,0:T(8,128)S(1)} %get-tuple-element.24), channel_id=1, source_target_pairs={{0,6},{1,7},{8,14},{9,15},{16,22},{17,23},{24,30},{25,31},{2,0},{3... | collective-permute-start | bytes 1277960 | tf_op jit(solution)/shard_map/ppermute | solution.py:199
  73.5 0.1 update.3
  73.6 0.7 collective-permute-start.26
  74.3 1.3 %collective-permute-start.27 = (f32[832,128]{1,0:T(8,128)S(1)}, f32[832,128]{1,0:T(8,128)S(1)}, u32[]{:S(2)}, u32[]{:S(2)}) collective-permute-start(f32[832,128]{1,0:T(8,128)S(1)} %get-tuple-element.30), channel_id=1, source_target_pairs={{6,2},{7,3},{14,10},{15,11},{22,18},{23,19},{30,26},{31,27},{4,0},... | collective-permute-start | bytes 1277960 | tf_op jit(solution)/shard_map/ppermute | solution.py:199
  75.6 16.7 %collective-permute-done.14.refs_1_ = f32[832,128]{1,0:T(8,128)S(1)} collective-permute-done((f32[832,128]{1,0:T(8,128)S(1)}, f32[832,128]{1,0:T(8,128)S(1)}, u32[]{:S(2)}, u32[]{:S(2)}) %collective-permute-start.14) | collective-permute-done | bytes 426016 | tf_op jit(solution)/shard_map/ppermute | solution.py:199
  92.3 1.3 %collective-permute-start.28 = (f32[832,128]{1,0:T(8,128)S(1)}, f32[832,128]{1,0:T(8,128)S(1)}, u32[]{:S(2)}, u32[]{:S(2)}) collective-permute-start(f32[832,128]{1,0:T(8,128)S(1)} %get-tuple-element.31), channel_id=1, source_target_pairs={{6,4},{7,5},{14,12},{15,13},{22,20},{23,21},{30,28},{31,29},{4,2},... | collective-permute-start | bytes 1277960 | tf_op jit(solution)/shard_map/ppermute | solution.py:199
  93.6 4.5 %collective-permute-done.15.refs_2_ = f32[832,128]{1,0:T(8,128)S(1)} collective-permute-done((f32[832,128]{1,0:T(8,128)S(1)}, f32[832,128]{1,0:T(8,128)S(1)}, u32[]{:S(2)}, u32[]{:S(2)}) %collective-permute-start.15) | collective-permute-done | bytes 426016 | tf_op jit(solution)/shard_map/ppermute | solution.py:199
  98.1 0.0 collective-permute-done.16.refs_3_
  98.1 0.0 collective-permute-done.26.refs_5_
  98.1 0.0 collective-permute-done.27.refs_6_
  98.1 14.9 %collective-permute-done.28.refs_7_ = f32[832,128]{1,0:T(8,128)S(1)} collective-permute-done((f32[832,128]{1,0:T(8,128)S(1)}, f32[832,128]{1,0:T(8,128)S(1)}, u32[]{:S(2)}, u32[]{:S(2)}) %collective-permute-start.28) | collective-permute-done | bytes 426016 | tf_op jit(solution)/shard_map/ppermute | solution.py:199
  113.0 1.0 add_up.1
  (5 shorter events, 0.1 us)
Async XLA Ops:
  1.5 7.4 %collective-permute-start = (f32[128,128]{1,0:T(8,128)S(1)}, f32[128,128]{1,0:T(8,128)S(1)}, u32[]{:S(2)}, u32[]{:S(2)}) collective-permute-start(f32[128,128]{1,0:T(8,128)S(1)} %slice_bitcast_fusion.1), channel_id=1, source_target_pairs={{1,0},{3,2},{5,4},{7,6},{0,1},{2,3},{4,5},{6,7},{9,8},{11,10},{13,... | collective-permute-start | bytes 196616 | tf_op jit(solution)/shard_map/ppermute | solution.py:199
  5.9 17.5 %collective-permute-start.6 = (f32[512,512]{1,0:T(8,128)S(1)}, f32[512,512]{1,0:T(8,128)S(1)}, u32[]{:S(2)}, u32[]{:S(2)}) collective-permute-start(f32[512,512]{1,0:T(8,128)S(1)} %slice_bitcast_fusion.near), channel_id=1, source_target_pairs={{10,0},{11,1},{13,14}} | collective-permute-start | bytes 3145736 | tf_op jit(solution)/shard_map/ppermute | solution.py:199
  8.9 14.5 %collective-permute-start.5 = (f32[512,512]{1,0:T(8,128)S(1)}, f32[512,512]{1,0:T(8,128)}, u32[]{:S(2)}, u32[]{:S(2)}) collective-permute-start(f32[512,512]{1,0:T(8,128)S(1)} %slice_bitcast_fusion.near), channel_id=1, source_target_pairs={{8,0},{9,1}} | collective-permute-start | bytes 3145736 | tf_op jit(solution)/shard_map/ppermute | solution.py:199
  10.6 12.8 %collective-permute-start.4 = (f32[512,512]{1,0:T(8,128)S(1)}, f32[512,512]{1,0:T(8,128)S(1)}, u32[]{:S(2)}, u32[]{:S(2)}) collective-permute-start(f32[512,512]{1,0:T(8,128)S(1)} %slice_bitcast_fusion.near), channel_id=1, source_target_pairs={{1,0},{13,15}} | collective-permute-start | bytes 3145736 | tf_op jit(solution)/shard_map/ppermute | solution.py:199
  12.2 3.8 %collective-permute-start.3 = (f32[2,128,128]{2,1,0:T(8,128)S(1)}, f32[2,128,128]{2,1,0:T(8,128)S(1)}, u32[]{:S(2)}, u32[]{:S(2)}) collective-permute-start(f32[2,128,128]{2,1,0:T(8,128)S(1)} %pad_maximum_fusion.own), channel_id=1, source_target_pairs={{6,0},{7,1},{8,14},{9,15}} | collective-permute-start | bytes 393224 | tf_op jit(solution)/shard_map/ppermute | solution.py:199
  12.9 6.1 %collective-permute-start.2 = (f32[2,128,128]{2,1,0:T(8,128)S(1)}, f32[2,128,128]{2,1,0:T(8,128)S(1)}, u32[]{:S(2)}, u32[]{:S(2)}) collective-permute-start(f32[2,128,128]{2,1,0:T(8,128)S(1)} %pad_maximum_fusion.own), channel_id=1, source_target_pairs={{4,0},{5,1},{10,14},{11,15}} | collective-permute-start | bytes 393224 | tf_op jit(solution)/shard_map/ppermute | solution.py:199
  16.0 2.9 %collective-permute-start.1 = (f32[2,128,128]{2,1,0:T(8,128)S(1)}, f32[2,128,128]{2,1,0:T(8,128)S(1)}, u32[]{:S(2)}, u32[]{:S(2)}) collective-permute-start(f32[2,128,128]{2,1,0:T(8,128)S(1)} %pad_maximum_fusion.own), channel_id=1, source_target_pairs={{2,0},{3,1},{12,14},{13,15}} | collective-permute-start | bytes 393224 | tf_op jit(solution)/shard_map/ppermute | solution.py:199
  24.6 2.7 %collective-permute-start.10 = (f32[128,512]{1,0:T(8,128)S(1)}, f32[128,512]{1,0:T(8,128)S(1)}, u32[]{:S(2)}, u32[]{:S(2)}) collective-permute-start(f32[128,512]{1,0:T(8,128)S(1)} %get-tuple-element.20), channel_id=1, source_target_pairs={{0,2},{1,3}} | collective-permute-start | bytes 786440 | tf_op jit(solution)/shard_map/ppermute | solution.py:199
  25.3 3.4 %collective-permute-start.18 = (f32[128,512]{1,0:T(8,128)S(1)}, f32[128,512]{1,0:T(8,128)S(1)}, u32[]{:S(2)}, u32[]{:S(2)}) collective-permute-start(f32[128,512]{1,0:T(8,128)S(1)} %get-tuple-element.25), channel_id=1, source_target_pairs={{0,15},{1,14}} | collective-permute-start | bytes 786440 | tf_op jit(solution)/shard_map/ppermute | solution.py:199
  26.0 2.8 %collective-permute-start.17 = (f32[128,512]{1,0:T(8,128)S(1)}, f32[128,512]{1,0:T(8,128)S(1)}, u32[]{:S(2)}, u32[]{:S(2)}) collective-permute-start(f32[128,512]{1,0:T(8,128)S(1)} %get-tuple-element.25), channel_id=1, source_target_pairs={{0,14},{1,15}} | collective-permute-start | bytes 786440 | tf_op jit(solution)/shard_map/ppermute | solution.py:199
  26.7 4.1 %collective-permute-start.7 = (f32[128,512]{1,0:T(8,128)S(1)}, f32[128,512]{1,0:T(8,128)S(1)}, u32[]{:S(2)}, u32[]{:S(2)}) collective-permute-start(f32[128,512]{1,0:T(8,128)S(1)} %get-tuple-element.19.refs_0_), channel_id=1, source_target_pairs={{0,16},{1,17}} | collective-permute-start | bytes 786440 | tf_op jit(solution)/shard_map/ppermute | solution.py:199
  27.4 4.1 %collective-permute-start.11 = (f32[128,512]{1,0:T(8,128)S(1)}, f32[128,512]{1,0:T(8,128)S(1)}, u32[]{:S(2)}, u32[]{:S(2)}) collective-permute-start(f32[128,512]{1,0:T(8,128)S(1)} %collective-permute-done.10.refs_4_), channel_id=1, source_target_pairs={{2,18},{3,19}} | collective-permute-start | bytes 786440 | tf_op jit(solution)/shard_map/ppermute | solution.py:199
  28.1 4.1 %collective-permute-start.8 = (f32[128,512]{1,0:T(8,128)S(1)}, f32[128,512]{1,0:T(8,128)S(1)}, u32[]{:S(2)}, u32[]{:S(2)}) collective-permute-start(f32[128,512]{1,0:T(8,128)S(1)} %get-tuple-element.19.refs_0_), channel_id=1, source_target_pairs={{0,8},{1,9}} | collective-permute-start | bytes 786440 | tf_op jit(solution)/shard_map/ppermute | solution.py:199
  28.8 4.1 %collective-permute-start.22 = (f32[128,512]{1,0:T(8,128)S(1)}, f32[128,512]{1,0:T(8,128)S(1)}, u32[]{:S(2)}, u32[]{:S(2)}) collective-permute-start(f32[128,512]{1,0:T(8,128)S(1)} %get-tuple-element.27), channel_id=1, source_target_pairs={{14,12},{15,13}} | collective-permute-start | bytes 786440 | tf_op jit(solution)/shard_map/ppermute | solution.py:199
  29.5 13.2 %collective-permute-start.12 = (f32[128,512]{1,0:T(8,128)S(1)}, f32[128,512]{1,0:T(8,128)S(1)}, u32[]{:S(2)}, u32[]{:S(2)}) collective-permute-start(f32[128,512]{1,0:T(8,128)S(1)} %collective-permute-done.10.refs_4_), channel_id=1, source_target_pairs={{2,10},{3,11}} | collective-permute-start | bytes 786440 | tf_op jit(solution)/shard_map/ppermute | solution.py:199
  30.8 11.9 %collective-permute-start.9 = (f32[128,512]{1,0:T(8,128)S(1)}, f32[128,512]{1,0:T(8,128)S(1)}, u32[]{:S(2)}, u32[]{:S(2)}) collective-permute-start(f32[128,512]{1,0:T(8,128)S(1)} %collective-permute-done.7.refs_1_), channel_id=1, source_target_pairs={{16,24},{17,25}} | collective-permute-start | bytes 786440 | tf_op jit(solution)/shard_map/ppermute | solution.py:199
  31.5 11.2 %collective-permute-start.13 = (f32[128,512]{1,0:T(8,128)S(1)}, f32[128,512]{1,0:T(8,128)S(1)}, u32[]{:S(2)}, u32[]{:S(2)}) collective-permute-start(f32[128,512]{1,0:T(8,128)S(1)} %collective-permute-done.11.refs_5_), channel_id=1, source_target_pairs={{18,26},{19,27}} | collective-permute-start | bytes 786440 | tf_op jit(solution)/shard_map/ppermute | solution.py:199
  32.2 34.8 %collective-permute-start.19 = (f32[128,512]{1,0:T(8,128)S(1)}, f32[128,512]{1,0:T(8,128)S(1)}, u32[]{:S(2)}, u32[]{:S(2)}) collective-permute-start(f32[128,512]{1,0:T(8,128)S(1)} %get-tuple-element.26.refs_0_), channel_id=1, source_target_pairs={{14,30},{15,31}} | collective-permute-start | bytes 786440 | tf_op jit(solution)/shard_map/ppermute | solution.py:199
  32.9 34.8 %collective-permute-start.23 = (f32[128,512]{1,0:T(8,128)S(1)}, f32[128,512]{1,0:T(8,128)S(1)}, u32[]{:S(2)}, u32[]{:S(2)}) collective-permute-start(f32[128,512]{1,0:T(8,128)S(1)} %collective-permute-done.22.refs_4_), channel_id=1, source_target_pairs={{12,28},{13,29}} | collective-permute-start | bytes 786440 | tf_op jit(solution)/shard_map/ppermute | solution.py:199
  46.5 66.4 %copy-start = (f32[6,1,1,128,128]{4,3,2,1,0:T(8,128)S(1)}, f32[6,1,1,128,128]{4,3,2,1,0:T(8,128)}, u32[]{:S(2)}) copy-start(f32[6,1,1,128,128]{4,3,2,1,0:T(8,128)} %param.4) | copy-start | bytes 1179652
  46.6 45.7 %collective-permute-start.14 = (f32[832,128]{1,0:T(8,128)S(1)}, f32[832,128]{1,0:T(8,128)S(1)}, u32[]{:S(2)}, u32[]{:S(2)}) collective-permute-start(f32[832,128]{1,0:T(8,128)S(1)} %get-tuple-element.22), channel_id=1, source_target_pairs={{0,2},{1,3},{8,10},{9,11},{16,18},{17,19},{24,26},{25,27},{2,4},{3... | collective-permute-start | bytes 1277960 | tf_op jit(solution)/shard_map/ppermute | solution.py:199
  65.7 2.8 %collective-permute-start.20 = (f32[128,512]{1,0:T(8,128)S(1)}, f32[128,512]{1,0:T(8,128)S(1)}, u32[]{:S(2)}, u32[]{:S(2)}) collective-permute-start(f32[128,512]{1,0:T(8,128)S(1)} %get-tuple-element.26.refs_0_), channel_id=1, source_target_pairs={{14,6},{15,7}} | collective-permute-start | bytes 786440 | tf_op jit(solution)/shard_map/ppermute | solution.py:199
  66.3 3.4 %collective-permute-start.24 = (f32[128,512]{1,0:T(8,128)S(1)}, f32[128,512]{1,0:T(8,128)S(1)}, u32[]{:S(2)}, u32[]{:S(2)}) collective-permute-start(f32[128,512]{1,0:T(8,128)S(1)} %collective-permute-done.22.refs_4_), channel_id=1, source_target_pairs={{12,4},{13,5}} | collective-permute-start | bytes 786440 | tf_op jit(solution)/shard_map/ppermute | solution.py:199
  67.0 6.5 %collective-permute-start.21 = (f32[128,512]{1,0:T(8,128)S(1)}, f32[128,512]{1,0:T(8,128)S(1)}, u32[]{:S(2)}, u32[]{:S(2)}) collective-permute-start(f32[128,512]{1,0:T(8,128)S(1)} %collective-permute-done.19.refs_1_), channel_id=1, source_target_pairs={{30,22},{31,23}} | collective-permute-start | bytes 786440 | tf_op jit(solution)/shard_map/ppermute | solution.py:199
  67.7 5.8 %collective-permute-start.25 = (f32[128,512]{1,0:T(8,128)S(1)}, f32[128,512]{1,0:T(8,128)S(1)}, u32[]{:S(2)}, u32[]{:S(2)}) collective-permute-start(f32[128,512]{1,0:T(8,128)S(1)} %collective-permute-done.23.refs_5_), channel_id=1, source_target_pairs={{28,20},{29,21}} | collective-permute-start | bytes 786440 | tf_op jit(solution)/shard_map/ppermute | solution.py:199
  68.4 29.7 %collective-permute-start.15 = (f32[832,128]{1,0:T(8,128)S(1)}, f32[832,128]{1,0:T(8,128)S(1)}, u32[]{:S(2)}, u32[]{:S(2)}) collective-permute-start(f32[832,128]{1,0:T(8,128)S(1)} %get-tuple-element.23), channel_id=1, source_target_pairs={{0,4},{1,5},{8,12},{9,13},{16,20},{17,21},{24,28},{25,29},{2,6},{3... | collective-permute-start | bytes 1277960 | tf_op jit(solution)/shard_map/ppermute | solution.py:199
  69.8 28.3 %collective-permute-start.16 = (f32[832,128]{1,0:T(8,128)S(1)}, f32[832,128]{1,0:T(8,128)S(1)}, u32[]{:S(2)}, u32[]{:S(2)}) collective-permute-start(f32[832,128]{1,0:T(8,128)S(1)} %get-tuple-element.24), channel_id=1, source_target_pairs={{0,6},{1,7},{8,14},{9,15},{16,22},{17,23},{24,30},{25,31},{2,0},{3... | collective-permute-start | bytes 1277960 | tf_op jit(solution)/shard_map/ppermute | solution.py:199
  73.6 24.5 %collective-permute-start.26 = (f32[832,128]{1,0:T(8,128)S(1)}, f32[832,128]{1,0:T(8,128)S(1)}, u32[]{:S(2)}, u32[]{:S(2)}) collective-permute-start(f32[832,128]{1,0:T(8,128)S(1)} %get-tuple-element.29), channel_id=1, source_target_pairs={{6,0},{7,1},{14,8},{15,9},{22,16},{23,17},{30,24},{31,25},{4,6},{5... | collective-permute-start | bytes 1277960 | tf_op jit(solution)/shard_map/ppermute | solution.py:199
  74.3 23.8 %collective-permute-start.27 = (f32[832,128]{1,0:T(8,128)S(1)}, f32[832,128]{1,0:T(8,128)S(1)}, u32[]{:S(2)}, u32[]{:S(2)}) collective-permute-start(f32[832,128]{1,0:T(8,128)S(1)} %get-tuple-element.30), channel_id=1, source_target_pairs={{6,2},{7,3},{14,10},{15,11},{22,18},{23,19},{30,26},{31,27},{4,0},... | collective-permute-start | bytes 1277960 | tf_op jit(solution)/shard_map/ppermute | solution.py:199
  92.3 20.7 %collective-permute-start.28 = (f32[832,128]{1,0:T(8,128)S(1)}, f32[832,128]{1,0:T(8,128)S(1)}, u32[]{:S(2)}, u32[]{:S(2)}) collective-permute-start(f32[832,128]{1,0:T(8,128)S(1)} %get-tuple-element.31), channel_id=1, source_target_pairs={{6,4},{7,5},{14,12},{15,13},{22,20},{23,21},{30,28},{31,29},{4,2},... | collective-permute-start | bytes 1277960 | tf_op jit(solution)/shard_map/ppermute | solution.py:199

commit v4 on v3

--- a/solution.py
+++ b/solution.py
@@ -92,7 +92,7 @@
 
 
 def update_kernel(cfg, *refs):
-    steps, groups, row_count, share, have, members, blocks = cfg
+    steps, groups, row_count, share, have, members, blocks, slots = cfg
     ways, panel = refs[:8], refs[8]
     outs, (tiles, s, full, sems) = refs[9: 9 + steps], refs[9 + steps:]
     quarter = full.shape[2] // steps
@@ -130,43 +130,52 @@
             block_id = (r * row_count + row) * groups + group
             keep = (block_id > member).astype(F32)
             full[r] = product(s[...], tiles[r]) * keep
-        for offset in range(steps):
-            to = lax.rem(member + offset, steps)
+        for slot in range(steps):
+            ends, nexts = slots
+            to = jnp.where(member == members[0], ends[slot], nexts[slot])
             columns = pl.ds(pl.multiple_of(to * quarter, quarter), quarter)
             for r in range(blocks):
-                outs[offset][pl.ds(r * quarter, quarter), :] = full[r, :, columns]
+                outs[slot][pl.ds(r * quarter, quarter), :] = full[r, :, columns]
             full[blocks, :, :quarter] = s[:, columns].T
             rows = pl.ds(pl.multiple_of(group * share, share), share)
-            outs[offset][blocks * quarter:, :] = full[blocks, rows, :quarter]
-
-
-def last_kernel(steps, groups, rhs, *refs):
-    sources, (solved, out) = refs[: 2 * steps], refs[2 * steps:]
-    lows, highs = sources[:steps], sources[steps:]
+            outs[slot][blocks * quarter:, :] = full[blocks, rows, :quarter]
+
+
+def join_kernel(cfg, mine, theirs, out):
+    groups, share, at = cfg
+    last = mine.shape[0] - share
+
+    @pl.when(lax.axis_index("col") // groups == at)
+    def _():
+        out[:last, :] = mine[:last, :] + theirs[:last, :]
+        out[pl.ds(last, share), :] = mine[last:, :]
+        out[pl.ds(last + share, share), :] = theirs[last:, :]
+
+
+def last_kernel(groups, rhs, *refs):
+    lows, highs, (solved, out) = refs[:5], refs[5:10], refs[10:]
     blocks, quarter = rhs.shape[0], rhs.shape[1]
+    last, share = blocks * quarter, solved.shape[1]
     member = lax.axis_index("col") // groups
 
-    def finish(own):
-        for r in range(blocks):
-            rows = pl.ds(r * quarter, quarter)
-            total = own[rows, :]
-            for part in lows[1:] + highs[1:]:
-                total = total + part[rows, :]
-            out[r] = rhs[r] - total.T
-        last = blocks * quarter
-        solved[member] = own[last:, :]
-        for offset in range(1, steps):
-            solved[lax.rem(member + steps - offset, steps)] = (
-                lows[offset][last:, :] + highs[offset][last:, :]
-            )
-
-    @pl.when(member < steps // 2)
-    def _():
-        finish(lows[0])
-
-    @pl.when(member >= steps // 2)
-    def _():
-        finish(highs[0])
+    def finish(at, parts, joined, joined_members):
+        @pl.when(member == at)
+        def _():
+            for r in range(blocks):
+                rows = pl.ds(r * quarter, quarter)
+                total = functools.reduce(jnp.add, [part[rows, :] for part, _ in parts])
+                if joined is not None:
+                    total = total + joined[rows, :]
+                out[r] = rhs[r] - total.T
+            for part, k in parts:
+                solved[k] = part[last:, :]
+            for i, k in enumerate(joined_members):
+                solved[k] = joined[pl.ds(last + i * share, share), :]
+
+    finish(0, [(lows[0], 0), (lows[2], 1)], highs[4], (2, 3))
+    finish(1, [(lows[0], 1), (lows[3], 0), (highs[1], 2), (highs[2], 3)], None, ())
+    finish(2, [(highs[0], 2), (highs[3], 3), (lows[1], 1), (lows[2], 0)], None, ())
+    finish(3, [(highs[0], 3), (highs[2], 2)], lows[4], (1, 0))
 
 
 def on_device(factor, rhs, inverses):
@@ -216,11 +225,12 @@
     ly = send(near, [(line(2, 1), low_homes[0]), (line(3, 1), low_homes[1]), (line(3, 2), high_homes[0])])
     later = lax.optimization_barrier((near, other))[0]
     la = send(later, [(line(1, 0), low_homes[0]), (line(3, 2), high_homes[1])])
-    lx = send(later, [(line(2, 0), low_homes[0]), (line(3, 0), low_homes[1])])
     gathered = [
         send(both, [(line(g, j), line(g, 0)) for g in (0, 1)] + [(line(g, top - j), line(g, top)) for g in (2, 3)])
         for j in range(1, steps)
     ]
+    later = lax.optimization_barrier((near, *gathered))[0]
+    lx = send(later, [(line(2, 0), low_homes[0]), (line(3, 0), low_homes[1])])
 
     vector = jax.ShapeDtypeStruct((nrhs, width), F32)
     two = [VMEM((2, width, width), F32), pltpu.SemaphoreType.DMA((2,))]
@@ -269,7 +279,12 @@
     def update(ways, lines, members):
         part = jax.ShapeDtypeStruct((blocks * quarter + share, nrhs), F32)
         have = [(g // groups, g % groups) for g in lines]
-        cfg = (steps, groups, row_count, share, have, members, blocks)
+        if members[0] == 0:
+            ends, nexts = (0, 3, 2, 1), (1, 2, 0, 3)
+        else:
+            ends, nexts = (3, 0, 1, 2), (2, 1, 3, 0)
+        slots = (ends, nexts)
+        cfg = (steps, groups, row_count, share, have, members, blocks, slots)
         parts = pl.pallas_call(
             functools.partial(update_kernel, cfg),
             in_specs=[vmem] * 8 + [hbm],
@@ -285,14 +300,26 @@
             cost_estimate=CHEAP,
             name="update",
         )(*ways, held_factor)
-        got = [parts[0]]
-        for offset in range(1, steps):
-            pairs = [
-                (dev(r, m, g), dev(r, (m + offset) % steps, g))
-                for m in members for r in range(row_count) for g in range(groups)
-            ]
-            got.append(send(parts[offset], pairs))
-        return got
+        across = [(r, g) for r in range(row_count) for g in range(groups)]
+
+        def route(hops):
+            return [(dev(r, a, g), dev(r, b, g)) for a, b in hops for r, g in across]
+
+        end, near_end = members
+        part_a = send(parts[1], route([(end, near_end), (near_end, nexts[1])]))
+        part_b = send(parts[2], route([(end, ends[2]), (near_end, nexts[2])]))
+        part_c = send(parts[3], route([(end, near_end)]))
+        joint = jax.ShapeDtypeStruct((blocks * quarter + 2 * share, nrhs), F32)
+        joined = pl.pallas_call(
+            functools.partial(join_kernel, (groups, share, near_end)),
+            in_specs=[vmem] * 2,
+            out_specs=vmem,
+            out_shape=joint,
+            compiler_params=PARAMS,
+            cost_estimate=CHEAP,
+            name="join",
+        )(parts[3], part_a)
+        return parts[0], part_a, part_b, part_c, send(joined, route([(near_end, ends[1])]))
 
     def both_planes(outer, inner, at, away, lines):
         moved = send(inner, [(line(g, at), line(g, away)) for g in lines])
@@ -302,8 +329,8 @@
     highs = update(both_planes(s_3, s_2, top, top - 1, (2, 3)), (2, 3), (top, top - 1))
 
     solved, remaining = pl.pallas_call(
-        functools.partial(last_kernel, steps, groups),
-        in_specs=[vmem] * (1 + 2 * steps),
+        functools.partial(last_kernel, groups),
+        in_specs=[vmem] * 11,
         out_specs=[vmem] * 2,
         out_shape=[
             jax.ShapeDtypeStruct((steps, share, nrhs), F32),

time: 115 us -> 117 us (1.017)
  the two profiles are of different devices: /device:TPU:9 before, /device:TPU:0 now
where the time goes in v4:
time: 117 us; the launch traced here: 115 us
  starting transfers between devices  67.6 us (58%)
  waiting for transfers between devices  35 us (30%)
  Pallas kernels  7.89 us (7%)
  local copies, waits for them, and re-layouts  2.15 us (2%)
    ppermute x31, starting transfers between devices, send(): return lax.ppermute(x, AXES, pairs)  67.6 us
    ppermute x31, waiting for transfers between devices, send(): return lax.ppermute(x, AXES, pairs)  35 us
    pallas_call x2, Pallas kernels, update(): pl.pallas_call(functools.partial(update_kernel, cfg), in_specs=[vmem] * 8...  3.94 us
    pallas_call x1, Pallas kernels, on_device(): pl.pallas_call(functools.partial(low_kernel, low_homes, col_count), in_sp...  2.94 us
  transfers between devices with their start and end apart: 31, of which 11 were waited for; matrix products, arithmetic and copies ran while one was open for 1% of the time, Pallas kernels for 3%

profile of v4, /device:TPU:0, one launch (start us, length us, event | category | flops | bytes accessed | tf_op | source)
XLA Modules:
  0.0 114.6 jit_solution(6280828826933567332)
XLA Ops:
  0.6 0.8 slice_bitcast_fusion.1
  1.5 4.9 %collective-permute-start = (f32[128,128]{1,0:T(8,128)S(1)}, f32[128,128]{1,0:T(8,128)S(1)}, u32[]{:S(2)}, u32[]{:S(2)}) collective-permute-start(f32[128,128]{1,0:T(8,128)S(1)} %slice_bitcast_fusion.1), channel_id=1, source_target_pairs={{1,0},{3,2},{5,4},{7,6},{0,1},{2,3},{4,5},{6,7},{9,8},{11,10},{13,... | collective-permute-start | bytes 196616 | tf_op jit(solution)/shard_map/ppermute | solution.py:208
  6.4 2.2 %collective-permute-done = f32[128,128]{1,0:T(8,128)S(1)} collective-permute-done((f32[128,128]{1,0:T(8,128)S(1)}, f32[128,128]{1,0:T(8,128)S(1)}, u32[]{:S(2)}, u32[]{:S(2)}) %collective-permute-start) | collective-permute-done | bytes 65568 | tf_op jit(solution)/shard_map/ppermute | solution.py:208
  8.6 0.9 select_bitcast_fusion.1
  9.4 1.3 %collective-permute-start.3 = (f32[2,128,128]{2,1,0:T(8,128)S(1)}, f32[2,128,128]{2,1,0:T(8,128)S(1)}, u32[]{:S(2)}, u32[]{:S(2)}) collective-permute-start(f32[2,128,128]{2,1,0:T(8,128)S(1)} %pad_maximum_fusion.own), channel_id=1, source_target_pairs={{6,0},{7,1},{8,14},{9,15}} | collective-permute-start | bytes 393224 | tf_op jit(solution)/shard_map/ppermute | solution.py:208
  10.7 1.3 %collective-permute-start.2 = (f32[2,128,128]{2,1,0:T(8,128)S(1)}, f32[2,128,128]{2,1,0:T(8,128)S(1)}, u32[]{:S(2)}, u32[]{:S(2)}) collective-permute-start(f32[2,128,128]{2,1,0:T(8,128)S(1)} %pad_maximum_fusion.own), channel_id=1, source_target_pairs={{4,0},{5,1},{10,14},{11,15}} | collective-permute-start | bytes 393224 | tf_op jit(solution)/shard_map/ppermute | solution.py:208
  12.0 1.3 %collective-permute-start.1 = (f32[2,128,128]{2,1,0:T(8,128)S(1)}, f32[2,128,128]{2,1,0:T(8,128)S(1)}, u32[]{:S(2)}, u32[]{:S(2)}) collective-permute-start(f32[2,128,128]{2,1,0:T(8,128)S(1)} %pad_maximum_fusion.own), channel_id=1, source_target_pairs={{2,0},{3,1},{12,14},{13,15}} | collective-permute-start | bytes 393224 | tf_op jit(solution)/shard_map/ppermute | solution.py:208
  13.3 1.3 %slice_bitcast_fusion.near = f32[512,512]{1,0:T(8,128)S(1)} fusion(f32[6,1,1,512,512]{4,3,2,1,0:T(8,128)} %refs_8_.3), kind=kLoop, calls=%fused_computation | loop fusion | bytes 2097152 | tf_op jit(solution)/shard_map/squeeze | solution.py:224
  14.6 1.3 %collective-permute-start.6 = (f32[512,512]{1,0:T(8,128)S(1)}, f32[512,512]{1,0:T(8,128)S(1)}, u32[]{:S(2)}, u32[]{:S(2)}) collective-permute-start(f32[512,512]{1,0:T(8,128)S(1)} %slice_bitcast_fusion.near), channel_id=1, source_target_pairs={{10,0},{11,1},{13,14}} | collective-permute-start | bytes 3145736 | tf_op jit(solution)/shard_map/ppermute | solution.py:208
  15.9 1.3 %collective-permute-start.4 = (f32[512,512]{1,0:T(8,128)S(1)}, f32[512,512]{1,0:T(8,128)S(1)}, u32[]{:S(2)}, u32[]{:S(2)}) collective-permute-start(f32[512,512]{1,0:T(8,128)S(1)} %slice_bitcast_fusion.near), channel_id=1, source_target_pairs={{1,0},{13,15}} | collective-permute-start | bytes 3145736 | tf_op jit(solution)/shard_map/ppermute | solution.py:208
  17.2 1.0 collective-permute-done.3.g3
  18.3 1.3 %collective-permute-done.2.g2 = f32[2,128,128]{2,1,0:T(8,128)S(1)} collective-permute-done((f32[2,128,128]{2,1,0:T(8,128)S(1)}, f32[2,128,128]{2,1,0:T(8,128)S(1)}, u32[]{:S(2)}, u32[]{:S(2)}) %collective-permute-start.2) | collective-permute-done | bytes 131104 | tf_op jit(solution)/shard_map/ppermute | solution.py:208
  19.6 2.4 %collective-permute-done.1.g1 = f32[2,128,128]{2,1,0:T(8,128)S(1)} collective-permute-done((f32[2,128,128]{2,1,0:T(8,128)S(1)}, f32[2,128,128]{2,1,0:T(8,128)S(1)}, u32[]{:S(2)}, u32[]{:S(2)}) %collective-permute-start.1) | collective-permute-done | bytes 131104 | tf_op jit(solution)/shard_map/ppermute | solution.py:208
  22.0 1.3 %collective-permute-start.5 = (f32[512,512]{1,0:T(8,128)S(1)}, f32[512,512]{1,0:T(8,128)S(1)}, u32[]{:S(2)}, u32[]{:S(2)}) collective-permute-start(f32[512,512]{1,0:T(8,128)S(1)} %slice_bitcast_fusion.near), channel_id=1, source_target_pairs={{8,0},{9,1}} | collective-permute-start | bytes 3145736 | tf_op jit(solution)/shard_map/ppermute | solution.py:208
  23.3 8.9 %collective-permute-done.6.ly.l_even = f32[512,512]{1,0:T(8,128)S(1)} collective-permute-done((f32[512,512]{1,0:T(8,128)S(1)}, f32[512,512]{1,0:T(8,128)S(1)}, u32[]{:S(2)}, u32[]{:S(2)}) %collective-permute-start.6) | collective-permute-done | bytes 1048608 | tf_op jit(solution)/shard_map/ppermute | solution.py:208
  32.2 0.5 collective-permute-done.4.la.l_odd
  32.6 0.0 collective-permute-done.5.lx
  32.6 2.9 %solve_low.1 = (f32[128,512]{1,0:T(8,128)S(1)}, f32[128,512]{1,0:T(8,128)S(1)}, f32[128,512]{1,0:T(8,128)S(1)}) custom-call(f32[2,128,128]{2,1,0:T(8,128)S(1)} %pad_maximum_fusion.own, f32[2,128,128]{2,1,0:T(8,128)S(1)} %collective-permute-done.1.g1, f32[2,128,128]{2,1,0:T(8,128)S(1)} %collective-permute-done.2.g2, ...), custom_call_target="tpu_custom_call" | custom-call | flops 1000 | bytes 1000 | tf_op jit(solution)/shard_map/solve_low/pallas_call | solution.py:237
  35.6 14.7 %collective-permute-start.19 = (f32[128,512]{1,0:T(8,128)S(1)}, f32[128,512]{1,0:T(8,128)S(1)}, u32[]{:S(2)}, u32[]{:S(2)}) collective-permute-start(f32[128,512]{1,0:T(8,128)S(1)} %get-tuple-element.27), channel_id=1, source_target_pairs={{0,15},{1,14}} | collective-permute-start | bytes 786440 | tf_op jit(solution)/shard_map/ppermute | solution.py:208
  50.3 1.3 %collective-permute-start.18 = (f32[128,512]{1,0:T(8,128)S(1)}, f32[128,512]{1,0:T(8,128)S(1)}, u32[]{:S(2)}, u32[]{:S(2)}) collective-permute-start(f32[128,512]{1,0:T(8,128)S(1)} %get-tuple-element.27), channel_id=1, source_target_pairs={{0,14},{1,15}} | collective-permute-start | bytes 786440 | tf_op jit(solution)/shard_map/ppermute | solution.py:208
  51.7 1.3 %collective-permute-start.10 = (f32[128,512]{1,0:T(8,128)S(1)}, f32[128,512]{1,0:T(8,128)S(1)}, u32[]{:S(2)}, u32[]{:S(2)}) collective-permute-start(f32[128,512]{1,0:T(8,128)S(1)} %get-tuple-element.22), channel_id=1, source_target_pairs={{0,2},{1,3}} | collective-permute-start | bytes 786440 | tf_op jit(solution)/shard_map/ppermute | solution.py:208
  53.0 1.3 %collective-permute-start.8 = (f32[128,512]{1,0:T(8,128)S(1)}, f32[128,512]{1,0:T(8,128)S(1)}, u32[]{:S(2)}, u32[]{:S(2)}) collective-permute-start(f32[128,512]{1,0:T(8,128)S(1)} %get-tuple-element.21.refs_0_), channel_id=1, source_target_pairs={{0,8},{1,9}} | collective-permute-start | bytes 786440 | tf_op jit(solution)/shard_map/ppermute | solution.py:208
  54.3 1.3 %collective-permute-start.7 = (f32[128,512]{1,0:T(8,128)S(1)}, f32[128,512]{1,0:T(8,128)S(1)}, u32[]{:S(2)}, u32[]{:S(2)}) collective-permute-start(f32[128,512]{1,0:T(8,128)S(1)} %get-tuple-element.21.refs_0_), channel_id=1, source_target_pairs={{0,16},{1,17}} | collective-permute-start | bytes 786440 | tf_op jit(solution)/shard_map/ppermute | solution.py:208
  55.6 0.0 collective-permute-done.19.w_2
  55.6 1.4 %collective-permute-done.18.w_1 = f32[128,512]{1,0:T(8,128)S(1)} collective-permute-done((f32[128,512]{1,0:T(8,128)S(1)}, f32[128,512]{1,0:T(8,128)S(1)}, u32[]{:S(2)}, u32[]{:S(2)}) %collective-permute-start.18) | collective-permute-done | bytes 262176 | tf_op jit(solution)/shard_map/ppermute | solution.py:208
  57.0 0.7 collective-permute-start.23
  57.7 2.1 %collective-permute-done.10.refs_4_ = f32[128,512]{1,0:T(8,128)S(1)} collective-permute-done((f32[128,512]{1,0:T(8,128)S(1)}, f32[128,512]{1,0:T(8,128)S(1)}, u32[]{:S(2)}, u32[]{:S(2)}) %collective-permute-start.10) | collective-permute-done | bytes 262176 | tf_op jit(solution)/shard_map/ppermute | solution.py:208
  59.8 0.7 collective-permute-start.11
  60.5 0.7 collective-permute-start.12
  61.2 0.0 collective-permute-done.8.refs_2_
  61.2 0.7 collective-permute-start.20
  61.9 0.0 collective-permute-done.7.refs_1_
  61.9 0.7 collective-permute-start.9
  62.6 0.0 collective-permute-done.23.refs_4_
  62.6 0.7 collective-permute-start.24
  63.3 0.0 collective-permute-done.11.refs_5_
  63.3 0.7 collective-permute-start.13
  64.0 0.7 collective-permute-start.21
  64.7 0.0 collective-permute-done.20.refs_1_
  64.7 0.7 collective-permute-start.25
  65.4 0.7 collective-permute-start.22
  66.1 0.0 collective-permute-done.24.refs_5_
  66.1 0.7 collective-permute-start.26
  66.8 3.9 %update.2 = (f32[832,128]{1,0:T(8,128)S(1)}, f32[832,128]{1,0:T(8,128)S(1)}, f32[832,128]{1,0:T(8,128)S(1)}, f32[832,128]{1,0:T(8,128)S(1)}) custom-call(f32[128,512]{1,0:T(8,128)S(1)} %get-tuple-element.21.refs_0_, f32[128,512]{1,0:T(8,128)S(1)} %collective-permute-done.7.refs_1_, f32[128,512]{1,0:T(8,128)S(1)} %collective-permute-done.8.refs_2_, ...), custom_call_target="tpu_custom_call" | custom-call | flops 1000 | bytes 1000 | tf_op jit(solution)/shard_map/update/pallas_call | solution.py:288
  70.6 0.0 copy-start
  70.6 6.2 %collective-permute-start.14 = (f32[832,128]{1,0:T(8,128)S(1)}, f32[832,128]{1,0:T(8,128)S(1)}, u32[]{:S(2)}, u32[]{:S(2)}) collective-permute-start(f32[832,128]{1,0:T(8,128)S(1)} %get-tuple-element.24), channel_id=1, source_target_pairs={{0,2},{1,3},{8,10},{9,11},{16,18},{17,19},{24,26},{25,27},{2,4},{3... | collective-permute-start | bytes 1277960 | tf_op jit(solution)/shard_map/ppermute | solution.py:208
  76.9 0.0 collective-permute-done.25.refs_6_
  76.9 0.0 collective-permute-done.22.refs_3_
  76.9 0.1 update.3
  77.0 0.7 collective-permute-start.27
  77.7 4.6 %collective-permute-start.15 = (f32[832,128]{1,0:T(8,128)S(1)}, f32[832,128]{1,0:T(8,128)S(1)}, u32[]{:S(2)}, u32[]{:S(2)}) collective-permute-start(f32[832,128]{1,0:T(8,128)S(1)} %get-tuple-element.25), channel_id=1, source_target_pairs={{0,4},{1,5},{8,12},{9,13},{16,20},{17,21},{24,28},{25,29},{2,0},{3... | collective-permute-start | bytes 1277960 | tf_op jit(solution)/shard_map/ppermute | solution.py:208
  82.3 2.6 %collective-permute-done.14.theirs.refs_1_ = f32[832,128]{1,0:T(8,128)S(1)} collective-permute-done((f32[832,128]{1,0:T(8,128)S(1)}, f32[832,128]{1,0:T(8,128)S(1)}, u32[]{:S(2)}, u32[]{:S(2)}) %collective-permute-start.14) | collective-permute-done | bytes 426016 | tf_op jit(solution)/shard_map/ppermute | solution.py:208
  84.9 0.7 collective-permute-start.17
  85.6 1.3 %collective-permute-start.30 = (f32[896,128]{1,0:T(8,128)S(1)}, f32[896,128]{1,0:T(8,128)S(1)}, u32[]{:S(2)}, u32[]{:S(2)}) collective-permute-start(f32[896,128]{1,0:T(8,128)S(1)} %join.3), channel_id=1, source_target_pairs={{4,0},{5,1},{12,8},{13,9},{20,16},{21,17},{28,24},{29,25}} | collective-permute-start | bytes 1376264 | tf_op jit(solution)/shard_map/ppermute | solution.py:208
  86.9 12.7 %collective-permute-start.16 = (f32[832,128]{1,0:T(8,128)S(1)}, f32[832,128]{1,0:T(8,128)S(1)}, u32[]{:S(2)}, u32[]{:S(2)}) collective-permute-start(f32[832,128]{1,0:T(8,128)S(1)} %get-tuple-element.26.mine), channel_id=1, source_target_pairs={{0,2},{1,3},{8,10},{9,11},{16,18},{17,19},{24,26},{25,27}} | collective-permute-start | bytes 1277960 | tf_op jit(solution)/shard_map/ppermute | solution.py:208
  99.6 0.7 collective-permute-start.28
  100.3 0.0 collective-permute-done.15.refs_2_
  100.3 0.7 collective-permute-start.29
  101.0 4.2 %collective-permute-done.16.refs_3_ = f32[832,128]{1,0:T(8,128)S(1)} collective-permute-done((f32[832,128]{1,0:T(8,128)S(1)}, f32[832,128]{1,0:T(8,128)S(1)}, u32[]{:S(2)}, u32[]{:S(2)}) %collective-permute-start.16) | collective-permute-done | bytes 426016 | tf_op jit(solution)/shard_map/ppermute | solution.py:208
  105.2 0.0 collective-permute-done.28.refs_7_
  105.2 0.0 collective-permute-done.29.refs_8_
  105.2 0.0 collective-permute-done.17.refs_4_
  105.2 8.4 %collective-permute-done.30.refs_9_ = f32[896,128]{1,0:T(8,128)S(1)} collective-permute-done((f32[896,128]{1,0:T(8,128)S(1)}, f32[896,128]{1,0:T(8,128)S(1)}, u32[]{:S(2)}, u32[]{:S(2)}) %collective-permute-start.30) | collective-permute-done | bytes 458784 | tf_op jit(solution)/shard_map/ppermute | solution.py:208
  113.6 1.0 add_up.1
  (11 shorter events, 0.1 us)
Async XLA Ops:
  1.5 7.1 %collective-permute-start = (f32[128,128]{1,0:T(8,128)S(1)}, f32[128,128]{1,0:T(8,128)S(1)}, u32[]{:S(2)}, u32[]{:S(2)}) collective-permute-start(f32[128,128]{1,0:T(8,128)S(1)} %slice_bitcast_fusion.1), channel_id=1, source_target_pairs={{1,0},{3,2},{5,4},{7,6},{0,1},{2,3},{4,5},{6,7},{9,8},{11,10},{13,... | collective-permute-start | bytes 196616 | tf_op jit(solution)/shard_map/ppermute | solution.py:208
  9.4 8.8 %collective-permute-start.3 = (f32[2,128,128]{2,1,0:T(8,128)S(1)}, f32[2,128,128]{2,1,0:T(8,128)S(1)}, u32[]{:S(2)}, u32[]{:S(2)}) collective-permute-start(f32[2,128,128]{2,1,0:T(8,128)S(1)} %pad_maximum_fusion.own), channel_id=1, source_target_pairs={{6,0},{7,1},{8,14},{9,15}} | collective-permute-start | bytes 393224 | tf_op jit(solution)/shard_map/ppermute | solution.py:208
  10.7 8.9 %collective-permute-start.2 = (f32[2,128,128]{2,1,0:T(8,128)S(1)}, f32[2,128,128]{2,1,0:T(8,128)S(1)}, u32[]{:S(2)}, u32[]{:S(2)}) collective-permute-start(f32[2,128,128]{2,1,0:T(8,128)S(1)} %pad_maximum_fusion.own), channel_id=1, source_target_pairs={{4,0},{5,1},{10,14},{11,15}} | collective-permute-start | bytes 393224 | tf_op jit(solution)/shard_map/ppermute | solution.py:208
  12.0 9.9 %collective-permute-start.1 = (f32[2,128,128]{2,1,0:T(8,128)S(1)}, f32[2,128,128]{2,1,0:T(8,128)S(1)}, u32[]{:S(2)}, u32[]{:S(2)}) collective-permute-start(f32[2,128,128]{2,1,0:T(8,128)S(1)} %pad_maximum_fusion.own), channel_id=1, source_target_pairs={{2,0},{3,1},{12,14},{13,15}} | collective-permute-start | bytes 393224 | tf_op jit(solution)/shard_map/ppermute | solution.py:208
  14.6 17.5 %collective-permute-start.6 = (f32[512,512]{1,0:T(8,128)S(1)}, f32[512,512]{1,0:T(8,128)S(1)}, u32[]{:S(2)}, u32[]{:S(2)}) collective-permute-start(f32[512,512]{1,0:T(8,128)S(1)} %slice_bitcast_fusion.near), channel_id=1, source_target_pairs={{10,0},{11,1},{13,14}} | collective-permute-start | bytes 3145736 | tf_op jit(solution)/shard_map/ppermute | solution.py:208
  15.9 16.7 %collective-permute-start.4 = (f32[512,512]{1,0:T(8,128)S(1)}, f32[512,512]{1,0:T(8,128)S(1)}, u32[]{:S(2)}, u32[]{:S(2)}) collective-permute-start(f32[512,512]{1,0:T(8,128)S(1)} %slice_bitcast_fusion.near), channel_id=1, source_target_pairs={{1,0},{13,15}} | collective-permute-start | bytes 3145736 | tf_op jit(solution)/shard_map/ppermute | solution.py:208
  22.0 10.6 %collective-permute-start.5 = (f32[512,512]{1,0:T(8,128)S(1)}, f32[512,512]{1,0:T(8,128)S(1)}, u32[]{:S(2)}, u32[]{:S(2)}) collective-permute-start(f32[512,512]{1,0:T(8,128)S(1)} %slice_bitcast_fusion.near), channel_id=1, source_target_pairs={{8,0},{9,1}} | collective-permute-start | bytes 3145736 | tf_op jit(solution)/shard_map/ppermute | solution.py:208
  35.6 20.0 %collective-permute-start.19 = (f32[128,512]{1,0:T(8,128)S(1)}, f32[128,512]{1,0:T(8,128)S(1)}, u32[]{:S(2)}, u32[]{:S(2)}) collective-permute-start(f32[128,512]{1,0:T(8,128)S(1)} %get-tuple-element.27), channel_id=1, source_target_pairs={{0,15},{1,14}} | collective-permute-start | bytes 786440 | tf_op jit(solution)/shard_map/ppermute | solution.py:208
  50.3 6.7 %collective-permute-start.18 = (f32[128,512]{1,0:T(8,128)S(1)}, f32[128,512]{1,0:T(8,128)S(1)}, u32[]{:S(2)}, u32[]{:S(2)}) collective-permute-start(f32[128,512]{1,0:T(8,128)S(1)} %get-tuple-element.27), channel_id=1, source_target_pairs={{0,14},{1,15}} | collective-permute-start | bytes 786440 | tf_op jit(solution)/shard_map/ppermute | solution.py:208
  51.7 8.2 %collective-permute-start.10 = (f32[128,512]{1,0:T(8,128)S(1)}, f32[128,512]{1,0:T(8,128)S(1)}, u32[]{:S(2)}, u32[]{:S(2)}) collective-permute-start(f32[128,512]{1,0:T(8,128)S(1)} %get-tuple-element.22), channel_id=1, source_target_pairs={{0,2},{1,3}} | collective-permute-start | bytes 786440 | tf_op jit(solution)/shard_map/ppermute | solution.py:208
  53.0 8.2 %collective-permute-start.8 = (f32[128,512]{1,0:T(8,128)S(1)}, f32[128,512]{1,0:T(8,128)S(1)}, u32[]{:S(2)}, u32[]{:S(2)}) collective-permute-start(f32[128,512]{1,0:T(8,128)S(1)} %get-tuple-element.21.refs_0_), channel_id=1, source_target_pairs={{0,8},{1,9}} | collective-permute-start | bytes 786440 | tf_op jit(solution)/shard_map/ppermute | solution.py:208
  54.3 7.6 %collective-permute-start.7 = (f32[128,512]{1,0:T(8,128)S(1)}, f32[128,512]{1,0:T(8,128)S(1)}, u32[]{:S(2)}, u32[]{:S(2)}) collective-permute-start(f32[128,512]{1,0:T(8,128)S(1)} %get-tuple-element.21.refs_0_), channel_id=1, source_target_pairs={{0,16},{1,17}} | collective-permute-start | bytes 786440 | tf_op jit(solution)/shard_map/ppermute | solution.py:208
  57.0 5.5 %collective-permute-start.23 = (f32[128,512]{1,0:T(8,128)S(1)}, f32[128,512]{1,0:T(8,128)S(1)}, u32[]{:S(2)}, u32[]{:S(2)}) collective-permute-start(f32[128,512]{1,0:T(8,128)S(1)} %get-tuple-element.29), channel_id=1, source_target_pairs={{14,12},{15,13}} | collective-permute-start | bytes 786440 | tf_op jit(solution)/shard_map/ppermute | solution.py:208
  59.8 3.4 %collective-permute-start.11 = (f32[128,512]{1,0:T(8,128)S(1)}, f32[128,512]{1,0:T(8,128)S(1)}, u32[]{:S(2)}, u32[]{:S(2)}) collective-permute-start(f32[128,512]{1,0:T(8,128)S(1)} %collective-permute-done.10.refs_4_), channel_id=1, source_target_pairs={{2,18},{3,19}} | collective-permute-start | bytes 786440 | tf_op jit(solution)/shard_map/ppermute | solution.py:208
  60.5 3.5 %collective-permute-start.12 = (f32[128,512]{1,0:T(8,128)S(1)}, f32[128,512]{1,0:T(8,128)S(1)}, u32[]{:S(2)}, u32[]{:S(2)}) collective-permute-start(f32[128,512]{1,0:T(8,128)S(1)} %collective-permute-done.10.refs_4_), channel_id=1, source_target_pairs={{2,10},{3,11}} | collective-permute-start | bytes 786440 | tf_op jit(solution)/shard_map/ppermute | solution.py:208
  61.2 3.5 %collective-permute-start.20 = (f32[128,512]{1,0:T(8,128)S(1)}, f32[128,512]{1,0:T(8,128)S(1)}, u32[]{:S(2)}, u32[]{:S(2)}) collective-permute-start(f32[128,512]{1,0:T(8,128)S(1)} %get-tuple-element.28.refs_0_), channel_id=1, source_target_pairs={{14,30},{15,31}} | collective-permute-start | bytes 786440 | tf_op jit(solution)/shard_map/ppermute | solution.py:208
  61.9 3.5 %collective-permute-start.9 = (f32[128,512]{1,0:T(8,128)S(1)}, f32[128,512]{1,0:T(8,128)S(1)}, u32[]{:S(2)}, u32[]{:S(2)}) collective-permute-start(f32[128,512]{1,0:T(8,128)S(1)} %collective-permute-done.7.refs_1_), channel_id=1, source_target_pairs={{16,24},{17,25}} | collective-permute-start | bytes 786440 | tf_op jit(solution)/shard_map/ppermute | solution.py:208
  62.6 3.5 %collective-permute-start.24 = (f32[128,512]{1,0:T(8,128)S(1)}, f32[128,512]{1,0:T(8,128)S(1)}, u32[]{:S(2)}, u32[]{:S(2)}) collective-permute-start(f32[128,512]{1,0:T(8,128)S(1)} %collective-permute-done.23.refs_4_), channel_id=1, source_target_pairs={{12,28},{13,29}} | collective-permute-start | bytes 786440 | tf_op jit(solution)/shard_map/ppermute | solution.py:208
  63.3 3.5 %collective-permute-start.13 = (f32[128,512]{1,0:T(8,128)S(1)}, f32[128,512]{1,0:T(8,128)S(1)}, u32[]{:S(2)}, u32[]{:S(2)}) collective-permute-start(f32[128,512]{1,0:T(8,128)S(1)} %collective-permute-done.11.refs_5_), channel_id=1, source_target_pairs={{18,26},{19,27}} | collective-permute-start | bytes 786440 | tf_op jit(solution)/shard_map/ppermute | solution.py:208
  64.0 12.9 %collective-permute-start.21 = (f32[128,512]{1,0:T(8,128)S(1)}, f32[128,512]{1,0:T(8,128)S(1)}, u32[]{:S(2)}, u32[]{:S(2)}) collective-permute-start(f32[128,512]{1,0:T(8,128)S(1)} %get-tuple-element.28.refs_0_), channel_id=1, source_target_pairs={{14,6},{15,7}} | collective-permute-start | bytes 786440 | tf_op jit(solution)/shard_map/ppermute | solution.py:208
  64.7 12.2 %collective-permute-start.25 = (f32[128,512]{1,0:T(8,128)S(1)}, f32[128,512]{1,0:T(8,128)S(1)}, u32[]{:S(2)}, u32[]{:S(2)}) collective-permute-start(f32[128,512]{1,0:T(8,128)S(1)} %collective-permute-done.23.refs_4_), channel_id=1, source_target_pairs={{12,4},{13,5}} | collective-permute-start | bytes 786440 | tf_op jit(solution)/shard_map/ppermute | solution.py:208
  65.4 11.5 %collective-permute-start.22 = (f32[128,512]{1,0:T(8,128)S(1)}, f32[128,512]{1,0:T(8,128)S(1)}, u32[]{:S(2)}, u32[]{:S(2)}) collective-permute-start(f32[128,512]{1,0:T(8,128)S(1)} %collective-permute-done.20.refs_1_), channel_id=1, source_target_pairs={{30,22},{31,23}} | collective-permute-start | bytes 786440 | tf_op jit(solution)/shard_map/ppermute | solution.py:208
  66.1 10.8 %collective-permute-start.26 = (f32[128,512]{1,0:T(8,128)S(1)}, f32[128,512]{1,0:T(8,128)S(1)}, u32[]{:S(2)}, u32[]{:S(2)}) collective-permute-start(f32[128,512]{1,0:T(8,128)S(1)} %collective-permute-done.24.refs_5_), channel_id=1, source_target_pairs={{28,20},{29,21}} | collective-permute-start | bytes 786440 | tf_op jit(solution)/shard_map/ppermute | solution.py:208
  70.6 43.0 %copy-start = (f32[6,1,1,128,128]{4,3,2,1,0:T(8,128)S(1)}, f32[6,1,1,128,128]{4,3,2,1,0:T(8,128)}, u32[]{:S(2)}) copy-start(f32[6,1,1,128,128]{4,3,2,1,0:T(8,128)} %param.4) | copy-start | bytes 1179652
  70.6 14.3 %collective-permute-start.14 = (f32[832,128]{1,0:T(8,128)S(1)}, f32[832,128]{1,0:T(8,128)S(1)}, u32[]{:S(2)}, u32[]{:S(2)}) collective-permute-start(f32[832,128]{1,0:T(8,128)S(1)} %get-tuple-element.24), channel_id=1, source_target_pairs={{0,2},{1,3},{8,10},{9,11},{16,18},{17,19},{24,26},{25,27},{2,4},{3... | collective-permute-start | bytes 1277960 | tf_op jit(solution)/shard_map/ppermute | solution.py:208
  77.0 8.6 %collective-permute-start.27 = (f32[832,128]{1,0:T(8,128)S(1)}, f32[832,128]{1,0:T(8,128)S(1)}, u32[]{:S(2)}, u32[]{:S(2)}) collective-permute-start(f32[832,128]{1,0:T(8,128)S(1)} %get-tuple-element.31), channel_id=1, source_target_pairs={{6,4},{7,5},{14,12},{15,13},{22,20},{23,21},{30,28},{31,29},{4,2},... | collective-permute-start | bytes 1277960 | tf_op jit(solution)/shard_map/ppermute | solution.py:208
  77.7 22.6 %collective-permute-start.15 = (f32[832,128]{1,0:T(8,128)S(1)}, f32[832,128]{1,0:T(8,128)S(1)}, u32[]{:S(2)}, u32[]{:S(2)}) collective-permute-start(f32[832,128]{1,0:T(8,128)S(1)} %get-tuple-element.25), channel_id=1, source_target_pairs={{0,4},{1,5},{8,12},{9,13},{16,20},{17,21},{24,28},{25,29},{2,0},{3... | collective-permute-start | bytes 1277960 | tf_op jit(solution)/shard_map/ppermute | solution.py:208
  84.9 20.4 %collective-permute-start.17 = (f32[896,128]{1,0:T(8,128)S(1)}, f32[896,128]{1,0:T(8,128)S(1)}, u32[]{:S(2)}, u32[]{:S(2)}) collective-permute-start(f32[896,128]{1,0:T(8,128)S(1)} %join.2), channel_id=1, source_target_pairs={{2,6},{3,7},{10,14},{11,15},{18,22},{19,23},{26,30},{27,31}} | collective-permute-start | bytes 1376264 | tf_op jit(solution)/shard_map/ppermute | solution.py:208
  85.6 28.0 %collective-permute-start.30 = (f32[896,128]{1,0:T(8,128)S(1)}, f32[896,128]{1,0:T(8,128)S(1)}, u32[]{:S(2)}, u32[]{:S(2)}) collective-permute-start(f32[896,128]{1,0:T(8,128)S(1)} %join.3), channel_id=1, source_target_pairs={{4,0},{5,1},{12,8},{13,9},{20,16},{21,17},{28,24},{29,25}} | collective-permute-start | bytes 1376264 | tf_op jit(solution)/shard_map/ppermute | solution.py:208
  86.9 18.3 %collective-permute-start.16 = (f32[832,128]{1,0:T(8,128)S(1)}, f32[832,128]{1,0:T(8,128)S(1)}, u32[]{:S(2)}, u32[]{:S(2)}) collective-permute-start(f32[832,128]{1,0:T(8,128)S(1)} %get-tuple-element.26.mine), channel_id=1, source_target_pairs={{0,2},{1,3},{8,10},{9,11},{16,18},{17,19},{24,26},{25,27}} | collective-permute-start | bytes 1277960 | tf_op jit(solution)/shard_map/ppermute | solution.py:208
  99.6 5.6 %collective-permute-start.28 = (f32[832,128]{1,0:T(8,128)S(1)}, f32[832,128]{1,0:T(8,128)S(1)}, u32[]{:S(2)}, u32[]{:S(2)}) collective-permute-start(f32[832,128]{1,0:T(8,128)S(1)} %get-tuple-element.32), channel_id=1, source_target_pairs={{6,2},{7,3},{14,10},{15,11},{22,18},{23,19},{30,26},{31,27},{4,6},... | collective-permute-start | bytes 1277960 | tf_op jit(solution)/shard_map/ppermute | solution.py:208
  100.3 4.9 %collective-permute-start.29 = (f32[832,128]{1,0:T(8,128)S(1)}, f32[832,128]{1,0:T(8,128)S(1)}, u32[]{:S(2)}, u32[]{:S(2)}) collective-permute-start(f32[832,128]{1,0:T(8,128)S(1)} %get-tuple-element.33.mine), channel_id=1, source_target_pairs={{6,4},{7,5},{14,12},{15,13},{22,20},{23,21},{30,28},{31,29}} | collective-permute-start | bytes 1277960 | tf_op jit(solution)/shard_map/ppermute | solution.py:208

commit v5 on v4

--- a/solution.py
+++ b/solution.py
@@ -66,47 +66,47 @@
         work(near)
 
 
-def high_kernel(homes, col_count, own, g1, g2, g3, l_even, l_odd, w_1, w_2, inverses, s_a, s_b, inv, sem):
+def high_kernel(homes, col_count, own, g1, g2, g3, block, w_1, w_2, inverses, s, inv, sem):
     me = position(col_count)
-
-    def work(block, w_even, w_odd):
-        copies = [pltpu.make_async_copy(inverses.at[2 + i], inv.at[i], sem.at[i]) for i in range(2)]
+    copies = [pltpu.make_async_copy(inverses.at[2 + i], inv.at[i], sem.at[i]) for i in range(2)]
+
+    @pl.when(me == homes[0])
+    def _():
+        copies[0].start()
+        right = stacked((g2, g1, own, g3), 0) - w_2[...]
+        copies[0].wait()
+        s[...] = product(right, inv[0], True)
+
+    @pl.when(me == homes[1])
+    def _():
         for copy in copies:
             copy.start()
         pieces = (g3, g2, g1, own)
-        right = stacked(pieces, 0) - w_even[...]
+        right = stacked(pieces, 0) - w_1[...]
         copies[0].wait()
         first = product(right, inv[0], True)
-        s_a[...] = first
-        right = stacked(pieces, 1) - w_odd[...] - product(first, block[...])
+        right = stacked(pieces, 1) - w_2[...] - product(first, block[...])
         copies[1].wait()
-        s_b[...] = product(right, inv[1], True)
-
-    @pl.when(me == homes[0])
-    def _():
-        work(l_even, w_1, w_2)
-
-    @pl.when(me == homes[1])
-    def _():
-        work(l_odd, w_2, w_1)
+        s[...] = product(right, inv[1], True)
 
 
 def update_kernel(cfg, *refs):
-    steps, groups, row_count, share, have, members, blocks, slots = cfg
-    ways, panel = refs[:8], refs[8]
-    outs, (tiles, s, full, sems) = refs[9: 9 + steps], refs[9 + steps:]
+    steps, groups, row_count, share, homes, members, blocks, slots = cfg
+    ways, panel = refs[:4], refs[4]
+    outs, (tiles, s, full, sems) = refs[5: 5 + steps], refs[5 + steps:]
     quarter = full.shape[2] // steps
     row = lax.axis_index("row")
     col = lax.axis_index("col")
     member = col // groups
     group = col % groups
 
-    def among(spots):
-        return functools.reduce(jnp.logical_or, [(row == r) & (group == g) for r, g in spots])
-
-    core = have[0][0] % 2
-    first, first_twin = among(have), among([(r ^ 1, g) for r, g in have])
-    same = lax.rem(row, 2) == core
+    def among(flip):
+        return functools.reduce(jnp.logical_or, [
+            (member == m) & (row == (r ^ flip)) & (group == g) for m in members for r, g in homes[m]
+        ])
+
+    first, first_twin = among(0), among(1)
+    same = lax.rem(row, 2) == homes[members[0]][0][0] % 2
     roles = (
         first, same & jnp.logical_not(first), first_twin,
         jnp.logical_not(same) & jnp.logical_not(first_twin),
@@ -119,11 +119,10 @@
         ]
         for copy in copies:
             copy.start()
-        for m, plane in enumerate(members):
-            for way, role in enumerate(roles):
-                @pl.when((member == plane) & role)
-                def _(src=ways[4 * m + way]):
-                    s[...] = src[...]
+        for way, role in zip(ways, roles):
+            @pl.when(role)
+            def _(src=way):
+                s[...] = src[...]
 
         for r in range(blocks):
             copies[r].wait()
@@ -202,7 +201,7 @@
         return dev(g // groups, mem, g % groups)
 
     low_homes = (line(0, 0), line(1, 0))
-    high_homes = (line(2, top), line(3, top))
+    high_homes = (line(2, top - 1), line(3, top))
 
     def send(x, pairs):
         return lax.ppermute(x, AXES, pairs)
@@ -218,19 +217,23 @@
     held_inverses = pltpu.with_memory_space_constraint(inverses, pltpu.HBM)
 
     mine = rhs[0, 0, 0]
-    other = send(mine, [(line(g ^ 1, m), line(g, m)) for g in range(4) for m in range(steps)])
+    near = factor[0, 0, 0]
+    lx = send(near, [(line(2, 0), low_homes[0]), (line(3, 0), low_homes[1])])
+    ly = send(near, [(line(2, 1), low_homes[0]), (line(3, 1), low_homes[1])])
+    other = send(mine, [(line(g ^ 1, m), line(g, m)) for g in (0, 1, 3) for m in range(steps)])
     even = group % 2 == 0
     both = jnp.stack([jnp.where(even, mine, other), jnp.where(even, other, mine)])
-    near = factor[0, 0, 0]
-    ly = send(near, [(line(2, 1), low_homes[0]), (line(3, 1), low_homes[1]), (line(3, 2), high_homes[0])])
+    both, lx = lax.optimization_barrier((both, lx))
     later = lax.optimization_barrier((near, other))[0]
     la = send(later, [(line(1, 0), low_homes[0]), (line(3, 2), high_homes[1])])
     gathered = [
-        send(both, [(line(g, j), line(g, 0)) for g in (0, 1)] + [(line(g, top - j), line(g, top)) for g in (2, 3)])
+        send(
+            both,
+            [(line(g, j), line(g, 0)) for g in (0, 1)]
+            + [(line(2, (top - 1 - j) % steps), high_homes[0]), (line(3, top - j), high_homes[1])],
+        )
         for j in range(1, steps)
     ]
-    later = lax.optimization_barrier((near, *gathered))[0]
-    lx = send(later, [(line(2, 0), low_homes[0]), (line(3, 0), low_homes[1])])
 
     vector = jax.ShapeDtypeStruct((nrhs, width), F32)
     two = [VMEM((2, width, width), F32), pltpu.SemaphoreType.DMA((2,))]
@@ -244,50 +247,65 @@
         cost_estimate=CHEAP,
         name="solve_low",
     )(both, *gathered, near, la, lx, ly, held_inverses)
-    w_1 = send(w, [(low_homes[0], high_homes[0]), (low_homes[1], high_homes[1])])
-    w_2 = send(w, [(low_homes[0], high_homes[1]), (low_homes[1], high_homes[0])])
-    s_2, s_3 = pl.pallas_call(
+    w_1 = send(w, [(low_homes[0], high_homes[1])])
+    w_2 = send(w, [(low_homes[1], high_homes[1]), (low_homes[0], high_homes[0])])
+    s_high = pl.pallas_call(
         functools.partial(high_kernel, high_homes, col_count),
-        in_specs=[vmem] * 8 + [hbm],
-        out_specs=[vmem] * 2,
-        out_shape=[vector] * 2,
+        in_specs=[vmem] * 7 + [hbm],
+        out_specs=vmem,
+        out_shape=vector,
         scratch_shapes=two,
         compiler_params=PARAMS,
         cost_estimate=CHEAP,
         name="solve_high",
-    )(both, *gathered, ly, la, w_1, w_2, held_inverses)
-
-    def spread(s, plane, lines):
-        have = [(g // groups, g % groups) for g in lines]
-        todo = [
-            (r, g) for r in range(row_count) for g in range(groups)
-            if r % 2 == have[0][0] % 2 and (r, g) not in have
-        ]
-        spots, far = list(have), None
-        while todo:
-            new, todo = todo[: len(spots)], todo[len(spots):]
-            pairs = [(dev(a[0], plane, a[1]), dev(b[0], plane, b[1])) for a, b in zip(spots, new)]
-            if far is None:
-                far = send(s, pairs)
-            else:
-                held = chosen([(0, dev(r, plane, g)) for r, g in have], s, far)
-                far = chosen(pairs, send(held, pairs), far)
-            spots = spots + new
-        twins = [(dev(r, plane, g), dev(r ^ 1, plane, g)) for r, g in spots]
-        return s, far, send(s, twins[: len(have)]), send(far, twins[len(have):])
-
-    def update(ways, lines, members):
+    )(both, *gathered, la, w_1, w_2, held_inverses)
+
+    def spread(s, homes):
+        have = {k: list(homes[k]) for k in homes}
+        todo = {
+            k: [
+                (r, g) for r in range(row_count) for g in range(groups)
+                if r % 2 == homes[k][0][0] % 2 and (r, g) not in homes[k]
+            ]
+            for k in homes
+        }
+        fan = 1 if all(len(spots) > 1 for spots in homes.values()) else 3
+        firsts = [(0, dev(r, k, g)) for k in homes for r, g in homes[k]]
+        far = None
+        while any(todo.values()):
+            held = s if far is None else chosen(firsts, s, far)
+            rounds = [[] for _ in range(fan)]
+            for k in homes:
+                spots = list(have[k])
+                for pairs in rounds:
+                    for a in spots:
+                        if todo[k]:
+                            b = todo[k].pop()
+                            have[k].append(b)
+                            pairs.append((dev(a[0], k, a[1]), dev(b[0], k, b[1])))
+            for pairs in rounds:
+                if pairs:
+                    got = send(held, pairs)
+                    far = got if far is None else chosen(pairs, got, far)
+        twins = {
+            k: [(dev(r, k, g), dev(r ^ 1, k, g)) for r, g in have[k]] for k in homes
+        }
+        near_twins = [pair for k in homes for pair in twins[k][: len(homes[k])]]
+        far_twins = [pair for k in homes for pair in twins[k][len(homes[k]):]]
+        return s, far, send(s, near_twins), send(far, far_twins)
+
+    def update(s, homes, members):
         part = jax.ShapeDtypeStruct((blocks * quarter + share, nrhs), F32)
-        have = [(g // groups, g % groups) for g in lines]
+        ways = spread(s, homes)
         if members[0] == 0:
             ends, nexts = (0, 3, 2, 1), (1, 2, 0, 3)
         else:
             ends, nexts = (3, 0, 1, 2), (2, 1, 3, 0)
         slots = (ends, nexts)
-        cfg = (steps, groups, row_count, share, have, members, blocks, slots)
+        cfg = (steps, groups, row_count, share, homes, members, blocks, slots)
         parts = pl.pallas_call(
             functools.partial(update_kernel, cfg),
-            in_specs=[vmem] * 8 + [hbm],
+            in_specs=[vmem] * 4 + [hbm],
             out_specs=[vmem] * steps,
             out_shape=[part] * steps,
             scratch_shapes=[
@@ -321,12 +339,11 @@
         )(parts[3], part_a)
         return parts[0], part_a, part_b, part_c, send(joined, route([(near_end, ends[1])]))
 
-    def both_planes(outer, inner, at, away, lines):
-        moved = send(inner, [(line(g, at), line(g, away)) for g in lines])
-        return spread(outer, at, lines) + spread(moved, away, lines)
-
-    lows = update(both_planes(s_0, s_1, 0, 1, (0, 1)), (0, 1), (0, 1))
-    highs = update(both_planes(s_3, s_2, top, top - 1, (2, 3)), (2, 3), (top, top - 1))
+    spots = [(g // groups, g % groups) for g in range(4)]
+    moved = send(s_1, [(line(g, 0), line(g, 1)) for g in (0, 1)])
+    s_low = jnp.where(member == 0, s_0, moved)
+    lows = update(s_low, {0: spots[:2], 1: spots[:2]}, (0, 1))
+    highs = update(s_high, {top: [spots[3]], top - 1: [spots[2]]}, (top, top - 1))
 
     solved, remaining = pl.pallas_call(
         functools.partial(last_kernel, groups),

time: 117 us -> 102 us (0.87); the launches traced: 115 us -> 101 us
  starting transfers between devices: 67.6 us -> 52.3 us
  Pallas kernels: 7.89 us -> 9.83 us
    ppermute x31 -> x26, starting transfers between devices: 67.6 us -> 52.3 us  [send(): return lax.ppermute(x, AXES, pairs)]
    pallas_call x1, Pallas kernels: 2.94 us -> 4.86 us  [on_device(): pl.pallas_call(functools.partial(low_kernel, low_homes, col_count), in_sp...]
    ppermute x31 -> x26, waiting for transfers between devices: 35 us -> 35 us  [send(): return lax.ppermute(x, AXES, pairs)]
  transfers between devices with their start and end apart: 31 -> 26, of which waited for: 11 -> 8; matrix products, arithmetic and copies ran while one was open for 1% -> 2% of each run, Pallas kernels for 3% -> 4%
where the time goes in v5:
time: 102 us; the launch traced here: 101 us
  starting transfers between devices  52.3 us (51%)
  waiting for transfers between devices  35 us (34%)
  Pallas kernels  9.83 us (10%)
  local copies, waits for them, and re-layouts  2.15 us (2%)
  between operations  1.09 us (1%)
    ppermute x26, starting transfers between devices, send(): return lax.ppermute(x, AXES, pairs)  52.3 us
    ppermute x26, waiting for transfers between devices, send(): return lax.ppermute(x, AXES, pairs)  35 us
    pallas_call x1, Pallas kernels, on_device(): pl.pallas_call(functools.partial(low_kernel, low_homes, col_count), in_sp...  4.86 us
    pallas_call x2, Pallas kernels, update(): pl.pallas_call(functools.partial(update_kernel, cfg), in_specs=[vmem] * 4...  3.94 us
  transfers between devices with their start and end apart: 26, of which 8 were waited for; matrix products, arithmetic and copies ran while one was open for 2% of the time, Pallas kernels for 4%

profile of v5, /device:TPU:0, one launch (start us, length us, event | category | flops | bytes accessed | tf_op | source)
XLA Modules:
  0.0 101.3 jit_solution(10220987025254408041)
XLA Ops:
  0.6 1.3 %slice_bitcast_fusion.near = f32[512,512]{1,0:T(8,128)S(1)} fusion(f32[6,1,1,512,512]{4,3,2,1,0:T(8,128)} %refs_4_.3), kind=kLoop, calls=%fused_computation | loop fusion | bytes 2097152 | tf_op jit(solution)/shard_map/squeeze | solution.py:220
  1.9 1.3 %collective-permute-start.1 = (f32[512,512]{1,0:T(8,128)S(1)}, f32[512,512]{1,0:T(8,128)S(1)}, u32[]{:S(2)}, u32[]{:S(2)}) collective-permute-start(f32[512,512]{1,0:T(8,128)S(1)} %slice_bitcast_fusion.near), channel_id=1, source_target_pairs={{8,0},{9,1}} | collective-permute-start | bytes 3145736 | tf_op jit(solution)/shard_map/ppermute | solution.py:207
  3.2 0.8 slice_bitcast_fusion.1
  4.1 4.9 %collective-permute-start = (f32[128,128]{1,0:T(8,128)S(1)}, f32[128,128]{1,0:T(8,128)S(1)}, u32[]{:S(2)}, u32[]{:S(2)}) collective-permute-start(f32[128,128]{1,0:T(8,128)S(1)} %slice_bitcast_fusion.1), channel_id=1, source_target_pairs={{1,0},{3,2},{5,4},{7,6},{0,1},{2,3},{4,5},{6,7},{8,9},{10,11},{12,... | collective-permute-start | bytes 196616 | tf_op jit(solution)/shard_map/ppermute | solution.py:207
  8.9 1.3 %collective-permute-start.6 = (f32[512,512]{1,0:T(8,128)S(1)}, f32[512,512]{1,0:T(8,128)}, u32[]{:S(2)}, u32[]{:S(2)}) collective-permute-start(f32[512,512]{1,0:T(8,128)S(1)} %slice_bitcast_fusion.near), channel_id=1, source_target_pairs={{10,0},{11,1}} | collective-permute-start | bytes 3145736 | tf_op jit(solution)/shard_map/ppermute | solution.py:207
  10.2 0.9 collective-permute-done
  11.2 1.3 %collective-permute-start.5 = (f32[512,512]{1,0:T(8,128)S(1)}, f32[512,512]{1,0:T(8,128)S(1)}, u32[]{:S(2)}, u32[]{:S(2)}) collective-permute-start(f32[512,512]{1,0:T(8,128)S(1)} %slice_bitcast_fusion.near), channel_id=1, source_target_pairs={{1,0},{13,15}} | collective-permute-start | bytes 3145736 | tf_op jit(solution)/shard_map/ppermute | solution.py:207
  12.5 0.9 select_bitcast_fusion.1
  13.4 0.0 collective-permute-done.1.lx
  13.4 1.3 %collective-permute-start.4 = (f32[2,128,128]{2,1,0:T(8,128)S(1)}, f32[2,128,128]{2,1,0:T(8,128)S(1)}, u32[]{:S(2)}, u32[]{:S(2)}) collective-permute-start(f32[2,128,128]{2,1,0:T(8,128)S(1)} %pad_maximum_fusion.own), channel_id=1, source_target_pairs={{6,0},{7,1},{14,12},{9,15}} | collective-permute-start | bytes 393224 | tf_op jit(solution)/shard_map/ppermute | solution.py:207
  14.7 1.3 %collective-permute-start.3 = (f32[2,128,128]{2,1,0:T(8,128)S(1)}, f32[2,128,128]{2,1,0:T(8,128)S(1)}, u32[]{:S(2)}, u32[]{:S(2)}) collective-permute-start(f32[2,128,128]{2,1,0:T(8,128)S(1)} %pad_maximum_fusion.own), channel_id=1, source_target_pairs={{4,0},{5,1},{8,12},{11,15}} | collective-permute-start | bytes 393224 | tf_op jit(solution)/shard_map/ppermute | solution.py:207
  16.0 1.3 %collective-permute-start.2 = (f32[2,128,128]{2,1,0:T(8,128)S(1)}, f32[2,128,128]{2,1,0:T(8,128)S(1)}, u32[]{:S(2)}, u32[]{:S(2)}) collective-permute-start(f32[2,128,128]{2,1,0:T(8,128)S(1)} %pad_maximum_fusion.own), channel_id=1, source_target_pairs={{2,0},{3,1},{10,12},{13,15}} | collective-permute-start | bytes 393224 | tf_op jit(solution)/shard_map/ppermute | solution.py:207
  17.3 12.1 %collective-permute-done.6.ly = f32[512,512]{1,0:T(8,128)} collective-permute-done((f32[512,512]{1,0:T(8,128)S(1)}, f32[512,512]{1,0:T(8,128)}, u32[]{:S(2)}, u32[]{:S(2)}) %collective-permute-start.6) | collective-permute-done | bytes 1048608 | tf_op jit(solution)/shard_map/ppermute | solution.py:207
  29.4 0.0 collective-permute-done.5.la.block
  29.4 0.0 collective-permute-done.4.g3
  29.4 0.0 collective-permute-done.3.g2
  29.4 0.0 collective-permute-done.2.g1
  29.4 4.9 %solve_low.1 = (f32[128,512]{1,0:T(8,128)S(1)}, f32[128,512]{1,0:T(8,128)S(1)}, f32[128,512]{1,0:T(8,128)}) custom-call(f32[2,128,128]{2,1,0:T(8,128)S(1)} %pad_maximum_fusion.own, f32[2,128,128]{2,1,0:T(8,128)S(1)} %collective-permute-done.2.g1, f32[2,128,128]{2,1,0:T(8,128)S(1)} %collective-permute-done.3.g2, ...), custom_call_target="tpu_custom_call" | custom-call | flops 1000 | bytes 1000 | tf_op jit(solution)/shard_map/solve_low/pallas_call | solution.py:240
  34.3 1.3 %collective-permute-start.16 = (f32[128,512]{1,0:T(8,128)S(1)}, f32[128,512]{1,0:T(8,128)S(1)}, u32[]{:S(2)}, u32[]{:S(2)}) collective-permute-start(f32[128,512]{1,0:T(8,128)S(1)} %get-tuple-element.27), channel_id=1, source_target_pairs={{1,15},{0,12}} | collective-permute-start | bytes 786440 | tf_op jit(solution)/shard_map/ppermute | solution.py:207
  35.6 3.3 %collective-permute-start.15 = (f32[128,512]{1,0:T(8,128)S(1)}, f32[128,512]{1,0:T(8,128)S(1)}, u32[]{:S(2)}, u32[]{:S(2)}) collective-permute-start(f32[128,512]{1,0:T(8,128)S(1)} %get-tuple-element.27), channel_id=1, source_target_pairs={{0,15}} | collective-permute-start | bytes 786440 | tf_op jit(solution)/shard_map/ppermute | solution.py:207
  38.9 1.3 %collective-permute-start.7 = (f32[128,512]{1,0:T(8,128)}, f32[128,512]{1,0:T(8,128)S(1)}, u32[]{:S(2)}, u32[]{:S(2)}) collective-permute-start(f32[128,512]{1,0:T(8,128)} %get-tuple-element.22), channel_id=1, source_target_pairs={{0,2},{1,3}} | collective-permute-start | bytes 786440 | tf_op jit(solution)/shard_map/ppermute | solution.py:207
  40.2 0.0 collective-permute-done.16.w_2
  40.2 2.5 %collective-permute-done.15.w_1 = f32[128,512]{1,0:T(8,128)S(1)} collective-permute-done((f32[128,512]{1,0:T(8,128)S(1)}, f32[128,512]{1,0:T(8,128)S(1)}, u32[]{:S(2)}, u32[]{:S(2)}) %collective-permute-start.15) | collective-permute-done | bytes 262176 | tf_op jit(solution)/shard_map/ppermute | solution.py:207
  42.8 0.7 collective-permute-start.19
  43.4 0.7 collective-permute-start.18
  44.1 0.7 collective-permute-start.17
  44.8 0.8 collective-permute-done.7
  45.7 1.3 %collective-permute-start.8 = (f32[128,512]{1,0:T(8,128)S(1)}, f32[128,512]{1,0:T(8,128)S(1)}, u32[]{:S(2)}, u32[]{:S(2)}) collective-permute-start(f32[128,512]{1,0:T(8,128)S(1)} %broadcast_select_fusion.refs_0_), channel_id=1, source_target_pairs={{0,17},{1,16},{2,19},{3,18}} | collective-permute-start | bytes 786440 | tf_op jit(solution)/shard_map/ppermute | solution.py:207
  47.0 0.7 collective-permute-start.20
  47.7 0.0 collective-permute-done.19
  47.7 0.0 collective-permute-done.18
  47.7 0.0 collective-permute-done.17
  47.7 0.1 select_select_fusion.refs_1_
  47.8 0.7 collective-permute-start.21
  48.5 1.3 %collective-permute-start.9 = (f32[128,512]{1,0:T(8,128)S(1)}, f32[128,512]{1,0:T(8,128)S(1)}, u32[]{:S(2)}, u32[]{:S(2)}) collective-permute-start(f32[128,512]{1,0:T(8,128)S(1)} %broadcast_select_fusion.refs_0_), channel_id=1, source_target_pairs={{0,8},{1,9},{2,10},{3,11}} | collective-permute-start | bytes 786440 | tf_op jit(solution)/shard_map/ppermute | solution.py:207
  49.8 1.1 %collective-permute-done.8.refs_1_ = f32[128,512]{1,0:T(8,128)S(1)} collective-permute-done((f32[128,512]{1,0:T(8,128)S(1)}, f32[128,512]{1,0:T(8,128)S(1)}, u32[]{:S(2)}, u32[]{:S(2)}) %collective-permute-start.8) | collective-permute-done | bytes 262176 | tf_op jit(solution)/shard_map/ppermute | solution.py:207
  50.9 0.7 collective-permute-start.10
  51.5 0.0 collective-permute-done.20.refs_2_
  51.5 0.0 collective-permute-done.21.refs_3_
  51.6 0.1 update.3
  51.6 0.0 copy-start
  51.7 0.8 collective-permute-start.22
  52.5 0.0 collective-permute-done.9.refs_2_
  52.5 0.0 collective-permute-done.10.refs_3_
  52.5 3.9 %update.2 = (f32[832,128]{1,0:T(8,128)S(1)}, f32[832,128]{1,0:T(8,128)S(1)}, f32[832,128]{1,0:T(8,128)S(1)}, f32[832,128]{1,0:T(8,128)S(1)}) custom-call(f32[128,512]{1,0:T(8,128)S(1)} %broadcast_select_fusion.refs_0_, f32[128,512]{1,0:T(8,128)S(1)} %collective-permute-done.8.refs_1_, f32[128,512]{1,0:T(8,128)S(1)} %collective-permute-done.9.refs_2_, ...), custom_call_target="tpu_custom_call" | custom-call | flops 1000 | bytes 1000 | tf_op jit(solution)/shard_map/update/pallas_call | solution.py:306
  56.4 4.9 %collective-permute-start.11 = (f32[832,128]{1,0:T(8,128)S(1)}, f32[832,128]{1,0:T(8,128)S(1)}, u32[]{:S(2)}, u32[]{:S(2)}) collective-permute-start(f32[832,128]{1,0:T(8,128)S(1)} %get-tuple-element.24), channel_id=1, source_target_pairs={{0,2},{1,3},{8,10},{9,11},{16,18},{17,19},{24,26},{25,27},{2,4},{3... | collective-permute-start | bytes 1277960 | tf_op jit(solution)/shard_map/ppermute | solution.py:207
  61.3 0.7 collective-permute-start.23
  62.0 0.0 collective-permute-done.22.theirs.refs_6_
  62.0 1.3 %collective-permute-start.25 = (f32[896,128]{1,0:T(8,128)S(1)}, f32[896,128]{1,0:T(8,128)S(1)}, u32[]{:S(2)}, u32[]{:S(2)}) collective-permute-start(f32[896,128]{1,0:T(8,128)S(1)} %join.3), channel_id=1, source_target_pairs={{4,0},{5,1},{12,8},{13,9},{20,16},{21,17},{28,24},{29,25}} | collective-permute-start | bytes 1376264 | tf_op jit(solution)/shard_map/ppermute | solution.py:207
  63.3 5.3 %collective-permute-done.11.theirs.refs_1_ = f32[832,128]{1,0:T(8,128)S(1)} collective-permute-done((f32[832,128]{1,0:T(8,128)S(1)}, f32[832,128]{1,0:T(8,128)S(1)}, u32[]{:S(2)}, u32[]{:S(2)}) %collective-permute-start.11) | collective-permute-done | bytes 426016 | tf_op jit(solution)/shard_map/ppermute | solution.py:207
  68.7 0.7 collective-permute-start.14
  69.3 0.7 collective-permute-start.24
  70.0 12.3 %collective-permute-start.12 = (f32[832,128]{1,0:T(8,128)S(1)}, f32[832,128]{1,0:T(8,128)S(1)}, u32[]{:S(2)}, u32[]{:S(2)}) collective-permute-start(f32[832,128]{1,0:T(8,128)S(1)} %get-tuple-element.25), channel_id=1, source_target_pairs={{0,4},{1,5},{8,12},{9,13},{16,20},{17,21},{24,28},{25,29},{2,0},{3... | collective-permute-start | bytes 1277960 | tf_op jit(solution)/shard_map/ppermute | solution.py:207
  82.3 0.0 collective-permute-done.23.refs_7_
  82.3 5.8 %collective-permute-start.13 = (f32[832,128]{1,0:T(8,128)S(1)}, f32[832,128]{1,0:T(8,128)S(1)}, u32[]{:S(2)}, u32[]{:S(2)}) collective-permute-start(f32[832,128]{1,0:T(8,128)S(1)} %get-tuple-element.26.mine), channel_id=1, source_target_pairs={{0,2},{1,3},{8,10},{9,11},{16,18},{17,19},{24,26},{25,27}} | collective-permute-start | bytes 1277960 | tf_op jit(solution)/shard_map/ppermute | solution.py:207
  88.1 0.0 collective-permute-done.24.refs_8_
  88.1 12.1 %collective-permute-done.12.refs_2_ = f32[832,128]{1,0:T(8,128)S(1)} collective-permute-done((f32[832,128]{1,0:T(8,128)S(1)}, f32[832,128]{1,0:T(8,128)S(1)}, u32[]{:S(2)}, u32[]{:S(2)}) %collective-permute-start.12) | collective-permute-done | bytes 426016 | tf_op jit(solution)/shard_map/ppermute | solution.py:207
  100.2 0.1 collective-permute-done.13.refs_3_
  100.3 0.0 collective-permute-done.25.refs_9_
  100.3 0.0 collective-permute-done.14.refs_4_
  100.3 0.0 copy-done
  100.3 1.0 add_up.1
  (5 shorter events, 0.1 us)
Async XLA Ops:
  1.9 11.5 %collective-permute-start.1 = (f32[512,512]{1,0:T(8,128)S(1)}, f32[512,512]{1,0:T(8,128)S(1)}, u32[]{:S(2)}, u32[]{:S(2)}) collective-permute-start(f32[512,512]{1,0:T(8,128)S(1)} %slice_bitcast_fusion.near), channel_id=1, source_target_pairs={{8,0},{9,1}} | collective-permute-start | bytes 3145736 | tf_op jit(solution)/shard_map/ppermute | solution.py:207
  4.1 7.1 %collective-permute-start = (f32[128,128]{1,0:T(8,128)S(1)}, f32[128,128]{1,0:T(8,128)S(1)}, u32[]{:S(2)}, u32[]{:S(2)}) collective-permute-start(f32[128,128]{1,0:T(8,128)S(1)} %slice_bitcast_fusion.1), channel_id=1, source_target_pairs={{1,0},{3,2},{5,4},{7,6},{0,1},{2,3},{4,5},{6,7},{8,9},{10,11},{12,... | collective-permute-start | bytes 196616 | tf_op jit(solution)/shard_map/ppermute | solution.py:207
  8.9 20.4 %collective-permute-start.6 = (f32[512,512]{1,0:T(8,128)S(1)}, f32[512,512]{1,0:T(8,128)}, u32[]{:S(2)}, u32[]{:S(2)}) collective-permute-start(f32[512,512]{1,0:T(8,128)S(1)} %slice_bitcast_fusion.near), channel_id=1, source_target_pairs={{10,0},{11,1}} | collective-permute-start | bytes 3145736 | tf_op jit(solution)/shard_map/ppermute | solution.py:207
  11.2 18.2 %collective-permute-start.5 = (f32[512,512]{1,0:T(8,128)S(1)}, f32[512,512]{1,0:T(8,128)S(1)}, u32[]{:S(2)}, u32[]{:S(2)}) collective-permute-start(f32[512,512]{1,0:T(8,128)S(1)} %slice_bitcast_fusion.near), channel_id=1, source_target_pairs={{1,0},{13,15}} | collective-permute-start | bytes 3145736 | tf_op jit(solution)/shard_map/ppermute | solution.py:207
  13.4 16.0 %collective-permute-start.4 = (f32[2,128,128]{2,1,0:T(8,128)S(1)}, f32[2,128,128]{2,1,0:T(8,128)S(1)}, u32[]{:S(2)}, u32[]{:S(2)}) collective-permute-start(f32[2,128,128]{2,1,0:T(8,128)S(1)} %pad_maximum_fusion.own), channel_id=1, source_target_pairs={{6,0},{7,1},{14,12},{9,15}} | collective-permute-start | bytes 393224 | tf_op jit(solution)/shard_map/ppermute | solution.py:207
  14.7 14.7 %collective-permute-start.3 = (f32[2,128,128]{2,1,0:T(8,128)S(1)}, f32[2,128,128]{2,1,0:T(8,128)S(1)}, u32[]{:S(2)}, u32[]{:S(2)}) collective-permute-start(f32[2,128,128]{2,1,0:T(8,128)S(1)} %pad_maximum_fusion.own), channel_id=1, source_target_pairs={{4,0},{5,1},{8,12},{11,15}} | collective-permute-start | bytes 393224 | tf_op jit(solution)/shard_map/ppermute | solution.py:207
  16.0 13.4 %collective-permute-start.2 = (f32[2,128,128]{2,1,0:T(8,128)S(1)}, f32[2,128,128]{2,1,0:T(8,128)S(1)}, u32[]{:S(2)}, u32[]{:S(2)}) collective-permute-start(f32[2,128,128]{2,1,0:T(8,128)S(1)} %pad_maximum_fusion.own), channel_id=1, source_target_pairs={{2,0},{3,1},{10,12},{13,15}} | collective-permute-start | bytes 393224 | tf_op jit(solution)/shard_map/ppermute | solution.py:207
  34.3 5.9 %collective-permute-start.16 = (f32[128,512]{1,0:T(8,128)S(1)}, f32[128,512]{1,0:T(8,128)S(1)}, u32[]{:S(2)}, u32[]{:S(2)}) collective-permute-start(f32[128,512]{1,0:T(8,128)S(1)} %get-tuple-element.27), channel_id=1, source_target_pairs={{1,15},{0,12}} | collective-permute-start | bytes 786440 | tf_op jit(solution)/shard_map/ppermute | solution.py:207
  35.6 7.1 %collective-permute-start.15 = (f32[128,512]{1,0:T(8,128)S(1)}, f32[128,512]{1,0:T(8,128)S(1)}, u32[]{:S(2)}, u32[]{:S(2)}) collective-permute-start(f32[128,512]{1,0:T(8,128)S(1)} %get-tuple-element.27), channel_id=1, source_target_pairs={{0,15}} | collective-permute-start | bytes 786440 | tf_op jit(solution)/shard_map/ppermute | solution.py:207
  38.9 6.8 %collective-permute-start.7 = (f32[128,512]{1,0:T(8,128)}, f32[128,512]{1,0:T(8,128)S(1)}, u32[]{:S(2)}, u32[]{:S(2)}) collective-permute-start(f32[128,512]{1,0:T(8,128)} %get-tuple-element.22), channel_id=1, source_target_pairs={{0,2},{1,3}} | collective-permute-start | bytes 786440 | tf_op jit(solution)/shard_map/ppermute | solution.py:207
  42.8 4.9 %collective-permute-start.19 = (f32[128,512]{1,0:T(8,128)S(1)}, f32[128,512]{1,0:T(8,128)S(1)}, u32[]{:S(2)}, u32[]{:S(2)}) collective-permute-start(f32[128,512]{1,0:T(8,128)S(1)} %solve_high.1.refs_0_), channel_id=1, source_target_pairs={{15,31},{12,29}} | collective-permute-start | bytes 786440 | tf_op jit(solution)/shard_map/ppermute | solution.py:207
  43.4 4.3 %collective-permute-start.18 = (f32[128,512]{1,0:T(8,128)S(1)}, f32[128,512]{1,0:T(8,128)S(1)}, u32[]{:S(2)}, u32[]{:S(2)}) collective-permute-start(f32[128,512]{1,0:T(8,128)S(1)} %solve_high.1.refs_0_), channel_id=1, source_target_pairs={{15,30},{12,28}} | collective-permute-start | bytes 786440 | tf_op jit(solution)/shard_map/ppermute | solution.py:207
  44.1 3.6 %collective-permute-start.17 = (f32[128,512]{1,0:T(8,128)S(1)}, f32[128,512]{1,0:T(8,128)S(1)}, u32[]{:S(2)}, u32[]{:S(2)}) collective-permute-start(f32[128,512]{1,0:T(8,128)S(1)} %solve_high.1.refs_0_), channel_id=1, source_target_pairs={{15,14},{12,13}} | collective-permute-start | bytes 786440 | tf_op jit(solution)/shard_map/ppermute | solution.py:207
  45.7 5.2 %collective-permute-start.8 = (f32[128,512]{1,0:T(8,128)S(1)}, f32[128,512]{1,0:T(8,128)S(1)}, u32[]{:S(2)}, u32[]{:S(2)}) collective-permute-start(f32[128,512]{1,0:T(8,128)S(1)} %broadcast_select_fusion.refs_0_), channel_id=1, source_target_pairs={{0,17},{1,16},{2,19},{3,18}} | collective-permute-start | bytes 786440 | tf_op jit(solution)/shard_map/ppermute | solution.py:207
  47.0 4.5 %collective-permute-start.20 = (f32[128,512]{1,0:T(8,128)S(1)}, f32[128,512]{1,0:T(8,128)S(1)}, u32[]{:S(2)}, u32[]{:S(2)}) collective-permute-start(f32[128,512]{1,0:T(8,128)S(1)} %solve_high.1.refs_0_), channel_id=1, source_target_pairs={{15,7},{12,4}} | collective-permute-start | bytes 786440 | tf_op jit(solution)/shard_map/ppermute | solution.py:207
  47.8 3.7 %collective-permute-start.21 = (f32[128,512]{1,0:T(8,128)S(1)}, f32[128,512]{1,0:T(8,128)S(1)}, u32[]{:S(2)}, u32[]{:S(2)}) collective-permute-start(f32[128,512]{1,0:T(8,128)S(1)} %select_select_fusion.refs_1_), channel_id=1, source_target_pairs={{31,23},{30,22},{14,6},{29,21},{28,20},{13,5}} | collective-permute-start | bytes 786440 | tf_op jit(solution)/shard_map/ppermute | solution.py:207
  48.5 4.0 %collective-permute-start.9 = (f32[128,512]{1,0:T(8,128)S(1)}, f32[128,512]{1,0:T(8,128)S(1)}, u32[]{:S(2)}, u32[]{:S(2)}) collective-permute-start(f32[128,512]{1,0:T(8,128)S(1)} %broadcast_select_fusion.refs_0_), channel_id=1, source_target_pairs={{0,8},{1,9},{2,10},{3,11}} | collective-permute-start | bytes 786440 | tf_op jit(solution)/shard_map/ppermute | solution.py:207
  50.9 1.6 %collective-permute-start.10 = (f32[128,512]{1,0:T(8,128)S(1)}, f32[128,512]{1,0:T(8,128)S(1)}, u32[]{:S(2)}, u32[]{:S(2)}) collective-permute-start(f32[128,512]{1,0:T(8,128)S(1)} %collective-permute-done.8.refs_1_), channel_id=1, source_target_pairs={{17,25},{16,24},{19,27},{18,26}} | collective-permute-start | bytes 786440 | tf_op jit(solution)/shard_map/ppermute | solution.py:207
  51.6 48.7 %copy-start = (f32[6,1,1,128,128]{4,3,2,1,0:T(8,128)S(1)}, f32[6,1,1,128,128]{4,3,2,1,0:T(8,128)}, u32[]{:S(2)}) copy-start(f32[6,1,1,128,128]{4,3,2,1,0:T(8,128)} %param.4) | copy-start | bytes 1179652
  51.7 10.3 %collective-permute-start.22 = (f32[832,128]{1,0:T(8,128)S(1)}, f32[832,128]{1,0:T(8,128)S(1)}, u32[]{:S(2)}, u32[]{:S(2)}) collective-permute-start(f32[832,128]{1,0:T(8,128)S(1)} %get-tuple-element.29), channel_id=1, source_target_pairs={{6,4},{7,5},{14,12},{15,13},{22,20},{23,21},{30,28},{31,29},{4,2},... | collective-permute-start | bytes 1277960 | tf_op jit(solution)/shard_map/ppermute | solution.py:207
  56.4 12.3 %collective-permute-start.11 = (f32[832,128]{1,0:T(8,128)S(1)}, f32[832,128]{1,0:T(8,128)S(1)}, u32[]{:S(2)}, u32[]{:S(2)}) collective-permute-start(f32[832,128]{1,0:T(8,128)S(1)} %get-tuple-element.24), channel_id=1, source_target_pairs={{0,2},{1,3},{8,10},{9,11},{16,18},{17,19},{24,26},{25,27},{2,4},{3... | collective-permute-start | bytes 1277960 | tf_op jit(solution)/shard_map/ppermute | solution.py:207
  61.3 21.0 %collective-permute-start.23 = (f32[832,128]{1,0:T(8,128)S(1)}, f32[832,128]{1,0:T(8,128)S(1)}, u32[]{:S(2)}, u32[]{:S(2)}) collective-permute-start(f32[832,128]{1,0:T(8,128)S(1)} %get-tuple-element.30), channel_id=1, source_target_pairs={{6,2},{7,3},{14,10},{15,11},{22,18},{23,19},{30,26},{31,27},{4,6},... | collective-permute-start | bytes 1277960 | tf_op jit(solution)/shard_map/ppermute | solution.py:207
  62.0 38.3 %collective-permute-start.25 = (f32[896,128]{1,0:T(8,128)S(1)}, f32[896,128]{1,0:T(8,128)S(1)}, u32[]{:S(2)}, u32[]{:S(2)}) collective-permute-start(f32[896,128]{1,0:T(8,128)S(1)} %join.3), channel_id=1, source_target_pairs={{4,0},{5,1},{12,8},{13,9},{20,16},{21,17},{28,24},{29,25}} | collective-permute-start | bytes 1376264 | tf_op jit(solution)/shard_map/ppermute | solution.py:207
  68.7 31.7 %collective-permute-start.14 = (f32[896,128]{1,0:T(8,128)S(1)}, f32[896,128]{1,0:T(8,128)S(1)}, u32[]{:S(2)}, u32[]{:S(2)}) collective-permute-start(f32[896,128]{1,0:T(8,128)S(1)} %join.2), channel_id=1, source_target_pairs={{2,6},{3,7},{10,14},{11,15},{18,22},{19,23},{26,30},{27,31}} | collective-permute-start | bytes 1376264 | tf_op jit(solution)/shard_map/ppermute | solution.py:207
  69.3 18.8 %collective-permute-start.24 = (f32[832,128]{1,0:T(8,128)S(1)}, f32[832,128]{1,0:T(8,128)S(1)}, u32[]{:S(2)}, u32[]{:S(2)}) collective-permute-start(f32[832,128]{1,0:T(8,128)S(1)} %get-tuple-element.31.mine), channel_id=1, source_target_pairs={{6,4},{7,5},{14,12},{15,13},{22,20},{23,21},{30,28},{31,29}} | collective-permute-start | bytes 1277960 | tf_op jit(solution)/shard_map/ppermute | solution.py:207
  70.0 30.2 %collective-permute-start.12 = (f32[832,128]{1,0:T(8,128)S(1)}, f32[832,128]{1,0:T(8,128)S(1)}, u32[]{:S(2)}, u32[]{:S(2)}) collective-permute-start(f32[832,128]{1,0:T(8,128)S(1)} %get-tuple-element.25), channel_id=1, source_target_pairs={{0,4},{1,5},{8,12},{9,13},{16,20},{17,21},{24,28},{25,29},{2,0},{3... | collective-permute-start | bytes 1277960 | tf_op jit(solution)/shard_map/ppermute | solution.py:207
  82.3 18.0 %collective-permute-start.13 = (f32[832,128]{1,0:T(8,128)S(1)}, f32[832,128]{1,0:T(8,128)S(1)}, u32[]{:S(2)}, u32[]{:S(2)}) collective-permute-start(f32[832,128]{1,0:T(8,128)S(1)} %get-tuple-element.26.mine), channel_id=1, source_target_pairs={{0,2},{1,3},{8,10},{9,11},{16,18},{17,19},{24,26},{25,27}} | collective-permute-start | bytes 1277960 | tf_op jit(solution)/shard_map/ppermute | solution.py:207

commit v6 on v5

v6 whole, which is shorter than its diff:
```python
import functools

import jax
import jax.numpy as jnp
from jax import lax
from jax.experimental import pallas as pl
from jax.experimental.pallas import tpu as pltpu
from jax.sharding import PartitionSpec as P

AXES = ("row", "col")
F32 = jnp.float32
VMEM = pltpu.VMEM
PARAMS = pltpu.CompilerParams(vmem_limit_bytes=20 * 2**20)
CHEAP = pl.CostEstimate(flops=1000, bytes_accessed=1000, transcendentals=0)


def split(x):
    high = x.astype(jnp.bfloat16)
    return high, (x - high.astype(F32)).astype(jnp.bfloat16)


def product(a, b, transposed=False):
    dims = (((1,), (1 if transposed else 0,)), ((), ()))
    a_high, a_low = split(a)
    b_high, b_low = split(b)
    n = a.shape[0]
    both = lax.dot_general(
        jnp.concatenate([a_high, a_low], 0), b_high, dims, preferred_element_type=F32
    )
    cross = lax.dot_general(a_high, b_low, dims, preferred_element_type=F32)
    return both[:n] + (both[n:] + cross)


def position(col_count):
    return lax.axis_index("row") * col_count + lax.axis_index("col")


def stacked(pieces, which):
    return jnp.concatenate([p[which].T for p in pieces], axis=1)


def low_kernel(homes, col_count, own, g1, g2, g3, near, la, inverses, s_a, s_b, inv, sem):
    me = position(col_count)

    def work(block):
        copies = [pltpu.make_async_copy(inverses.at[i], inv.at[i], sem.at[i]) for i in range(2)]
        for copy in copies:
            copy.start()
        pieces = (own, g1, g2, g3)
        right = stacked(pieces, 0)
        copies[0].wait()
        first = product(right, inv[0], True)
        s_a[...] = first
        right = stacked(pieces, 1) - product(first, block[...])
        copies[1].wait()
        s_b[...] = product(right, inv[1], True)

    @pl.when(me == homes[0])
    def _():
        work(la)

    @pl.when(me == homes[1])
    def _():
        work(near)


def reduce_kernel(homes, col_count, s_a, s_b, lx, ly, w):
    me = position(col_count)

    @pl.when((me == homes[0]) | (me == homes[1]))
    def _():
        w[...] = product(s_a[...], lx[...]) + product(s_b[...], ly[...])


def high_kernel(homes, col_count, own, g1, g2, g3, block, w_1, w_2, inverses, s, inv, sem):
    me = position(col_count)
    copies = [pltpu.make_async_copy(inverses.at[2 + i], inv.at[i], sem.at[i]) for i in range(2)]

    @pl.when(me == homes[0])
    def _():
        copies[0].start()
        right = stacked((g2, g1, own, g3), 0) - w_2[...]
        copies[0].wait()
        s[...] = product(right, inv[0], True)

    @pl.when(me == homes[1])
    def _():
        for copy in copies:
            copy.start()
        pieces = (g3, g2, g1, own)
        right = stacked(pieces, 0) - w_1[...]
        copies[0].wait()
        first = product(right, inv[0], True)
        right = stacked(pieces, 1) - w_2[...] - product(first, block[...])
        copies[1].wait()
        s[...] = product(right, inv[1], True)


def update_kernel(cfg, *refs):
    groups, row_count, share, homes, slots, blocks = cfg
    steps = len(homes)
    ways, panel, refs = refs[:8], refs[8], refs[9:]
    outs, (tiles, s, turned, sems) = refs[:2], refs[2:]
    quarter = turned.shape[0]
    row = lax.axis_index("row")
    col = lax.axis_index("col")
    member = col // groups
    group = col % groups
    columns = []
    for table in slots:
        to = functools.reduce(jnp.add, [jnp.where(member == m, p, 0) for m, p in enumerate(table)])
        columns.append(pl.ds(pl.multiple_of(to * quarter, quarter), quarter))
    copies = [
        [
            pltpu.make_async_copy(
                panel.at[r, 0, 0, :, columns[i]],
                tiles.at[r, :, pl.ds(i * quarter, quarter)],
                sems.at[2 * r + i],
            )
            for i in range(2)
        ]
        for r in range(blocks)
    ]
    for pair in copies:
        for copy in pair:
            copy.start()

    for half in range(2):
        planes = [m for m in range(steps) if m // (steps // 2) == half]

        def among(flip):
            return functools.reduce(jnp.logical_or, [
                (member == m) & (row == (r ^ flip)) & (group == g)
                for m in planes for r, g in homes[m]
            ])

        first, first_twin = among(0), among(1)
        here = functools.reduce(jnp.logical_or, [member == m for m in planes])
        same = here & (lax.rem(row, 2) == homes[planes[0]][0][0] % 2)
        other = here & (lax.rem(row, 2) != homes[planes[0]][0][0] % 2)
        roles = (
            first, same & jnp.logical_not(first), first_twin, other & jnp.logical_not(first_twin)
        )
        for way, role in zip(ways[4 * half:], roles):
            @pl.when(role)
            def _(src=way):
                s[...] = src[...]

    for r in range(blocks):
        for copy in copies[r]:
            copy.wait()
        block_id = (r * row_count + row) * groups + group
        keep = (block_id > member).astype(F32)
        full = product(s[...], tiles[r]) * keep
        for i, out in enumerate(outs):
            out[pl.ds(r * quarter, quarter), :] = full[:, i * quarter: (i + 1) * quarter]
    for i, out in enumerate(outs):
        turned[...] = s[:, columns[i]].T
        rows = pl.ds(pl.multiple_of(group * share, share), share)
        out[blocks * quarter:, :] = turned[rows, :]


def join_kernel(cfg, mine, theirs, got_2, got_4, out):
    del got_2, got_4
    groups, share = cfg
    last = mine.shape[0] - share
    member = lax.axis_index("col") // groups

    @pl.when((member == 1) | (member == 2))
    def _():
        out[:last, :] = mine[:last, :] + theirs[:last, :]
        out[pl.ds(last, share), :] = mine[last:, :]
        out[pl.ds(last + share, share), :] = theirs[last:, :]


def last_kernel(groups, rhs, own, got_1, got_2, got_3, got_4, joined, solved, out):
    blocks, quarter = rhs.shape[0], rhs.shape[1]
    last, share = blocks * quarter, solved.shape[1]
    member = lax.axis_index("col") // groups

    def finish(at, parts, joined_members=()):
        @pl.when(member == at)
        def _():
            for r in range(blocks):
                rows = pl.ds(r * quarter, quarter)
                total = functools.reduce(jnp.add, [part[rows, :] for part, _ in parts])
                if joined_members:
                    total = total + joined[rows, :]
                out[r] = rhs[r] - total.T
            for part, k in parts:
                solved[k] = part[last:, :]
            for i, k in enumerate(joined_members):
                solved[k] = joined[pl.ds(last + i * share, share), :]

    finish(0, [(own, 0), (got_1, 1)], (2, 3))
    finish(1, [(own, 1), (got_2, 3), (got_3, 0), (got_4, 2)])
    finish(2, [(own, 2), (got_2, 0), (got_3, 3), (got_4, 1)])
    finish(3, [(own, 3), (got_1, 2)], (1, 0))


def on_device(factor, rhs, inverses):
    steps = inverses.shape[0]
    blocks = factor.shape[0]
    width = factor.shape[3]
    quarter = rhs.shape[3]
    nrhs = rhs.shape[4]
    row_count = lax.axis_size("row")
    col_count = lax.axis_size("col")
    groups = col_count // steps
    row_pos = lax.axis_index("row")
    col_pos = lax.axis_index("col")
    member = col_pos // groups
    group = col_pos % groups
    share = width // col_count
    top = steps - 1
    me = row_pos * col_count + col_pos

    def dev(row, mem, grp):
        return row * col_count + mem * groups + grp

    def line(g, mem):
        return dev(g // groups, mem, g % groups)

    low_homes = (line(0, 0), line(1, 0))
    high_homes = (line(2, top - 1), line(3, top))

    def send(x, pairs):
        return lax.ppermute(x, AXES, pairs)

    def chosen(pairs, new, old):
        here = functools.reduce(jnp.logical_or, [me == d for _, d in pairs])
        return jnp.where(here, new, old)

    vmem = pl.BlockSpec(memory_space=VMEM)
    hbm = pl.BlockSpec(memory_space=pltpu.HBM)

    held_factor = pltpu.with_memory_space_constraint(factor, pltpu.HBM)
    held_inverses = pltpu.with_memory_space_constraint(inverses, pltpu.HBM)

    mine = rhs[0, 0, 0]
    near = factor[0, 0, 0]
    lx = send(near, [(line(2, 0), low_homes[0]), (line(3, 0), low_homes[1])])
    ly = send(near, [(line(2, 1), low_homes[0]), (line(3, 1), low_homes[1])])
    other = send(mine, [(line(g ^ 1, m), line(g, m)) for g in (0, 1, 3) for m in range(steps)])
    even = group % 2 == 0
    both = jnp.stack([jnp.where(even, mine, other), jnp.where(even, other, mine)])
    both, lx = lax.optimization_barrier((both, lx))
    later = lax.optimization_barrier((near, other))[0]
    la = send(later, [(line(1, 0), low_homes[0]), (line(3, 2), high_homes[1])])
    gathered = [
        send(
            both,
            [(line(g, j), line(g, 0)) for g in (0, 1)]
            + [(line(2, (top - 1 - j) % steps), high_homes[0]), (line(3, top - j), high_homes[1])],
        )
        for j in range(1, steps)
    ]

    vector = jax.ShapeDtypeStruct((nrhs, width), F32)
    two = [VMEM((2, width, width), F32), pltpu.SemaphoreType.DMA((2,))]
    s_0, s_1 = pl.pallas_call(
        functools.partial(low_kernel, low_homes, col_count),
        in_specs=[vmem] * 6 + [hbm],
        out_specs=[vmem] * 2,
        out_shape=[vector] * 2,
        scratch_shapes=two,
        compiler_params=PARAMS,
        cost_estimate=CHEAP,
        name="solve_low",
    )(both, *gathered, near, la, held_inverses)
    w = pl.pallas_call(
        functools.partial(reduce_kernel, low_homes, col_count),
        in_specs=[vmem] * 4,
        out_specs=vmem,
        out_shape=vector,
        compiler_params=PARAMS,
        cost_estimate=CHEAP,
        name="reduce_low",
    )(s_0, s_1, lx, ly)
    w_1 = send(w, [(low_homes[0], high_homes[1])])
    w_2 = send(w, [(low_homes[1], high_homes[1]), (low_homes[0], high_homes[0])])
    s_high = pl.pallas_call(
        functools.partial(high_kernel, high_homes, col_count),
        in_specs=[vmem] * 7 + [hbm],
        out_specs=vmem,
        out_shape=vector,
        scratch_shapes=two,
        compiler_params=PARAMS,
        cost_estimate=CHEAP,
        name="solve_high",
    )(both, *gathered, la, w_1, w_2, held_inverses)

    def spread(s, homes):
        have = {k: list(homes[k]) for k in homes}
        todo = {
            k: sorted(
                [
                    (r, g) for r in range(row_count) for g in range(groups)
                    if r % 2 == homes[k][0][0] % 2 and (r, g) not in homes[k]
                ],
                key=lambda spot: -(spot[0] != homes[k][0][0]) - (spot[1] != homes[k][0][1]),
            )
            for k in homes
        }
        fan = 1 if all(len(spots) > 1 for spots in homes.values()) else 3
        firsts = [(0, dev(r, k, g)) for k in homes for r, g in homes[k]]
        far = None
        while any(todo.values()):
            held = s if far is None else chosen(firsts, s, far)
            rounds = [[] for _ in range(fan)]
            for k in homes:
                spots = list(have[k])
                for pairs in rounds:
                    for a in spots:
                        if todo[k]:
                            b = todo[k].pop()
                            have[k].append(b)
                            pairs.append((dev(a[0], k, a[1]), dev(b[0], k, b[1])))
            for pairs in rounds:
                if pairs:
                    got = send(held, pairs)
                    far = got if far is None else chosen(pairs, got, far)
        twins = {
            k: [(dev(r, k, g), dev(r ^ 1, k, g)) for r, g in have[k]] for k in homes
        }
        near_twins = [pair for k in homes for pair in twins[k][: len(homes[k])]]
        far_twins = [pair for k in homes for pair in twins[k][len(homes[k]):]]
        return s, far, send(s, near_twins), send(far, far_twins)

    spots = [(g // groups, g % groups) for g in range(4)]
    homes = (tuple(spots[:2]), tuple(spots[:2]), (spots[2],), (spots[3],))
    moved = send(s_1, [(line(g, 0), line(g, 1)) for g in (0, 1)])
    s_low = jnp.where(member == 0, s_0, moved)
    ways = spread(s_low, {0: homes[0], 1: homes[1]}) + spread(s_high, {2: homes[2], 3: homes[3]})

    part = jax.ShapeDtypeStruct((blocks * quarter + share, nrhs), F32)

    def update(name, *slots):
        return pl.pallas_call(
            functools.partial(update_kernel, (groups, row_count, share, homes, slots, blocks)),
            in_specs=[vmem] * 8 + [hbm],
            out_specs=[vmem] * 2,
            out_shape=[part] * 2,
            scratch_shapes=[
                VMEM((blocks, width, 2 * quarter), F32),
                VMEM((nrhs, width), F32),
                VMEM((quarter, nrhs), F32),
                pltpu.SemaphoreType.DMA((2 * blocks,)),
            ],
            compiler_params=PARAMS,
            cost_estimate=CHEAP,
            name=name,
        )(*ways, held_factor)

    part_a, part_b = update("update_first", (3, 0, 3, 0), (2, 2, 1, 1))
    own, part_c = update("update_second", (0, 1, 2, 3), (1, 3, 0, 2))
    across = [(r, g) for r in range(row_count) for g in range(groups)]

    def route(*hops):
        return [(dev(r, a, g), dev(r, b, g)) for a, b in hops for r, g in across]

    got_1 = send(part_a, route((3, 2), (0, 1), (1, 0), (2, 3)))
    got_4 = send(part_b, route((2, 1), (1, 2)))
    got_3 = send(part_c, route((3, 2), (0, 1)))
    got_2 = send(part_b, route((3, 1), (0, 2)))
    joint = jax.ShapeDtypeStruct((blocks * quarter + 2 * share, nrhs), F32)
    joined = pl.pallas_call(
        functools.partial(join_kernel, (groups, share)),
        in_specs=[vmem] * 2 + [pl.BlockSpec(memory_space=pl.ANY)] * 2,
        out_specs=vmem,
        out_shape=joint,
        compiler_params=PARAMS,
        cost_estimate=CHEAP,
        name="join",
    )(part_c, got_1, got_2, got_4)
    joined = send(joined, route((2, 0), (1, 3)))

    solved, remaining = pl.pallas_call(
        functools.partial(last_kernel, groups),
        in_specs=[vmem] * 7,
        out_specs=[vmem] * 2,
        out_shape=[
            jax.ShapeDtypeStruct((steps, share, nrhs), F32),
            jax.ShapeDtypeStruct((blocks, quarter, nrhs), F32),
        ],
        compiler_params=PARAMS,
        cost_estimate=CHEAP,
        name="add_up",
    )(rhs[:, 0, 0], own, got_1, got_2, got_3, got_4, joined)
    return solved, remaining[:, None, None]


def solution(mesh):
    in_specs = (P(None, "row", "col", None, None), P(None, "row", "col", None, None), P())
    out_specs = (P(None, "col", None), P(None, "row", "col", None, None))
    return jax.shard_map(
        on_device, mesh=mesh, in_specs=in_specs, out_specs=out_specs, check_vma=False
    )
```

time: 102 us -> 99 us (0.971)
  starting transfers between devices: 52.3 us -> 48.6 us
  Pallas kernels: 9.83 us -> 12.7 us
  waiting for transfers between devices: 35 us -> 32.4 us
    pallas_call x4, Pallas kernels: 3.96 us -> 8.49 us  [the longest x2 6.6 us: update(): pl.pallas_call(functools.partial(update_kernel, (groups, row_count, share...]
    ppermute x26 -> x23, starting transfers between devices: 52.3 us -> 48.6 us  [send(): return lax.ppermute(x, AXES, pairs)]
    ppermute x26 -> x23, waiting for transfers between devices: 35 us -> 32.4 us  [send(): return lax.ppermute(x, AXES, pairs)]
    pallas_call x1, Pallas kernels: 4.86 us -> 3.2 us  [on_device(): pl.pallas_call(functools.partial(low_kernel, low_homes, col_count), in_sp...]
  transfers between devices with their start and end apart: 26 -> 23, of which waited for: 8 -> 9; matrix products, arithmetic and copies ran while one was open for 2% -> 2% of each run, Pallas kernels for 4% -> 7%
where the time goes in v6:
time: 99 us; the launch traced here: 97.8 us
  starting transfers between devices  48.6 us (49%)
  waiting for transfers between devices  32.4 us (33%)
  Pallas kernels  12.7 us (13%)
  local copies, waits for them, and re-layouts  2.15 us (2%)
  between operations  1.04 us (1%)
    ppermute x23, starting transfers between devices, send(): return lax.ppermute(x, AXES, pairs)  48.6 us
    ppermute x23, waiting for transfers between devices, send(): return lax.ppermute(x, AXES, pairs)  32.4 us
    pallas_call x2, Pallas kernels, update(): pl.pallas_call(functools.partial(update_kernel, (groups, row_count, share...  6.6 us
    pallas_call x1, Pallas kernels, on_device(): pl.pallas_call(functools.partial(low_kernel, low_homes, col_count), in_sp...  3.2 us
  transfers between devices with their start and end apart: 23, of which 9 were waited for; matrix products, arithmetic and copies ran while one was open for 2% of the time, Pallas kernels for 7%

profile of v6, /device:TPU:0, one launch (start us, length us, event | category | flops | bytes accessed | tf_op | source)
XLA Modules:
  0.0 97.8 jit_solution(10419618247112757757)
XLA Ops:
  0.6 1.3 %slice_bitcast_fusion.near = f32[512,512]{1,0:T(8,128)S(1)} fusion(f32[6,1,1,512,512]{4,3,2,1,0:T(8,128)} %refs_8_.3), kind=kLoop, calls=%fused_computation | loop fusion | bytes 2097152 | tf_op jit(solution)/shard_map/squeeze | solution.py:241
  1.9 1.3 %collective-permute-start.1 = (f32[512,512]{1,0:T(8,128)S(1)}, f32[512,512]{1,0:T(8,128)S(1)}, u32[]{:S(2)}, u32[]{:S(2)}) collective-permute-start(f32[512,512]{1,0:T(8,128)S(1)} %slice_bitcast_fusion.near), channel_id=1, source_target_pairs={{8,0},{9,1}} | collective-permute-start | bytes 3145736 | tf_op jit(solution)/shard_map/ppermute | solution.py:228
  3.2 0.8 slice_bitcast_fusion.1
  4.1 4.9 %collective-permute-start = (f32[128,128]{1,0:T(8,128)S(1)}, f32[128,128]{1,0:T(8,128)S(1)}, u32[]{:S(2)}, u32[]{:S(2)}) collective-permute-start(f32[128,128]{1,0:T(8,128)S(1)} %slice_bitcast_fusion.1), channel_id=1, source_target_pairs={{1,0},{3,2},{5,4},{7,6},{0,1},{2,3},{4,5},{6,7},{8,9},{10,11},{12,... | collective-permute-start | bytes 196616 | tf_op jit(solution)/shard_map/ppermute | solution.py:228
  8.9 2.2 %collective-permute-done = f32[128,128]{1,0:T(8,128)S(1)} collective-permute-done((f32[128,128]{1,0:T(8,128)S(1)}, f32[128,128]{1,0:T(8,128)S(1)}, u32[]{:S(2)}, u32[]{:S(2)}) %collective-permute-start) | collective-permute-done | bytes 65568 | tf_op jit(solution)/shard_map/ppermute | solution.py:228
  11.2 1.3 %collective-permute-start.5 = (f32[512,512]{1,0:T(8,128)S(1)}, f32[512,512]{1,0:T(8,128)S(1)}, u32[]{:S(2)}, u32[]{:S(2)}) collective-permute-start(f32[512,512]{1,0:T(8,128)S(1)} %slice_bitcast_fusion.near), channel_id=1, source_target_pairs={{1,0},{13,15}} | collective-permute-start | bytes 3145736 | tf_op jit(solution)/shard_map/ppermute | solution.py:228
  12.5 1.3 %collective-permute-start.10 = (f32[512,512]{1,0:T(8,128)S(1)}, f32[512,512]{1,0:T(8,128)}, u32[]{:S(2)}, u32[]{:S(2)}) collective-permute-start(f32[512,512]{1,0:T(8,128)S(1)} %slice_bitcast_fusion.near), channel_id=1, source_target_pairs={{10,0},{11,1}} | collective-permute-start | bytes 3145736 | tf_op jit(solution)/shard_map/ppermute | solution.py:228
  13.8 0.9 select_bitcast_fusion.1
  14.7 0.0 collective-permute-done.1.lx
  14.7 1.3 %collective-permute-start.4 = (f32[2,128,128]{2,1,0:T(8,128)S(1)}, f32[2,128,128]{2,1,0:T(8,128)S(1)}, u32[]{:S(2)}, u32[]{:S(2)}) collective-permute-start(f32[2,128,128]{2,1,0:T(8,128)S(1)} %pad_maximum_fusion.own), channel_id=1, source_target_pairs={{6,0},{7,1},{14,12},{9,15}} | collective-permute-start | bytes 393224 | tf_op jit(solution)/shard_map/ppermute | solution.py:228
  16.0 1.3 %collective-permute-start.3 = (f32[2,128,128]{2,1,0:T(8,128)S(1)}, f32[2,128,128]{2,1,0:T(8,128)S(1)}, u32[]{:S(2)}, u32[]{:S(2)}) collective-permute-start(f32[2,128,128]{2,1,0:T(8,128)S(1)} %pad_maximum_fusion.own), channel_id=1, source_target_pairs={{4,0},{5,1},{8,12},{11,15}} | collective-permute-start | bytes 393224 | tf_op jit(solution)/shard_map/ppermute | solution.py:228
  17.3 1.3 %collective-permute-start.2 = (f32[2,128,128]{2,1,0:T(8,128)S(1)}, f32[2,128,128]{2,1,0:T(8,128)S(1)}, u32[]{:S(2)}, u32[]{:S(2)}) collective-permute-start(f32[2,128,128]{2,1,0:T(8,128)S(1)} %pad_maximum_fusion.own), channel_id=1, source_target_pairs={{2,0},{3,1},{10,12},{13,15}} | collective-permute-start | bytes 393224 | tf_op jit(solution)/shard_map/ppermute | solution.py:228
  18.6 9.3 %collective-permute-done.5.la.block = f32[512,512]{1,0:T(8,128)S(1)} collective-permute-done((f32[512,512]{1,0:T(8,128)S(1)}, f32[512,512]{1,0:T(8,128)S(1)}, u32[]{:S(2)}, u32[]{:S(2)}) %collective-permute-start.5) | collective-permute-done | bytes 1048608 | tf_op jit(solution)/shard_map/ppermute | solution.py:228
  27.9 0.0 collective-permute-done.4.g3
  27.9 0.0 collective-permute-done.3.g2
  27.9 0.0 collective-permute-done.2.g1
  27.9 3.2 %solve_low.1 = (f32[128,512]{1,0:T(8,128)S(1)}, f32[128,512]{1,0:T(8,128)}) custom-call(f32[2,128,128]{2,1,0:T(8,128)S(1)} %pad_maximum_fusion.own, f32[2,128,128]{2,1,0:T(8,128)S(1)} %collective-permute-done.2.g1, f32[2,128,128]{2,1,0:T(8,128)S(1)} %collective-permute-done.3.g2, f32[2,128,128]{2,1,0:T(8,128)S(1)} %collective-permute-done.4.g3, ...), custom_call_target="tpu_custom_call" | custom-call | flops 1000 | bytes 1000 | tf_op jit(solution)/shard_map/solve_low/pallas_call | solution.py:261
  31.1 1.8 %collective-permute-done.10.ly = f32[512,512]{1,0:T(8,128)} collective-permute-done((f32[512,512]{1,0:T(8,128)S(1)}, f32[512,512]{1,0:T(8,128)}, u32[]{:S(2)}, u32[]{:S(2)}) %collective-permute-start.10) | collective-permute-done | bytes 1048608 | tf_op jit(solution)/shard_map/ppermute | solution.py:228
  32.9 1.9 %reduce_low.1 = f32[128,512]{1,0:T(8,128)S(1)} custom-call(f32[128,512]{1,0:T(8,128)S(1)} %get-tuple-element.15.s_a, f32[128,512]{1,0:T(8,128)} %get-tuple-element.16.s_b, f32[512,512]{1,0:T(8,128)S(1)} %collective-permute-done.1.lx, f32[512,512]{1,0:T(8,128)} %collective-permute-done.10.ly), custom_call_target="tpu_custom_call" | custom-call | flops 1000 | bytes 1000 | tf_op jit(solution)/shard_map/reduce_low/pallas_call | solution.py:271
  34.8 1.3 %collective-permute-start.12 = (f32[128,512]{1,0:T(8,128)S(1)}, f32[128,512]{1,0:T(8,128)S(1)}, u32[]{:S(2)}, u32[]{:S(2)}) collective-permute-start(f32[128,512]{1,0:T(8,128)S(1)} %reduce_low.1), channel_id=1, source_target_pairs={{1,15},{0,12}} | collective-permute-start | bytes 786440 | tf_op jit(solution)/shard_map/ppermute | solution.py:228
  36.1 2.8 %collective-permute-start.11 = (f32[128,512]{1,0:T(8,128)S(1)}, f32[128,512]{1,0:T(8,128)S(1)}, u32[]{:S(2)}, u32[]{:S(2)}) collective-permute-start(f32[128,512]{1,0:T(8,128)S(1)} %reduce_low.1), channel_id=1, source_target_pairs={{0,15}} | collective-permute-start | bytes 786440 | tf_op jit(solution)/shard_map/ppermute | solution.py:228
  39.0 1.3 %collective-permute-start.6 = (f32[128,512]{1,0:T(8,128)}, f32[128,512]{1,0:T(8,128)S(1)}, u32[]{:S(2)}, u32[]{:S(2)}) collective-permute-start(f32[128,512]{1,0:T(8,128)} %get-tuple-element.16.s_b), channel_id=1, source_target_pairs={{0,2},{1,3}} | collective-permute-start | bytes 786440 | tf_op jit(solution)/shard_map/ppermute | solution.py:228
  40.3 0.0 collective-permute-done.12.w_2
  40.3 2.5 %collective-permute-done.11.w_1 = f32[128,512]{1,0:T(8,128)S(1)} collective-permute-done((f32[128,512]{1,0:T(8,128)S(1)}, f32[128,512]{1,0:T(8,128)S(1)}, u32[]{:S(2)}, u32[]{:S(2)}) %collective-permute-start.11) | collective-permute-done | bytes 262176 | tf_op jit(solution)/shard_map/ppermute | solution.py:228
  42.9 0.7 collective-permute-start.15
  43.5 0.7 collective-permute-start.14
  44.2 0.7 collective-permute-start.13
  44.9 0.8 collective-permute-done.6
  45.8 1.3 %collective-permute-start.7 = (f32[128,512]{1,0:T(8,128)S(1)}, f32[128,512]{1,0:T(8,128)S(1)}, u32[]{:S(2)}, u32[]{:S(2)}) collective-permute-start(f32[128,512]{1,0:T(8,128)S(1)} %broadcast_select_fusion.refs_0_), channel_id=1, source_target_pairs={{0,16},{1,17},{2,18},{3,19}} | collective-permute-start | bytes 786440 | tf_op jit(solution)/shard_map/ppermute | solution.py:228
  47.1 0.7 collective-permute-start.16
  47.8 0.0 collective-permute-done.15
  47.8 1.3 %collective-permute-start.8 = (f32[128,512]{1,0:T(8,128)S(1)}, f32[128,512]{1,0:T(8,128)S(1)}, u32[]{:S(2)}, u32[]{:S(2)}) collective-permute-start(f32[128,512]{1,0:T(8,128)S(1)} %broadcast_select_fusion.refs_0_), channel_id=1, source_target_pairs={{0,8},{1,9},{2,10},{3,11}} | collective-permute-start | bytes 786440 | tf_op jit(solution)/shard_map/ppermute | solution.py:228
  49.1 0.0 collective-permute-done.14
  49.1 0.0 collective-permute-done.13
  49.1 0.1 select_select_fusion.refs_5_
  49.2 0.7 collective-permute-start.17
  49.9 1.1 %collective-permute-done.7.refs_1_ = f32[128,512]{1,0:T(8,128)S(1)} collective-permute-done((f32[128,512]{1,0:T(8,128)S(1)}, f32[128,512]{1,0:T(8,128)S(1)}, u32[]{:S(2)}, u32[]{:S(2)}) %collective-permute-start.7) | collective-permute-done | bytes 262176 | tf_op jit(solution)/shard_map/ppermute | solution.py:228
  51.0 0.7 collective-permute-start.9
  51.6 0.0 collective-permute-done.16.refs_6_
  51.6 0.0 collective-permute-done.8.refs_2_
  51.6 0.0 collective-permute-done.17.refs_7_
  51.7 0.0 collective-permute-done.9.refs_3_
  51.7 3.3 %update_first.1 = (f32[832,128]{1,0:T(8,128)S(1)}, f32[832,128]{1,0:T(8,128)S(1)}) custom-call(f32[128,512]{1,0:T(8,128)S(1)} %broadcast_select_fusion.refs_0_, f32[128,512]{1,0:T(8,128)S(1)} %collective-permute-done.7.refs_1_, f32[128,512]{1,0:T(8,128)S(1)} %collective-permute-done.8.refs_2_, f32[128,512]{1,0:T(8,128)S(1)} %collective-permute-done.9.refs_3_, ...), custom_call_target="tpu_custom_call" | custom-call | flops 1000 | bytes 1000 | tf_op jit(solution)/shard_map/update_first/pallas_call | solution.py:339
  55.0 0.0 copy-start
  55.0 2.4 %collective-permute-start.18 = (f32[832,128]{1,0:T(8,128)S(1)}, f32[832,128]{1,0:T(8,128)S(1)}, u32[]{:S(2)}, u32[]{:S(2)}) collective-permute-start(f32[832,128]{1,0:T(8,128)S(1)} %get-tuple-element.19), channel_id=1, source_target_pairs={{6,4},{7,5},{14,12},{15,13},{22,20},{23,21},{30,28},{31,29},{0,2},... | collective-permute-start | bytes 1277960 | tf_op jit(solution)/shard_map/ppermute | solution.py:228
  57.4 0.7 collective-permute-start.21
  58.1 9.0 %collective-permute-start.19 = (f32[832,128]{1,0:T(8,128)S(1)}, f32[832,128]{1,0:T(8,128)S(1)}, u32[]{:S(2)}, u32[]{:S(2)}) collective-permute-start(f32[832,128]{1,0:T(8,128)S(1)} %get-tuple-element.20), channel_id=1, source_target_pairs={{6,2},{7,3},{14,10},{15,11},{22,18},{23,19},{30,26},{31,27},{0,4},... | collective-permute-start | bytes 1277960 | tf_op jit(solution)/shard_map/ppermute | solution.py:228
  67.1 3.3 %update_second.1 = (f32[832,128]{1,0:T(8,128)S(1)}, f32[832,128]{1,0:T(8,128)S(1)}) custom-call(f32[128,512]{1,0:T(8,128)S(1)} %broadcast_select_fusion.refs_0_, f32[128,512]{1,0:T(8,128)S(1)} %collective-permute-done.7.refs_1_, f32[128,512]{1,0:T(8,128)S(1)} %collective-permute-done.8.refs_2_, f32[128,512]{1,0:T(8,128)S(1)} %collective-permute-done.9.refs_3_, ...), custom_call_target="tpu_custom_call" | custom-call | flops 1000 | bytes 1000 | tf_op jit(solution)/shard_map/update_second/pallas_call | solution.py:339
  70.4 0.0 collective-permute-done.18.theirs.got_1
  70.4 0.0 collective-permute-done.21.got_4
  70.4 5.8 %collective-permute-done.19.got_2 = f32[832,128]{1,0:T(8,128)S(1)} collective-permute-done((f32[832,128]{1,0:T(8,128)S(1)}, f32[832,128]{1,0:T(8,128)S(1)}, u32[]{:S(2)}, u32[]{:S(2)}) %collective-permute-start.19) | collective-permute-done | bytes 426016 | tf_op jit(solution)/shard_map/ppermute | solution.py:228
  76.2 1.3 %collective-permute-start.22 = (f32[896,128]{1,0:T(8,128)S(1)}, f32[896,128]{1,0:T(8,128)S(1)}, u32[]{:S(2)}, u32[]{:S(2)}) collective-permute-start(f32[896,128]{1,0:T(8,128)S(1)} %join.1), channel_id=1, source_target_pairs={{4,0},{5,1},{12,8},{13,9},{20,16},{21,17},{28,24},{29,25},{2,6},{3... | collective-permute-start | bytes 1376264 | tf_op jit(solution)/shard_map/ppermute | solution.py:228
  77.5 10.5 %collective-permute-start.20 = (f32[832,128]{1,0:T(8,128)S(1)}, f32[832,128]{1,0:T(8,128)S(1)}, u32[]{:S(2)}, u32[]{:S(2)}) collective-permute-start(f32[832,128]{1,0:T(8,128)S(1)} %get-tuple-element.21.mine), channel_id=1, source_target_pairs={{6,4},{7,5},{14,12},{15,13},{22,20},{23,21},{30,28},{31,29},{0,2},... | collective-permute-start | bytes 1277960 | tf_op jit(solution)/shard_map/ppermute | solution.py:228
  88.0 8.5 %collective-permute-done.20.got_3 = f32[832,128]{1,0:T(8,128)S(1)} collective-permute-done((f32[832,128]{1,0:T(8,128)S(1)}, f32[832,128]{1,0:T(8,128)S(1)}, u32[]{:S(2)}, u32[]{:S(2)}) %collective-permute-start.20) | collective-permute-done | bytes 426016 | tf_op jit(solution)/shard_map/ppermute | solution.py:228
  96.5 0.3 collective-permute-done.22.joined
  96.8 0.0 copy-done
  96.8 1.0 add_up.1
  (4 shorter events, 0.1 us)
Async XLA Ops:
  1.9 12.8 %collective-permute-start.1 = (f32[512,512]{1,0:T(8,128)S(1)}, f32[512,512]{1,0:T(8,128)S(1)}, u32[]{:S(2)}, u32[]{:S(2)}) collective-permute-start(f32[512,512]{1,0:T(8,128)S(1)} %slice_bitcast_fusion.near), channel_id=1, source_target_pairs={{8,0},{9,1}} | collective-permute-start | bytes 3145736 | tf_op jit(solution)/shard_map/ppermute | solution.py:228
  4.1 7.1 %collective-permute-start = (f32[128,128]{1,0:T(8,128)S(1)}, f32[128,128]{1,0:T(8,128)S(1)}, u32[]{:S(2)}, u32[]{:S(2)}) collective-permute-start(f32[128,128]{1,0:T(8,128)S(1)} %slice_bitcast_fusion.1), channel_id=1, source_target_pairs={{1,0},{3,2},{5,4},{7,6},{0,1},{2,3},{4,5},{6,7},{8,9},{10,11},{12,... | collective-permute-start | bytes 196616 | tf_op jit(solution)/shard_map/ppermute | solution.py:228
  11.2 16.7 %collective-permute-start.5 = (f32[512,512]{1,0:T(8,128)S(1)}, f32[512,512]{1,0:T(8,128)S(1)}, u32[]{:S(2)}, u32[]{:S(2)}) collective-permute-start(f32[512,512]{1,0:T(8,128)S(1)} %slice_bitcast_fusion.near), channel_id=1, source_target_pairs={{1,0},{13,15}} | collective-permute-start | bytes 3145736 | tf_op jit(solution)/shard_map/ppermute | solution.py:228
  12.5 20.4 %collective-permute-start.10 = (f32[512,512]{1,0:T(8,128)S(1)}, f32[512,512]{1,0:T(8,128)}, u32[]{:S(2)}, u32[]{:S(2)}) collective-permute-start(f32[512,512]{1,0:T(8,128)S(1)} %slice_bitcast_fusion.near), channel_id=1, source_target_pairs={{10,0},{11,1}} | collective-permute-start | bytes 3145736 | tf_op jit(solution)/shard_map/ppermute | solution.py:228
  14.7 13.2 %collective-permute-start.4 = (f32[2,128,128]{2,1,0:T(8,128)S(1)}, f32[2,128,128]{2,1,0:T(8,128)S(1)}, u32[]{:S(2)}, u32[]{:S(2)}) collective-permute-start(f32[2,128,128]{2,1,0:T(8,128)S(1)} %pad_maximum_fusion.own), channel_id=1, source_target_pairs={{6,0},{7,1},{14,12},{9,15}} | collective-permute-start | bytes 393224 | tf_op jit(solution)/shard_map/ppermute | solution.py:228
  16.0 11.9 %collective-permute-start.3 = (f32[2,128,128]{2,1,0:T(8,128)S(1)}, f32[2,128,128]{2,1,0:T(8,128)S(1)}, u32[]{:S(2)}, u32[]{:S(2)}) collective-permute-start(f32[2,128,128]{2,1,0:T(8,128)S(1)} %pad_maximum_fusion.own), channel_id=1, source_target_pairs={{4,0},{5,1},{8,12},{11,15}} | collective-permute-start | bytes 393224 | tf_op jit(solution)/shard_map/ppermute | solution.py:228
  17.3 10.6 %collective-permute-start.2 = (f32[2,128,128]{2,1,0:T(8,128)S(1)}, f32[2,128,128]{2,1,0:T(8,128)S(1)}, u32[]{:S(2)}, u32[]{:S(2)}) collective-permute-start(f32[2,128,128]{2,1,0:T(8,128)S(1)} %pad_maximum_fusion.own), channel_id=1, source_target_pairs={{2,0},{3,1},{10,12},{13,15}} | collective-permute-start | bytes 393224 | tf_op jit(solution)/shard_map/ppermute | solution.py:228
  34.8 5.5 %collective-permute-start.12 = (f32[128,512]{1,0:T(8,128)S(1)}, f32[128,512]{1,0:T(8,128)S(1)}, u32[]{:S(2)}, u32[]{:S(2)}) collective-permute-start(f32[128,512]{1,0:T(8,128)S(1)} %reduce_low.1), channel_id=1, source_target_pairs={{1,15},{0,12}} | collective-permute-start | bytes 786440 | tf_op jit(solution)/shard_map/ppermute | solution.py:228
  36.1 6.7 %collective-permute-start.11 = (f32[128,512]{1,0:T(8,128)S(1)}, f32[128,512]{1,0:T(8,128)S(1)}, u32[]{:S(2)}, u32[]{:S(2)}) collective-permute-start(f32[128,512]{1,0:T(8,128)S(1)} %reduce_low.1), channel_id=1, source_target_pairs={{0,15}} | collective-permute-start | bytes 786440 | tf_op jit(solution)/shard_map/ppermute | solution.py:228
  39.0 6.8 %collective-permute-start.6 = (f32[128,512]{1,0:T(8,128)}, f32[128,512]{1,0:T(8,128)S(1)}, u32[]{:S(2)}, u32[]{:S(2)}) collective-permute-start(f32[128,512]{1,0:T(8,128)} %get-tuple-element.16.s_b), channel_id=1, source_target_pairs={{0,2},{1,3}} | collective-permute-start | bytes 786440 | tf_op jit(solution)/shard_map/ppermute | solution.py:228
  42.9 4.9 %collective-permute-start.15 = (f32[128,512]{1,0:T(8,128)S(1)}, f32[128,512]{1,0:T(8,128)S(1)}, u32[]{:S(2)}, u32[]{:S(2)}) collective-permute-start(f32[128,512]{1,0:T(8,128)S(1)} %solve_high.1.refs_4_), channel_id=1, source_target_pairs={{12,28},{15,31}} | collective-permute-start | bytes 786440 | tf_op jit(solution)/shard_map/ppermute | solution.py:228
  43.5 5.6 %collective-permute-start.14 = (f32[128,512]{1,0:T(8,128)S(1)}, f32[128,512]{1,0:T(8,128)S(1)}, u32[]{:S(2)}, u32[]{:S(2)}) collective-permute-start(f32[128,512]{1,0:T(8,128)S(1)} %solve_high.1.refs_4_), channel_id=1, source_target_pairs={{12,13},{15,14}} | collective-permute-start | bytes 786440 | tf_op jit(solution)/shard_map/ppermute | solution.py:228
  44.2 4.9 %collective-permute-start.13 = (f32[128,512]{1,0:T(8,128)S(1)}, f32[128,512]{1,0:T(8,128)S(1)}, u32[]{:S(2)}, u32[]{:S(2)}) collective-permute-start(f32[128,512]{1,0:T(8,128)S(1)} %solve_high.1.refs_4_), channel_id=1, source_target_pairs={{12,29},{15,30}} | collective-permute-start | bytes 786440 | tf_op jit(solution)/shard_map/ppermute | solution.py:228
  45.8 5.2 %collective-permute-start.7 = (f32[128,512]{1,0:T(8,128)S(1)}, f32[128,512]{1,0:T(8,128)S(1)}, u32[]{:S(2)}, u32[]{:S(2)}) collective-permute-start(f32[128,512]{1,0:T(8,128)S(1)} %broadcast_select_fusion.refs_0_), channel_id=1, source_target_pairs={{0,16},{1,17},{2,18},{3,19}} | collective-permute-start | bytes 786440 | tf_op jit(solution)/shard_map/ppermute | solution.py:228
  47.1 4.5 %collective-permute-start.16 = (f32[128,512]{1,0:T(8,128)S(1)}, f32[128,512]{1,0:T(8,128)S(1)}, u32[]{:S(2)}, u32[]{:S(2)}) collective-permute-start(f32[128,512]{1,0:T(8,128)S(1)} %solve_high.1.refs_4_), channel_id=1, source_target_pairs={{12,4},{15,7}} | collective-permute-start | bytes 786440 | tf_op jit(solution)/shard_map/ppermute | solution.py:228
  47.8 3.8 %collective-permute-start.8 = (f32[128,512]{1,0:T(8,128)S(1)}, f32[128,512]{1,0:T(8,128)S(1)}, u32[]{:S(2)}, u32[]{:S(2)}) collective-permute-start(f32[128,512]{1,0:T(8,128)S(1)} %broadcast_select_fusion.refs_0_), channel_id=1, source_target_pairs={{0,8},{1,9},{2,10},{3,11}} | collective-permute-start | bytes 786440 | tf_op jit(solution)/shard_map/ppermute | solution.py:228
  49.2 2.4 %collective-permute-start.17 = (f32[128,512]{1,0:T(8,128)S(1)}, f32[128,512]{1,0:T(8,128)S(1)}, u32[]{:S(2)}, u32[]{:S(2)}) collective-permute-start(f32[128,512]{1,0:T(8,128)S(1)} %select_select_fusion.refs_5_), channel_id=1, source_target_pairs={{28,20},{13,5},{29,21},{31,23},{14,6},{30,22}} | collective-permute-start | bytes 786440 | tf_op jit(solution)/shard_map/ppermute | solution.py:228
  51.0 0.7 collective-permute-start.9
  55.0 41.9 %copy-start = (f32[6,1,1,128,128]{4,3,2,1,0:T(8,128)S(1)}, f32[6,1,1,128,128]{4,3,2,1,0:T(8,128)}, u32[]{:S(2)}) copy-start(f32[6,1,1,128,128]{4,3,2,1,0:T(8,128)} %param.4) | copy-start | bytes 1179652
  55.0 15.4 %collective-permute-start.18 = (f32[832,128]{1,0:T(8,128)S(1)}, f32[832,128]{1,0:T(8,128)S(1)}, u32[]{:S(2)}, u32[]{:S(2)}) collective-permute-start(f32[832,128]{1,0:T(8,128)S(1)} %get-tuple-element.19), channel_id=1, source_target_pairs={{6,4},{7,5},{14,12},{15,13},{22,20},{23,21},{30,28},{31,29},{0,2},... | collective-permute-start | bytes 1277960 | tf_op jit(solution)/shard_map/ppermute | solution.py:228
  57.4 13.0 %collective-permute-start.21 = (f32[832,128]{1,0:T(8,128)S(1)}, f32[832,128]{1,0:T(8,128)S(1)}, u32[]{:S(2)}, u32[]{:S(2)}) collective-permute-start(f32[832,128]{1,0:T(8,128)S(1)} %get-tuple-element.20), channel_id=1, source_target_pairs={{4,2},{5,3},{12,10},{13,11},{20,18},{21,19},{28,26},{29,27},{2,4},... | collective-permute-start | bytes 1277960 | tf_op jit(solution)/shard_map/ppermute | solution.py:228
  58.1 18.1 %collective-permute-start.19 = (f32[832,128]{1,0:T(8,128)S(1)}, f32[832,128]{1,0:T(8,128)S(1)}, u32[]{:S(2)}, u32[]{:S(2)}) collective-permute-start(f32[832,128]{1,0:T(8,128)S(1)} %get-tuple-element.20), channel_id=1, source_target_pairs={{6,2},{7,3},{14,10},{15,11},{22,18},{23,19},{30,26},{31,27},{0,4},... | collective-permute-start | bytes 1277960 | tf_op jit(solution)/shard_map/ppermute | solution.py:228
  76.2 20.6 %collective-permute-start.22 = (f32[896,128]{1,0:T(8,128)S(1)}, f32[896,128]{1,0:T(8,128)S(1)}, u32[]{:S(2)}, u32[]{:S(2)}) collective-permute-start(f32[896,128]{1,0:T(8,128)S(1)} %join.1), channel_id=1, source_target_pairs={{4,0},{5,1},{12,8},{13,9},{20,16},{21,17},{28,24},{29,25},{2,6},{3... | collective-permute-start | bytes 1376264 | tf_op jit(solution)/shard_map/ppermute | solution.py:228
  77.5 19.0 %collective-permute-start.20 = (f32[832,128]{1,0:T(8,128)S(1)}, f32[832,128]{1,0:T(8,128)S(1)}, u32[]{:S(2)}, u32[]{:S(2)}) collective-permute-start(f32[832,128]{1,0:T(8,128)S(1)} %get-tuple-element.21.mine), channel_id=1, source_target_pairs={{6,4},{7,5},{14,12},{15,13},{22,20},{23,21},{30,28},{31,29},{0,2},... | collective-permute-start | bytes 1277960 | tf_op jit(solution)/shard_map/ppermute | solution.py:228

commit v7 on v6

--- a/solution.py
+++ b/solution.py
@@ -35,63 +35,74 @@
     return lax.axis_index("row") * col_count + lax.axis_index("col")
 
 
-def stacked(pieces, which):
-    return jnp.concatenate([p[which].T for p in pieces], axis=1)
-
-
-def low_kernel(homes, col_count, own, g1, g2, g3, near, la, inverses, s_a, s_b, inv, sem):
+def turn_kernel(order, solver, col_count, own, g1, g2, g3, inverses, out, inv, sem):
     me = position(col_count)
 
-    def work(block):
-        copies = [pltpu.make_async_copy(inverses.at[i], inv.at[i], sem.at[i]) for i in range(2)]
+    def joined(pieces):
+        return jnp.concatenate([piece[...].T for piece in pieces], axis=1)
+
+    @pl.when(me == solver)
+    def _():
+        copy = pltpu.make_async_copy(inverses.at[0], inv, sem)
+        copy.start()
+        right = joined((own, g1, g2, g3))
+        copy.wait()
+        out[...] = product(right, inv[...], True)
+
+    for device, places in order:
+        @pl.when(me == device)
+        def _(places=places):
+            refs = (own, g1, g2, g3)
+            out[...] = joined([refs[i] for i in places])
+
+
+def low_kernel(homes, col_count, out, swapped, near, la, inverses, s_a, s_b, inv, sem):
+    me = position(col_count)
+
+    def work(first, right, block):
+        copy = pltpu.make_async_copy(inverses.at[1], inv, sem)
+        copy.start()
+        s_a[...] = first[...]
+        left = right[...] - product(first[...], block[...])
+        copy.wait()
+        s_b[...] = product(left, inv[...], True)
+
+    @pl.when(me == homes[0])
+    def _():
+        work(out, swapped, la)
+
+    @pl.when(me == homes[1])
+    def _():
+        work(swapped, out, near)
+
+
+def reduce_kernel(homes, col_count, s_a, s_b, lx, ly, w):
+    me = position(col_count)
+
+    @pl.when((me == homes[0]) | (me == homes[1]))
+    def _():
+        w[...] = product(s_a[...], lx[...]) + product(s_b[...], ly[...])
+
+
+def high_kernel(homes, col_count, own, swapped, block, w_1, w_2, inverses, s, inv, sem):
+    me = position(col_count)
+    copies = [pltpu.make_async_copy(inverses.at[2 + i], inv.at[i], sem.at[i]) for i in range(2)]
+
+    @pl.when(me == homes[0])
+    def _():
+        copies[0].start()
+        right = own[...] - w_2[...]
+        copies[0].wait()
+        s[...] = product(right, inv[0], True)
+
+    @pl.when(me == homes[1])
+    def _():
         for copy in copies:
             copy.start()
-        pieces = (own, g1, g2, g3)
-        right = stacked(pieces, 0)
+        right = swapped[...] - w_1[...]
         copies[0].wait()
         first = product(right, inv[0], True)
-        s_a[...] = first
-        right = stacked(pieces, 1) - product(first, block[...])
-        copies[1].wait()
-        s_b[...] = product(right, inv[1], True)
-
-    @pl.when(me == homes[0])
-    def _():
-        work(la)
-
-    @pl.when(me == homes[1])
-    def _():
-        work(near)
-
-
-def reduce_kernel(homes, col_count, s_a, s_b, lx, ly, w):
-    me = position(col_count)
-
-    @pl.when((me == homes[0]) | (me == homes[1]))
-    def _():
-        w[...] = product(s_a[...], lx[...]) + product(s_b[...], ly[...])
-
-
-def high_kernel(homes, col_count, own, g1, g2, g3, block, w_1, w_2, inverses, s, inv, sem):
-    me = position(col_count)
-    copies = [pltpu.make_async_copy(inverses.at[2 + i], inv.at[i], sem.at[i]) for i in range(2)]
-
-    @pl.when(me == homes[0])
-    def _():
-        copies[0].start()
-        right = stacked((g2, g1, own, g3), 0) - w_2[...]
-        copies[0].wait()
-        s[...] = product(right, inv[0], True)
-
-    @pl.when(me == homes[1])
-    def _():
-        for copy in copies:
-            copy.start()
-        pieces = (g3, g2, g1, own)
-        right = stacked(pieces, 0) - w_1[...]
-        copies[0].wait()
-        first = product(right, inv[0], True)
-        right = stacked(pieces, 1) - w_2[...] - product(first, block[...])
+        right = own[...] - w_2[...] - product(first, block[...])
         copies[1].wait()
         s[...] = product(right, inv[1], True)
 
@@ -238,36 +249,45 @@
     held_inverses = pltpu.with_memory_space_constraint(inverses, pltpu.HBM)
 
     mine = rhs[0, 0, 0]
-    near = factor[0, 0, 0]
-    lx = send(near, [(line(2, 0), low_homes[0]), (line(3, 0), low_homes[1])])
-    ly = send(near, [(line(2, 1), low_homes[0]), (line(3, 1), low_homes[1])])
-    other = send(mine, [(line(g ^ 1, m), line(g, m)) for g in (0, 1, 3) for m in range(steps)])
-    even = group % 2 == 0
-    both = jnp.stack([jnp.where(even, mine, other), jnp.where(even, other, mine)])
-    both, lx = lax.optimization_barrier((both, lx))
-    later = lax.optimization_barrier((near, other))[0]
-    la = send(later, [(line(1, 0), low_homes[0]), (line(3, 2), high_homes[1])])
     gathered = [
         send(
-            both,
+            mine,
             [(line(g, j), line(g, 0)) for g in (0, 1)]
             + [(line(2, (top - 1 - j) % steps), high_homes[0]), (line(3, top - j), high_homes[1])],
         )
         for j in range(1, steps)
     ]
+    near = factor[0, 0, 0]
+    la = send(near, [(line(1, 0), low_homes[0]), (line(3, 2), high_homes[1])])
+    ly = send(near, [(line(2, 1), low_homes[0]), (line(3, 1), low_homes[1])])
 
     vector = jax.ShapeDtypeStruct((nrhs, width), F32)
+    one = [VMEM((width, width), F32), pltpu.SemaphoreType.DMA]
     two = [VMEM((2, width, width), F32), pltpu.SemaphoreType.DMA((2,))]
+    order = ((low_homes[1], (0, 1, 2, 3)), (high_homes[0], (2, 1, 0, 3)), (high_homes[1], (3, 2, 1, 0)))
+    turned = pl.pallas_call(
+        functools.partial(turn_kernel, order, low_homes[0], col_count),
+        in_specs=[vmem] * 4 + [hbm],
+        out_specs=vmem,
+        out_shape=vector,
+        scratch_shapes=one,
+        compiler_params=PARAMS,
+        cost_estimate=CHEAP,
+        name="turn",
+    )(mine, *gathered, held_inverses)
+    swapped = send(turned, [low_homes, low_homes[::-1], high_homes])
+    later = lax.optimization_barrier((near, turned))[0]
+    lx = send(later, [(line(2, 0), low_homes[0]), (line(3, 0), low_homes[1])])
     s_0, s_1 = pl.pallas_call(
         functools.partial(low_kernel, low_homes, col_count),
-        in_specs=[vmem] * 6 + [hbm],
+        in_specs=[vmem] * 4 + [hbm],
         out_specs=[vmem] * 2,
         out_shape=[vector] * 2,
-        scratch_shapes=two,
+        scratch_shapes=one,
         compiler_params=PARAMS,
         cost_estimate=CHEAP,
         name="solve_low",
-    )(both, *gathered, near, la, held_inverses)
+    )(turned, swapped, near, la, held_inverses)
     w = pl.pallas_call(
         functools.partial(reduce_kernel, low_homes, col_count),
         in_specs=[vmem] * 4,
@@ -281,14 +301,14 @@
     w_2 = send(w, [(low_homes[1], high_homes[1]), (low_homes[0], high_homes[0])])
     s_high = pl.pallas_call(
         functools.partial(high_kernel, high_homes, col_count),
-        in_specs=[vmem] * 7 + [hbm],
+        in_specs=[vmem] * 5 + [hbm],
         out_specs=vmem,
         out_shape=vector,
         scratch_shapes=two,
         compiler_params=PARAMS,
         cost_estimate=CHEAP,
         name="solve_high",
-    )(both, *gathered, la, w_1, w_2, held_inverses)
+    )(turned, swapped, la, w_1, w_2, held_inverses)
 
     def spread(s, homes):
         have = {k: list(homes[k]) for k in homes}

time: 99 us -> 97.9 us (0.989)
  starting transfers between devices: 48.6 us -> 55 us
  waiting for transfers between devices: 32.4 us -> 26.6 us
    ppermute x23, starting transfers between devices: 48.6 us -> 55 us  [send(): return lax.ppermute(x, AXES, pairs)]
    ppermute x23, waiting for transfers between devices: 32.4 us -> 26.6 us  [send(): return lax.ppermute(x, AXES, pairs)]
    pallas_call x0 -> x1, Pallas kernels: none -> 1.7 us  [on_device(): pl.pallas_call(functools.partial(turn_kernel, order, low_homes[0], col_co...]
    pallas_call x1, Pallas kernels: 1.9 us -> 0.59 us  [on_device(): pl.pallas_call(functools.partial(reduce_kernel, low_homes, col_count), in...]
    pallas_call x1, Pallas kernels: 3.2 us -> 1.93 us  [on_device(): pl.pallas_call(functools.partial(low_kernel, low_homes, col_count), in_sp...]
  transfers between devices with their start and end apart: 23 -> 23, of which waited for: 9 -> 8; matrix products, arithmetic and copies ran while one was open for 2% -> 1% of each run, Pallas kernels for 7% -> 8%
where the time goes in v7:
time: 97.9 us; the launch traced here: 96.7 us
  starting transfers between devices  55 us (56%)
  waiting for transfers between devices  26.6 us (27%)
  Pallas kernels  11.8 us (12%)
  local copies, waits for them, and re-layouts  2.15 us (2%)
  between operations  1.04 us (1%)
    ppermute x23, starting transfers between devices, send(): return lax.ppermute(x, AXES, pairs)  55 us
    ppermute x23, waiting for transfers between devices, send(): return lax.ppermute(x, AXES, pairs)  26.6 us
    pallas_call x2, Pallas kernels, update(): pl.pallas_call(functools.partial(update_kernel, (groups, row_count, share...  6.6 us
  transfers between devices with their start and end apart: 23, of which 8 were waited for; matrix products, arithmetic and copies ran while one was open for 1% of the time, Pallas kernels for 8%

profile of v7, /device:TPU:0, one launch (start us, length us, event | category | flops | bytes accessed | tf_op | source)
XLA Modules:
  0.0 96.7 jit_solution(7288448188589067155)
XLA Ops:
  0.6 1.3 %slice_bitcast_fusion.near = f32[512,512]{1,0:T(8,128)S(1)} fusion(f32[6,1,1,512,512]{4,3,2,1,0:T(8,128)} %refs_8_.3), kind=kLoop, calls=%fused_computation | loop fusion | bytes 2097152 | tf_op jit(solution)/shard_map/squeeze | solution.py:260
  1.9 1.3 %collective-permute-start.4 = (f32[512,512]{1,0:T(8,128)S(1)}, f32[512,512]{1,0:T(8,128)S(1)}, u32[]{:S(2)}, u32[]{:S(2)}) collective-permute-start(f32[512,512]{1,0:T(8,128)S(1)} %slice_bitcast_fusion.near), channel_id=1, source_target_pairs={{1,0},{13,15}} | collective-permute-start | bytes 3145736 | tf_op jit(solution)/shard_map/ppermute | solution.py:239
  3.2 0.8 slice_bitcast_fusion.1.own
  4.1 1.3 %collective-permute-start.2 = (f32[128,128]{1,0:T(8,128)S(1)}, f32[128,128]{1,0:T(8,128)S(1)}, u32[]{:S(2)}, u32[]{:S(2)}) collective-permute-start(f32[128,128]{1,0:T(8,128)S(1)} %slice_bitcast_fusion.1.own), channel_id=1, source_target_pairs={{6,0},{7,1},{14,12},{9,15}} | collective-permute-start | bytes 196616 | tf_op jit(solution)/shard_map/ppermute | solution.py:239
  5.4 1.3 %collective-permute-start.1 = (f32[128,128]{1,0:T(8,128)S(1)}, f32[128,128]{1,0:T(8,128)S(1)}, u32[]{:S(2)}, u32[]{:S(2)}) collective-permute-start(f32[128,128]{1,0:T(8,128)S(1)} %slice_bitcast_fusion.1.own), channel_id=1, source_target_pairs={{4,0},{5,1},{8,12},{11,15}} | collective-permute-start | bytes 196616 | tf_op jit(solution)/shard_map/ppermute | solution.py:239
  6.7 1.3 %collective-permute-start = (f32[128,128]{1,0:T(8,128)S(1)}, f32[128,128]{1,0:T(8,128)S(1)}, u32[]{:S(2)}, u32[]{:S(2)}) collective-permute-start(f32[128,128]{1,0:T(8,128)S(1)} %slice_bitcast_fusion.1.own), channel_id=1, source_target_pairs={{2,0},{3,1},{10,12},{13,15}} | collective-permute-start | bytes 196616 | tf_op jit(solution)/shard_map/ppermute | solution.py:239
  8.0 1.3 %collective-permute-start.10 = (f32[512,512]{1,0:T(8,128)S(1)}, f32[512,512]{1,0:T(8,128)S(1)}, u32[]{:S(2)}, u32[]{:S(2)}) collective-permute-start(f32[512,512]{1,0:T(8,128)S(1)} %slice_bitcast_fusion.near), channel_id=1, source_target_pairs={{10,0},{11,1}} | collective-permute-start | bytes 3145736 | tf_op jit(solution)/shard_map/ppermute | solution.py:239
  9.3 3.6 %collective-permute-done.2.g3 = f32[128,128]{1,0:T(8,128)S(1)} collective-permute-done((f32[128,128]{1,0:T(8,128)S(1)}, f32[128,128]{1,0:T(8,128)S(1)}, u32[]{:S(2)}, u32[]{:S(2)}) %collective-permute-start.2) | collective-permute-done | bytes 65568 | tf_op jit(solution)/shard_map/ppermute | solution.py:239
  12.9 0.2 collective-permute-done.1.g2
  13.0 0.6 collective-permute-done.g1
  13.7 1.7 %turn.1.out.own = f32[128,512]{1,0:T(8,128)S(1)} custom-call(f32[128,128]{1,0:T(8,128)S(1)} %slice_bitcast_fusion.1.own, f32[128,128]{1,0:T(8,128)S(1)} %collective-permute-done.g1, f32[128,128]{1,0:T(8,128)S(1)} %collective-permute-done.1.g2, f32[128,128]{1,0:T(8,128)S(1)} %collective-permute-done.2.g3, f32[4,512,512]{2,1,0:T(8,128)} %inverses.5), custom_call_target="tpu_custom_call" | custom-call | flops 1000 | bytes 1000 | tf_op jit(solution)/shard_map/turn/pallas_call | solution.py:268
  15.4 1.3 %collective-permute-start.9 = (f32[512,512]{1,0:T(8,128)S(1)}, f32[512,512]{1,0:T(8,128)S(1)}, u32[]{:S(2)}, u32[]{:S(2)}) collective-permute-start(f32[512,512]{1,0:T(8,128)S(1)} %slice_bitcast_fusion.near), channel_id=1, source_target_pairs={{8,0},{9,1}} | collective-permute-start | bytes 3145736 | tf_op jit(solution)/shard_map/ppermute | solution.py:239
  16.7 3.2 %collective-permute-start.3 = (f32[128,512]{1,0:T(8,128)S(1)}, f32[128,512]{1,0:T(8,128)S(1)}, u32[]{:S(2)}, u32[]{:S(2)}) collective-permute-start(f32[128,512]{1,0:T(8,128)S(1)} %turn.1.out.own), channel_id=1, source_target_pairs={{0,1},{1,0},{12,15}} | collective-permute-start | bytes 786440 | tf_op jit(solution)/shard_map/ppermute | solution.py:239
  19.8 5.1 %collective-permute-done.3.swapped = f32[128,512]{1,0:T(8,128)S(1)} collective-permute-done((f32[128,512]{1,0:T(8,128)S(1)}, f32[128,512]{1,0:T(8,128)S(1)}, u32[]{:S(2)}, u32[]{:S(2)}) %collective-permute-start.3) | collective-permute-done | bytes 262176 | tf_op jit(solution)/shard_map/ppermute | solution.py:239
  24.9 0.0 collective-permute-done.4.la.block
  24.9 1.9 %solve_low.1 = (f32[128,512]{1,0:T(8,128)S(1)}, f32[128,512]{1,0:T(8,128)S(1)}) custom-call(f32[128,512]{1,0:T(8,128)S(1)} %turn.1.out.own, f32[128,512]{1,0:T(8,128)S(1)} %collective-permute-done.3.swapped, f32[512,512]{1,0:T(8,128)S(1)} %slice_bitcast_fusion.near, f32[512,512]{1,0:T(8,128)S(1)} %collective-permute-done.4.la.block, f32[4,512,512]{2,1,0:T(8,128)} %inverses.5), custom_call_target="tpu_custom_call" | custom-call | flops 1000 | bytes 1000 | tf_op jit(solution)/shard_map/solve_low/pallas_call | solution.py:281
  26.9 1.3 %collective-permute-start.5 = (f32[128,512]{1,0:T(8,128)S(1)}, f32[128,512]{1,0:T(8,128)S(1)}, u32[]{:S(2)}, u32[]{:S(2)}) collective-permute-start(f32[128,512]{1,0:T(8,128)S(1)} %get-tuple-element.12.s_b), channel_id=1, source_target_pairs={{0,2},{1,3}} | collective-permute-start | bytes 786440 | tf_op jit(solution)/shard_map/ppermute | solution.py:239
  28.2 0.0 collective-permute-done.10.ly
  28.2 0.0 collective-permute-done.9.lx
  28.2 0.6 reduce_low.1
  28.8 5.3 %collective-permute-start.12 = (f32[128,512]{1,0:T(8,128)S(1)}, f32[128,512]{1,0:T(8,128)S(1)}, u32[]{:S(2)}, u32[]{:S(2)}) collective-permute-start(f32[128,512]{1,0:T(8,128)S(1)} %reduce_low.1), channel_id=1, source_target_pairs={{1,15},{0,12}} | collective-permute-start | bytes 786440 | tf_op jit(solution)/shard_map/ppermute | solution.py:239
  34.1 3.8 %collective-permute-start.11 = (f32[128,512]{1,0:T(8,128)S(1)}, f32[128,512]{1,0:T(8,128)S(1)}, u32[]{:S(2)}, u32[]{:S(2)}) collective-permute-start(f32[128,512]{1,0:T(8,128)S(1)} %reduce_low.1), channel_id=1, source_target_pairs={{0,15}} | collective-permute-start | bytes 786440 | tf_op jit(solution)/shard_map/ppermute | solution.py:239
  37.9 0.0 collective-permute-done.5
  38.0 1.3 %collective-permute-start.6 = (f32[128,512]{1,0:T(8,128)S(1)}, f32[128,512]{1,0:T(8,128)S(1)}, u32[]{:S(2)}, u32[]{:S(2)}) collective-permute-start(f32[128,512]{1,0:T(8,128)S(1)} %broadcast_select_fusion.refs_0_), channel_id=1, source_target_pairs={{0,16},{1,17},{2,18},{3,19}} | collective-permute-start | bytes 786440 | tf_op jit(solution)/shard_map/ppermute | solution.py:239
  39.3 0.0 collective-permute-done.12.w_2
  39.3 2.5 %collective-permute-done.11.w_1 = f32[128,512]{1,0:T(8,128)S(1)} collective-permute-done((f32[128,512]{1,0:T(8,128)S(1)}, f32[128,512]{1,0:T(8,128)S(1)}, u32[]{:S(2)}, u32[]{:S(2)}) %collective-permute-start.11) | collective-permute-done | bytes 262176 | tf_op jit(solution)/shard_map/ppermute | solution.py:239
  41.8 0.7 collective-permute-start.15
  42.5 0.7 collective-permute-start.14
  43.2 0.7 collective-permute-start.13
  43.9 1.3 %collective-permute-start.7 = (f32[128,512]{1,0:T(8,128)S(1)}, f32[128,512]{1,0:T(8,128)S(1)}, u32[]{:S(2)}, u32[]{:S(2)}) collective-permute-start(f32[128,512]{1,0:T(8,128)S(1)} %broadcast_select_fusion.refs_0_), channel_id=1, source_target_pairs={{0,8},{1,9},{2,10},{3,11}} | collective-permute-start | bytes 786440 | tf_op jit(solution)/shard_map/ppermute | solution.py:239
  45.2 0.0 collective-permute-done.6.refs_1_
  45.2 0.7 collective-permute-start.16
  45.9 0.0 collective-permute-done.15
  45.9 0.7 collective-permute-start.8
  46.6 0.0 collective-permute-done.14
  46.6 0.0 collective-permute-done.13
  46.6 0.1 select_select_fusion.refs_5_
  46.7 0.7 collective-permute-start.17
  47.3 0.0 collective-permute-done.7.refs_2_
  47.3 0.0 collective-permute-done.16.refs_6_
  47.4 0.0 collective-permute-done.8.refs_3_
  47.4 0.0 collective-permute-done.17.refs_7_
  47.4 3.3 %update_first.1 = (f32[832,128]{1,0:T(8,128)S(1)}, f32[832,128]{1,0:T(8,128)S(1)}) custom-call(f32[128,512]{1,0:T(8,128)S(1)} %broadcast_select_fusion.refs_0_, f32[128,512]{1,0:T(8,128)S(1)} %collective-permute-done.6.refs_1_, f32[128,512]{1,0:T(8,128)S(1)} %collective-permute-done.7.refs_2_, f32[128,512]{1,0:T(8,128)S(1)} %collective-permute-done.8.refs_3_, ...), custom_call_target="tpu_custom_call" | custom-call | flops 1000 | bytes 1000 | tf_op jit(solution)/shard_map/update_first/pallas_call | solution.py:359
  50.7 0.0 copy-start
  50.7 0.1 collective-permute-start.18
  50.8 0.8 collective-permute-start.21
  51.6 14.4 %collective-permute-start.19 = (f32[832,128]{1,0:T(8,128)S(1)}, f32[832,128]{1,0:T(8,128)S(1)}, u32[]{:S(2)}, u32[]{:S(2)}) collective-permute-start(f32[832,128]{1,0:T(8,128)S(1)} %get-tuple-element.16), channel_id=1, source_target_pairs={{6,2},{7,3},{14,10},{15,11},{22,18},{23,19},{30,26},{31,27},{0,4},... | collective-permute-start | bytes 1277960 | tf_op jit(solution)/shard_map/ppermute | solution.py:239
  66.0 3.3 %update_second.1 = (f32[832,128]{1,0:T(8,128)S(1)}, f32[832,128]{1,0:T(8,128)S(1)}) custom-call(f32[128,512]{1,0:T(8,128)S(1)} %broadcast_select_fusion.refs_0_, f32[128,512]{1,0:T(8,128)S(1)} %collective-permute-done.6.refs_1_, f32[128,512]{1,0:T(8,128)S(1)} %collective-permute-done.7.refs_2_, f32[128,512]{1,0:T(8,128)S(1)} %collective-permute-done.8.refs_3_, ...), custom_call_target="tpu_custom_call" | custom-call | flops 1000 | bytes 1000 | tf_op jit(solution)/shard_map/update_second/pallas_call | solution.py:359
  69.3 0.0 collective-permute-done.18.theirs.got_1
  69.3 0.0 collective-permute-done.21.got_4
  69.3 5.8 %collective-permute-done.19.got_2 = f32[832,128]{1,0:T(8,128)S(1)} collective-permute-done((f32[832,128]{1,0:T(8,128)S(1)}, f32[832,128]{1,0:T(8,128)S(1)}, u32[]{:S(2)}, u32[]{:S(2)}) %collective-permute-start.19) | collective-permute-done | bytes 426016 | tf_op jit(solution)/shard_map/ppermute | solution.py:239
  75.1 1.3 %collective-permute-start.22 = (f32[896,128]{1,0:T(8,128)S(1)}, f32[896,128]{1,0:T(8,128)S(1)}, u32[]{:S(2)}, u32[]{:S(2)}) collective-permute-start(f32[896,128]{1,0:T(8,128)S(1)} %join.1), channel_id=1, source_target_pairs={{4,0},{5,1},{12,8},{13,9},{20,16},{21,17},{28,24},{29,25},{2,6},{3... | collective-permute-start | bytes 1376264 | tf_op jit(solution)/shard_map/ppermute | solution.py:239
  76.4 10.5 %collective-permute-start.20 = (f32[832,128]{1,0:T(8,128)S(1)}, f32[832,128]{1,0:T(8,128)S(1)}, u32[]{:S(2)}, u32[]{:S(2)}) collective-permute-start(f32[832,128]{1,0:T(8,128)S(1)} %get-tuple-element.17.mine), channel_id=1, source_target_pairs={{6,4},{7,5},{14,12},{15,13},{22,20},{23,21},{30,28},{31,29},{0,2},... | collective-permute-start | bytes 1277960 | tf_op jit(solution)/shard_map/ppermute | solution.py:239
  86.9 8.5 %collective-permute-done.20.got_3 = f32[832,128]{1,0:T(8,128)S(1)} collective-permute-done((f32[832,128]{1,0:T(8,128)S(1)}, f32[832,128]{1,0:T(8,128)S(1)}, u32[]{:S(2)}, u32[]{:S(2)}) %collective-permute-start.20) | collective-permute-done | bytes 426016 | tf_op jit(solution)/shard_map/ppermute | solution.py:239
  95.4 0.3 collective-permute-done.22.joined
  95.8 0.0 copy-done
  95.8 1.0 %add_up.1 = (f32[4,64,128]{2,1,0:T(8,128)}, f32[6,128,128]{2,1,0:T(8,128)}) custom-call(f32[6,128,128]{2,1,0:T(8,128)S(1)} %bitcast.8, f32[832,128]{1,0:T(8,128)S(1)} %get-tuple-element.14.own, f32[832,128]{1,0:T(8,128)S(1)} %collective-permute-done.18.theirs.got_1, f32[832,128]{1,0:T(8,128)S(1)} %collective-permute-done.19.got_2, ...), custom_call_target="tpu_custom_call" | custom-call | flops 1000 | bytes 1000 | tf_op jit(solution)/shard_map/add_up/pallas_call | solution.py:398
  (3 shorter events, 0.1 us)
Async XLA Ops:
  1.9 23.0 %collective-permute-start.4 = (f32[512,512]{1,0:T(8,128)S(1)}, f32[512,512]{1,0:T(8,128)S(1)}, u32[]{:S(2)}, u32[]{:S(2)}) collective-permute-start(f32[512,512]{1,0:T(8,128)S(1)} %slice_bitcast_fusion.near), channel_id=1, source_target_pairs={{1,0},{13,15}} | collective-permute-start | bytes 3145736 | tf_op jit(solution)/shard_map/ppermute | solution.py:239
  4.1 8.8 %collective-permute-start.2 = (f32[128,128]{1,0:T(8,128)S(1)}, f32[128,128]{1,0:T(8,128)S(1)}, u32[]{:S(2)}, u32[]{:S(2)}) collective-permute-start(f32[128,128]{1,0:T(8,128)S(1)} %slice_bitcast_fusion.1.own), channel_id=1, source_target_pairs={{6,0},{7,1},{14,12},{9,15}} | collective-permute-start | bytes 196616 | tf_op jit(solution)/shard_map/ppermute | solution.py:239
  5.4 7.7 %collective-permute-start.1 = (f32[128,128]{1,0:T(8,128)S(1)}, f32[128,128]{1,0:T(8,128)S(1)}, u32[]{:S(2)}, u32[]{:S(2)}) collective-permute-start(f32[128,128]{1,0:T(8,128)S(1)} %slice_bitcast_fusion.1.own), channel_id=1, source_target_pairs={{4,0},{5,1},{8,12},{11,15}} | collective-permute-start | bytes 196616 | tf_op jit(solution)/shard_map/ppermute | solution.py:239
  6.7 7.0 %collective-permute-start = (f32[128,128]{1,0:T(8,128)S(1)}, f32[128,128]{1,0:T(8,128)S(1)}, u32[]{:S(2)}, u32[]{:S(2)}) collective-permute-start(f32[128,128]{1,0:T(8,128)S(1)} %slice_bitcast_fusion.1.own), channel_id=1, source_target_pairs={{2,0},{3,1},{10,12},{13,15}} | collective-permute-start | bytes 196616 | tf_op jit(solution)/shard_map/ppermute | solution.py:239
  8.0 20.2 %collective-permute-start.10 = (f32[512,512]{1,0:T(8,128)S(1)}, f32[512,512]{1,0:T(8,128)S(1)}, u32[]{:S(2)}, u32[]{:S(2)}) collective-permute-start(f32[512,512]{1,0:T(8,128)S(1)} %slice_bitcast_fusion.near), channel_id=1, source_target_pairs={{10,0},{11,1}} | collective-permute-start | bytes 3145736 | tf_op jit(solution)/shard_map/ppermute | solution.py:239
  15.4 12.8 %collective-permute-start.9 = (f32[512,512]{1,0:T(8,128)S(1)}, f32[512,512]{1,0:T(8,128)S(1)}, u32[]{:S(2)}, u32[]{:S(2)}) collective-permute-start(f32[512,512]{1,0:T(8,128)S(1)} %slice_bitcast_fusion.near), channel_id=1, source_target_pairs={{8,0},{9,1}} | collective-permute-start | bytes 3145736 | tf_op jit(solution)/shard_map/ppermute | solution.py:239
  16.7 8.3 %collective-permute-start.3 = (f32[128,512]{1,0:T(8,128)S(1)}, f32[128,512]{1,0:T(8,128)S(1)}, u32[]{:S(2)}, u32[]{:S(2)}) collective-permute-start(f32[128,512]{1,0:T(8,128)S(1)} %turn.1.out.own), channel_id=1, source_target_pairs={{0,1},{1,0},{12,15}} | collective-permute-start | bytes 786440 | tf_op jit(solution)/shard_map/ppermute | solution.py:239
  26.9 11.1 %collective-permute-start.5 = (f32[128,512]{1,0:T(8,128)S(1)}, f32[128,512]{1,0:T(8,128)S(1)}, u32[]{:S(2)}, u32[]{:S(2)}) collective-permute-start(f32[128,512]{1,0:T(8,128)S(1)} %get-tuple-element.12.s_b), channel_id=1, source_target_pairs={{0,2},{1,3}} | collective-permute-start | bytes 786440 | tf_op jit(solution)/shard_map/ppermute | solution.py:239
  28.8 10.5 %collective-permute-start.12 = (f32[128,512]{1,0:T(8,128)S(1)}, f32[128,512]{1,0:T(8,128)S(1)}, u32[]{:S(2)}, u32[]{:S(2)}) collective-permute-start(f32[128,512]{1,0:T(8,128)S(1)} %reduce_low.1), channel_id=1, source_target_pairs={{1,15},{0,12}} | collective-permute-start | bytes 786440 | tf_op jit(solution)/shard_map/ppermute | solution.py:239
  34.1 7.7 %collective-permute-start.11 = (f32[128,512]{1,0:T(8,128)S(1)}, f32[128,512]{1,0:T(8,128)S(1)}, u32[]{:S(2)}, u32[]{:S(2)}) collective-permute-start(f32[128,512]{1,0:T(8,128)S(1)} %reduce_low.1), channel_id=1, source_target_pairs={{0,15}} | collective-permute-start | bytes 786440 | tf_op jit(solution)/shard_map/ppermute | solution.py:239
  38.0 7.2 %collective-permute-start.6 = (f32[128,512]{1,0:T(8,128)S(1)}, f32[128,512]{1,0:T(8,128)S(1)}, u32[]{:S(2)}, u32[]{:S(2)}) collective-permute-start(f32[128,512]{1,0:T(8,128)S(1)} %broadcast_select_fusion.refs_0_), channel_id=1, source_target_pairs={{0,16},{1,17},{2,18},{3,19}} | collective-permute-start | bytes 786440 | tf_op jit(solution)/shard_map/ppermute | solution.py:239
  41.8 4.1 %collective-permute-start.15 = (f32[128,512]{1,0:T(8,128)S(1)}, f32[128,512]{1,0:T(8,128)S(1)}, u32[]{:S(2)}, u32[]{:S(2)}) collective-permute-start(f32[128,512]{1,0:T(8,128)S(1)} %solve_high.1.refs_4_), channel_id=1, source_target_pairs={{12,28},{15,31}} | collective-permute-start | bytes 786440 | tf_op jit(solution)/shard_map/ppermute | solution.py:239
  42.5 4.1 %collective-permute-start.14 = (f32[128,512]{1,0:T(8,128)S(1)}, f32[128,512]{1,0:T(8,128)S(1)}, u32[]{:S(2)}, u32[]{:S(2)}) collective-permute-start(f32[128,512]{1,0:T(8,128)S(1)} %solve_high.1.refs_4_), channel_id=1, source_target_pairs={{12,13},{15,14}} | collective-permute-start | bytes 786440 | tf_op jit(solution)/shard_map/ppermute | solution.py:239
  43.2 3.4 %collective-permute-start.13 = (f32[128,512]{1,0:T(8,128)S(1)}, f32[128,512]{1,0:T(8,128)S(1)}, u32[]{:S(2)}, u32[]{:S(2)}) collective-permute-start(f32[128,512]{1,0:T(8,128)S(1)} %solve_high.1.refs_4_), channel_id=1, source_target_pairs={{12,29},{15,30}} | collective-permute-start | bytes 786440 | tf_op jit(solution)/shard_map/ppermute | solution.py:239
  43.9 3.5 %collective-permute-start.7 = (f32[128,512]{1,0:T(8,128)S(1)}, f32[128,512]{1,0:T(8,128)S(1)}, u32[]{:S(2)}, u32[]{:S(2)}) collective-permute-start(f32[128,512]{1,0:T(8,128)S(1)} %broadcast_select_fusion.refs_0_), channel_id=1, source_target_pairs={{0,8},{1,9},{2,10},{3,11}} | collective-permute-start | bytes 786440 | tf_op jit(solution)/shard_map/ppermute | solution.py:239
  45.2 2.2 %collective-permute-start.16 = (f32[128,512]{1,0:T(8,128)S(1)}, f32[128,512]{1,0:T(8,128)S(1)}, u32[]{:S(2)}, u32[]{:S(2)}) collective-permute-start(f32[128,512]{1,0:T(8,128)S(1)} %solve_high.1.refs_4_), channel_id=1, source_target_pairs={{12,4},{15,7}} | collective-permute-start | bytes 786440 | tf_op jit(solution)/shard_map/ppermute | solution.py:239
  45.9 1.5 %collective-permute-start.8 = (f32[128,512]{1,0:T(8,128)S(1)}, f32[128,512]{1,0:T(8,128)S(1)}, u32[]{:S(2)}, u32[]{:S(2)}) collective-permute-start(f32[128,512]{1,0:T(8,128)S(1)} %collective-permute-done.6.refs_1_), channel_id=1, source_target_pairs={{16,24},{17,25},{18,26},{19,27}} | collective-permute-start | bytes 786440 | tf_op jit(solution)/shard_map/ppermute | solution.py:239
  46.7 0.7 collective-permute-start.17
  50.7 45.1 %copy-start = (f32[6,1,1,128,128]{4,3,2,1,0:T(8,128)S(1)}, f32[6,1,1,128,128]{4,3,2,1,0:T(8,128)}, u32[]{:S(2)}) copy-start(f32[6,1,1,128,128]{4,3,2,1,0:T(8,128)} %param.4) | copy-start | bytes 1179652
  50.7 18.6 %collective-permute-start.18 = (f32[832,128]{1,0:T(8,128)S(1)}, f32[832,128]{1,0:T(8,128)S(1)}, u32[]{:S(2)}, u32[]{:S(2)}) collective-permute-start(f32[832,128]{1,0:T(8,128)S(1)} %get-tuple-element.15), channel_id=1, source_target_pairs={{6,4},{7,5},{14,12},{15,13},{22,20},{23,21},{30,28},{31,29},{0,2},... | collective-permute-start | bytes 1277960 | tf_op jit(solution)/shard_map/ppermute | solution.py:239
  50.8 18.6 %collective-permute-start.21 = (f32[832,128]{1,0:T(8,128)S(1)}, f32[832,128]{1,0:T(8,128)S(1)}, u32[]{:S(2)}, u32[]{:S(2)}) collective-permute-start(f32[832,128]{1,0:T(8,128)S(1)} %get-tuple-element.16), channel_id=1, source_target_pairs={{4,2},{5,3},{12,10},{13,11},{20,18},{21,19},{28,26},{29,27},{2,4},... | collective-permute-start | bytes 1277960 | tf_op jit(solution)/shard_map/ppermute | solution.py:239
  51.6 23.5 %collective-permute-start.19 = (f32[832,128]{1,0:T(8,128)S(1)}, f32[832,128]{1,0:T(8,128)S(1)}, u32[]{:S(2)}, u32[]{:S(2)}) collective-permute-start(f32[832,128]{1,0:T(8,128)S(1)} %get-tuple-element.16), channel_id=1, source_target_pairs={{6,2},{7,3},{14,10},{15,11},{22,18},{23,19},{30,26},{31,27},{0,4},... | collective-permute-start | bytes 1277960 | tf_op jit(solution)/shard_map/ppermute | solution.py:239
  75.1 20.6 %collective-permute-start.22 = (f32[896,128]{1,0:T(8,128)S(1)}, f32[896,128]{1,0:T(8,128)S(1)}, u32[]{:S(2)}, u32[]{:S(2)}) collective-permute-start(f32[896,128]{1,0:T(8,128)S(1)} %join.1), channel_id=1, source_target_pairs={{4,0},{5,1},{12,8},{13,9},{20,16},{21,17},{28,24},{29,25},{2,6},{3... | collective-permute-start | bytes 1376264 | tf_op jit(solution)/shard_map/ppermute | solution.py:239
  76.4 19.0 %collective-permute-start.20 = (f32[832,128]{1,0:T(8,128)S(1)}, f32[832,128]{1,0:T(8,128)S(1)}, u32[]{:S(2)}, u32[]{:S(2)}) collective-permute-start(f32[832,128]{1,0:T(8,128)S(1)} %get-tuple-element.17.mine), channel_id=1, source_target_pairs={{6,4},{7,5},{14,12},{15,13},{22,20},{23,21},{30,28},{31,29},{0,2},... | collective-permute-start | bytes 1277960 | tf_op jit(solution)/shard_map/ppermute | solution.py:239

commit v8 on v7

--- a/solution.py
+++ b/solution.py
@@ -168,23 +168,23 @@
     for i, out in enumerate(outs):
         turned[...] = s[:, columns[i]].T
         rows = pl.ds(pl.multiple_of(group * share, share), share)
-        out[blocks * quarter:, :] = turned[rows, :]
+        out[pl.ds(blocks * quarter, share), :] = turned[rows, :]
 
 
 def join_kernel(cfg, mine, theirs, got_2, got_4, out):
     del got_2, got_4
     groups, share = cfg
-    last = mine.shape[0] - share
+    last = theirs.shape[0] - share
     member = lax.axis_index("col") // groups
+    out[...] = mine[...]
 
     @pl.when((member == 1) | (member == 2))
     def _():
         out[:last, :] = mine[:last, :] + theirs[:last, :]
-        out[pl.ds(last, share), :] = mine[last:, :]
         out[pl.ds(last + share, share), :] = theirs[last:, :]
 
 
-def last_kernel(groups, rhs, own, got_1, got_2, got_3, got_4, joined, solved, out):
+def last_kernel(groups, rhs, own, got_1, got_2, got_4, got_3, solved, out):
     blocks, quarter = rhs.shape[0], rhs.shape[1]
     last, share = blocks * quarter, solved.shape[1]
     member = lax.axis_index("col") // groups
@@ -196,12 +196,12 @@
                 rows = pl.ds(r * quarter, quarter)
                 total = functools.reduce(jnp.add, [part[rows, :] for part, _ in parts])
                 if joined_members:
-                    total = total + joined[rows, :]
+                    total = total + got_3[rows, :]
                 out[r] = rhs[r] - total.T
             for part, k in parts:
-                solved[k] = part[last:, :]
+                solved[k] = part[pl.ds(last, share), :]
             for i, k in enumerate(joined_members):
-                solved[k] = joined[pl.ds(last + i * share, share), :]
+                solved[k] = got_3[pl.ds(last + i * share, share), :]
 
     finish(0, [(own, 0), (got_1, 1)], (2, 3))
     finish(1, [(own, 1), (got_2, 3), (got_3, 0), (got_4, 2)])
@@ -236,7 +236,14 @@
     high_homes = (line(2, top - 1), line(3, top))
 
     def send(x, pairs):
-        return lax.ppermute(x, AXES, pairs)
+        onward = dict(pairs)
+        for start in sorted(set(onward) - set(onward.values())):
+            stop = onward[start]
+            while stop in onward:
+                stop = onward[stop]
+            onward[stop] = start
+        everyone = range(row_count * col_count)
+        return lax.ppermute(x, AXES, [(i, onward.get(i, i)) for i in everyone])
 
     def chosen(pairs, new, old):
         here = functools.reduce(jnp.logical_or, [me == d for _, d in pairs])
@@ -258,8 +265,8 @@
         for j in range(1, steps)
     ]
     near = factor[0, 0, 0]
-    la = send(near, [(line(1, 0), low_homes[0]), (line(3, 2), high_homes[1])])
-    ly = send(near, [(line(2, 1), low_homes[0]), (line(3, 1), low_homes[1])])
+    la = send(near, [(line(1, 0), low_homes[0])])
+    ly = send(near, [(line(2, 1), low_homes[0]), (line(3, 1), low_homes[1]), (line(3, 2), high_homes[1])])
 
     vector = jax.ShapeDtypeStruct((nrhs, width), F32)
     one = [VMEM((width, width), F32), pltpu.SemaphoreType.DMA]
@@ -308,7 +315,7 @@
         compiler_params=PARAMS,
         cost_estimate=CHEAP,
         name="solve_high",
-    )(turned, swapped, la, w_1, w_2, held_inverses)
+    )(turned, swapped, ly, w_1, w_2, held_inverses)
 
     def spread(s, homes):
         have = {k: list(homes[k]) for k in homes}
@@ -353,14 +360,16 @@
     s_low = jnp.where(member == 0, s_0, moved)
     ways = spread(s_low, {0: homes[0], 1: homes[1]}) + spread(s_high, {2: homes[2], 3: homes[3]})
 
-    part = jax.ShapeDtypeStruct((blocks * quarter + share, nrhs), F32)
-
-    def update(name, *slots):
+    part, joint = [
+        jax.ShapeDtypeStruct((blocks * quarter + n * share, nrhs), F32) for n in (1, 2)
+    ]
+
+    def update(name, shapes, *slots):
         return pl.pallas_call(
             functools.partial(update_kernel, (groups, row_count, share, homes, slots, blocks)),
             in_specs=[vmem] * 8 + [hbm],
             out_specs=[vmem] * 2,
-            out_shape=[part] * 2,
+            out_shape=shapes,
             scratch_shapes=[
                 VMEM((blocks, width, 2 * quarter), F32),
                 VMEM((nrhs, width), F32),
@@ -372,8 +381,8 @@
             name=name,
         )(*ways, held_factor)
 
-    part_a, part_b = update("update_first", (3, 0, 3, 0), (2, 2, 1, 1))
-    own, part_c = update("update_second", (0, 1, 2, 3), (1, 3, 0, 2))
+    part_a, part_b = update("update_first", [part, part], (3, 0, 3, 0), (2, 2, 1, 1))
+    own, part_c = update("update_second", [part, joint], (0, 1, 2, 3), (1, 3, 0, 2))
     across = [(r, g) for r in range(row_count) for g in range(groups)]
 
     def route(*hops):
@@ -381,9 +390,7 @@
 
     got_1 = send(part_a, route((3, 2), (0, 1), (1, 0), (2, 3)))
     got_4 = send(part_b, route((2, 1), (1, 2)))
-    got_3 = send(part_c, route((3, 2), (0, 1)))
-    got_2 = send(part_b, route((3, 1), (0, 2)))
-    joint = jax.ShapeDtypeStruct((blocks * quarter + 2 * share, nrhs), F32)
+    got_2 = send(part_b, route((3, 1), (1, 0), (0, 2), (2, 3)))
     joined = pl.pallas_call(
         functools.partial(join_kernel, (groups, share)),
         in_specs=[vmem] * 2 + [pl.BlockSpec(memory_space=pl.ANY)] * 2,
@@ -393,11 +400,11 @@
         cost_estimate=CHEAP,
         name="join",
     )(part_c, got_1, got_2, got_4)
-    joined = send(joined, route((2, 0), (1, 3)))
+    got_3 = send(joined, route((3, 2), (0, 1), (2, 0), (1, 3)))
 
     solved, remaining = pl.pallas_call(
         functools.partial(last_kernel, groups),
-        in_specs=[vmem] * 7,
+        in_specs=[vmem] * 6,
         out_specs=[vmem] * 2,
         out_shape=[
             jax.ShapeDtypeStruct((steps, share, nrhs), F32),
@@ -406,7 +413,7 @@
         compiler_params=PARAMS,
         cost_estimate=CHEAP,
         name="add_up",
-    )(rhs[:, 0, 0], own, got_1, got_2, got_3, got_4, joined)
+    )(rhs[:, 0, 0], own, got_1, got_2, got_4, got_3)
     return solved, remaining[:, None, None]
 
 

time: 97.9 us -> 105 us (1.073)
  waiting for transfers between devices: 26.6 us -> 31.4 us
  starting transfers between devices: 55 us -> 58.1 us
    ppermute x23 -> x22, waiting for transfers between devices: 26.6 us -> 31.4 us  [send(): return lax.ppermute(x, AXES, [(i, onward.get(i, i)) for i in everyone])]
    ppermute x23 -> x22, starting transfers between devices: 55 us -> 58.1 us  [send(): return lax.ppermute(x, AXES, [(i, onward.get(i, i)) for i in everyone])]
  transfers between devices with their start and end apart: 23 -> 22, of which waited for: 8 -> 8; matrix products, arithmetic and copies ran while one was open for 1% -> 1% of each run, Pallas kernels for 8% -> 7%
where the time goes in v8:
time: 105 us
  starting transfers between devices  58.1 us (55%)
  waiting for transfers between devices  31.4 us (30%)
  Pallas kernels  11.8 us (11%)
  local copies, waits for them, and re-layouts  2.15 us (2%)
    ppermute x22, starting transfers between devices, send(): return lax.ppermute(x, AXES, [(i, onward.get(i, i)) for i in everyone])  58.1 us
    ppermute x22, waiting for transfers between devices, send(): return lax.ppermute(x, AXES, [(i, onward.get(i, i)) for i in everyone])  31.4 us
    pallas_call x2, Pallas kernels, update(): pl.pallas_call(functools.partial(update_kernel, (groups, row_count, share...  6.6 us
  transfers between devices with their start and end apart: 22, of which 8 were waited for; matrix products, arithmetic and copies ran while one was open for 1% of the time, Pallas kernels for 7%

profile of v8, /device:TPU:0, one launch (start us, length us, event | category | flops | bytes accessed | tf_op | source)
XLA Modules:
  0.0 104.6 jit_solution(3705149076049752429)
XLA Ops:
  0.6 1.3 %slice_bitcast_fusion.near = f32[512,512]{1,0:T(8,128)S(1)} fusion(f32[6,1,1,512,512]{4,3,2,1,0:T(8,128)} %refs_8_.3), kind=kLoop, calls=%fused_computation | loop fusion | bytes 2097152 | tf_op jit(solution)/shard_map/squeeze | solution.py:267
  1.9 4.9 %collective-permute-start.4 = (f32[512,512]{1,0:T(8,128)S(1)}, f32[512,512]{1,0:T(8,128)S(1)}, u32[]{:S(2)}, u32[]{:S(2)}) collective-permute-start(f32[512,512]{1,0:T(8,128)S(1)} %slice_bitcast_fusion.near), channel_id=1, source_target_pairs={{0,1},{1,0},{2,2},{3,3},{4,4},{5,5},{6,6},{7,7},{8,8},{9,9},{10,10... | collective-permute-start | bytes 3145736 | tf_op jit(solution)/shard_map/ppermute | solution.py:246
  6.8 0.8 slice_bitcast_fusion.1.own
  7.7 1.9 %collective-permute-start = (f32[128,128]{1,0:T(8,128)S(1)}, f32[128,128]{1,0:T(8,128)S(1)}, u32[]{:S(2)}, u32[]{:S(2)}) collective-permute-start(f32[128,128]{1,0:T(8,128)S(1)} %slice_bitcast_fusion.1.own), channel_id=1, source_target_pairs={{0,2},{1,3},{2,0},{3,1},{4,4},{5,5},{6,6},{7,7},{8,8},{9,9},{10,12... | collective-permute-start | bytes 196616 | tf_op jit(solution)/shard_map/ppermute | solution.py:246
  9.6 1.9 %collective-permute-start.1 = (f32[128,128]{1,0:T(8,128)S(1)}, f32[128,128]{1,0:T(8,128)S(1)}, u32[]{:S(2)}, u32[]{:S(2)}) collective-permute-start(f32[128,128]{1,0:T(8,128)S(1)} %slice_bitcast_fusion.1.own), channel_id=1, source_target_pairs={{0,4},{1,5},{2,2},{3,3},{4,0},{5,1},{6,6},{7,7},{8,12},{9,9},{10,1... | collective-permute-start | bytes 196616 | tf_op jit(solution)/shard_map/ppermute | solution.py:246
  11.5 1.9 %collective-permute-start.2 = (f32[128,128]{1,0:T(8,128)S(1)}, f32[128,128]{1,0:T(8,128)S(1)}, u32[]{:S(2)}, u32[]{:S(2)}) collective-permute-start(f32[128,128]{1,0:T(8,128)S(1)} %slice_bitcast_fusion.1.own), channel_id=1, source_target_pairs={{0,6},{1,7},{2,2},{3,3},{4,4},{5,5},{6,0},{7,1},{8,8},{9,15},{10,1... | collective-permute-start | bytes 196616 | tf_op jit(solution)/shard_map/ppermute | solution.py:246
  13.4 1.9 %collective-permute-start.9 = (f32[512,512]{1,0:T(8,128)S(1)}, f32[512,512]{1,0:T(8,128)S(1)}, u32[]{:S(2)}, u32[]{:S(2)}) collective-permute-start(f32[512,512]{1,0:T(8,128)S(1)} %slice_bitcast_fusion.near), channel_id=1, source_target_pairs={{0,10},{1,11},{2,2},{3,3},{4,4},{5,5},{6,6},{7,7},{8,8},{9,9},{10,... | collective-permute-start | bytes 3145736 | tf_op jit(solution)/shard_map/ppermute | solution.py:246
  15.4 0.0 collective-permute-done.g1
  15.4 1.3 %collective-permute-done.1.g2 = f32[128,128]{1,0:T(8,128)S(1)} collective-permute-done((f32[128,128]{1,0:T(8,128)S(1)}, f32[128,128]{1,0:T(8,128)S(1)}, u32[]{:S(2)}, u32[]{:S(2)}) %collective-permute-start.1) | collective-permute-done | bytes 65568 | tf_op jit(solution)/shard_map/ppermute | solution.py:246
  16.6 2.9 %collective-permute-done.2.g3 = f32[128,128]{1,0:T(8,128)S(1)} collective-permute-done((f32[128,128]{1,0:T(8,128)S(1)}, f32[128,128]{1,0:T(8,128)S(1)}, u32[]{:S(2)}, u32[]{:S(2)}) %collective-permute-start.2) | collective-permute-done | bytes 65568 | tf_op jit(solution)/shard_map/ppermute | solution.py:246
  19.6 1.7 %turn.1.out.own = f32[128,512]{1,0:T(8,128)S(1)} custom-call(f32[128,128]{1,0:T(8,128)S(1)} %slice_bitcast_fusion.1.own, f32[128,128]{1,0:T(8,128)S(1)} %collective-permute-done.g1, f32[128,128]{1,0:T(8,128)S(1)} %collective-permute-done.1.g2, f32[128,128]{1,0:T(8,128)S(1)} %collective-permute-done.2.g3, f32[4,512,512]{2,1,0:T(8,128)} %inverses.5), custom_call_target="tpu_custom_call" | custom-call | flops 1000 | bytes 1000 | tf_op jit(solution)/shard_map/turn/pallas_call | solution.py:275
  21.3 1.9 %collective-permute-start.10 = (f32[512,512]{1,0:T(8,128)S(1)}, f32[512,512]{1,0:T(8,128)S(1)}, u32[]{:S(2)}, u32[]{:S(2)}) collective-permute-start(f32[512,512]{1,0:T(8,128)S(1)} %slice_bitcast_fusion.near), channel_id=1, source_target_pairs={{0,8},{1,9},{2,2},{3,3},{4,4},{5,5},{6,6},{7,7},{8,0},{9,1},{10,10... | collective-permute-start | bytes 3145736 | tf_op jit(solution)/shard_map/ppermute | solution.py:246
  23.2 1.9 %collective-permute-start.3 = (f32[128,512]{1,0:T(8,128)S(1)}, f32[128,512]{1,0:T(8,128)S(1)}, u32[]{:S(2)}, u32[]{:S(2)}) collective-permute-start(f32[128,512]{1,0:T(8,128)S(1)} %turn.1.out.own), channel_id=1, source_target_pairs={{0,1},{1,0},{2,2},{3,3},{4,4},{5,5},{6,6},{7,7},{8,8},{9,9},{10,10... | collective-permute-start | bytes 786440 | tf_op jit(solution)/shard_map/ppermute | solution.py:246
  25.1 6.3 %collective-permute-done.3.swapped = f32[128,512]{1,0:T(8,128)S(1)} collective-permute-done((f32[128,512]{1,0:T(8,128)S(1)}, f32[128,512]{1,0:T(8,128)S(1)}, u32[]{:S(2)}, u32[]{:S(2)}) %collective-permute-start.3) | collective-permute-done | bytes 262176 | tf_op jit(solution)/shard_map/ppermute | solution.py:246
  31.5 0.0 collective-permute-done.4.la
  31.5 1.9 %solve_low.1 = (f32[128,512]{1,0:T(8,128)S(1)}, f32[128,512]{1,0:T(8,128)S(1)}) custom-call(f32[128,512]{1,0:T(8,128)S(1)} %turn.1.out.own, f32[128,512]{1,0:T(8,128)S(1)} %collective-permute-done.3.swapped, f32[512,512]{1,0:T(8,128)S(1)} %slice_bitcast_fusion.near, f32[512,512]{1,0:T(8,128)S(1)} %collective-permute-done.4.la, f32[4,512,512]{2,1,0:T(8,128)} %inverses.5), custom_call_target="tpu_custom_call" | custom-call | flops 1000 | bytes 1000 | tf_op jit(solution)/shard_map/solve_low/pallas_call | solution.py:288
  33.4 1.9 %collective-permute-start.5 = (f32[128,512]{1,0:T(8,128)S(1)}, f32[128,512]{1,0:T(8,128)S(1)}, u32[]{:S(2)}, u32[]{:S(2)}) collective-permute-start(f32[128,512]{1,0:T(8,128)S(1)} %get-tuple-element.12.s_b), channel_id=1, source_target_pairs={{0,2},{1,3},{2,0},{3,1},{4,4},{5,5},{6,6},{7,7},{8,8},{9,9},{10,10... | collective-permute-start | bytes 786440 | tf_op jit(solution)/shard_map/ppermute | solution.py:246
  35.3 0.0 collective-permute-done.9.ly.block
  35.3 0.0 collective-permute-done.10.lx
  35.4 0.6 reduce_low.1
  36.0 1.9 %collective-permute-start.11 = (f32[128,512]{1,0:T(8,128)S(1)}, f32[128,512]{1,0:T(8,128)S(1)}, u32[]{:S(2)}, u32[]{:S(2)}) collective-permute-start(f32[128,512]{1,0:T(8,128)S(1)} %reduce_low.1), channel_id=1, source_target_pairs={{0,15},{1,1},{2,2},{3,3},{4,4},{5,5},{6,6},{7,7},{8,8},{9,9},{10,1... | collective-permute-start | bytes 786440 | tf_op jit(solution)/shard_map/ppermute | solution.py:246
  37.9 1.9 %collective-permute-start.12 = (f32[128,512]{1,0:T(8,128)S(1)}, f32[128,512]{1,0:T(8,128)S(1)}, u32[]{:S(2)}, u32[]{:S(2)}) collective-permute-start(f32[128,512]{1,0:T(8,128)S(1)} %reduce_low.1), channel_id=1, source_target_pairs={{0,12},{1,15},{2,2},{3,3},{4,4},{5,5},{6,6},{7,7},{8,8},{9,9},{10,... | collective-permute-start | bytes 786440 | tf_op jit(solution)/shard_map/ppermute | solution.py:246
  39.8 1.8 %collective-permute-done.5 = f32[128,512]{1,0:T(8,128)S(1)} collective-permute-done((f32[128,512]{1,0:T(8,128)S(1)}, f32[128,512]{1,0:T(8,128)S(1)}, u32[]{:S(2)}, u32[]{:S(2)}) %collective-permute-start.5) | collective-permute-done | bytes 262176 | tf_op jit(solution)/shard_map/ppermute | solution.py:246
  41.7 1.9 %collective-permute-start.6 = (f32[128,512]{1,0:T(8,128)S(1)}, f32[128,512]{1,0:T(8,128)S(1)}, u32[]{:S(2)}, u32[]{:S(2)}) collective-permute-start(f32[128,512]{1,0:T(8,128)S(1)} %broadcast_select_fusion.refs_0_), channel_id=1, source_target_pairs={{0,16},{1,17},{2,18},{3,19},{4,4},{5,5},{6,6},{7,7},{8,8},{9,9},{1... | collective-permute-start | bytes 786440 | tf_op jit(solution)/shard_map/ppermute | solution.py:246
  43.6 2.7 %collective-permute-done.11.w_1 = f32[128,512]{1,0:T(8,128)S(1)} collective-permute-done((f32[128,512]{1,0:T(8,128)S(1)}, f32[128,512]{1,0:T(8,128)S(1)}, u32[]{:S(2)}, u32[]{:S(2)}) %collective-permute-start.11) | collective-permute-done | bytes 262176 | tf_op jit(solution)/shard_map/ppermute | solution.py:246
  46.3 0.1 collective-permute-done.12.w_2
  46.5 0.7 collective-permute-start.13
  47.2 0.7 collective-permute-start.14
  47.9 0.7 collective-permute-start.15
  48.6 1.9 %collective-permute-start.7 = (f32[128,512]{1,0:T(8,128)S(1)}, f32[128,512]{1,0:T(8,128)S(1)}, u32[]{:S(2)}, u32[]{:S(2)}) collective-permute-start(f32[128,512]{1,0:T(8,128)S(1)} %broadcast_select_fusion.refs_0_), channel_id=1, source_target_pairs={{0,8},{1,9},{2,10},{3,11},{4,4},{5,5},{6,6},{7,7},{8,0},{9,1},{10,... | collective-permute-start | bytes 786440 | tf_op jit(solution)/shard_map/ppermute | solution.py:246
  50.5 0.0 collective-permute-done.6.refs_1_
  50.5 0.7 collective-permute-start.16
  51.2 0.0 collective-permute-done.13
  51.2 0.7 collective-permute-start.8
  51.9 0.0 collective-permute-done.14
  51.9 0.0 collective-permute-done.15
  51.9 0.1 select_select_fusion.refs_5_
  52.0 0.7 collective-permute-start.17
  52.7 0.0 collective-permute-done.7.refs_2_
  52.7 0.0 collective-permute-done.16.refs_6_
  52.7 0.0 collective-permute-done.8.refs_3_
  52.7 0.0 collective-permute-done.17.refs_7_
  52.7 3.3 %update_first.1 = (f32[832,128]{1,0:T(8,128)S(1)}, f32[832,128]{1,0:T(8,128)S(1)}) custom-call(f32[128,512]{1,0:T(8,128)S(1)} %broadcast_select_fusion.refs_0_, f32[128,512]{1,0:T(8,128)S(1)} %collective-permute-done.6.refs_1_, f32[128,512]{1,0:T(8,128)S(1)} %collective-permute-done.7.refs_2_, f32[128,512]{1,0:T(8,128)S(1)} %collective-permute-done.8.refs_3_, ...), custom_call_target="tpu_custom_call" | custom-call | flops 1000 | bytes 1000 | tf_op jit(solution)/shard_map/update_first/pallas_call | solution.py:368
  56.0 0.0 copy-start
  56.0 0.1 collective-permute-start.18
  56.1 14.8 %collective-permute-start.19 = (f32[832,128]{1,0:T(8,128)S(1)}, f32[832,128]{1,0:T(8,128)S(1)}, u32[]{:S(2)}, u32[]{:S(2)}) collective-permute-start(f32[832,128]{1,0:T(8,128)S(1)} %get-tuple-element.16), channel_id=1, source_target_pairs={{0,4},{1,5},{2,0},{3,1},{4,6},{5,7},{6,2},{7,3},{8,12},{9,13},{10,... | collective-permute-start | bytes 1277960 | tf_op jit(solution)/shard_map/ppermute | solution.py:246
  70.9 0.7 collective-permute-start.20
  71.6 3.3 %update_second.1 = (f32[832,128]{1,0:T(8,128)S(1)}, f32[896,128]{1,0:T(8,128)S(1)}) custom-call(f32[128,512]{1,0:T(8,128)S(1)} %broadcast_select_fusion.refs_0_, f32[128,512]{1,0:T(8,128)S(1)} %collective-permute-done.6.refs_1_, f32[128,512]{1,0:T(8,128)S(1)} %collective-permute-done.7.refs_2_, f32[128,512]{1,0:T(8,128)S(1)} %collective-permute-done.8.refs_3_, ...), custom_call_target="tpu_custom_call" | custom-call | flops 1000 | bytes 1000 | tf_op jit(solution)/shard_map/update_second/pallas_call | solution.py:368
  74.9 0.0 collective-permute-done.18.theirs.got_1
  74.9 5.4 %collective-permute-done.19.got_2 = f32[832,128]{1,0:T(8,128)S(1)} collective-permute-done((f32[832,128]{1,0:T(8,128)S(1)}, f32[832,128]{1,0:T(8,128)S(1)}, u32[]{:S(2)}, u32[]{:S(2)}) %collective-permute-start.19) | collective-permute-done | bytes 426016 | tf_op jit(solution)/shard_map/ppermute | solution.py:246
  80.3 0.0 collective-permute-done.20.got_4
  80.3 12.4 %collective-permute-start.21 = (f32[896,128]{1,0:T(8,128)S(1)}, f32[896,128]{1,0:T(8,128)S(1)}, u32[]{:S(2)}, u32[]{:S(2)}) collective-permute-start(f32[896,128]{1,0:T(8,128)S(1)} %join.1), channel_id=1, source_target_pairs={{0,2},{1,3},{2,6},{3,7},{4,0},{5,1},{6,4},{7,5},{8,10},{9,11},{10,... | collective-permute-start | bytes 1376264 | tf_op jit(solution)/shard_map/ppermute | solution.py:246
  92.8 10.8 %collective-permute-done.21.got_3 = f32[896,128]{1,0:T(8,128)S(1)} collective-permute-done((f32[896,128]{1,0:T(8,128)S(1)}, f32[896,128]{1,0:T(8,128)S(1)}, u32[]{:S(2)}, u32[]{:S(2)}) %collective-permute-start.21) | collective-permute-done | bytes 458784 | tf_op jit(solution)/shard_map/ppermute | solution.py:246
  103.6 0.0 copy-done
  103.6 1.0 add_up.1
  (3 shorter events, 0.1 us)
Async XLA Ops:
  1.9 29.5 %collective-permute-start.4 = (f32[512,512]{1,0:T(8,128)S(1)}, f32[512,512]{1,0:T(8,128)S(1)}, u32[]{:S(2)}, u32[]{:S(2)}) collective-permute-start(f32[512,512]{1,0:T(8,128)S(1)} %slice_bitcast_fusion.near), channel_id=1, source_target_pairs={{0,1},{1,0},{2,2},{3,3},{4,4},{5,5},{6,6},{7,7},{8,8},{9,9},{10,10... | collective-permute-start | bytes 3145736 | tf_op jit(solution)/shard_map/ppermute | solution.py:246
  7.7 7.7 %collective-permute-start = (f32[128,128]{1,0:T(8,128)S(1)}, f32[128,128]{1,0:T(8,128)S(1)}, u32[]{:S(2)}, u32[]{:S(2)}) collective-permute-start(f32[128,128]{1,0:T(8,128)S(1)} %slice_bitcast_fusion.1.own), channel_id=1, source_target_pairs={{0,2},{1,3},{2,0},{3,1},{4,4},{5,5},{6,6},{7,7},{8,8},{9,9},{10,12... | collective-permute-start | bytes 196616 | tf_op jit(solution)/shard_map/ppermute | solution.py:246
  9.6 7.1 %collective-permute-start.1 = (f32[128,128]{1,0:T(8,128)S(1)}, f32[128,128]{1,0:T(8,128)S(1)}, u32[]{:S(2)}, u32[]{:S(2)}) collective-permute-start(f32[128,128]{1,0:T(8,128)S(1)} %slice_bitcast_fusion.1.own), channel_id=1, source_target_pairs={{0,4},{1,5},{2,2},{3,3},{4,0},{5,1},{6,6},{7,7},{8,12},{9,9},{10,1... | collective-permute-start | bytes 196616 | tf_op jit(solution)/shard_map/ppermute | solution.py:246
  11.5 8.1 %collective-permute-start.2 = (f32[128,128]{1,0:T(8,128)S(1)}, f32[128,128]{1,0:T(8,128)S(1)}, u32[]{:S(2)}, u32[]{:S(2)}) collective-permute-start(f32[128,128]{1,0:T(8,128)S(1)} %slice_bitcast_fusion.1.own), channel_id=1, source_target_pairs={{0,6},{1,7},{2,2},{3,3},{4,4},{5,5},{6,0},{7,1},{8,8},{9,15},{10,1... | collective-permute-start | bytes 196616 | tf_op jit(solution)/shard_map/ppermute | solution.py:246
  13.4 21.9 %collective-permute-start.9 = (f32[512,512]{1,0:T(8,128)S(1)}, f32[512,512]{1,0:T(8,128)S(1)}, u32[]{:S(2)}, u32[]{:S(2)}) collective-permute-start(f32[512,512]{1,0:T(8,128)S(1)} %slice_bitcast_fusion.near), channel_id=1, source_target_pairs={{0,10},{1,11},{2,2},{3,3},{4,4},{5,5},{6,6},{7,7},{8,8},{9,9},{10,... | collective-permute-start | bytes 3145736 | tf_op jit(solution)/shard_map/ppermute | solution.py:246
  21.3 14.1 %collective-permute-start.10 = (f32[512,512]{1,0:T(8,128)S(1)}, f32[512,512]{1,0:T(8,128)S(1)}, u32[]{:S(2)}, u32[]{:S(2)}) collective-permute-start(f32[512,512]{1,0:T(8,128)S(1)} %slice_bitcast_fusion.near), channel_id=1, source_target_pairs={{0,8},{1,9},{2,2},{3,3},{4,4},{5,5},{6,6},{7,7},{8,0},{9,1},{10,10... | collective-permute-start | bytes 3145736 | tf_op jit(solution)/shard_map/ppermute | solution.py:246
  23.2 8.3 %collective-permute-start.3 = (f32[128,512]{1,0:T(8,128)S(1)}, f32[128,512]{1,0:T(8,128)S(1)}, u32[]{:S(2)}, u32[]{:S(2)}) collective-permute-start(f32[128,512]{1,0:T(8,128)S(1)} %turn.1.out.own), channel_id=1, source_target_pairs={{0,1},{1,0},{2,2},{3,3},{4,4},{5,5},{6,6},{7,7},{8,8},{9,9},{10,10... | collective-permute-start | bytes 786440 | tf_op jit(solution)/shard_map/ppermute | solution.py:246
  33.4 8.3 %collective-permute-start.5 = (f32[128,512]{1,0:T(8,128)S(1)}, f32[128,512]{1,0:T(8,128)S(1)}, u32[]{:S(2)}, u32[]{:S(2)}) collective-permute-start(f32[128,512]{1,0:T(8,128)S(1)} %get-tuple-element.12.s_b), channel_id=1, source_target_pairs={{0,2},{1,3},{2,0},{3,1},{4,4},{5,5},{6,6},{7,7},{8,8},{9,9},{10,10... | collective-permute-start | bytes 786440 | tf_op jit(solution)/shard_map/ppermute | solution.py:246
  36.0 10.4 %collective-permute-start.11 = (f32[128,512]{1,0:T(8,128)S(1)}, f32[128,512]{1,0:T(8,128)S(1)}, u32[]{:S(2)}, u32[]{:S(2)}) collective-permute-start(f32[128,512]{1,0:T(8,128)S(1)} %reduce_low.1), channel_id=1, source_target_pairs={{0,15},{1,1},{2,2},{3,3},{4,4},{5,5},{6,6},{7,7},{8,8},{9,9},{10,1... | collective-permute-start | bytes 786440 | tf_op jit(solution)/shard_map/ppermute | solution.py:246
  37.9 8.6 %collective-permute-start.12 = (f32[128,512]{1,0:T(8,128)S(1)}, f32[128,512]{1,0:T(8,128)S(1)}, u32[]{:S(2)}, u32[]{:S(2)}) collective-permute-start(f32[128,512]{1,0:T(8,128)S(1)} %reduce_low.1), channel_id=1, source_target_pairs={{0,12},{1,15},{2,2},{3,3},{4,4},{5,5},{6,6},{7,7},{8,8},{9,9},{10,... | collective-permute-start | bytes 786440 | tf_op jit(solution)/shard_map/ppermute | solution.py:246
  41.7 8.8 %collective-permute-start.6 = (f32[128,512]{1,0:T(8,128)S(1)}, f32[128,512]{1,0:T(8,128)S(1)}, u32[]{:S(2)}, u32[]{:S(2)}) collective-permute-start(f32[128,512]{1,0:T(8,128)S(1)} %broadcast_select_fusion.refs_0_), channel_id=1, source_target_pairs={{0,16},{1,17},{2,18},{3,19},{4,4},{5,5},{6,6},{7,7},{8,8},{9,9},{1... | collective-permute-start | bytes 786440 | tf_op jit(solution)/shard_map/ppermute | solution.py:246
  46.5 4.7 %collective-permute-start.13 = (f32[128,512]{1,0:T(8,128)S(1)}, f32[128,512]{1,0:T(8,128)S(1)}, u32[]{:S(2)}, u32[]{:S(2)}) collective-permute-start(f32[128,512]{1,0:T(8,128)S(1)} %solve_high.1.refs_4_), channel_id=1, source_target_pairs={{0,0},{1,1},{2,2},{3,3},{4,4},{5,5},{6,6},{7,7},{8,8},{9,9},{10,10... | collective-permute-start | bytes 786440 | tf_op jit(solution)/shard_map/ppermute | solution.py:246
  47.2 4.7 %collective-permute-start.14 = (f32[128,512]{1,0:T(8,128)S(1)}, f32[128,512]{1,0:T(8,128)S(1)}, u32[]{:S(2)}, u32[]{:S(2)}) collective-permute-start(f32[128,512]{1,0:T(8,128)S(1)} %solve_high.1.refs_4_), channel_id=1, source_target_pairs={{0,0},{1,1},{2,2},{3,3},{4,4},{5,5},{6,6},{7,7},{8,8},{9,9},{10,10... | collective-permute-start | bytes 786440 | tf_op jit(solution)/shard_map/ppermute | solution.py:246
  47.9 4.0 %collective-permute-start.15 = (f32[128,512]{1,0:T(8,128)S(1)}, f32[128,512]{1,0:T(8,128)S(1)}, u32[]{:S(2)}, u32[]{:S(2)}) collective-permute-start(f32[128,512]{1,0:T(8,128)S(1)} %solve_high.1.refs_4_), channel_id=1, source_target_pairs={{0,0},{1,1},{2,2},{3,3},{4,4},{5,5},{6,6},{7,7},{8,8},{9,9},{10,10... | collective-permute-start | bytes 786440 | tf_op jit(solution)/shard_map/ppermute | solution.py:246
  48.6 4.1 %collective-permute-start.7 = (f32[128,512]{1,0:T(8,128)S(1)}, f32[128,512]{1,0:T(8,128)S(1)}, u32[]{:S(2)}, u32[]{:S(2)}) collective-permute-start(f32[128,512]{1,0:T(8,128)S(1)} %broadcast_select_fusion.refs_0_), channel_id=1, source_target_pairs={{0,8},{1,9},{2,10},{3,11},{4,4},{5,5},{6,6},{7,7},{8,0},{9,1},{10,... | collective-permute-start | bytes 786440 | tf_op jit(solution)/shard_map/ppermute | solution.py:246
  50.5 2.2 %collective-permute-start.16 = (f32[128,512]{1,0:T(8,128)S(1)}, f32[128,512]{1,0:T(8,128)S(1)}, u32[]{:S(2)}, u32[]{:S(2)}) collective-permute-start(f32[128,512]{1,0:T(8,128)S(1)} %solve_high.1.refs_4_), channel_id=1, source_target_pairs={{0,0},{1,1},{2,2},{3,3},{4,12},{5,5},{6,6},{7,15},{8,8},{9,9},{10,... | collective-permute-start | bytes 786440 | tf_op jit(solution)/shard_map/ppermute | solution.py:246
  51.2 1.5 %collective-permute-start.8 = (f32[128,512]{1,0:T(8,128)S(1)}, f32[128,512]{1,0:T(8,128)S(1)}, u32[]{:S(2)}, u32[]{:S(2)}) collective-permute-start(f32[128,512]{1,0:T(8,128)S(1)} %collective-permute-done.6.refs_1_), channel_id=1, source_target_pairs={{0,0},{1,1},{2,2},{3,3},{4,4},{5,5},{6,6},{7,7},{8,8},{9,9},{10,10... | collective-permute-start | bytes 786440 | tf_op jit(solution)/shard_map/ppermute | solution.py:246
  52.0 0.7 collective-permute-start.17
  56.0 47.6 %copy-start = (f32[6,1,1,128,128]{4,3,2,1,0:T(8,128)S(1)}, f32[6,1,1,128,128]{4,3,2,1,0:T(8,128)}, u32[]{:S(2)}) copy-start(f32[6,1,1,128,128]{4,3,2,1,0:T(8,128)} %param.4) | copy-start | bytes 1179652
  56.0 18.9 %collective-permute-start.18 = (f32[832,128]{1,0:T(8,128)S(1)}, f32[832,128]{1,0:T(8,128)S(1)}, u32[]{:S(2)}, u32[]{:S(2)}) collective-permute-start(f32[832,128]{1,0:T(8,128)S(1)} %get-tuple-element.15), channel_id=1, source_target_pairs={{0,2},{1,3},{2,0},{3,1},{4,6},{5,7},{6,4},{7,5},{8,10},{9,11},{10,... | collective-permute-start | bytes 1277960 | tf_op jit(solution)/shard_map/ppermute | solution.py:246
  56.1 24.2 %collective-permute-start.19 = (f32[832,128]{1,0:T(8,128)S(1)}, f32[832,128]{1,0:T(8,128)S(1)}, u32[]{:S(2)}, u32[]{:S(2)}) collective-permute-start(f32[832,128]{1,0:T(8,128)S(1)} %get-tuple-element.16), channel_id=1, source_target_pairs={{0,4},{1,5},{2,0},{3,1},{4,6},{5,7},{6,2},{7,3},{8,12},{9,13},{10,... | collective-permute-start | bytes 1277960 | tf_op jit(solution)/shard_map/ppermute | solution.py:246
  70.9 9.4 %collective-permute-start.20 = (f32[832,128]{1,0:T(8,128)S(1)}, f32[832,128]{1,0:T(8,128)S(1)}, u32[]{:S(2)}, u32[]{:S(2)}) collective-permute-start(f32[832,128]{1,0:T(8,128)S(1)} %get-tuple-element.16), channel_id=1, source_target_pairs={{0,0},{1,1},{2,4},{3,5},{4,2},{5,3},{6,6},{7,7},{8,8},{9,9},{10,12... | collective-permute-start | bytes 1277960 | tf_op jit(solution)/shard_map/ppermute | solution.py:246
  80.3 23.3 %collective-permute-start.21 = (f32[896,128]{1,0:T(8,128)S(1)}, f32[896,128]{1,0:T(8,128)S(1)}, u32[]{:S(2)}, u32[]{:S(2)}) collective-permute-start(f32[896,128]{1,0:T(8,128)S(1)} %join.1), channel_id=1, source_target_pairs={{0,2},{1,3},{2,6},{3,7},{4,0},{5,1},{6,4},{7,5},{8,10},{9,11},{10,... | collective-permute-start | bytes 1376264 | tf_op jit(solution)/shard_map/ppermute | solution.py:246

commit v9 on v8

--- a/solution.py
+++ b/solution.py
@@ -242,8 +242,23 @@
             while stop in onward:
                 stop = onward[stop]
             onward[stop] = start
-        everyone = range(row_count * col_count)
-        return lax.ppermute(x, AXES, [(i, onward.get(i, i)) for i in everyone])
+        idle = [i for i in range(row_count * col_count) if i not in onward]
+        rest = []
+        for i in idle:
+            twin = i + col_count if (i // col_count) % 2 == 0 else i - col_count
+            if twin in idle:
+                onward[i] = twin
+            else:
+                rest.append(i)
+        rest.sort(key=lambda i: i % col_count)
+        while rest:
+            ring, rest = (rest, []) if len(rest) == 3 else (rest[:2], rest[2:])
+            for i, j in zip(ring, ring[1:] + ring[:1]):
+                onward[i] = j
+        return lax.ppermute(x, AXES, sorted(onward.items()))
+
+    def send_some(x, pairs):
+        return lax.ppermute(x, AXES, pairs)
 
     def chosen(pairs, new, old):
         here = functools.reduce(jnp.logical_or, [me == d for _, d in pairs])
@@ -265,8 +280,8 @@
         for j in range(1, steps)
     ]
     near = factor[0, 0, 0]
-    la = send(near, [(line(1, 0), low_homes[0])])
-    ly = send(near, [(line(2, 1), low_homes[0]), (line(3, 1), low_homes[1]), (line(3, 2), high_homes[1])])
+    la = send_some(near, [(line(1, 0), low_homes[0])])
+    ly = send_some(near, [(line(2, 1), low_homes[0]), (line(3, 1), low_homes[1]), (line(3, 2), high_homes[1])])
 
     vector = jax.ShapeDtypeStruct((nrhs, width), F32)
     one = [VMEM((width, width), F32), pltpu.SemaphoreType.DMA]
@@ -284,7 +299,7 @@
     )(mine, *gathered, held_inverses)
     swapped = send(turned, [low_homes, low_homes[::-1], high_homes])
     later = lax.optimization_barrier((near, turned))[0]
-    lx = send(later, [(line(2, 0), low_homes[0]), (line(3, 0), low_homes[1])])
+    lx = send_some(later, [(line(2, 0), low_homes[0]), (line(3, 0), low_homes[1])])
     s_0, s_1 = pl.pallas_call(
         functools.partial(low_kernel, low_homes, col_count),
         in_specs=[vmem] * 4 + [hbm],

time: 105 us -> 97.4 us (0.928)
  starting transfers between devices: 58.1 us -> 37 us
  waiting for transfers between devices: 31.4 us -> 45.2 us
    ppermute x22, starting transfers between devices: 58.1 us -> 37 us  [the longest x19 33.2 us: send(): return lax.ppermute(x, AXES, sorted(onward.items()))]
    ppermute x22, waiting for transfers between devices: 31.4 us -> 45.2 us  [the longest x19 45.1 us: send(): return lax.ppermute(x, AXES, sorted(onward.items()))]
  transfers between devices with their start and end apart: 22 -> 22, of which waited for: 8 -> 11; matrix products, arithmetic and copies ran while one was open for 1% -> 1% of each run, Pallas kernels for 7% -> 8%
where the time goes in v9:
time: 97.4 us; the launch traced here: 97.1 us
  waiting for transfers between devices  45.2 us (46%)
  starting transfers between devices  37 us (38%)
  Pallas kernels  11.8 us (12%)
  local copies, waits for them, and re-layouts  2.15 us (2%)
    ppermute x19, waiting for transfers between devices, send(): return lax.ppermute(x, AXES, sorted(onward.items()))  45.1 us
    ppermute x19, starting transfers between devices, send(): return lax.ppermute(x, AXES, sorted(onward.items()))  33.2 us
    pallas_call x2, Pallas kernels, update(): pl.pallas_call(functools.partial(update_kernel, (groups, row_count, share...  6.55 us
    ppermute x3, starting transfers between devices, send_some(): return lax.ppermute(x, AXES, pairs)  3.86 us
  transfers between devices with their start and end apart: 22, of which 11 were waited for; matrix products, arithmetic and copies ran while one was open for 1% of the time, Pallas kernels for 8%

profile of v9, /device:TPU:0, one launch (start us, length us, event | category | flops | bytes accessed | tf_op | source)
XLA Modules:
  0.0 97.1 jit_solution(10029339725544057047)
XLA Ops:
  0.6 1.3 %slice_bitcast_fusion.near = f32[512,512]{1,0:T(8,128)S(1)} fusion(f32[6,1,1,512,512]{4,3,2,1,0:T(8,128)} %refs_8_.3), kind=kLoop, calls=%fused_computation | loop fusion | bytes 2097152 | tf_op jit(solution)/shard_map/squeeze | solution.py:282
  1.9 1.3 %collective-permute-start.4 = (f32[512,512]{1,0:T(8,128)S(1)}, f32[512,512]{1,0:T(8,128)S(1)}, u32[]{:S(2)}, u32[]{:S(2)}) collective-permute-start(f32[512,512]{1,0:T(8,128)S(1)} %slice_bitcast_fusion.near), channel_id=1, source_target_pairs={{1,0}} | collective-permute-start | bytes 3145736 | tf_op jit(solution)/shard_map/ppermute | solution.py:261
  3.2 0.8 slice_bitcast_fusion.1.own
  4.1 2.5 %collective-permute-start = (f32[128,128]{1,0:T(8,128)S(1)}, f32[128,128]{1,0:T(8,128)S(1)}, u32[]{:S(2)}, u32[]{:S(2)}) collective-permute-start(f32[128,128]{1,0:T(8,128)S(1)} %slice_bitcast_fusion.1.own), channel_id=1, source_target_pairs={{0,2},{1,3},{2,0},{3,1},{4,11},{5,7},{6,14},{7,5},{8,9},{9,8},{10,... | collective-permute-start | bytes 196616 | tf_op jit(solution)/shard_map/ppermute | solution.py:258
  6.5 1.9 %collective-permute-start.1 = (f32[128,128]{1,0:T(8,128)S(1)}, f32[128,128]{1,0:T(8,128)S(1)}, u32[]{:S(2)}, u32[]{:S(2)}) collective-permute-start(f32[128,128]{1,0:T(8,128)S(1)} %slice_bitcast_fusion.1.own), channel_id=1, source_target_pairs={{0,4},{1,5},{2,10},{3,9},{4,0},{5,1},{6,14},{7,13},{8,12},{9,3},{1... | collective-permute-start | bytes 196616 | tf_op jit(solution)/shard_map/ppermute | solution.py:258
  8.4 0.7 collective-permute-start.2
  9.1 1.3 %collective-permute-start.9 = (f32[512,512]{1,0:T(8,128)S(1)}, f32[512,512]{1,0:T(8,128)S(1)}, u32[]{:S(2)}, u32[]{:S(2)}) collective-permute-start(f32[512,512]{1,0:T(8,128)S(1)} %slice_bitcast_fusion.near), channel_id=1, source_target_pairs={{10,0},{11,1},{13,15}} | collective-permute-start | bytes 3145736 | tf_op jit(solution)/shard_map/ppermute | solution.py:261
  10.4 0.0 collective-permute-done.g1
  10.4 1.3 %collective-permute-done.1.g2 = f32[128,128]{1,0:T(8,128)S(1)} collective-permute-done((f32[128,128]{1,0:T(8,128)S(1)}, f32[128,128]{1,0:T(8,128)S(1)}, u32[]{:S(2)}, u32[]{:S(2)}) %collective-permute-start.1) | collective-permute-done | bytes 65568 | tf_op jit(solution)/shard_map/ppermute | solution.py:258
  11.7 2.8 %collective-permute-done.2.g3 = f32[128,128]{1,0:T(8,128)S(1)} collective-permute-done((f32[128,128]{1,0:T(8,128)S(1)}, f32[128,128]{1,0:T(8,128)S(1)}, u32[]{:S(2)}, u32[]{:S(2)}) %collective-permute-start.2) | collective-permute-done | bytes 65568 | tf_op jit(solution)/shard_map/ppermute | solution.py:258
  14.5 1.7 %turn.1.out.own = f32[128,512]{1,0:T(8,128)S(1)} custom-call(f32[128,128]{1,0:T(8,128)S(1)} %slice_bitcast_fusion.1.own, f32[128,128]{1,0:T(8,128)S(1)} %collective-permute-done.g1, f32[128,128]{1,0:T(8,128)S(1)} %collective-permute-done.1.g2, f32[128,128]{1,0:T(8,128)S(1)} %collective-permute-done.2.g3, f32[4,512,512]{2,1,0:T(8,128)} %inverses.5), custom_call_target="tpu_custom_call" | custom-call | flops 1000 | bytes 1000 | tf_op jit(solution)/shard_map/turn/pallas_call | solution.py:290
  16.2 1.3 %collective-permute-start.10 = (f32[512,512]{1,0:T(8,128)S(1)}, f32[512,512]{1,0:T(8,128)S(1)}, u32[]{:S(2)}, u32[]{:S(2)}) collective-permute-start(f32[512,512]{1,0:T(8,128)S(1)} %slice_bitcast_fusion.near), channel_id=1, source_target_pairs={{8,0},{9,1}} | collective-permute-start | bytes 3145736 | tf_op jit(solution)/shard_map/ppermute | solution.py:261
  17.5 0.8 collective-permute-start.3
  18.3 8.3 %collective-permute-done.3.swapped = f32[128,512]{1,0:T(8,128)S(1)} collective-permute-done((f32[128,512]{1,0:T(8,128)S(1)}, f32[128,512]{1,0:T(8,128)S(1)}, u32[]{:S(2)}, u32[]{:S(2)}) %collective-permute-start.3) | collective-permute-done | bytes 262176 | tf_op jit(solution)/shard_map/ppermute | solution.py:258
  26.5 0.0 collective-permute-done.4.la
  26.6 1.9 %solve_low.1 = (f32[128,512]{1,0:T(8,128)S(1)}, f32[128,512]{1,0:T(8,128)S(1)}) custom-call(f32[128,512]{1,0:T(8,128)S(1)} %turn.1.out.own, f32[128,512]{1,0:T(8,128)S(1)} %collective-permute-done.3.swapped, f32[512,512]{1,0:T(8,128)S(1)} %slice_bitcast_fusion.near, f32[512,512]{1,0:T(8,128)S(1)} %collective-permute-done.4.la, f32[4,512,512]{2,1,0:T(8,128)} %inverses.5), custom_call_target="tpu_custom_call" | custom-call | flops 1000 | bytes 1000 | tf_op jit(solution)/shard_map/solve_low/pallas_call | solution.py:303
  28.5 0.1 collective-permute-start.5
  28.6 0.0 collective-permute-done.9.ly.block
  28.6 0.0 collective-permute-done.10.lx
  28.6 0.6 reduce_low.1
  29.2 0.1 collective-permute-start.11
  29.3 0.1 collective-permute-start.12
  29.4 8.4 %collective-permute-done.5 = f32[128,512]{1,0:T(8,128)S(1)} collective-permute-done((f32[128,512]{1,0:T(8,128)S(1)}, f32[128,512]{1,0:T(8,128)S(1)}, u32[]{:S(2)}, u32[]{:S(2)}) %collective-permute-start.5) | collective-permute-done | bytes 262176 | tf_op jit(solution)/shard_map/ppermute | solution.py:258
  37.8 0.1 collective-permute-start.6
  37.9 2.8 %collective-permute-done.11.w_1 = f32[128,512]{1,0:T(8,128)S(1)} collective-permute-done((f32[128,512]{1,0:T(8,128)S(1)}, f32[128,512]{1,0:T(8,128)S(1)}, u32[]{:S(2)}, u32[]{:S(2)}) %collective-permute-start.11) | collective-permute-done | bytes 262176 | tf_op jit(solution)/shard_map/ppermute | solution.py:258
  40.6 0.0 collective-permute-done.12.w_2
  40.7 0.1 collective-permute-start.13
  40.7 0.5 collective-permute-start.14
  41.2 0.1 collective-permute-start.15
  41.3 0.4 collective-permute-start.7
  41.7 2.5 %collective-permute-done.6.refs_1_ = f32[128,512]{1,0:T(8,128)S(1)} collective-permute-done((f32[128,512]{1,0:T(8,128)S(1)}, f32[128,512]{1,0:T(8,128)S(1)}, u32[]{:S(2)}, u32[]{:S(2)}) %collective-permute-start.6) | collective-permute-done | bytes 262176 | tf_op jit(solution)/shard_map/ppermute | solution.py:258
  44.2 0.0 collective-permute-start.16
  44.2 0.0 collective-permute-done.13
  44.2 0.5 collective-permute-start.8
  44.7 0.0 collective-permute-done.14
  44.7 0.0 collective-permute-done.15
  44.7 0.1 select_select_fusion.refs_5_
  44.8 0.1 collective-permute-start.17
  44.9 0.0 collective-permute-done.7.refs_2_
  44.9 0.9 collective-permute-done.16.refs_6_
  45.7 0.4 collective-permute-done.8.refs_3_
  46.1 0.4 collective-permute-done.17.refs_7_
  46.5 3.3 %update_first.1 = (f32[832,128]{1,0:T(8,128)S(1)}, f32[832,128]{1,0:T(8,128)S(1)}) custom-call(f32[128,512]{1,0:T(8,128)S(1)} %broadcast_select_fusion.refs_0_, f32[128,512]{1,0:T(8,128)S(1)} %collective-permute-done.6.refs_1_, f32[128,512]{1,0:T(8,128)S(1)} %collective-permute-done.7.refs_2_, f32[128,512]{1,0:T(8,128)S(1)} %collective-permute-done.8.refs_3_, ...), custom_call_target="tpu_custom_call" | custom-call | flops 1000 | bytes 1000 | tf_op jit(solution)/shard_map/update_first/pallas_call | solution.py:383
  49.8 0.0 copy-start
  49.8 0.1 collective-permute-start.18
  49.9 13.5 %collective-permute-start.19 = (f32[832,128]{1,0:T(8,128)S(1)}, f32[832,128]{1,0:T(8,128)S(1)}, u32[]{:S(2)}, u32[]{:S(2)}) collective-permute-start(f32[832,128]{1,0:T(8,128)S(1)} %get-tuple-element.16), channel_id=1, source_target_pairs={{0,4},{1,5},{2,0},{3,1},{4,6},{5,7},{6,2},{7,3},{8,12},{9,13},{10,... | collective-permute-start | bytes 1277960 | tf_op jit(solution)/shard_map/ppermute | solution.py:258
  63.4 0.0 collective-permute-start.20
  63.4 3.3 %update_second.1 = (f32[832,128]{1,0:T(8,128)S(1)}, f32[896,128]{1,0:T(8,128)S(1)}) custom-call(f32[128,512]{1,0:T(8,128)S(1)} %broadcast_select_fusion.refs_0_, f32[128,512]{1,0:T(8,128)S(1)} %collective-permute-done.6.refs_1_, f32[128,512]{1,0:T(8,128)S(1)} %collective-permute-done.7.refs_2_, f32[128,512]{1,0:T(8,128)S(1)} %collective-permute-done.8.refs_3_, ...), custom_call_target="tpu_custom_call" | custom-call | flops 1000 | bytes 1000 | tf_op jit(solution)/shard_map/update_second/pallas_call | solution.py:383
  66.6 0.0 collective-permute-done.18.theirs.got_1
  66.7 6.1 %collective-permute-done.19.got_2 = f32[832,128]{1,0:T(8,128)S(1)} collective-permute-done((f32[832,128]{1,0:T(8,128)S(1)}, f32[832,128]{1,0:T(8,128)S(1)}, u32[]{:S(2)}, u32[]{:S(2)}) %collective-permute-start.19) | collective-permute-done | bytes 426016 | tf_op jit(solution)/shard_map/ppermute | solution.py:258
  72.8 0.0 collective-permute-done.20.got_4
  72.8 11.9 %collective-permute-start.21 = (f32[896,128]{1,0:T(8,128)S(1)}, f32[896,128]{1,0:T(8,128)S(1)}, u32[]{:S(2)}, u32[]{:S(2)}) collective-permute-start(f32[896,128]{1,0:T(8,128)S(1)} %join.1), channel_id=1, source_target_pairs={{0,2},{1,3},{2,6},{3,7},{4,0},{5,1},{6,4},{7,5},{8,10},{9,11},{10,... | collective-permute-start | bytes 1376264 | tf_op jit(solution)/shard_map/ppermute | solution.py:258
  84.7 11.4 %collective-permute-done.21.got_3 = f32[896,128]{1,0:T(8,128)S(1)} collective-permute-done((f32[896,128]{1,0:T(8,128)S(1)}, f32[896,128]{1,0:T(8,128)S(1)}, u32[]{:S(2)}, u32[]{:S(2)}) %collective-permute-start.21) | collective-permute-done | bytes 458784 | tf_op jit(solution)/shard_map/ppermute | solution.py:258
  96.1 0.0 copy-done
  96.1 1.0 %add_up.1 = (f32[4,64,128]{2,1,0:T(8,128)}, f32[6,128,128]{2,1,0:T(8,128)}) custom-call(f32[6,128,128]{2,1,0:T(8,128)S(1)} %bitcast.8, f32[832,128]{1,0:T(8,128)S(1)} %get-tuple-element.14.own, f32[832,128]{1,0:T(8,128)S(1)} %collective-permute-done.18.theirs.got_1, f32[832,128]{1,0:T(8,128)S(1)} %collective-permute-done.19.got_2, ...), custom_call_target="tpu_custom_call" | custom-call | flops 1000 | bytes 1000 | tf_op jit(solution)/shard_map/add_up/pallas_call | solution.py:420
  (3 shorter events, 0.1 us)
Async XLA Ops:
  1.9 24.6 %collective-permute-start.4 = (f32[512,512]{1,0:T(8,128)S(1)}, f32[512,512]{1,0:T(8,128)S(1)}, u32[]{:S(2)}, u32[]{:S(2)}) collective-permute-start(f32[512,512]{1,0:T(8,128)S(1)} %slice_bitcast_fusion.near), channel_id=1, source_target_pairs={{1,0}} | collective-permute-start | bytes 3145736 | tf_op jit(solution)/shard_map/ppermute | solution.py:261
  4.1 6.3 %collective-permute-start = (f32[128,128]{1,0:T(8,128)S(1)}, f32[128,128]{1,0:T(8,128)S(1)}, u32[]{:S(2)}, u32[]{:S(2)}) collective-permute-start(f32[128,128]{1,0:T(8,128)S(1)} %slice_bitcast_fusion.1.own), channel_id=1, source_target_pairs={{0,2},{1,3},{2,0},{3,1},{4,11},{5,7},{6,14},{7,5},{8,9},{9,8},{10,... | collective-permute-start | bytes 196616 | tf_op jit(solution)/shard_map/ppermute | solution.py:258
  6.5 5.2 %collective-permute-start.1 = (f32[128,128]{1,0:T(8,128)S(1)}, f32[128,128]{1,0:T(8,128)S(1)}, u32[]{:S(2)}, u32[]{:S(2)}) collective-permute-start(f32[128,128]{1,0:T(8,128)S(1)} %slice_bitcast_fusion.1.own), channel_id=1, source_target_pairs={{0,4},{1,5},{2,10},{3,9},{4,0},{5,1},{6,14},{7,13},{8,12},{9,3},{1... | collective-permute-start | bytes 196616 | tf_op jit(solution)/shard_map/ppermute | solution.py:258
  8.4 6.1 %collective-permute-start.2 = (f32[128,128]{1,0:T(8,128)S(1)}, f32[128,128]{1,0:T(8,128)S(1)}, u32[]{:S(2)}, u32[]{:S(2)}) collective-permute-start(f32[128,128]{1,0:T(8,128)S(1)} %slice_bitcast_fusion.1.own), channel_id=1, source_target_pairs={{0,6},{1,7},{2,10},{3,11},{4,8},{5,13},{6,0},{7,1},{8,4},{9,15},{1... | collective-permute-start | bytes 196616 | tf_op jit(solution)/shard_map/ppermute | solution.py:258
  9.1 19.5 %collective-permute-start.9 = (f32[512,512]{1,0:T(8,128)S(1)}, f32[512,512]{1,0:T(8,128)S(1)}, u32[]{:S(2)}, u32[]{:S(2)}) collective-permute-start(f32[512,512]{1,0:T(8,128)S(1)} %slice_bitcast_fusion.near), channel_id=1, source_target_pairs={{10,0},{11,1},{13,15}} | collective-permute-start | bytes 3145736 | tf_op jit(solution)/shard_map/ppermute | solution.py:261
  16.2 12.4 %collective-permute-start.10 = (f32[512,512]{1,0:T(8,128)S(1)}, f32[512,512]{1,0:T(8,128)S(1)}, u32[]{:S(2)}, u32[]{:S(2)}) collective-permute-start(f32[512,512]{1,0:T(8,128)S(1)} %slice_bitcast_fusion.near), channel_id=1, source_target_pairs={{8,0},{9,1}} | collective-permute-start | bytes 3145736 | tf_op jit(solution)/shard_map/ppermute | solution.py:261
  17.5 9.0 %collective-permute-start.3 = (f32[128,512]{1,0:T(8,128)S(1)}, f32[128,512]{1,0:T(8,128)S(1)}, u32[]{:S(2)}, u32[]{:S(2)}) collective-permute-start(f32[128,512]{1,0:T(8,128)S(1)} %turn.1.out.own), channel_id=1, source_target_pairs={{0,1},{1,0},{2,10},{3,11},{4,7},{5,13},{6,14},{7,4},{8,9},{9,8},{1... | collective-permute-start | bytes 786440 | tf_op jit(solution)/shard_map/ppermute | solution.py:258
  28.5 9.2 %collective-permute-start.5 = (f32[128,512]{1,0:T(8,128)S(1)}, f32[128,512]{1,0:T(8,128)S(1)}, u32[]{:S(2)}, u32[]{:S(2)}) collective-permute-start(f32[128,512]{1,0:T(8,128)S(1)} %get-tuple-element.12.s_b), channel_id=1, source_target_pairs={{0,2},{1,3},{2,0},{3,1},{4,12},{5,13},{6,14},{7,15},{8,9},{9,8},{1... | collective-permute-start | bytes 786440 | tf_op jit(solution)/shard_map/ppermute | solution.py:258
  29.2 11.4 %collective-permute-start.11 = (f32[128,512]{1,0:T(8,128)S(1)}, f32[128,512]{1,0:T(8,128)S(1)}, u32[]{:S(2)}, u32[]{:S(2)}) collective-permute-start(f32[128,512]{1,0:T(8,128)S(1)} %reduce_low.1), channel_id=1, source_target_pairs={{0,15},{1,9},{2,10},{3,11},{4,12},{5,13},{6,14},{7,8},{8,7},{9,1},... | collective-permute-start | bytes 786440 | tf_op jit(solution)/shard_map/ppermute | solution.py:258
  29.3 11.4 %collective-permute-start.12 = (f32[128,512]{1,0:T(8,128)S(1)}, f32[128,512]{1,0:T(8,128)S(1)}, u32[]{:S(2)}, u32[]{:S(2)}) collective-permute-start(f32[128,512]{1,0:T(8,128)S(1)} %reduce_low.1), channel_id=1, source_target_pairs={{0,12},{1,15},{2,10},{3,11},{4,7},{5,13},{6,14},{7,4},{8,9},{9,8},... | collective-permute-start | bytes 786440 | tf_op jit(solution)/shard_map/ppermute | solution.py:258
  37.8 6.4 %collective-permute-start.6 = (f32[128,512]{1,0:T(8,128)S(1)}, f32[128,512]{1,0:T(8,128)S(1)}, u32[]{:S(2)}, u32[]{:S(2)}) collective-permute-start(f32[128,512]{1,0:T(8,128)S(1)} %broadcast_select_fusion.refs_0_), channel_id=1, source_target_pairs={{0,16},{1,17},{2,18},{3,19},{4,12},{5,13},{6,14},{7,15},{8,24},{9,... | collective-permute-start | bytes 786440 | tf_op jit(solution)/shard_map/ppermute | solution.py:258
  40.7 3.6 %collective-permute-start.13 = (f32[128,512]{1,0:T(8,128)S(1)}, f32[128,512]{1,0:T(8,128)S(1)}, u32[]{:S(2)}, u32[]{:S(2)}) collective-permute-start(f32[128,512]{1,0:T(8,128)S(1)} %solve_high.1.refs_4_), channel_id=1, source_target_pairs={{0,8},{1,9},{2,10},{3,11},{4,21},{5,13},{6,14},{7,22},{8,0},{9,1},... | collective-permute-start | bytes 786440 | tf_op jit(solution)/shard_map/ppermute | solution.py:258
  40.7 4.0 %collective-permute-start.14 = (f32[128,512]{1,0:T(8,128)S(1)}, f32[128,512]{1,0:T(8,128)S(1)}, u32[]{:S(2)}, u32[]{:S(2)}) collective-permute-start(f32[128,512]{1,0:T(8,128)S(1)} %solve_high.1.refs_4_), channel_id=1, source_target_pairs={{0,8},{1,9},{2,10},{3,11},{4,5},{5,4},{6,7},{7,6},{8,0},{9,1},{10,... | collective-permute-start | bytes 786440 | tf_op jit(solution)/shard_map/ppermute | solution.py:258
  41.2 3.5 %collective-permute-start.15 = (f32[128,512]{1,0:T(8,128)S(1)}, f32[128,512]{1,0:T(8,128)S(1)}, u32[]{:S(2)}, u32[]{:S(2)}) collective-permute-start(f32[128,512]{1,0:T(8,128)S(1)} %solve_high.1.refs_4_), channel_id=1, source_target_pairs={{0,8},{1,9},{2,10},{3,11},{4,20},{5,13},{6,14},{7,23},{8,0},{9,1},... | collective-permute-start | bytes 786440 | tf_op jit(solution)/shard_map/ppermute | solution.py:258
  41.3 3.6 %collective-permute-start.7 = (f32[128,512]{1,0:T(8,128)S(1)}, f32[128,512]{1,0:T(8,128)S(1)}, u32[]{:S(2)}, u32[]{:S(2)}) collective-permute-start(f32[128,512]{1,0:T(8,128)S(1)} %broadcast_select_fusion.refs_0_), channel_id=1, source_target_pairs={{0,8},{1,9},{2,10},{3,11},{4,12},{5,13},{6,14},{7,15},{8,0},{9,1},... | collective-permute-start | bytes 786440 | tf_op jit(solution)/shard_map/ppermute | solution.py:258
  44.2 1.5 %collective-permute-start.16 = (f32[128,512]{1,0:T(8,128)S(1)}, f32[128,512]{1,0:T(8,128)S(1)}, u32[]{:S(2)}, u32[]{:S(2)}) collective-permute-start(f32[128,512]{1,0:T(8,128)S(1)} %solve_high.1.refs_4_), channel_id=1, source_target_pairs={{0,8},{1,9},{2,10},{3,11},{4,12},{5,13},{6,14},{7,15},{8,0},{9,1},... | collective-permute-start | bytes 786440 | tf_op jit(solution)/shard_map/ppermute | solution.py:258
  44.2 1.9 %collective-permute-start.8 = (f32[128,512]{1,0:T(8,128)S(1)}, f32[128,512]{1,0:T(8,128)S(1)}, u32[]{:S(2)}, u32[]{:S(2)}) collective-permute-start(f32[128,512]{1,0:T(8,128)S(1)} %collective-permute-done.6.refs_1_), channel_id=1, source_target_pairs={{0,8},{1,9},{2,10},{3,11},{4,12},{5,13},{6,14},{7,15},{8,0},{9,1},... | collective-permute-start | bytes 786440 | tf_op jit(solution)/shard_map/ppermute | solution.py:258
  44.8 1.7 %collective-permute-start.17 = (f32[128,512]{1,0:T(8,128)S(1)}, f32[128,512]{1,0:T(8,128)S(1)}, u32[]{:S(2)}, u32[]{:S(2)}) collective-permute-start(f32[128,512]{1,0:T(8,128)S(1)} %select_select_fusion.refs_5_), channel_id=1, source_target_pairs={{0,8},{1,9},{2,10},{3,11},{4,12},{5,13},{6,14},{7,15},{8,0},{9,1},... | collective-permute-start | bytes 786440 | tf_op jit(solution)/shard_map/ppermute | solution.py:258
  49.8 46.3 %copy-start = (f32[6,1,1,128,128]{4,3,2,1,0:T(8,128)S(1)}, f32[6,1,1,128,128]{4,3,2,1,0:T(8,128)}, u32[]{:S(2)}) copy-start(f32[6,1,1,128,128]{4,3,2,1,0:T(8,128)} %param.4) | copy-start | bytes 1179652
  49.8 16.9 %collective-permute-start.18 = (f32[832,128]{1,0:T(8,128)S(1)}, f32[832,128]{1,0:T(8,128)S(1)}, u32[]{:S(2)}, u32[]{:S(2)}) collective-permute-start(f32[832,128]{1,0:T(8,128)S(1)} %get-tuple-element.15), channel_id=1, source_target_pairs={{0,2},{1,3},{2,0},{3,1},{4,6},{5,7},{6,4},{7,5},{8,10},{9,11},{10,... | collective-permute-start | bytes 1277960 | tf_op jit(solution)/shard_map/ppermute | solution.py:258
  49.9 22.9 %collective-permute-start.19 = (f32[832,128]{1,0:T(8,128)S(1)}, f32[832,128]{1,0:T(8,128)S(1)}, u32[]{:S(2)}, u32[]{:S(2)}) collective-permute-start(f32[832,128]{1,0:T(8,128)S(1)} %get-tuple-element.16), channel_id=1, source_target_pairs={{0,4},{1,5},{2,0},{3,1},{4,6},{5,7},{6,2},{7,3},{8,12},{9,13},{10,... | collective-permute-start | bytes 1277960 | tf_op jit(solution)/shard_map/ppermute | solution.py:258
  63.4 9.4 %collective-permute-start.20 = (f32[832,128]{1,0:T(8,128)S(1)}, f32[832,128]{1,0:T(8,128)S(1)}, u32[]{:S(2)}, u32[]{:S(2)}) collective-permute-start(f32[832,128]{1,0:T(8,128)S(1)} %get-tuple-element.16), channel_id=1, source_target_pairs={{0,8},{1,9},{2,4},{3,5},{4,2},{5,3},{6,14},{7,15},{8,0},{9,1},{10,... | collective-permute-start | bytes 1277960 | tf_op jit(solution)/shard_map/ppermute | solution.py:258
  72.8 23.3 %collective-permute-start.21 = (f32[896,128]{1,0:T(8,128)S(1)}, f32[896,128]{1,0:T(8,128)S(1)}, u32[]{:S(2)}, u32[]{:S(2)}) collective-permute-start(f32[896,128]{1,0:T(8,128)S(1)} %join.1), channel_id=1, source_target_pairs={{0,2},{1,3},{2,6},{3,7},{4,0},{5,1},{6,4},{7,5},{8,10},{9,11},{10,... | collective-permute-start | bytes 1376264 | tf_op jit(solution)/shard_map/ppermute | solution.py:258

commit v10 on v8

--- a/solution.py
+++ b/solution.py
@@ -111,7 +111,7 @@
     groups, row_count, share, homes, slots, blocks = cfg
     steps = len(homes)
     ways, panel, refs = refs[:8], refs[8], refs[9:]
-    outs, (tiles, s, turned, sems) = refs[:2], refs[2:]
+    outs, shares, (tiles, s, turned, sems) = refs[:2], refs[2:-4], refs[-4:]
     quarter = turned.shape[0]
     row = lax.axis_index("row")
     col = lax.axis_index("col")
@@ -128,7 +128,7 @@
                 tiles.at[r, :, pl.ds(i * quarter, quarter)],
                 sems.at[2 * r + i],
             )
-            for i in range(2)
+            for i in range(len(outs))
         ]
         for r in range(blocks)
     ]
@@ -165,48 +165,45 @@
         full = product(s[...], tiles[r]) * keep
         for i, out in enumerate(outs):
             out[pl.ds(r * quarter, quarter), :] = full[:, i * quarter: (i + 1) * quarter]
-    for i, out in enumerate(outs):
-        turned[...] = s[:, columns[i]].T
+    for place, out in zip(columns, outs + shares):
+        turned[...] = s[:, place].T
         rows = pl.ds(pl.multiple_of(group * share, share), share)
-        out[pl.ds(blocks * quarter, share), :] = turned[rows, :]
-
-
-def join_kernel(cfg, mine, theirs, got_2, got_4, out):
-    del got_2, got_4
+        first = blocks * quarter if out.shape[0] > share else 0
+        out[pl.ds(first, share), :] = turned[rows, :]
+
+
+def join_kernel(cfg, mine, theirs, out):
     groups, share = cfg
-    last = theirs.shape[0] - share
+    last = out.shape[0] - share
     member = lax.axis_index("col") // groups
-    out[...] = mine[...]
 
     @pl.when((member == 1) | (member == 2))
     def _():
         out[:last, :] = mine[:last, :] + theirs[:last, :]
-        out[pl.ds(last + share, share), :] = theirs[last:, :]
-
-
-def last_kernel(groups, rhs, own, got_1, got_2, got_4, got_3, solved, out):
+        out[last:, :] = mine[pl.ds(last, share), :]
+
+
+def last_kernel(groups, rhs, own, got_1, got_2, got_3, got_4, joined, far, solved, out):
     blocks, quarter = rhs.shape[0], rhs.shape[1]
     last, share = blocks * quarter, solved.shape[1]
     member = lax.axis_index("col") // groups
 
-    def finish(at, parts, joined_members=()):
+    def finish(at, *parts):
         @pl.when(member == at)
         def _():
             for r in range(blocks):
                 rows = pl.ds(r * quarter, quarter)
                 total = functools.reduce(jnp.add, [part[rows, :] for part, _ in parts])
-                if joined_members:
-                    total = total + got_3[rows, :]
                 out[r] = rhs[r] - total.T
             for part, k in parts:
                 solved[k] = part[pl.ds(last, share), :]
-            for i, k in enumerate(joined_members):
-                solved[k] = got_3[pl.ds(last + i * share, share), :]
-
-    finish(0, [(own, 0), (got_1, 1)], (2, 3))
-    finish(1, [(own, 1), (got_2, 3), (got_3, 0), (got_4, 2)])
-    finish(2, [(own, 2), (got_2, 0), (got_3, 3), (got_4, 1)])
-    finish(3, [(own, 3), (got_1, 2)], (1, 0))
+            if at in (0, 3):
+                solved[3 - at] = far[...]
+
+    finish(0, (own, 0), (got_1, 1), (joined, 2))
+    finish(1, (own, 1), (got_2, 3), (got_3, 0), (got_4, 2))
+    finish(2, (own, 2), (got_2, 0), (got_3, 3), (got_4, 1))
+    finish(3, (own, 3), (got_1, 2), (joined, 1))
 
 
 def on_device(factor, rhs, inverses):
@@ -236,14 +233,37 @@
     high_homes = (line(2, top - 1), line(3, top))
 
     def send(x, pairs):
+        def twin(i):
+            return i + col_count if (i // col_count) % 2 == 0 else i - col_count
+
         onward = dict(pairs)
+        taken = set(onward) | set(onward.values())
         for start in sorted(set(onward) - set(onward.values())):
             stop = onward[start]
             while stop in onward:
                 stop = onward[stop]
-            onward[stop] = start
-        everyone = range(row_count * col_count)
-        return lax.ppermute(x, AXES, [(i, onward.get(i, i)) for i in everyone])
+            back = [twin(stop), twin(start)]
+            if twin(start) == stop or taken & set(back):
+                onward[stop] = start
+            else:
+                onward[stop], onward[back[0]], onward[back[1]] = back[0], back[1], start
+                taken |= set(back)
+        left = []
+        for i in range(row_count * col_count):
+            if i not in onward:
+                if twin(i) in taken:
+                    left.append(i)
+                else:
+                    onward[i] = twin(i)
+        paired = [i for i in sorted(onward) if onward[i] == twin(i) and i not in taken]
+        for i in left:
+            j = min(paired, key=lambda j: (j % col_count != i % col_count, abs(j - i)))
+            onward[i], onward[j] = onward[j], i
+            paired.remove(j)
+        return lax.ppermute(x, AXES, sorted(onward.items()))
+
+    def send_some(x, pairs):
+        return lax.ppermute(x, AXES, pairs)
 
     def chosen(pairs, new, old):
         here = functools.reduce(jnp.logical_or, [me == d for _, d in pairs])
@@ -360,15 +380,16 @@
     s_low = jnp.where(member == 0, s_0, moved)
     ways = spread(s_low, {0: homes[0], 1: homes[1]}) + spread(s_high, {2: homes[2], 3: homes[3]})
 
-    part, joint = [
-        jax.ShapeDtypeStruct((blocks * quarter + n * share, nrhs), F32) for n in (1, 2)
+    far_share, part, longer = [
+        jax.ShapeDtypeStruct((n, nrhs), F32)
+        for n in (share, blocks * quarter + share, blocks * quarter + share + 8)
     ]
 
     def update(name, shapes, *slots):
         return pl.pallas_call(
             functools.partial(update_kernel, (groups, row_count, share, homes, slots, blocks)),
             in_specs=[vmem] * 8 + [hbm],
-            out_specs=[vmem] * 2,
+            out_specs=[vmem] * len(shapes),
             out_shape=shapes,
             scratch_shapes=[
                 VMEM((blocks, width, 2 * quarter), F32),
@@ -381,8 +402,10 @@
             name=name,
         )(*ways, held_factor)
 
-    part_a, part_b = update("update_first", [part, part], (3, 0, 3, 0), (2, 2, 1, 1))
-    own, part_c = update("update_second", [part, joint], (0, 1, 2, 3), (1, 3, 0, 2))
+    part_a, part_b, far = update(
+        "update_first", [part, longer, far_share], (3, 0, 3, 0), (2, 2, 1, 1), (3, 0, 0, 0)
+    )
+    own, part_c = update("update_second", [part, longer], (0, 1, 2, 3), (1, 3, 0, 2))
     across = [(r, g) for r in range(row_count) for g in range(groups)]
 
     def route(*hops):
@@ -391,20 +414,22 @@
     got_1 = send(part_a, route((3, 2), (0, 1), (1, 0), (2, 3)))
     got_4 = send(part_b, route((2, 1), (1, 2)))
     got_2 = send(part_b, route((3, 1), (1, 0), (0, 2), (2, 3)))
+    got_3 = send_some(part_c, route((3, 2), (0, 1)))
     joined = pl.pallas_call(
         functools.partial(join_kernel, (groups, share)),
-        in_specs=[vmem] * 2 + [pl.BlockSpec(memory_space=pl.ANY)] * 2,
+        in_specs=[vmem] * 2,
         out_specs=vmem,
-        out_shape=joint,
+        out_shape=part,
         compiler_params=PARAMS,
         cost_estimate=CHEAP,
         name="join",
-    )(part_c, got_1, got_2, got_4)
-    got_3 = send(joined, route((3, 2), (0, 1), (2, 0), (1, 3)))
+    )(part_c, got_1)
+    joined = send_some(joined, route((2, 0), (1, 3)))
+    far = send(far, route((3, 0), (0, 3), (1, 2), (2, 1)))
 
     solved, remaining = pl.pallas_call(
         functools.partial(last_kernel, groups),
-        in_specs=[vmem] * 6,
+        in_specs=[vmem] * 8,
         out_specs=[vmem] * 2,
         out_shape=[
             jax.ShapeDtypeStruct((steps, share, nrhs), F32),
@@ -413,7 +438,7 @@
         compiler_params=PARAMS,
         cost_estimate=CHEAP,
         name="add_up",
-    )(rhs[:, 0, 0], own, got_1, got_2, got_4, got_3)
+    )(rhs[:, 0, 0], own, got_1, got_2, got_3, got_4, joined, far)
     return solved, remaining[:, None, None]
 
 

time: 105 us -> 83.4 us (0.79)
  starting transfers between devices: 58.1 us -> 30.2 us
  waiting for transfers between devices: 31.4 us -> 38 us
    ppermute x22 -> x24, starting transfers between devices: 58.1 us -> 30.2 us  [the longest x22 24.5 us: send(): return lax.ppermute(x, AXES, sorted(onward.items()))]
    ppermute x22 -> x24, waiting for transfers between devices: 31.4 us -> 38 us  [the longest x22 37.7 us: send(): return lax.ppermute(x, AXES, sorted(onward.items()))]
  transfers between devices with their start and end apart: 22 -> 24, of which waited for: 8 -> 14; matrix products, arithmetic and copies ran while one was open for 1% -> 1% of each run, Pallas kernels for 7% -> 9%
where the time goes in v10:
time: 83.4 us; the launch traced here: 83.1 us
  waiting for transfers between devices  38 us (46%)
  starting transfers between devices  30.2 us (36%)
  Pallas kernels  11.8 us (14%)
  local copies, waits for them, and re-layouts  2.15 us (3%)
    ppermute x22, waiting for transfers between devices, send(): return lax.ppermute(x, AXES, sorted(onward.items()))  37.7 us
    ppermute x22, starting transfers between devices, send(): return lax.ppermute(x, AXES, sorted(onward.items()))  24.5 us
    pallas_call x2, Pallas kernels, update(): pl.pallas_call(functools.partial(update_kernel, (groups, row_count, share...  6.55 us
    ppermute x2, starting transfers between devices, send_some(): return lax.ppermute(x, AXES, pairs)  5.74 us
    pallas_call x1, Pallas kernels, on_device(): pl.pallas_call(functools.partial(low_kernel, low_homes, col_count), in_sp...  1.93 us
    pallas_call x1, Pallas kernels, on_device(): pl.pallas_call(functools.partial(turn_kernel, order, low_homes[0], col_co...  1.7 us
  transfers between devices with their start and end apart: 24, of which 14 were waited for; matrix products, arithmetic and copies ran while one was open for 1% of the time, Pallas kernels for 9%

profile of v10, /device:TPU:0, one launch (start us, length us, event | category | flops | bytes accessed | tf_op | source)
XLA Modules:
  0.0 83.1 jit_solution(17851804018371967823)
XLA Ops:
  0.6 1.3 %slice_bitcast_fusion.near = f32[512,512]{1,0:T(8,128)S(1)} fusion(f32[6,1,1,512,512]{4,3,2,1,0:T(8,128)} %refs_8_.3), kind=kLoop, calls=%fused_computation | loop fusion | bytes 2097152 | tf_op jit(solution)/shard_map/squeeze | solution.py:287
  1.9 0.5 collective-permute-start.4
  2.5 0.8 %slice_bitcast_fusion.1.own = f32[128,128]{1,0:T(8,128)S(1)} fusion(f32[6,1,1,128,128]{4,3,2,1,0:T(8,128)} %param.4), kind=kLoop, calls=%fused_computation.3 | loop fusion | bytes 131072 | tf_op jit(solution)/shard_map/squeeze | solution.py:278
  3.3 2.6 %collective-permute-start = (f32[128,128]{1,0:T(8,128)S(1)}, f32[128,128]{1,0:T(8,128)S(1)}, u32[]{:S(2)}, u32[]{:S(2)}) collective-permute-start(f32[128,128]{1,0:T(8,128)S(1)} %slice_bitcast_fusion.1.own), channel_id=1, source_target_pairs={{0,2},{1,9},{2,0},{3,1},{4,28},{5,13},{6,14},{7,5},{8,24},{9,11},{... | collective-permute-start | bytes 196616 | tf_op jit(solution)/shard_map/ppermute | solution.py:263
  5.9 2.6 %collective-permute-start.1 = (f32[128,128]{1,0:T(8,128)S(1)}, f32[128,128]{1,0:T(8,128)S(1)}, u32[]{:S(2)}, u32[]{:S(2)}) collective-permute-start(f32[128,128]{1,0:T(8,128)S(1)} %slice_bitcast_fusion.1.own), channel_id=1, source_target_pairs={{0,4},{1,9},{2,10},{3,11},{4,0},{5,1},{6,14},{7,3},{8,12},{9,13},{... | collective-permute-start | bytes 196616 | tf_op jit(solution)/shard_map/ppermute | solution.py:263
  8.5 0.0 collective-permute-start.2
  8.5 0.0 collective-permute-start.9
  8.5 0.0 collective-permute-done.g1
  8.5 2.6 %collective-permute-done.1.g2 = f32[128,128]{1,0:T(8,128)S(1)} collective-permute-done((f32[128,128]{1,0:T(8,128)S(1)}, f32[128,128]{1,0:T(8,128)S(1)}, u32[]{:S(2)}, u32[]{:S(2)}) %collective-permute-start.1) | collective-permute-done | bytes 65568 | tf_op jit(solution)/shard_map/ppermute | solution.py:263
  11.1 3.6 %collective-permute-done.2.g3 = f32[128,128]{1,0:T(8,128)S(1)} collective-permute-done((f32[128,128]{1,0:T(8,128)S(1)}, f32[128,128]{1,0:T(8,128)S(1)}, u32[]{:S(2)}, u32[]{:S(2)}) %collective-permute-start.2) | collective-permute-done | bytes 65568 | tf_op jit(solution)/shard_map/ppermute | solution.py:263
  14.6 1.7 %turn.1.out.own = f32[128,512]{1,0:T(8,128)S(1)} custom-call(f32[128,128]{1,0:T(8,128)S(1)} %slice_bitcast_fusion.1.own, f32[128,128]{1,0:T(8,128)S(1)} %collective-permute-done.g1, f32[128,128]{1,0:T(8,128)S(1)} %collective-permute-done.1.g2, f32[128,128]{1,0:T(8,128)S(1)} %collective-permute-done.2.g3, f32[4,512,512]{2,1,0:T(8,128)} %inverses.5), custom_call_target="tpu_custom_call" | custom-call | flops 1000 | bytes 1000 | tf_op jit(solution)/shard_map/turn/pallas_call | solution.py:295
  16.3 0.1 collective-permute-start.10
  16.4 0.1 collective-permute-start.3
  16.5 6.4 %collective-permute-done.3.swapped = f32[128,512]{1,0:T(8,128)S(1)} collective-permute-done((f32[128,512]{1,0:T(8,128)S(1)}, f32[128,512]{1,0:T(8,128)S(1)}, u32[]{:S(2)}, u32[]{:S(2)}) %collective-permute-start.3) | collective-permute-done | bytes 262176 | tf_op jit(solution)/shard_map/ppermute | solution.py:263
  22.8 0.0 collective-permute-done.4.la
  22.8 1.9 %solve_low.1 = (f32[128,512]{1,0:T(8,128)S(1)}, f32[128,512]{1,0:T(8,128)S(1)}) custom-call(f32[128,512]{1,0:T(8,128)S(1)} %turn.1.out.own, f32[128,512]{1,0:T(8,128)S(1)} %collective-permute-done.3.swapped, f32[512,512]{1,0:T(8,128)S(1)} %slice_bitcast_fusion.near, f32[512,512]{1,0:T(8,128)S(1)} %collective-permute-done.4.la, f32[4,512,512]{2,1,0:T(8,128)} %inverses.5), custom_call_target="tpu_custom_call" | custom-call | flops 1000 | bytes 1000 | tf_op jit(solution)/shard_map/solve_low/pallas_call | solution.py:308
  24.8 0.1 collective-permute-start.5
  24.9 0.0 collective-permute-done.9.ly.block
  24.9 0.0 collective-permute-done.10.lx
  24.9 0.6 reduce_low.1
  25.5 2.1 %collective-permute-start.11 = (f32[128,512]{1,0:T(8,128)S(1)}, f32[128,512]{1,0:T(8,128)S(1)}, u32[]{:S(2)}, u32[]{:S(2)}) collective-permute-start(f32[128,512]{1,0:T(8,128)S(1)} %reduce_low.1), channel_id=1, source_target_pairs={{0,15},{1,9},{2,10},{3,11},{4,12},{5,13},{6,14},{7,8},{8,0},{9,1},... | collective-permute-start | bytes 786440 | tf_op jit(solution)/shard_map/ppermute | solution.py:263
  27.6 1.1 %collective-permute-start.12 = (f32[128,512]{1,0:T(8,128)S(1)}, f32[128,512]{1,0:T(8,128)S(1)}, u32[]{:S(2)}, u32[]{:S(2)}) collective-permute-start(f32[128,512]{1,0:T(8,128)S(1)} %reduce_low.1), channel_id=1, source_target_pairs={{0,12},{1,15},{2,10},{3,11},{4,8},{5,13},{6,14},{7,9},{8,0},{9,1},... | collective-permute-start | bytes 786440 | tf_op jit(solution)/shard_map/ppermute | solution.py:263
  28.7 0.0 collective-permute-done.5
  28.8 0.1 collective-permute-start.6
  28.9 2.7 %collective-permute-done.11.w_1 = f32[128,512]{1,0:T(8,128)S(1)} collective-permute-done((f32[128,512]{1,0:T(8,128)S(1)}, f32[128,512]{1,0:T(8,128)S(1)}, u32[]{:S(2)}, u32[]{:S(2)}) %collective-permute-start.11) | collective-permute-done | bytes 262176 | tf_op jit(solution)/shard_map/ppermute | solution.py:263
  31.6 2.8 %collective-permute-done.12.w_2 = f32[128,512]{1,0:T(8,128)S(1)} collective-permute-done((f32[128,512]{1,0:T(8,128)S(1)}, f32[128,512]{1,0:T(8,128)S(1)}, u32[]{:S(2)}, u32[]{:S(2)}) %collective-permute-start.12) | collective-permute-done | bytes 262176 | tf_op jit(solution)/shard_map/ppermute | solution.py:263
  34.4 0.0 collective-permute-start.13
  34.5 0.5 collective-permute-start.14
  34.9 0.1 collective-permute-start.15
  35.0 0.5 collective-permute-start.7
  35.5 0.0 collective-permute-done.6.refs_1_
  35.5 0.1 collective-permute-start.16
  35.5 0.5 collective-permute-done.13
  36.0 0.1 collective-permute-start.8
  36.1 0.2 collective-permute-done.14
  36.3 0.4 collective-permute-done.15
  36.7 0.1 select_select_fusion.refs_5_
  36.8 0.2 collective-permute-start.17
  37.0 0.1 collective-permute-done.7.refs_2_
  37.1 0.4 collective-permute-done.16.refs_6_
  37.5 0.4 collective-permute-done.8.refs_3_
  37.8 0.5 collective-permute-done.17.refs_7_
  38.4 3.3 %update_first.1 = (f32[832,128]{1,0:T(8,128)S(1)}, f32[840,128]{1,0:T(8,128)S(1)}, f32[64,128]{1,0:T(8,128)S(1)}) custom-call(f32[128,512]{1,0:T(8,128)S(1)} %broadcast_select_fusion.refs_0_, f32[128,512]{1,0:T(8,128)S(1)} %collective-permute-done.6.refs_1_, f32[128,512]{1,0:T(8,128)S(1)} %collective-permute-done.7.refs_2_, ...), custom_call_target="tpu_custom_call" | custom-call | flops 1000 | bytes 1000 | tf_op jit(solution)/shard_map/update_first/pallas_call | solution.py:389
  41.7 0.0 copy-start
  41.7 0.1 collective-permute-start.18
  41.8 9.5 %collective-permute-start.19 = (f32[840,128]{1,0:T(8,128)S(1)}, f32[840,128]{1,0:T(8,128)S(1)}, u32[]{:S(2)}, u32[]{:S(2)}) collective-permute-start(f32[840,128]{1,0:T(8,128)S(1)} %get-tuple-element.17), channel_id=1, source_target_pairs={{0,4},{1,5},{2,0},{3,1},{4,6},{5,7},{6,2},{7,3},{8,12},{9,13},{10,... | collective-permute-start | bytes 1290248 | tf_op jit(solution)/shard_map/ppermute | solution.py:263
  51.2 0.0 collective-permute-start.21
  51.2 3.3 %update_second.1 = (f32[832,128]{1,0:T(8,128)S(1)}, f32[840,128]{1,0:T(8,128)S(1)}) custom-call(f32[128,512]{1,0:T(8,128)S(1)} %broadcast_select_fusion.refs_0_, f32[128,512]{1,0:T(8,128)S(1)} %collective-permute-done.6.refs_1_, f32[128,512]{1,0:T(8,128)S(1)} %collective-permute-done.7.refs_2_, f32[128,512]{1,0:T(8,128)S(1)} %collective-permute-done.8.refs_3_, ...), custom_call_target="tpu_custom_call" | custom-call | flops 1000 | bytes 1000 | tf_op jit(solution)/shard_map/update_second/pallas_call | solution.py:389
  54.5 4.5 %collective-permute-start.20 = (f32[840,128]{1,0:T(8,128)S(1)}, f32[840,128]{1,0:T(8,128)S(1)}, u32[]{:S(2)}, u32[]{:S(2)}) collective-permute-start(f32[840,128]{1,0:T(8,128)S(1)} %get-tuple-element.18.mine), channel_id=1, source_target_pairs={{6,4},{7,5},{14,12},{15,13},{22,20},{23,21},{30,28},{31,29},{0,2},... | collective-permute-start | bytes 1290248 | tf_op jit(solution)/shard_map/ppermute | solution.py:266
  59.0 0.0 collective-permute-done.18.theirs.got_1
  59.0 1.3 %collective-permute-start.22 = (f32[832,128]{1,0:T(8,128)S(1)}, f32[832,128]{1,0:T(8,128)S(1)}, u32[]{:S(2)}, u32[]{:S(2)}) collective-permute-start(f32[832,128]{1,0:T(8,128)S(1)} %join.1), channel_id=1, source_target_pairs={{4,0},{5,1},{12,8},{13,9},{20,16},{21,17},{28,24},{29,25},{2,6},{3... | collective-permute-start | bytes 1277960 | tf_op jit(solution)/shard_map/ppermute | solution.py:266
  60.3 4.3 %collective-permute-start.23 = (f32[64,128]{1,0:T(8,128)S(1)}, f32[64,128]{1,0:T(8,128)S(1)}, u32[]{:S(2)}, u32[]{:S(2)}) collective-permute-start(f32[64,128]{1,0:T(8,128)S(1)} %get-tuple-element.19), channel_id=1, source_target_pairs={{0,6},{1,7},{2,4},{3,5},{4,2},{5,3},{6,0},{7,1},{8,14},{9,15},{10,... | collective-permute-start | bytes 98312 | tf_op jit(solution)/shard_map/ppermute | solution.py:263
  64.6 17.2 %collective-permute-done.23.far = f32[64,128]{1,0:T(8,128)S(1)} collective-permute-done((f32[64,128]{1,0:T(8,128)S(1)}, f32[64,128]{1,0:T(8,128)S(1)}, u32[]{:S(2)}, u32[]{:S(2)}) %collective-permute-start.23) | collective-permute-done | bytes 32800 | tf_op jit(solution)/shard_map/ppermute | solution.py:263
  81.7 0.0 collective-permute-done.19.got_2
  81.7 0.0 collective-permute-done.21.got_4
  81.7 0.0 collective-permute-done.20.got_3
  81.7 0.3 collective-permute-done.22.joined
  82.1 0.0 copy-done
  82.1 1.0 %add_up.1 = (f32[4,64,128]{2,1,0:T(8,128)}, f32[6,128,128]{2,1,0:T(8,128)}) custom-call(f32[6,128,128]{2,1,0:T(8,128)S(1)} %bitcast.8, f32[832,128]{1,0:T(8,128)S(1)} %get-tuple-element.15.own, f32[832,128]{1,0:T(8,128)S(1)} %collective-permute-done.18.theirs.got_1, f32[840,128]{1,0:T(8,128)S(1)} %collective-permute-done.19.got_2, ...), custom_call_target="tpu_custom_call" | custom-call | flops 1000 | bytes 1000 | tf_op jit(solution)/shard_map/add_up/pallas_call | solution.py:430
  (3 shorter events, 0.1 us)
Async XLA Ops:
  1.9 20.9 %collective-permute-start.4 = (f32[512,512]{1,0:T(8,128)S(1)}, f32[512,512]{1,0:T(8,128)S(1)}, u32[]{:S(2)}, u32[]{:S(2)}) collective-permute-start(f32[512,512]{1,0:T(8,128)S(1)} %slice_bitcast_fusion.near), channel_id=1, source_target_pairs={{0,8},{1,0},{2,10},{3,11},{4,12},{5,13},{6,14},{7,15},{8,9},{9,1},... | collective-permute-start | bytes 3145736 | tf_op jit(solution)/shard_map/ppermute | solution.py:263
  3.3 5.2 %collective-permute-start = (f32[128,128]{1,0:T(8,128)S(1)}, f32[128,128]{1,0:T(8,128)S(1)}, u32[]{:S(2)}, u32[]{:S(2)}) collective-permute-start(f32[128,128]{1,0:T(8,128)S(1)} %slice_bitcast_fusion.1.own), channel_id=1, source_target_pairs={{0,2},{1,9},{2,0},{3,1},{4,28},{5,13},{6,14},{7,5},{8,24},{9,11},{... | collective-permute-start | bytes 196616 | tf_op jit(solution)/shard_map/ppermute | solution.py:263
  5.9 5.2 %collective-permute-start.1 = (f32[128,128]{1,0:T(8,128)S(1)}, f32[128,128]{1,0:T(8,128)S(1)}, u32[]{:S(2)}, u32[]{:S(2)}) collective-permute-start(f32[128,128]{1,0:T(8,128)S(1)} %slice_bitcast_fusion.1.own), channel_id=1, source_target_pairs={{0,4},{1,9},{2,10},{3,11},{4,0},{5,1},{6,14},{7,3},{8,12},{9,13},{... | collective-permute-start | bytes 196616 | tf_op jit(solution)/shard_map/ppermute | solution.py:263
  8.5 6.2 %collective-permute-start.2 = (f32[128,128]{1,0:T(8,128)S(1)}, f32[128,128]{1,0:T(8,128)S(1)}, u32[]{:S(2)}, u32[]{:S(2)}) collective-permute-start(f32[128,128]{1,0:T(8,128)S(1)} %slice_bitcast_fusion.1.own), channel_id=1, source_target_pairs={{0,6},{1,7},{2,10},{3,11},{4,28},{5,13},{6,0},{7,1},{8,24},{9,15},... | collective-permute-start | bytes 196616 | tf_op jit(solution)/shard_map/ppermute | solution.py:263
  8.5 16.4 %collective-permute-start.9 = (f32[512,512]{1,0:T(8,128)S(1)}, f32[512,512]{1,0:T(8,128)S(1)}, u32[]{:S(2)}, u32[]{:S(2)}) collective-permute-start(f32[512,512]{1,0:T(8,128)S(1)} %slice_bitcast_fusion.near), channel_id=1, source_target_pairs={{0,8},{1,9},{2,10},{3,11},{4,12},{5,13},{6,14},{7,5},{8,2},{9,3},{... | collective-permute-start | bytes 3145736 | tf_op jit(solution)/shard_map/ppermute | solution.py:263
  16.3 8.6 %collective-permute-start.10 = (f32[512,512]{1,0:T(8,128)S(1)}, f32[512,512]{1,0:T(8,128)S(1)}, u32[]{:S(2)}, u32[]{:S(2)}) collective-permute-start(f32[512,512]{1,0:T(8,128)S(1)} %slice_bitcast_fusion.near), channel_id=1, source_target_pairs={{0,8},{1,9},{2,10},{3,11},{4,12},{5,13},{6,14},{7,15},{8,0},{9,1},... | collective-permute-start | bytes 3145736 | tf_op jit(solution)/shard_map/ppermute | solution.py:263
  16.4 6.4 %collective-permute-start.3 = (f32[128,512]{1,0:T(8,128)S(1)}, f32[128,512]{1,0:T(8,128)S(1)}, u32[]{:S(2)}, u32[]{:S(2)}) collective-permute-start(f32[128,512]{1,0:T(8,128)S(1)} %turn.1.out.own), channel_id=1, source_target_pairs={{0,1},{1,0},{2,10},{3,11},{4,12},{5,13},{6,14},{7,4},{8,24},{9,25}... | collective-permute-start | bytes 786440 | tf_op jit(solution)/shard_map/ppermute | solution.py:263
  24.8 4.0 %collective-permute-start.5 = (f32[128,512]{1,0:T(8,128)S(1)}, f32[128,512]{1,0:T(8,128)S(1)}, u32[]{:S(2)}, u32[]{:S(2)}) collective-permute-start(f32[128,512]{1,0:T(8,128)S(1)} %get-tuple-element.13.s_b), channel_id=1, source_target_pairs={{0,2},{1,3},{2,10},{3,11},{4,12},{5,13},{6,14},{7,15},{8,0},{9,1},... | collective-permute-start | bytes 786440 | tf_op jit(solution)/shard_map/ppermute | solution.py:263
  25.5 6.1 %collective-permute-start.11 = (f32[128,512]{1,0:T(8,128)S(1)}, f32[128,512]{1,0:T(8,128)S(1)}, u32[]{:S(2)}, u32[]{:S(2)}) collective-permute-start(f32[128,512]{1,0:T(8,128)S(1)} %reduce_low.1), channel_id=1, source_target_pairs={{0,15},{1,9},{2,10},{3,11},{4,12},{5,13},{6,14},{7,8},{8,0},{9,1},... | collective-permute-start | bytes 786440 | tf_op jit(solution)/shard_map/ppermute | solution.py:263
  27.6 6.8 %collective-permute-start.12 = (f32[128,512]{1,0:T(8,128)S(1)}, f32[128,512]{1,0:T(8,128)S(1)}, u32[]{:S(2)}, u32[]{:S(2)}) collective-permute-start(f32[128,512]{1,0:T(8,128)S(1)} %reduce_low.1), channel_id=1, source_target_pairs={{0,12},{1,15},{2,10},{3,11},{4,8},{5,13},{6,14},{7,9},{8,0},{9,1},... | collective-permute-start | bytes 786440 | tf_op jit(solution)/shard_map/ppermute | solution.py:263
  28.8 6.7 %collective-permute-start.6 = (f32[128,512]{1,0:T(8,128)S(1)}, f32[128,512]{1,0:T(8,128)S(1)}, u32[]{:S(2)}, u32[]{:S(2)}) collective-permute-start(f32[128,512]{1,0:T(8,128)S(1)} %broadcast_select_fusion.refs_0_), channel_id=1, source_target_pairs={{0,16},{1,17},{2,18},{3,19},{4,12},{5,13},{6,14},{7,15},{8,0},{9,1... | collective-permute-start | bytes 786440 | tf_op jit(solution)/shard_map/ppermute | solution.py:263
  34.4 1.6 %collective-permute-start.13 = (f32[128,512]{1,0:T(8,128)S(1)}, f32[128,512]{1,0:T(8,128)S(1)}, u32[]{:S(2)}, u32[]{:S(2)}) collective-permute-start(f32[128,512]{1,0:T(8,128)S(1)} %solve_high.1.refs_4_), channel_id=1, source_target_pairs={{0,8},{1,9},{2,10},{3,11},{4,12},{5,13},{6,14},{7,15},{8,0},{9,1},... | collective-permute-start | bytes 786440 | tf_op jit(solution)/shard_map/ppermute | solution.py:263
  34.5 1.9 %collective-permute-start.14 = (f32[128,512]{1,0:T(8,128)S(1)}, f32[128,512]{1,0:T(8,128)S(1)}, u32[]{:S(2)}, u32[]{:S(2)}) collective-permute-start(f32[128,512]{1,0:T(8,128)S(1)} %solve_high.1.refs_4_), channel_id=1, source_target_pairs={{0,8},{1,9},{2,10},{3,11},{4,12},{5,4},{6,7},{7,15},{8,0},{9,1},{1... | collective-permute-start | bytes 786440 | tf_op jit(solution)/shard_map/ppermute | solution.py:263
  34.9 1.8 %collective-permute-start.15 = (f32[128,512]{1,0:T(8,128)S(1)}, f32[128,512]{1,0:T(8,128)S(1)}, u32[]{:S(2)}, u32[]{:S(2)}) collective-permute-start(f32[128,512]{1,0:T(8,128)S(1)} %solve_high.1.refs_4_), channel_id=1, source_target_pairs={{0,8},{1,9},{2,10},{3,11},{4,12},{5,13},{6,14},{7,15},{8,0},{9,1},... | collective-permute-start | bytes 786440 | tf_op jit(solution)/shard_map/ppermute | solution.py:263
  35.0 2.1 %collective-permute-start.7 = (f32[128,512]{1,0:T(8,128)S(1)}, f32[128,512]{1,0:T(8,128)S(1)}, u32[]{:S(2)}, u32[]{:S(2)}) collective-permute-start(f32[128,512]{1,0:T(8,128)S(1)} %broadcast_select_fusion.refs_0_), channel_id=1, source_target_pairs={{0,8},{1,9},{2,10},{3,11},{4,12},{5,13},{6,14},{7,15},{8,0},{9,1},... | collective-permute-start | bytes 786440 | tf_op jit(solution)/shard_map/ppermute | solution.py:263
  35.5 2.0 %collective-permute-start.16 = (f32[128,512]{1,0:T(8,128)S(1)}, f32[128,512]{1,0:T(8,128)S(1)}, u32[]{:S(2)}, u32[]{:S(2)}) collective-permute-start(f32[128,512]{1,0:T(8,128)S(1)} %solve_high.1.refs_4_), channel_id=1, source_target_pairs={{0,8},{1,9},{2,10},{3,11},{4,12},{5,13},{6,14},{7,15},{8,0},{9,1},... | collective-permute-start | bytes 786440 | tf_op jit(solution)/shard_map/ppermute | solution.py:263
  36.0 1.9 %collective-permute-start.8 = (f32[128,512]{1,0:T(8,128)S(1)}, f32[128,512]{1,0:T(8,128)S(1)}, u32[]{:S(2)}, u32[]{:S(2)}) collective-permute-start(f32[128,512]{1,0:T(8,128)S(1)} %collective-permute-done.6.refs_1_), channel_id=1, source_target_pairs={{0,8},{1,9},{2,10},{3,11},{4,12},{5,13},{6,14},{7,15},{8,0},{9,1},... | collective-permute-start | bytes 786440 | tf_op jit(solution)/shard_map/ppermute | solution.py:263
  36.8 1.6 %collective-permute-start.17 = (f32[128,512]{1,0:T(8,128)S(1)}, f32[128,512]{1,0:T(8,128)S(1)}, u32[]{:S(2)}, u32[]{:S(2)}) collective-permute-start(f32[128,512]{1,0:T(8,128)S(1)} %select_select_fusion.refs_5_), channel_id=1, source_target_pairs={{0,8},{1,9},{2,10},{3,11},{4,12},{5,13},{6,14},{7,15},{8,0},{9,1},... | collective-permute-start | bytes 786440 | tf_op jit(solution)/shard_map/ppermute | solution.py:263
  41.7 40.4 %copy-start = (f32[6,1,1,128,128]{4,3,2,1,0:T(8,128)S(1)}, f32[6,1,1,128,128]{4,3,2,1,0:T(8,128)}, u32[]{:S(2)}) copy-start(f32[6,1,1,128,128]{4,3,2,1,0:T(8,128)} %param.4) | copy-start | bytes 1179652
  41.7 17.3 %collective-permute-start.18 = (f32[832,128]{1,0:T(8,128)S(1)}, f32[832,128]{1,0:T(8,128)S(1)}, u32[]{:S(2)}, u32[]{:S(2)}) collective-permute-start(f32[832,128]{1,0:T(8,128)S(1)} %get-tuple-element.16), channel_id=1, source_target_pairs={{0,2},{1,3},{2,0},{3,1},{4,6},{5,7},{6,4},{7,5},{8,10},{9,11},{10,... | collective-permute-start | bytes 1277960 | tf_op jit(solution)/shard_map/ppermute | solution.py:263
  41.8 40.0 %collective-permute-start.19 = (f32[840,128]{1,0:T(8,128)S(1)}, f32[840,128]{1,0:T(8,128)S(1)}, u32[]{:S(2)}, u32[]{:S(2)}) collective-permute-start(f32[840,128]{1,0:T(8,128)S(1)} %get-tuple-element.17), channel_id=1, source_target_pairs={{0,4},{1,5},{2,0},{3,1},{4,6},{5,7},{6,2},{7,3},{8,12},{9,13},{10,... | collective-permute-start | bytes 1290248 | tf_op jit(solution)/shard_map/ppermute | solution.py:263
  51.2 30.5 %collective-permute-start.21 = (f32[840,128]{1,0:T(8,128)S(1)}, f32[840,128]{1,0:T(8,128)S(1)}, u32[]{:S(2)}, u32[]{:S(2)}) collective-permute-start(f32[840,128]{1,0:T(8,128)S(1)} %get-tuple-element.17), channel_id=1, source_target_pairs={{0,8},{1,9},{2,4},{3,5},{4,2},{5,3},{6,14},{7,15},{8,0},{9,1},{10,... | collective-permute-start | bytes 1290248 | tf_op jit(solution)/shard_map/ppermute | solution.py:263
  54.5 27.2 %collective-permute-start.20 = (f32[840,128]{1,0:T(8,128)S(1)}, f32[840,128]{1,0:T(8,128)S(1)}, u32[]{:S(2)}, u32[]{:S(2)}) collective-permute-start(f32[840,128]{1,0:T(8,128)S(1)} %get-tuple-element.18.mine), channel_id=1, source_target_pairs={{6,4},{7,5},{14,12},{15,13},{22,20},{23,21},{30,28},{31,29},{0,2},... | collective-permute-start | bytes 1290248 | tf_op jit(solution)/shard_map/ppermute | solution.py:266
  59.0 23.1 %collective-permute-start.22 = (f32[832,128]{1,0:T(8,128)S(1)}, f32[832,128]{1,0:T(8,128)S(1)}, u32[]{:S(2)}, u32[]{:S(2)}) collective-permute-start(f32[832,128]{1,0:T(8,128)S(1)} %join.1), channel_id=1, source_target_pairs={{4,0},{5,1},{12,8},{13,9},{20,16},{21,17},{28,24},{29,25},{2,6},{3... | collective-permute-start | bytes 1277960 | tf_op jit(solution)/shard_map/ppermute | solution.py:266
  60.3 21.4 %collective-permute-start.23 = (f32[64,128]{1,0:T(8,128)S(1)}, f32[64,128]{1,0:T(8,128)S(1)}, u32[]{:S(2)}, u32[]{:S(2)}) collective-permute-start(f32[64,128]{1,0:T(8,128)S(1)} %get-tuple-element.19), channel_id=1, source_target_pairs={{0,6},{1,7},{2,4},{3,5},{4,2},{5,3},{6,0},{7,1},{8,14},{9,15},{10,... | collective-permute-start | bytes 98312 | tf_op jit(solution)/shard_map/ppermute | solution.py:263

commit v11 on v10

--- a/solution.py
+++ b/solution.py
@@ -20,9 +20,9 @@
 
 
 def product(a, b, transposed=False):
+    b_high, b_low = b if isinstance(b, tuple) else split(b)
     dims = (((1,), (1 if transposed else 0,)), ((), ()))
     a_high, a_low = split(a)
-    b_high, b_low = split(b)
     n = a.shape[0]
     both = lax.dot_general(
         jnp.concatenate([a_high, a_low], 0), b_high, dims, preferred_element_type=F32
@@ -35,7 +35,66 @@
     return lax.axis_index("row") * col_count + lax.axis_index("col")
 
 
-def turn_kernel(order, solver, col_count, own, g1, g2, g3, inverses, out, inv, sem):
+def fetch_kernel(factor, rhs, near, mine, sem):
+    copies = [
+        pltpu.make_async_copy(rhs.at[0, 0, 0], mine, sem.at[0]),
+        pltpu.make_async_copy(factor.at[0, 0, 0], near, sem.at[1]),
+    ]
+    for copy in copies:
+        copy.start()
+    for copy in copies:
+        copy.wait()
+
+
+def ready_kernel(solvers, col_count, inverses, high, low, inv, sem):
+    me = position(col_count)
+    for devices, first in zip(solvers, (0, 2)):
+        @pl.when((me == devices[0]) | (me == devices[1]))
+        def _(first=first):
+            copies = [
+                pltpu.make_async_copy(inverses.at[first + i], inv.at[i], sem.at[i]) for i in range(2)
+            ]
+            for copy in copies:
+                copy.start()
+            for i, copy in enumerate(copies):
+                copy.wait()
+                high[i], low[i] = split(inv[i])
+
+
+def ahead_kernel(groups, table_pair, panel, high, low, tiles, sems):
+    blocks, quarter = tiles.shape[0], tiles.shape[2] // 2
+    copies = column_copies(groups, table_pair, panel, tiles, sems)
+    for pair in copies:
+        for copy in pair:
+            copy.start()
+    for r in range(blocks):
+        for copy in copies[r]:
+            copy.wait()
+        high[r], low[r] = split(tiles[r])
+
+
+def piece_columns(groups, table, quarter):
+    member = lax.axis_index("col") // groups
+    to = functools.reduce(jnp.add, [jnp.where(member == m, p, 0) for m, p in enumerate(table)])
+    return pl.ds(pl.multiple_of(to * quarter, quarter), quarter)
+
+
+def column_copies(groups, table_pair, panel, tiles, sems):
+    quarter = tiles.shape[2] // 2
+    return [
+        [
+            pltpu.make_async_copy(
+                panel.at[r, 0, 0, :, piece_columns(groups, table, quarter)],
+                tiles.at[r, :, pl.ds(i * quarter, quarter)],
+                sems.at[2 * r + i],
+            )
+            for i, table in enumerate(table_pair)
+        ]
+        for r in range(tiles.shape[0])
+    ]
+
+
+def turn_kernel(order, solver, col_count, own, g1, g2, g3, high, low, out):
     me = position(col_count)
 
     def joined(pieces):
@@ -43,11 +102,7 @@
 
     @pl.when(me == solver)
     def _():
-        copy = pltpu.make_async_copy(inverses.at[0], inv, sem)
-        copy.start()
-        right = joined((own, g1, g2, g3))
-        copy.wait()
-        out[...] = product(right, inv[...], True)
+        out[...] = product(joined((own, g1, g2, g3)), (high[0], low[0]), True)
 
     for device, places in order:
         @pl.when(me == device)
@@ -56,16 +111,13 @@
             out[...] = joined([refs[i] for i in places])
 
 
-def low_kernel(homes, col_count, out, swapped, near, la, inverses, s_a, s_b, inv, sem):
+def low_kernel(homes, col_count, out, swapped, near, la, high, low, s_a, s_b):
     me = position(col_count)
 
     def work(first, right, block):
-        copy = pltpu.make_async_copy(inverses.at[1], inv, sem)
-        copy.start()
         s_a[...] = first[...]
         left = right[...] - product(first[...], block[...])
-        copy.wait()
-        s_b[...] = product(left, inv[...], True)
+        s_b[...] = product(left, (high[1], low[1]), True)
 
     @pl.when(me == homes[0])
     def _():
@@ -84,57 +136,41 @@
         w[...] = product(s_a[...], lx[...]) + product(s_b[...], ly[...])
 
 
-def high_kernel(homes, col_count, own, swapped, block, w_1, w_2, inverses, s, inv, sem):
+def high_kernel(homes, col_count, own, swapped, block, w_1, w_2, high, low, early_high, early_low, s):
+    del early_high, early_low
     me = position(col_count)
-    copies = [pltpu.make_async_copy(inverses.at[2 + i], inv.at[i], sem.at[i]) for i in range(2)]
 
     @pl.when(me == homes[0])
     def _():
-        copies[0].start()
-        right = own[...] - w_2[...]
-        copies[0].wait()
-        s[...] = product(right, inv[0], True)
+        s[...] = product(own[...] - w_2[...], (high[0], low[0]), True)
 
     @pl.when(me == homes[1])
     def _():
-        for copy in copies:
-            copy.start()
-        right = swapped[...] - w_1[...]
-        copies[0].wait()
-        first = product(right, inv[0], True)
-        right = own[...] - w_2[...] - product(first, block[...])
-        copies[1].wait()
-        s[...] = product(right, inv[1], True)
+        first = product(swapped[...] - w_1[...], (high[0], low[0]), True)
+        left = own[...] - w_2[...] - product(first, block[...])
+        s[...] = product(left, (high[1], low[1]), True)
 
 
 def update_kernel(cfg, *refs):
-    groups, row_count, share, homes, slots, blocks = cfg
+    groups, row_count, share, homes, slots, blocks, early = cfg
     steps = len(homes)
-    ways, panel, refs = refs[:8], refs[8], refs[9:]
-    outs, shares, (tiles, s, turned, sems) = refs[:2], refs[2:-4], refs[-4:]
+    ways, refs = refs[:8], refs[8:]
+    if early:
+        (high, low), refs = refs[:2], refs[2:]
+        s, turned = refs[-2:]
+        outs, shares = refs[:2], refs[2:-2]
+    else:
+        panel, outs, shares, (s, turned, tiles, sems) = refs[0], refs[1:3], refs[3:-4], refs[-4:]
+        copies = column_copies(groups, slots, panel, tiles, sems)
+        for pair in copies:
+            for copy in pair:
+                copy.start()
     quarter = turned.shape[0]
     row = lax.axis_index("row")
     col = lax.axis_index("col")
     member = col // groups
     group = col % groups
-    columns = []
-    for table in slots:
-        to = functools.reduce(jnp.add, [jnp.where(member == m, p, 0) for m, p in enumerate(table)])
-        columns.append(pl.ds(pl.multiple_of(to * quarter, quarter), quarter))
-    copies = [
-        [
-            pltpu.make_async_copy(
-                panel.at[r, 0, 0, :, columns[i]],
-                tiles.at[r, :, pl.ds(i * quarter, quarter)],
-                sems.at[2 * r + i],
-            )
-            for i in range(len(outs))
-        ]
-        for r in range(blocks)
-    ]
-    for pair in copies:
-        for copy in pair:
-            copy.start()
+    columns = [piece_columns(groups, table, quarter) for table in slots]
 
     for half in range(2):
         planes = [m for m in range(steps) if m // (steps // 2) == half]
@@ -158,11 +194,15 @@
                 s[...] = src[...]
 
     for r in range(blocks):
-        for copy in copies[r]:
-            copy.wait()
+        if early:
+            block = (high[r], low[r])
+        else:
+            for copy in copies[r]:
+                copy.wait()
+            block = tiles[r]
         block_id = (r * row_count + row) * groups + group
         keep = (block_id > member).astype(F32)
-        full = product(s[...], tiles[r]) * keep
+        full = product(s[...], block) * keep
         for i, out in enumerate(outs):
             out[pl.ds(r * quarter, quarter), :] = full[:, i * quarter: (i + 1) * quarter]
     for place, out in zip(columns, outs + shares):
@@ -275,7 +315,29 @@
     held_factor = pltpu.with_memory_space_constraint(factor, pltpu.HBM)
     held_inverses = pltpu.with_memory_space_constraint(inverses, pltpu.HBM)
 
-    mine = rhs[0, 0, 0]
+    half = jax.ShapeDtypeStruct((2, width, width), jnp.bfloat16)
+    near, mine = pl.pallas_call(
+        fetch_kernel,
+        in_specs=[hbm] * 2,
+        out_specs=[vmem] * 2,
+        out_shape=[
+            jax.ShapeDtypeStruct((width, width), F32), jax.ShapeDtypeStruct((quarter, nrhs), F32)
+        ],
+        scratch_shapes=[pltpu.SemaphoreType.DMA((2,))],
+        compiler_params=PARAMS,
+        cost_estimate=CHEAP,
+        name="fetch",
+    )(held_factor, pltpu.with_memory_space_constraint(rhs, pltpu.HBM))
+    ready = pl.pallas_call(
+        functools.partial(ready_kernel, (low_homes, high_homes), col_count),
+        in_specs=[hbm],
+        out_specs=[vmem] * 2,
+        out_shape=[half] * 2,
+        scratch_shapes=[VMEM((2, width, width), F32), pltpu.SemaphoreType.DMA((2,))],
+        compiler_params=PARAMS,
+        cost_estimate=CHEAP,
+        name="ready",
+    )(held_inverses)
     gathered = [
         send(
             mine,
@@ -284,37 +346,32 @@
         )
         for j in range(1, steps)
     ]
-    near = factor[0, 0, 0]
     la = send(near, [(line(1, 0), low_homes[0])])
-    ly = send(near, [(line(2, 1), low_homes[0]), (line(3, 1), low_homes[1]), (line(3, 2), high_homes[1])])
+    ly = send_some(near, [(line(2, 1), low_homes[0]), (line(3, 1), low_homes[1]), (line(3, 2), high_homes[1])])
 
     vector = jax.ShapeDtypeStruct((nrhs, width), F32)
-    one = [VMEM((width, width), F32), pltpu.SemaphoreType.DMA]
-    two = [VMEM((2, width, width), F32), pltpu.SemaphoreType.DMA((2,))]
     order = ((low_homes[1], (0, 1, 2, 3)), (high_homes[0], (2, 1, 0, 3)), (high_homes[1], (3, 2, 1, 0)))
     turned = pl.pallas_call(
         functools.partial(turn_kernel, order, low_homes[0], col_count),
-        in_specs=[vmem] * 4 + [hbm],
+        in_specs=[vmem] * 6,
         out_specs=vmem,
         out_shape=vector,
-        scratch_shapes=one,
         compiler_params=PARAMS,
         cost_estimate=CHEAP,
         name="turn",
-    )(mine, *gathered, held_inverses)
+    )(mine, *gathered, *ready)
     swapped = send(turned, [low_homes, low_homes[::-1], high_homes])
     later = lax.optimization_barrier((near, turned))[0]
     lx = send(later, [(line(2, 0), low_homes[0]), (line(3, 0), low_homes[1])])
     s_0, s_1 = pl.pallas_call(
         functools.partial(low_kernel, low_homes, col_count),
-        in_specs=[vmem] * 4 + [hbm],
+        in_specs=[vmem] * 6,
         out_specs=[vmem] * 2,
         out_shape=[vector] * 2,
-        scratch_shapes=one,
         compiler_params=PARAMS,
         cost_estimate=CHEAP,
         name="solve_low",
-    )(turned, swapped, near, la, held_inverses)
+    )(turned, swapped, near, la, *ready)
     w = pl.pallas_call(
         functools.partial(reduce_kernel, low_homes, col_count),
         in_specs=[vmem] * 4,
@@ -326,16 +383,27 @@
     )(s_0, s_1, lx, ly)
     w_1 = send(w, [(low_homes[0], high_homes[1])])
     w_2 = send(w, [(low_homes[1], high_homes[1]), (low_homes[0], high_homes[0])])
+    first_slots, second_slots = ((3, 0, 3, 0), (2, 2, 1, 1)), ((0, 1, 2, 3), (1, 3, 0, 2))
+    loads = [VMEM((blocks, width, 2 * quarter), F32), pltpu.SemaphoreType.DMA((2 * blocks,))]
+    early = pl.pallas_call(
+        functools.partial(ahead_kernel, groups, first_slots),
+        in_specs=[hbm],
+        out_specs=[vmem] * 2,
+        out_shape=[jax.ShapeDtypeStruct((blocks, width, 2 * quarter), jnp.bfloat16)] * 2,
+        scratch_shapes=loads,
+        compiler_params=PARAMS,
+        cost_estimate=CHEAP,
+        name="ahead",
+    )(lax.optimization_barrier((held_factor, w))[0])
     s_high = pl.pallas_call(
         functools.partial(high_kernel, high_homes, col_count),
-        in_specs=[vmem] * 5 + [hbm],
+        in_specs=[vmem] * 7 + [pl.BlockSpec(memory_space=pl.ANY)] * 2,
         out_specs=vmem,
         out_shape=vector,
-        scratch_shapes=two,
         compiler_params=PARAMS,
         cost_estimate=CHEAP,
         name="solve_high",
-    )(turned, swapped, ly, w_1, w_2, held_inverses)
+    )(turned, swapped, ly, w_1, w_2, *ready, *early)
 
     def spread(s, homes):
         have = {k: list(homes[k]) for k in homes}
@@ -385,27 +453,24 @@
         for n in (share, blocks * quarter + share, blocks * quarter + share + 8)
     ]
 
-    def update(name, shapes, *slots):
+    def update(name, shapes, slots, *block):
+        cfg = (groups, row_count, share, homes, slots, blocks, len(block) == 2)
         return pl.pallas_call(
-            functools.partial(update_kernel, (groups, row_count, share, homes, slots, blocks)),
-            in_specs=[vmem] * 8 + [hbm],
+            functools.partial(update_kernel, cfg),
+            in_specs=[vmem] * 8 + ([vmem] * 2 if len(block) == 2 else [hbm]),
             out_specs=[vmem] * len(shapes),
             out_shape=shapes,
-            scratch_shapes=[
-                VMEM((blocks, width, 2 * quarter), F32),
-                VMEM((nrhs, width), F32),
-                VMEM((quarter, nrhs), F32),
-                pltpu.SemaphoreType.DMA((2 * blocks,)),
-            ],
+            scratch_shapes=[VMEM((nrhs, width), F32), VMEM((quarter, nrhs), F32)]
+            + (loads if len(block) == 1 else []),
             compiler_params=PARAMS,
             cost_estimate=CHEAP,
             name=name,
-        )(*ways, held_factor)
+        )(*ways, *block)
 
     part_a, part_b, far = update(
-        "update_first", [part, longer, far_share], (3, 0, 3, 0), (2, 2, 1, 1), (3, 0, 0, 0)
+        "update_first", [part, longer, far_share], first_slots + ((3, 0, 0, 0),), *early
     )
-    own, part_c = update("update_second", [part, longer], (0, 1, 2, 3), (1, 3, 0, 2))
+    own, part_c = update("update_second", [part, longer], second_slots, held_factor)
     across = [(r, g) for r in range(row_count) for g in range(groups)]
 
     def route(*hops):

time: 83.4 us -> 87.6 us (1.050)
  Pallas kernels: 11.8 us -> 16.5 us
  starting transfers between devices: 30.2 us -> 27.4 us
  local copies, waits for them, and re-layouts: 2.15 us -> 4.75 us
    unnamed x2 -> x22, local copies, waits for them, and re-layouts: 0.01 us -> 4.75 us
    pallas_call x2 -> x5, Pallas kernels: 6.55 us -> 11.3 us  [the longest x2 6.17 us: update(): pl.pallas_call(functools.partial(update_kernel, cfg), in_specs=[vmem] * 8...]
    ppermute x22 -> x21, starting transfers between devices: 24.5 us -> 20.3 us  [send(): return lax.ppermute(x, AXES, sorted(onward.items()))]
    ppermute x22 -> x21, waiting for transfers between devices: 37.7 us -> 34.4 us  [send(): return lax.ppermute(x, AXES, sorted(onward.items()))]
    ppermute x2 -> x3, waiting for transfers between devices: 0.34 us -> 3.12 us  [send_some(): return lax.ppermute(x, AXES, pairs)]
    squeeze x2 -> x0, local copies, waits for them, and re-layouts: 2.14 us -> none  [the longest x1 1.3 us: on_device(): near = factor[0, 0, 0]]
    pallas_call x1, Pallas kernels: 0.02 us -> 1.73 us  [on_device(): pl.pallas_call(functools.partial(high_kernel, high_homes, col_count), in_...]
    ppermute x2 -> x3, starting transfers between devices: 5.74 us -> 7.01 us  [send_some(): return lax.ppermute(x, AXES, pairs)]
  transfers between devices with their start and end apart: 24 -> 24, of which waited for: 14 -> 13; matrix products, arithmetic and copies ran while one was open for 1% -> 0% of each run, Pallas kernels for 9% -> 14%
where the time goes in v11:
time: 87.6 us; the launch traced here: 87.2 us
  waiting for transfers between devices  37.6 us (43%)
  starting transfers between devices  27.4 us (31%)
  Pallas kernels  16.5 us (19%)
  local copies, waits for them, and re-layouts  4.75 us (5%)
  between operations  0.89 us (1%)
    ppermute x21, waiting for transfers between devices, send(): return lax.ppermute(x, AXES, sorted(onward.items()))  34.4 us
    ppermute x21, starting transfers between devices, send(): return lax.ppermute(x, AXES, sorted(onward.items()))  20.3 us
    ppermute x3, starting transfers between devices, send_some(): return lax.ppermute(x, AXES, pairs)  7.01 us
    pallas_call x2, Pallas kernels, update(): pl.pallas_call(functools.partial(update_kernel, cfg), in_specs=[vmem] * 8...  6.17 us
    unnamed x22, local copies, waits for them, and re-layouts  4.75 us
    ppermute x3, waiting for transfers between devices, send_some(): return lax.ppermute(x, AXES, pairs)  3.12 us
    pallas_call x1, Pallas kernels, on_device(): pl.pallas_call(functools.partial(ahead_kernel, groups, first_slots), in_s...  2.1 us
  transfers between devices with their start and end apart: 24, of which 13 were waited for; matrix products, arithmetic and copies ran while one was open for 0% of the time, Pallas kernels for 14%

profile of v11, /device:TPU:0, one launch (start us, length us, event | category | flops | bytes accessed | tf_op | source)
XLA Modules:
  0.0 87.2 jit_solution(18089856860833998676)
XLA Ops:
  0.6 1.3 %fetch.1 = (f32[512,512]{1,0:T(8,128)S(1)}, f32[128,128]{1,0:T(8,128)S(1)}) custom-call(f32[6,1,1,512,512]{4,3,2,1,0:T(8,128)} %refs_8_.1, f32[6,1,1,128,128]{4,3,2,1,0:T(8,128)} %rhs.1), custom_call_target="tpu_custom_call" | custom-call | flops 1000 | bytes 1000 | tf_op jit(solution)/shard_map/fetch/pallas_call | solution.py:319
  1.9 0.5 collective-permute-start.4
  2.5 2.6 %collective-permute-start = (f32[128,128]{1,0:T(8,128)S(1)}, f32[128,128]{1,0:T(8,128)S(1)}, u32[]{:S(2)}, u32[]{:S(2)}) collective-permute-start(f32[128,128]{1,0:T(8,128)S(1)} %get-tuple-element.19.own), channel_id=1, source_target_pairs={{0,2},{1,9},{2,0},{3,1},{4,28},{5,13},{6,14},{7,5},{8,24},{9,11},{... | collective-permute-start | bytes 196616 | tf_op jit(solution)/shard_map/ppermute | solution.py:303
  5.1 2.5 %collective-permute-start.1 = (f32[128,128]{1,0:T(8,128)S(1)}, f32[128,128]{1,0:T(8,128)S(1)}, u32[]{:S(2)}, u32[]{:S(2)}) collective-permute-start(f32[128,128]{1,0:T(8,128)S(1)} %get-tuple-element.19.own), channel_id=1, source_target_pairs={{0,4},{1,9},{2,10},{3,11},{4,0},{5,1},{6,14},{7,3},{8,12},{9,13},{... | collective-permute-start | bytes 196616 | tf_op jit(solution)/shard_map/ppermute | solution.py:303
  7.6 0.0 collective-permute-start.2
  7.6 1.3 %collective-permute-start.9 = (f32[512,512]{1,0:T(8,128)S(1)}, f32[512,512]{1,0:T(8,128)S(1)}, u32[]{:S(2)}, u32[]{:S(2)}) collective-permute-start(f32[512,512]{1,0:T(8,128)S(1)} %get-tuple-element.25.near), channel_id=1, source_target_pairs={{10,0},{11,1},{13,15}} | collective-permute-start | bytes 3145736 | tf_op jit(solution)/shard_map/ppermute | solution.py:306
  8.9 1.7 %ready.1 = (bf16[2,512,512]{2,1,0:T(8,128)(2,1)S(1)}, bf16[2,512,512]{2,1,0:T(8,128)(2,1)S(1)}) custom-call(f32[4,512,512]{2,1,0:T(8,128)} %inverses.1), custom_call_target="tpu_custom_call" | custom-call | flops 1000 | bytes 1000 | tf_op jit(solution)/shard_map/ready/pallas_call | solution.py:331
  10.6 0.0 collective-permute-done.g1
  10.6 0.0 collective-permute-done.1.g2
  10.6 3.1 %collective-permute-done.2.g3 = f32[128,128]{1,0:T(8,128)S(1)} collective-permute-done((f32[128,128]{1,0:T(8,128)S(1)}, f32[128,128]{1,0:T(8,128)S(1)}, u32[]{:S(2)}, u32[]{:S(2)}) %collective-permute-start.2) | collective-permute-done | bytes 65568 | tf_op jit(solution)/shard_map/ppermute | solution.py:303
  13.8 0.5 turn.1.out.own
  14.3 0.1 collective-permute-start.10
  14.3 0.1 collective-permute-start.3
  14.4 6.4 %collective-permute-done.3.swapped = f32[128,512]{1,0:T(8,128)S(1)} collective-permute-done((f32[128,512]{1,0:T(8,128)S(1)}, f32[128,512]{1,0:T(8,128)S(1)}, u32[]{:S(2)}, u32[]{:S(2)}) %collective-permute-start.3) | collective-permute-done | bytes 262176 | tf_op jit(solution)/shard_map/ppermute | solution.py:303
  20.8 0.0 collective-permute-done.4.la
  20.8 0.8 solve_low.1
  21.5 0.0 copy-start.7
  21.5 0.1 collective-permute-start.5
  21.6 2.8 %collective-permute-done.9.ly.block = f32[512,512]{1,0:T(8,128)S(1)} collective-permute-done((f32[512,512]{1,0:T(8,128)S(1)}, f32[512,512]{1,0:T(8,128)S(1)}, u32[]{:S(2)}, u32[]{:S(2)}) %collective-permute-start.9) | collective-permute-done | bytes 1048608 | tf_op jit(solution)/shard_map/ppermute | solution.py:306
  24.4 0.0 collective-permute-done.10.lx
  24.4 1.3 %reduce_low.1 = f32[128,512]{1,0:T(8,128)} custom-call(f32[128,512]{1,0:T(8,128)S(1)} %get-tuple-element.23.s_a, f32[128,512]{1,0:T(8,128)S(1)} %get-tuple-element.24.s_b, f32[512,512]{1,0:T(8,128)S(1)} %collective-permute-done.10.lx, f32[512,512]{1,0:T(8,128)S(1)} %collective-permute-done.9.ly.block), custom_call_target="tpu_custom_call" | custom-call | flops 1000 | bytes 1000 | tf_op jit(solution)/shard_map/reduce_low/pallas_call | solution.py:375
  25.7 2.2 %collective-permute-start.11 = (f32[128,512]{1,0:T(8,128)}, f32[128,512]{1,0:T(8,128)}, u32[]{:S(2)}, u32[]{:S(2)}) collective-permute-start(f32[128,512]{1,0:T(8,128)} %reduce_low.1), channel_id=1, source_target_pairs={{0,15},{1,9},{2,10},{3,11},{4,12},{5,13},{6,14},{7,8},{8,0},{9,1},... | collective-permute-start | bytes 786440 | tf_op jit(solution)/shard_map/ppermute | solution.py:303
  27.9 0.0 collective-permute-start.12
  27.9 2.1 %ahead.1 = (bf16[6,512,256]{2,1,0:T(8,128)(2,1)S(1)}, bf16[6,512,256]{2,1,0:T(8,128)(2,1)S(1)}) custom-call(f32[6,1,1,512,512]{4,3,2,1,0:T(8,128)} %refs_8_.1), custom_call_target="tpu_custom_call" | custom-call | flops 1000 | bytes 1000 | tf_op jit(solution)/shard_map/ahead/pallas_call | solution.py:388
  30.0 0.0 collective-permute-done.5
  30.1 0.1 collective-permute-start.6
  30.2 1.9 %collective-permute-done.11.w_1 = f32[128,512]{1,0:T(8,128)} collective-permute-done((f32[128,512]{1,0:T(8,128)}, f32[128,512]{1,0:T(8,128)}, u32[]{:S(2)}, u32[]{:S(2)}) %collective-permute-start.11) | collective-permute-done | bytes 262176 | tf_op jit(solution)/shard_map/ppermute | solution.py:303
  32.1 2.8 %collective-permute-done.12.w_2 = f32[128,512]{1,0:T(8,128)} collective-permute-done((f32[128,512]{1,0:T(8,128)}, f32[128,512]{1,0:T(8,128)}, u32[]{:S(2)}, u32[]{:S(2)}) %collective-permute-start.12) | collective-permute-done | bytes 262176 | tf_op jit(solution)/shard_map/ppermute | solution.py:303
  34.9 0.9 %copy-done.5 = f32[128,512]{1,0:T(8,128)S(1)} copy-done((f32[128,512]{1,0:T(8,128)S(1)}, f32[128,512]{1,0:T(8,128)}, u32[]{:S(2)}) %copy-start.5) | copy-done | bytes 262168
  35.9 0.9 %copy-done.10 = f32[128,512]{1,0:T(8,128)S(1)} copy-done((f32[128,512]{1,0:T(8,128)S(1)}, f32[128,512]{1,0:T(8,128)}, u32[]{:S(2)}) %copy-start.10) | copy-done | bytes 262168
  36.8 1.7 %solve_high.1.refs_4_ = f32[128,512]{1,0:T(8,128)} custom-call(f32[128,512]{1,0:T(8,128)S(1)} %copy-done.5, f32[128,512]{1,0:T(8,128)S(1)} %copy-done.10, f32[512,512]{1,0:T(8,128)S(1)} %collective-permute-done.9.ly.block, f32[128,512]{1,0:T(8,128)} %collective-permute-done.11.w_1, f32[128,512]{1,0:T(8,128)} %collective-permute-done.12.w_2, ...), custom_call_target="tpu_custom_call" | custom-call | flops 1000 | bytes 1000 | tf_op jit(solution)/shard_map/solve_high/pallas_call | solution.py:398
  38.5 0.0 collective-permute-start.13
  38.5 0.5 collective-permute-start.14
  39.1 0.0 collective-permute-start.15
  39.1 0.5 collective-permute-start.7
  39.6 0.0 collective-permute-done.6.refs_1_
  39.6 0.0 collective-permute-start.16
  39.6 0.7 collective-permute-done.13
  40.3 0.1 collective-permute-start.8
  40.4 0.2 collective-permute-done.14
  40.7 0.7 collective-permute-done.15
  41.4 0.1 select_select_fusion.refs_5_
  41.5 0.2 collective-permute-start.17
  41.7 0.0 collective-permute-done.7.refs_2_
  41.7 0.1 collective-permute-done.16.refs_6_
  41.8 0.4 collective-permute-done.8.refs_3_
  42.2 0.9 %collective-permute-done.17.refs_7_ = f32[128,512]{1,0:T(8,128)S(1)} collective-permute-done((f32[128,512]{1,0:T(8,128)S(1)}, f32[128,512]{1,0:T(8,128)S(1)}, u32[]{:S(2)}, u32[]{:S(2)}) %collective-permute-start.17) | collective-permute-done | bytes 262176 | tf_op jit(solution)/shard_map/ppermute | solution.py:303
  43.1 1.4 %copy-done.1 = bf16[6,512,256]{2,1,0:T(8,128)(2,1)S(1)} copy-done((bf16[6,512,256]{2,1,0:T(8,128)(2,1)S(1)}, bf16[6,512,256]{2,1,0:T(8,128)(2,1)}, u32[]{:S(2)}) %copy-start.1) | copy-done | bytes 1572888
  44.5 1.4 %copy-done.3 = bf16[6,512,256]{2,1,0:T(8,128)(2,1)S(1)} copy-done((bf16[6,512,256]{2,1,0:T(8,128)(2,1)S(1)}, bf16[6,512,256]{2,1,0:T(8,128)(2,1)}, u32[]{:S(2)}) %copy-start.3) | copy-done | bytes 1572888
  45.9 1.9 %update_first.1 = (f32[832,128]{1,0:T(8,128)S(1)}, f32[840,128]{1,0:T(8,128)S(1)}, f32[64,128]{1,0:T(8,128)S(1)}) custom-call(f32[128,512]{1,0:T(8,128)S(1)} %broadcast_select_fusion.refs_0_, f32[128,512]{1,0:T(8,128)} %collective-permute-done.6.refs_1_, f32[128,512]{1,0:T(8,128)S(1)} %collective-permute-done.7.refs_2_, ...), custom_call_target="tpu_custom_call" | custom-call | flops 1000 | bytes 1000 | tf_op jit(solution)/shard_map/update_first/pallas_call | solution.py:458
  47.8 0.1 collective-permute-start.18
  47.8 0.0 copy-start.6
  47.9 7.5 %collective-permute-start.19 = (f32[840,128]{1,0:T(8,128)S(1)}, f32[840,128]{1,0:T(8,128)S(1)}, u32[]{:S(2)}, u32[]{:S(2)}) collective-permute-start(f32[840,128]{1,0:T(8,128)S(1)} %get-tuple-element.31), channel_id=1, source_target_pairs={{0,4},{1,5},{2,0},{3,1},{4,6},{5,7},{6,2},{7,3},{8,12},{9,13},{10,... | collective-permute-start | bytes 1290248 | tf_op jit(solution)/shard_map/ppermute | solution.py:303
  55.3 0.0 collective-permute-start.21
  55.3 4.3 %update_second.1 = (f32[832,128]{1,0:T(8,128)S(1)}, f32[840,128]{1,0:T(8,128)S(1)}) custom-call(f32[128,512]{1,0:T(8,128)S(1)} %broadcast_select_fusion.refs_0_, f32[128,512]{1,0:T(8,128)} %collective-permute-done.6.refs_1_, f32[128,512]{1,0:T(8,128)S(1)} %collective-permute-done.7.refs_2_, f32[128,512]{1,0:T(8,128)S(1)} %collective-permute-done.8.refs_3_, ...), custom_call_target="tpu_custom_call" | custom-call | flops 1000 | bytes 1000 | tf_op jit(solution)/shard_map/update_second/pallas_call | solution.py:458
  59.6 4.4 %collective-permute-start.20 = (f32[840,128]{1,0:T(8,128)S(1)}, f32[840,128]{1,0:T(8,128)S(1)}, u32[]{:S(2)}, u32[]{:S(2)}) collective-permute-start(f32[840,128]{1,0:T(8,128)S(1)} %get-tuple-element.32.mine), channel_id=1, source_target_pairs={{6,4},{7,5},{14,12},{15,13},{22,20},{23,21},{30,28},{31,29},{0,2},... | collective-permute-start | bytes 1290248 | tf_op jit(solution)/shard_map/ppermute | solution.py:306
  64.1 0.0 collective-permute-done.18.theirs.got_1
  64.1 1.3 %collective-permute-start.22 = (f32[832,128]{1,0:T(8,128)S(1)}, f32[832,128]{1,0:T(8,128)S(1)}, u32[]{:S(2)}, u32[]{:S(2)}) collective-permute-start(f32[832,128]{1,0:T(8,128)S(1)} %join.1), channel_id=1, source_target_pairs={{4,0},{5,1},{12,8},{13,9},{20,16},{21,17},{28,24},{29,25},{2,6},{3... | collective-permute-start | bytes 1277960 | tf_op jit(solution)/shard_map/ppermute | solution.py:306
  65.4 3.2 %collective-permute-start.23 = (f32[64,128]{1,0:T(8,128)S(1)}, f32[64,128]{1,0:T(8,128)S(1)}, u32[]{:S(2)}, u32[]{:S(2)}) collective-permute-start(f32[64,128]{1,0:T(8,128)S(1)} %get-tuple-element.33), channel_id=1, source_target_pairs={{0,6},{1,7},{2,4},{3,5},{4,2},{5,3},{6,0},{7,1},{8,14},{9,15},{10,... | collective-permute-start | bytes 98312 | tf_op jit(solution)/shard_map/ppermute | solution.py:303
  68.7 17.2 %collective-permute-done.23.far = f32[64,128]{1,0:T(8,128)S(1)} collective-permute-done((f32[64,128]{1,0:T(8,128)S(1)}, f32[64,128]{1,0:T(8,128)S(1)}, u32[]{:S(2)}, u32[]{:S(2)}) %collective-permute-start.23) | collective-permute-done | bytes 32800 | tf_op jit(solution)/shard_map/ppermute | solution.py:303
  85.8 0.0 collective-permute-done.19.got_2
  85.8 0.0 collective-permute-done.21.got_4
  85.8 0.3 collective-permute-done.22.joined
  86.2 1.0 %add_up.1 = (f32[4,64,128]{2,1,0:T(8,128)}, f32[6,128,128]{2,1,0:T(8,128)}) custom-call(f32[6,128,128]{2,1,0:T(8,128)S(1)} %bitcast.4, f32[832,128]{1,0:T(8,128)S(1)} %get-tuple-element.29.own, f32[832,128]{1,0:T(8,128)S(1)} %collective-permute-done.18.theirs.got_1, f32[840,128]{1,0:T(8,128)S(1)} %collective-permute-done.19.got_2, ...), custom_call_target="tpu_custom_call" | custom-call | flops 1000 | bytes 1000 | tf_op jit(solution)/shard_map/add_up/pallas_call | solution.py:495
  (19 shorter events, 0.1 us)
Async XLA Ops:
  1.9 18.8 %collective-permute-start.4 = (f32[512,512]{1,0:T(8,128)S(1)}, f32[512,512]{1,0:T(8,128)S(1)}, u32[]{:S(2)}, u32[]{:S(2)}) collective-permute-start(f32[512,512]{1,0:T(8,128)S(1)} %get-tuple-element.25.near), channel_id=1, source_target_pairs={{0,8},{1,0},{2,10},{3,11},{4,12},{5,13},{6,14},{7,15},{8,9},{9,1},... | collective-permute-start | bytes 3145736 | tf_op jit(solution)/shard_map/ppermute | solution.py:303
  2.5 8.2 %collective-permute-start = (f32[128,128]{1,0:T(8,128)S(1)}, f32[128,128]{1,0:T(8,128)S(1)}, u32[]{:S(2)}, u32[]{:S(2)}) collective-permute-start(f32[128,128]{1,0:T(8,128)S(1)} %get-tuple-element.19.own), channel_id=1, source_target_pairs={{0,2},{1,9},{2,0},{3,1},{4,28},{5,13},{6,14},{7,5},{8,24},{9,11},{... | collective-permute-start | bytes 196616 | tf_op jit(solution)/shard_map/ppermute | solution.py:303
  5.1 5.5 %collective-permute-start.1 = (f32[128,128]{1,0:T(8,128)S(1)}, f32[128,128]{1,0:T(8,128)S(1)}, u32[]{:S(2)}, u32[]{:S(2)}) collective-permute-start(f32[128,128]{1,0:T(8,128)S(1)} %get-tuple-element.19.own), channel_id=1, source_target_pairs={{0,4},{1,9},{2,10},{3,11},{4,0},{5,1},{6,14},{7,3},{8,12},{9,13},{... | collective-permute-start | bytes 196616 | tf_op jit(solution)/shard_map/ppermute | solution.py:303
  7.6 6.2 %collective-permute-start.2 = (f32[128,128]{1,0:T(8,128)S(1)}, f32[128,128]{1,0:T(8,128)S(1)}, u32[]{:S(2)}, u32[]{:S(2)}) collective-permute-start(f32[128,128]{1,0:T(8,128)S(1)} %get-tuple-element.19.own), channel_id=1, source_target_pairs={{0,6},{1,7},{2,10},{3,11},{4,28},{5,13},{6,0},{7,1},{8,24},{9,15},... | collective-permute-start | bytes 196616 | tf_op jit(solution)/shard_map/ppermute | solution.py:303
  7.6 16.8 %collective-permute-start.9 = (f32[512,512]{1,0:T(8,128)S(1)}, f32[512,512]{1,0:T(8,128)S(1)}, u32[]{:S(2)}, u32[]{:S(2)}) collective-permute-start(f32[512,512]{1,0:T(8,128)S(1)} %get-tuple-element.25.near), channel_id=1, source_target_pairs={{10,0},{11,1},{13,15}} | collective-permute-start | bytes 3145736 | tf_op jit(solution)/shard_map/ppermute | solution.py:306
  14.3 10.2 %copy-start.4 = (f32[128,512]{1,0:T(8,128)}, f32[128,512]{1,0:T(8,128)S(1)}, u32[]{:S(2)}) copy-start(f32[128,512]{1,0:T(8,128)S(1)} %turn.1.out.own) | copy-start | bytes 786436
  14.3 10.2 %collective-permute-start.10 = (f32[512,512]{1,0:T(8,128)S(1)}, f32[512,512]{1,0:T(8,128)S(1)}, u32[]{:S(2)}, u32[]{:S(2)}) collective-permute-start(f32[512,512]{1,0:T(8,128)S(1)} %get-tuple-element.25.near), channel_id=1, source_target_pairs={{0,8},{1,9},{2,10},{3,11},{4,12},{5,13},{6,14},{7,15},{8,0},{9,1},... | collective-permute-start | bytes 3145736 | tf_op jit(solution)/shard_map/ppermute | solution.py:303
  14.3 6.4 %collective-permute-start.3 = (f32[128,512]{1,0:T(8,128)S(1)}, f32[128,512]{1,0:T(8,128)S(1)}, u32[]{:S(2)}, u32[]{:S(2)}) collective-permute-start(f32[128,512]{1,0:T(8,128)S(1)} %turn.1.out.own), channel_id=1, source_target_pairs={{0,1},{1,0},{2,10},{3,11},{4,12},{5,13},{6,14},{7,4},{8,24},{9,25}... | collective-permute-start | bytes 786440 | tf_op jit(solution)/shard_map/ppermute | solution.py:303
  20.8 3.7 %copy-start.9 = (f32[128,512]{1,0:T(8,128)}, f32[128,512]{1,0:T(8,128)S(1)}, u32[]{:S(2)}) copy-start(f32[128,512]{1,0:T(8,128)S(1)} %collective-permute-done.3.swapped) | copy-start | bytes 786436
  21.5 4.2 %copy-start.7 = (f32[128,512]{1,0:T(8,128)}, f32[128,512]{1,0:T(8,128)S(1)}, u32[]{:S(2)}) copy-start(f32[128,512]{1,0:T(8,128)S(1)} %get-tuple-element.23.s_a) | copy-start | bytes 786436
  21.5 8.5 %collective-permute-start.5 = (f32[128,512]{1,0:T(8,128)S(1)}, f32[128,512]{1,0:T(8,128)}, u32[]{:S(2)}, u32[]{:S(2)}) collective-permute-start(f32[128,512]{1,0:T(8,128)S(1)} %get-tuple-element.24.s_b), channel_id=1, source_target_pairs={{0,2},{1,3},{2,10},{3,11},{4,12},{5,13},{6,14},{7,15},{8,0},{9,1},... | collective-permute-start | bytes 786440 | tf_op jit(solution)/shard_map/ppermute | solution.py:303
  25.7 6.4 %collective-permute-start.11 = (f32[128,512]{1,0:T(8,128)}, f32[128,512]{1,0:T(8,128)}, u32[]{:S(2)}, u32[]{:S(2)}) collective-permute-start(f32[128,512]{1,0:T(8,128)} %reduce_low.1), channel_id=1, source_target_pairs={{0,15},{1,9},{2,10},{3,11},{4,12},{5,13},{6,14},{7,8},{8,0},{9,1},... | collective-permute-start | bytes 786440 | tf_op jit(solution)/shard_map/ppermute | solution.py:303
  27.9 7.0 %collective-permute-start.12 = (f32[128,512]{1,0:T(8,128)}, f32[128,512]{1,0:T(8,128)}, u32[]{:S(2)}, u32[]{:S(2)}) collective-permute-start(f32[128,512]{1,0:T(8,128)} %reduce_low.1), channel_id=1, source_target_pairs={{0,12},{1,15},{2,10},{3,11},{4,8},{5,13},{6,14},{7,9},{8,0},{9,1},... | collective-permute-start | bytes 786440 | tf_op jit(solution)/shard_map/ppermute | solution.py:303
  27.9 2.1 %copy-start.8 = (f32[128,512]{1,0:T(8,128)S(1)}, f32[128,512]{1,0:T(8,128)}, u32[]{:S(2)}) copy-start(f32[128,512]{1,0:T(8,128)} %copy-done.7) | copy-start | bytes 786436
  30.0 8.5 %copy-start = (bf16[6,512,256]{2,1,0:T(8,128)(2,1)}, bf16[6,512,256]{2,1,0:T(8,128)(2,1)S(1)}, u32[]{:S(2)}) copy-start(bf16[6,512,256]{2,1,0:T(8,128)(2,1)S(1)} %get-tuple-element.27.early_high.refs_8_) | copy-start | bytes 4718596
  30.0 8.5 %copy-start.2 = (bf16[6,512,256]{2,1,0:T(8,128)(2,1)}, bf16[6,512,256]{2,1,0:T(8,128)(2,1)S(1)}, u32[]{:S(2)}) copy-start(bf16[6,512,256]{2,1,0:T(8,128)(2,1)S(1)} %get-tuple-element.28.early_low.refs_9_) | copy-start | bytes 4718596
  30.1 9.5 %collective-permute-start.6 = (f32[128,512]{1,0:T(8,128)S(1)}, f32[128,512]{1,0:T(8,128)}, u32[]{:S(2)}, u32[]{:S(2)}) collective-permute-start(f32[128,512]{1,0:T(8,128)S(1)} %broadcast_select_fusion.refs_0_), channel_id=1, source_target_pairs={{0,16},{1,17},{2,18},{3,19},{4,12},{5,13},{6,14},{7,15},{8,0},{9,1... | collective-permute-start | bytes 786440 | tf_op jit(solution)/shard_map/ppermute | solution.py:303
  34.9 0.9 %copy-start.5 = (f32[128,512]{1,0:T(8,128)S(1)}, f32[128,512]{1,0:T(8,128)}, u32[]{:S(2)}) copy-start(f32[128,512]{1,0:T(8,128)} %copy-done.4) | copy-start | bytes 786436
  35.9 0.9 %copy-start.10 = (f32[128,512]{1,0:T(8,128)S(1)}, f32[128,512]{1,0:T(8,128)}, u32[]{:S(2)}) copy-start(f32[128,512]{1,0:T(8,128)} %copy-done.9) | copy-start | bytes 786436
  38.5 1.7 %collective-permute-start.13 = (f32[128,512]{1,0:T(8,128)}, f32[128,512]{1,0:T(8,128)S(1)}, u32[]{:S(2)}, u32[]{:S(2)}) collective-permute-start(f32[128,512]{1,0:T(8,128)} %solve_high.1.refs_4_), channel_id=1, source_target_pairs={{0,8},{1,9},{2,10},{3,11},{4,12},{5,13},{6,14},{7,15},{8,0},{9,1},... | collective-permute-start | bytes 786440 | tf_op jit(solution)/shard_map/ppermute | solution.py:303
  38.5 2.1 %collective-permute-start.14 = (f32[128,512]{1,0:T(8,128)}, f32[128,512]{1,0:T(8,128)S(1)}, u32[]{:S(2)}, u32[]{:S(2)}) collective-permute-start(f32[128,512]{1,0:T(8,128)} %solve_high.1.refs_4_), channel_id=1, source_target_pairs={{0,8},{1,9},{2,10},{3,11},{4,12},{5,4},{6,7},{7,15},{8,0},{9,1},{1... | collective-permute-start | bytes 786440 | tf_op jit(solution)/shard_map/ppermute | solution.py:303
  39.1 2.4 %collective-permute-start.15 = (f32[128,512]{1,0:T(8,128)}, f32[128,512]{1,0:T(8,128)S(1)}, u32[]{:S(2)}, u32[]{:S(2)}) collective-permute-start(f32[128,512]{1,0:T(8,128)} %solve_high.1.refs_4_), channel_id=1, source_target_pairs={{0,8},{1,9},{2,10},{3,11},{4,12},{5,13},{6,14},{7,15},{8,0},{9,1},... | collective-permute-start | bytes 786440 | tf_op jit(solution)/shard_map/ppermute | solution.py:303
  39.1 2.6 %collective-permute-start.7 = (f32[128,512]{1,0:T(8,128)S(1)}, f32[128,512]{1,0:T(8,128)S(1)}, u32[]{:S(2)}, u32[]{:S(2)}) collective-permute-start(f32[128,512]{1,0:T(8,128)S(1)} %broadcast_select_fusion.refs_0_), channel_id=1, source_target_pairs={{0,8},{1,9},{2,10},{3,11},{4,12},{5,13},{6,14},{7,15},{8,0},{9,1},... | collective-permute-start | bytes 786440 | tf_op jit(solution)/shard_map/ppermute | solution.py:303
  39.6 2.2 %collective-permute-start.16 = (f32[128,512]{1,0:T(8,128)}, f32[128,512]{1,0:T(8,128)S(1)}, u32[]{:S(2)}, u32[]{:S(2)}) collective-permute-start(f32[128,512]{1,0:T(8,128)} %solve_high.1.refs_4_), channel_id=1, source_target_pairs={{0,8},{1,9},{2,10},{3,11},{4,12},{5,13},{6,14},{7,15},{8,0},{9,1},... | collective-permute-start | bytes 786440 | tf_op jit(solution)/shard_map/ppermute | solution.py:303
  40.3 1.9 %collective-permute-start.8 = (f32[128,512]{1,0:T(8,128)}, f32[128,512]{1,0:T(8,128)S(1)}, u32[]{:S(2)}, u32[]{:S(2)}) collective-permute-start(f32[128,512]{1,0:T(8,128)} %collective-permute-done.6.refs_1_), channel_id=1, source_target_pairs={{0,8},{1,9},{2,10},{3,11},{4,12},{5,13},{6,14},{7,15},{8,0},{9,1},... | collective-permute-start | bytes 786440 | tf_op jit(solution)/shard_map/ppermute | solution.py:303
  41.5 1.6 %collective-permute-start.17 = (f32[128,512]{1,0:T(8,128)S(1)}, f32[128,512]{1,0:T(8,128)S(1)}, u32[]{:S(2)}, u32[]{:S(2)}) collective-permute-start(f32[128,512]{1,0:T(8,128)S(1)} %select_select_fusion.refs_5_), channel_id=1, source_target_pairs={{0,8},{1,9},{2,10},{3,11},{4,12},{5,13},{6,14},{7,15},{8,0},{9,1},... | collective-permute-start | bytes 786440 | tf_op jit(solution)/shard_map/ppermute | solution.py:303
  43.1 1.4 %copy-start.1 = (bf16[6,512,256]{2,1,0:T(8,128)(2,1)S(1)}, bf16[6,512,256]{2,1,0:T(8,128)(2,1)}, u32[]{:S(2)}) copy-start(bf16[6,512,256]{2,1,0:T(8,128)(2,1)} %copy-done) | copy-start | bytes 4718596
  44.5 1.4 %copy-start.3 = (bf16[6,512,256]{2,1,0:T(8,128)(2,1)S(1)}, bf16[6,512,256]{2,1,0:T(8,128)(2,1)}, u32[]{:S(2)}) copy-start(bf16[6,512,256]{2,1,0:T(8,128)(2,1)} %copy-done.2) | copy-start | bytes 4718596
  47.8 16.3 %collective-permute-start.18 = (f32[832,128]{1,0:T(8,128)S(1)}, f32[832,128]{1,0:T(8,128)S(1)}, u32[]{:S(2)}, u32[]{:S(2)}) collective-permute-start(f32[832,128]{1,0:T(8,128)S(1)} %get-tuple-element.30), channel_id=1, source_target_pairs={{0,2},{1,3},{2,0},{3,1},{4,6},{5,7},{6,4},{7,5},{8,10},{9,11},{10,... | collective-permute-start | bytes 1277960 | tf_op jit(solution)/shard_map/ppermute | solution.py:303
  47.8 38.3 %copy-start.6 = (f32[6,1,1,128,128]{4,3,2,1,0:T(8,128)S(1)}, f32[6,1,1,128,128]{4,3,2,1,0:T(8,128)}, u32[]{:S(2)}) copy-start(f32[6,1,1,128,128]{4,3,2,1,0:T(8,128)} %rhs.1) | copy-start | bytes 1179652
  47.9 38.0 %collective-permute-start.19 = (f32[840,128]{1,0:T(8,128)S(1)}, f32[840,128]{1,0:T(8,128)S(1)}, u32[]{:S(2)}, u32[]{:S(2)}) collective-permute-start(f32[840,128]{1,0:T(8,128)S(1)} %get-tuple-element.31), channel_id=1, source_target_pairs={{0,4},{1,5},{2,0},{3,1},{4,6},{5,7},{6,2},{7,3},{8,12},{9,13},{10,... | collective-permute-start | bytes 1290248 | tf_op jit(solution)/shard_map/ppermute | solution.py:303
  55.3 30.5 %collective-permute-start.21 = (f32[840,128]{1,0:T(8,128)S(1)}, f32[840,128]{1,0:T(8,128)S(1)}, u32[]{:S(2)}, u32[]{:S(2)}) collective-permute-start(f32[840,128]{1,0:T(8,128)S(1)} %get-tuple-element.31), channel_id=1, source_target_pairs={{0,8},{1,9},{2,4},{3,5},{4,2},{5,3},{6,14},{7,15},{8,0},{9,1},{10,... | collective-permute-start | bytes 1290248 | tf_op jit(solution)/shard_map/ppermute | solution.py:303
  59.6 26.2 %collective-permute-start.20 = (f32[840,128]{1,0:T(8,128)S(1)}, f32[840,128]{1,0:T(8,128)S(1)}, u32[]{:S(2)}, u32[]{:S(2)}) collective-permute-start(f32[840,128]{1,0:T(8,128)S(1)} %get-tuple-element.32.mine), channel_id=1, source_target_pairs={{6,4},{7,5},{14,12},{15,13},{22,20},{23,21},{30,28},{31,29},{0,2},... | collective-permute-start | bytes 1290248 | tf_op jit(solution)/shard_map/ppermute | solution.py:306
  64.1 22.1 %collective-permute-start.22 = (f32[832,128]{1,0:T(8,128)S(1)}, f32[832,128]{1,0:T(8,128)S(1)}, u32[]{:S(2)}, u32[]{:S(2)}) collective-permute-start(f32[832,128]{1,0:T(8,128)S(1)} %join.1), channel_id=1, source_target_pairs={{4,0},{5,1},{12,8},{13,9},{20,16},{21,17},{28,24},{29,25},{2,6},{3... | collective-permute-start | bytes 1277960 | tf_op jit(solution)/shard_map/ppermute | solution.py:306
  65.4 20.4 %collective-permute-start.23 = (f32[64,128]{1,0:T(8,128)S(1)}, f32[64,128]{1,0:T(8,128)S(1)}, u32[]{:S(2)}, u32[]{:S(2)}) collective-permute-start(f32[64,128]{1,0:T(8,128)S(1)} %get-tuple-element.33), channel_id=1, source_target_pairs={{0,6},{1,7},{2,4},{3,5},{4,2},{5,3},{6,0},{7,1},{8,14},{9,15},{10,... | collective-permute-start | bytes 98312 | tf_op jit(solution)/shard_map/ppermute | solution.py:303

commit v12 on v11

--- a/solution.py
+++ b/solution.py
@@ -22,8 +22,8 @@
 def product(a, b, transposed=False):
     b_high, b_low = b if isinstance(b, tuple) else split(b)
     dims = (((1,), (1 if transposed else 0,)), ((), ()))
-    a_high, a_low = split(a)
-    n = a.shape[0]
+    a_high, a_low = a if isinstance(a, tuple) else split(a)
+    n = a_high.shape[0]
     both = lax.dot_general(
         jnp.concatenate([a_high, a_low], 0), b_high, dims, preferred_element_type=F32
     )
@@ -48,29 +48,15 @@
 
 def ready_kernel(solvers, col_count, inverses, high, low, inv, sem):
     me = position(col_count)
-    for devices, first in zip(solvers, (0, 2)):
-        @pl.when((me == devices[0]) | (me == devices[1]))
-        def _(first=first):
-            copies = [
-                pltpu.make_async_copy(inverses.at[first + i], inv.at[i], sem.at[i]) for i in range(2)
-            ]
-            for copy in copies:
-                copy.start()
-            for i, copy in enumerate(copies):
-                copy.wait()
-                high[i], low[i] = split(inv[i])
-
-
-def ahead_kernel(groups, table_pair, panel, high, low, tiles, sems):
-    blocks, quarter = tiles.shape[0], tiles.shape[2] // 2
-    copies = column_copies(groups, table_pair, panel, tiles, sems)
-    for pair in copies:
-        for copy in pair:
+
+    @pl.when((me == solvers[0]) | (me == solvers[1]))
+    def _():
+        copies = [pltpu.make_async_copy(inverses.at[i], inv.at[i], sem.at[i]) for i in range(2)]
+        for copy in copies:
             copy.start()
-    for r in range(blocks):
-        for copy in copies[r]:
+        for i, copy in enumerate(copies):
             copy.wait()
-        high[r], low[r] = split(tiles[r])
+            high[i], low[i] = split(inv[i])
 
 
 def piece_columns(groups, table, quarter):
@@ -111,7 +97,8 @@
             out[...] = joined([refs[i] for i in places])
 
 
-def low_kernel(homes, col_count, out, swapped, near, la, high, low, s_a, s_b):
+def low_kernel(homes, col_count, out, swapped, near, la, high, low, ly, s_a, s_b):
+    del ly
     me = position(col_count)
 
     def work(first, right, block):
@@ -136,35 +123,38 @@
         w[...] = product(s_a[...], lx[...]) + product(s_b[...], ly[...])
 
 
-def high_kernel(homes, col_count, own, swapped, block, w_1, w_2, high, low, early_high, early_low, s):
-    del early_high, early_low
+def high_kernel(homes, col_count, own, swapped, block, w_1, w_2, inverses, s, inv, sem):
     me = position(col_count)
+    copies = [pltpu.make_async_copy(inverses.at[2 + i], inv.at[i], sem.at[i]) for i in range(2)]
 
     @pl.when(me == homes[0])
     def _():
-        s[...] = product(own[...] - w_2[...], (high[0], low[0]), True)
+        copies[0].start()
+        right = own[...] - w_2[...]
+        copies[0].wait()
+        s[...] = product(right, inv[0], True)
 
     @pl.when(me == homes[1])
     def _():
-        first = product(swapped[...] - w_1[...], (high[0], low[0]), True)
-        left = own[...] - w_2[...] - product(first, block[...])
-        s[...] = product(left, (high[1], low[1]), True)
+        for copy in copies:
+            copy.start()
+        right = swapped[...] - w_1[...]
+        copies[0].wait()
+        first = product(right, inv[0], True)
+        right = own[...] - w_2[...] - product(first, block[...])
+        copies[1].wait()
+        s[...] = product(right, inv[1], True)
 
 
 def update_kernel(cfg, *refs):
-    groups, row_count, share, homes, slots, blocks, early = cfg
+    groups, row_count, share, homes, slots, blocks = cfg
     steps = len(homes)
-    ways, refs = refs[:8], refs[8:]
-    if early:
-        (high, low), refs = refs[:2], refs[2:]
-        s, turned = refs[-2:]
-        outs, shares = refs[:2], refs[2:-2]
-    else:
-        panel, outs, shares, (s, turned, tiles, sems) = refs[0], refs[1:3], refs[3:-4], refs[-4:]
-        copies = column_copies(groups, slots, panel, tiles, sems)
-        for pair in copies:
-            for copy in pair:
-                copy.start()
+    ways, panel, refs = refs[:8], refs[8], refs[9:]
+    outs, shares, (s, turned, tiles, sems) = refs[:2], refs[2:-4], refs[-4:]
+    copies = column_copies(groups, slots[:2], panel, tiles, sems)
+    for pair in copies:
+        for copy in pair:
+            copy.start()
     quarter = turned.shape[0]
     row = lax.axis_index("row")
     col = lax.axis_index("col")
@@ -193,16 +183,13 @@
             def _(src=way):
                 s[...] = src[...]
 
+    parts = split(s[...])
     for r in range(blocks):
-        if early:
-            block = (high[r], low[r])
-        else:
-            for copy in copies[r]:
-                copy.wait()
-            block = tiles[r]
+        for copy in copies[r]:
+            copy.wait()
         block_id = (r * row_count + row) * groups + group
         keep = (block_id > member).astype(F32)
-        full = product(s[...], block) * keep
+        full = product(parts, tiles[r]) * keep
         for i, out in enumerate(outs):
             out[pl.ds(r * quarter, quarter), :] = full[:, i * quarter: (i + 1) * quarter]
     for place, out in zip(columns, outs + shares):
@@ -329,7 +316,7 @@
         name="fetch",
     )(held_factor, pltpu.with_memory_space_constraint(rhs, pltpu.HBM))
     ready = pl.pallas_call(
-        functools.partial(ready_kernel, (low_homes, high_homes), col_count),
+        functools.partial(ready_kernel, low_homes, col_count),
         in_specs=[hbm],
         out_specs=[vmem] * 2,
         out_shape=[half] * 2,
@@ -365,13 +352,13 @@
     lx = send(later, [(line(2, 0), low_homes[0]), (line(3, 0), low_homes[1])])
     s_0, s_1 = pl.pallas_call(
         functools.partial(low_kernel, low_homes, col_count),
-        in_specs=[vmem] * 6,
+        in_specs=[vmem] * 6 + [pl.BlockSpec(memory_space=pl.ANY)],
         out_specs=[vmem] * 2,
         out_shape=[vector] * 2,
         compiler_params=PARAMS,
         cost_estimate=CHEAP,
         name="solve_low",
-    )(turned, swapped, near, la, *ready)
+    )(turned, swapped, near, la, *ready, ly)
     w = pl.pallas_call(
         functools.partial(reduce_kernel, low_homes, col_count),
         in_specs=[vmem] * 4,
@@ -384,26 +371,16 @@
     w_1 = send(w, [(low_homes[0], high_homes[1])])
     w_2 = send(w, [(low_homes[1], high_homes[1]), (low_homes[0], high_homes[0])])
     first_slots, second_slots = ((3, 0, 3, 0), (2, 2, 1, 1)), ((0, 1, 2, 3), (1, 3, 0, 2))
-    loads = [VMEM((blocks, width, 2 * quarter), F32), pltpu.SemaphoreType.DMA((2 * blocks,))]
-    early = pl.pallas_call(
-        functools.partial(ahead_kernel, groups, first_slots),
-        in_specs=[hbm],
-        out_specs=[vmem] * 2,
-        out_shape=[jax.ShapeDtypeStruct((blocks, width, 2 * quarter), jnp.bfloat16)] * 2,
-        scratch_shapes=loads,
-        compiler_params=PARAMS,
-        cost_estimate=CHEAP,
-        name="ahead",
-    )(lax.optimization_barrier((held_factor, w))[0])
     s_high = pl.pallas_call(
         functools.partial(high_kernel, high_homes, col_count),
-        in_specs=[vmem] * 7 + [pl.BlockSpec(memory_space=pl.ANY)] * 2,
+        in_specs=[vmem] * 5 + [hbm],
         out_specs=vmem,
         out_shape=vector,
+        scratch_shapes=[VMEM((2, width, width), F32), pltpu.SemaphoreType.DMA((2,))],
         compiler_params=PARAMS,
         cost_estimate=CHEAP,
         name="solve_high",
-    )(turned, swapped, ly, w_1, w_2, *ready, *early)
+    )(turned, swapped, ly, w_1, w_2, held_inverses)
 
     def spread(s, homes):
         have = {k: list(homes[k]) for k in homes}
@@ -453,24 +430,27 @@
         for n in (share, blocks * quarter + share, blocks * quarter + share + 8)
     ]
 
-    def update(name, shapes, slots, *block):
-        cfg = (groups, row_count, share, homes, slots, blocks, len(block) == 2)
+    def update(name, shapes, slots):
         return pl.pallas_call(
-            functools.partial(update_kernel, cfg),
-            in_specs=[vmem] * 8 + ([vmem] * 2 if len(block) == 2 else [hbm]),
+            functools.partial(update_kernel, (groups, row_count, share, homes, slots, blocks)),
+            in_specs=[vmem] * 8 + [hbm],
             out_specs=[vmem] * len(shapes),
             out_shape=shapes,
-            scratch_shapes=[VMEM((nrhs, width), F32), VMEM((quarter, nrhs), F32)]
-            + (loads if len(block) == 1 else []),
+            scratch_shapes=[
+                VMEM((nrhs, width), F32),
+                VMEM((quarter, nrhs), F32),
+                VMEM((blocks, width, 2 * quarter), F32),
+                pltpu.SemaphoreType.DMA((2 * blocks,)),
+            ],
             compiler_params=PARAMS,
             cost_estimate=CHEAP,
             name=name,
-        )(*ways, *block)
+        )(*ways, held_factor)
 
     part_a, part_b, far = update(
-        "update_first", [part, longer, far_share], first_slots + ((3, 0, 0, 0),), *early
+        "update_first", [part, longer, far_share], first_slots + ((3, 0, 0, 0),)
     )
-    own, part_c = update("update_second", [part, longer], second_slots, held_factor)
+    own, part_c = update("update_second", [part, longer], second_slots)
     across = [(r, g) for r in range(row_count) for g in range(groups)]
 
     def route(*hops):

time: 87.6 us -> 87.9 us (level)
  starting transfers between devices: 27.4 us -> 38.3 us
  local copies, waits for them, and re-layouts: 4.75 us -> 0.01 us
  Pallas kernels: 16.5 us -> 12.4 us
  waiting for transfers between devices: 37.6 us -> 36 us
    ppermute x21, starting transfers between devices: 20.3 us -> 31.3 us  [send(): return lax.ppermute(x, AXES, sorted(onward.items()))]
    unnamed x22 -> x2, local copies, waits for them, and re-layouts: 4.75 us -> 0.01 us
    ppermute x3, waiting for transfers between devices: 3.12 us -> 0.34 us  [send_some(): return lax.ppermute(x, AXES, pairs)]
    pallas_call x4 -> x3, Pallas kernels: 9.98 us -> 8.24 us  [the longest x2 6.55 us: update(): pl.pallas_call(functools.partial(update_kernel, (groups, row_count, share...]
    pallas_call x1, Pallas kernels: 1.73 us -> 0.02 us  [on_device(): pl.pallas_call(functools.partial(high_kernel, high_homes, col_count), in_...]
    ppermute x21, waiting for transfers between devices: 34.4 us -> 35.7 us  [send(): return lax.ppermute(x, AXES, sorted(onward.items()))]
  transfers between devices with their start and end apart: 24 -> 24, of which waited for: 13 -> 14; matrix products, arithmetic and copies ran while one was open for 0% -> 0% of each run, Pallas kernels for 14% -> 8%
where the time goes in v12:
time: 87.9 us; the launch traced here: 87.6 us
  starting transfers between devices  38.3 us (44%)
  waiting for transfers between devices  36 us (41%)
  Pallas kernels  12.4 us (14%)
    ppermute x21, waiting for transfers between devices, send(): return lax.ppermute(x, AXES, sorted(onward.items()))  35.7 us
    ppermute x21, starting transfers between devices, send(): return lax.ppermute(x, AXES, sorted(onward.items()))  31.3 us
    ppermute x3, starting transfers between devices, send_some(): return lax.ppermute(x, AXES, pairs)  7.04 us
    pallas_call x2, Pallas kernels, update(): pl.pallas_call(functools.partial(update_kernel, (groups, row_count, share...  6.55 us
  transfers between devices with their start and end apart: 24, of which 14 were waited for; matrix products, arithmetic and copies ran while one was open for 0% of the time, Pallas kernels for 8%

profile of v12, /device:TPU:0, one launch (start us, length us, event | category | flops | bytes accessed | tf_op | source)
XLA Modules:
  0.0 87.6 jit_solution(11992723620319524478)
XLA Ops:
  0.6 1.3 %fetch.1 = (f32[512,512]{1,0:T(8,128)S(1)}, f32[128,128]{1,0:T(8,128)S(1)}) custom-call(f32[6,1,1,512,512]{4,3,2,1,0:T(8,128)} %refs_8_.3, f32[6,1,1,128,128]{4,3,2,1,0:T(8,128)} %rhs.1), custom_call_target="tpu_custom_call" | custom-call | flops 1000 | bytes 1000 | tf_op jit(solution)/shard_map/fetch/pallas_call | solution.py:306
  1.9 1.3 %collective-permute-start.5 = (f32[512,512]{1,0:T(8,128)S(1)}, f32[512,512]{1,0:T(8,128)S(1)}, u32[]{:S(2)}, u32[]{:S(2)}) collective-permute-start(f32[512,512]{1,0:T(8,128)S(1)} %get-tuple-element.22.near), channel_id=1, source_target_pairs={{10,0},{11,1},{13,15}} | collective-permute-start | bytes 3145736 | tf_op jit(solution)/shard_map/ppermute | solution.py:293
  3.2 0.1 collective-permute-start.4
  3.3 2.9 %collective-permute-start = (f32[128,128]{1,0:T(8,128)S(1)}, f32[128,128]{1,0:T(8,128)S(1)}, u32[]{:S(2)}, u32[]{:S(2)}) collective-permute-start(f32[128,128]{1,0:T(8,128)S(1)} %get-tuple-element.16.own), channel_id=1, source_target_pairs={{0,2},{1,9},{2,0},{3,1},{4,28},{5,13},{6,14},{7,5},{8,24},{9,11},{... | collective-permute-start | bytes 196616 | tf_op jit(solution)/shard_map/ppermute | solution.py:290
  6.2 2.1 %collective-permute-start.1 = (f32[128,128]{1,0:T(8,128)S(1)}, f32[128,128]{1,0:T(8,128)S(1)}, u32[]{:S(2)}, u32[]{:S(2)}) collective-permute-start(f32[128,128]{1,0:T(8,128)S(1)} %get-tuple-element.16.own), channel_id=1, source_target_pairs={{0,4},{1,9},{2,10},{3,11},{4,0},{5,1},{6,14},{7,3},{8,12},{9,13},{... | collective-permute-start | bytes 196616 | tf_op jit(solution)/shard_map/ppermute | solution.py:290
  8.3 0.0 collective-permute-start.2
  8.3 1.7 %ready.1 = (bf16[2,512,512]{2,1,0:T(8,128)(2,1)S(1)}, bf16[2,512,512]{2,1,0:T(8,128)(2,1)S(1)}) custom-call(f32[4,512,512]{2,1,0:T(8,128)} %inverses.3), custom_call_target="tpu_custom_call" | custom-call | flops 1000 | bytes 1000 | tf_op jit(solution)/shard_map/ready/pallas_call | solution.py:318
  10.0 0.0 collective-permute-done.g1
  10.1 1.4 %collective-permute-done.1.g2 = f32[128,128]{1,0:T(8,128)S(1)} collective-permute-done((f32[128,128]{1,0:T(8,128)S(1)}, f32[128,128]{1,0:T(8,128)S(1)}, u32[]{:S(2)}, u32[]{:S(2)}) %collective-permute-start.1) | collective-permute-done | bytes 65568 | tf_op jit(solution)/shard_map/ppermute | solution.py:290
  11.5 3.0 %collective-permute-done.2.g3 = f32[128,128]{1,0:T(8,128)S(1)} collective-permute-done((f32[128,128]{1,0:T(8,128)S(1)}, f32[128,128]{1,0:T(8,128)S(1)}, u32[]{:S(2)}, u32[]{:S(2)}) %collective-permute-start.2) | collective-permute-done | bytes 65568 | tf_op jit(solution)/shard_map/ppermute | solution.py:290
  14.5 0.5 turn.1.out.own
  15.0 0.1 collective-permute-start.10
  15.1 1.8 %collective-permute-start.3 = (f32[128,512]{1,0:T(8,128)S(1)}, f32[128,512]{1,0:T(8,128)S(1)}, u32[]{:S(2)}, u32[]{:S(2)}) collective-permute-start(f32[128,512]{1,0:T(8,128)S(1)} %turn.1.out.own), channel_id=1, source_target_pairs={{0,1},{1,0},{2,10},{3,11},{4,12},{5,13},{6,14},{7,4},{8,24},{9,25}... | collective-permute-start | bytes 786440 | tf_op jit(solution)/shard_map/ppermute | solution.py:290
  16.8 5.0 %collective-permute-done.3.swapped = f32[128,512]{1,0:T(8,128)S(1)} collective-permute-done((f32[128,512]{1,0:T(8,128)S(1)}, f32[128,512]{1,0:T(8,128)S(1)}, u32[]{:S(2)}, u32[]{:S(2)}) %collective-permute-start.3) | collective-permute-done | bytes 262176 | tf_op jit(solution)/shard_map/ppermute | solution.py:290
  21.9 0.0 collective-permute-done.5.ly.block
  21.9 0.0 collective-permute-done.4.la
  21.9 0.8 solve_low.1
  22.6 0.1 collective-permute-start.6
  22.7 0.0 collective-permute-done.10.lx
  22.7 0.6 reduce_low.1
  23.3 8.9 %collective-permute-start.11 = (f32[128,512]{1,0:T(8,128)S(1)}, f32[128,512]{1,0:T(8,128)S(1)}, u32[]{:S(2)}, u32[]{:S(2)}) collective-permute-start(f32[128,512]{1,0:T(8,128)S(1)} %reduce_low.1), channel_id=1, source_target_pairs={{0,15},{1,9},{2,10},{3,11},{4,12},{5,13},{6,14},{7,8},{8,0},{9,1},... | collective-permute-start | bytes 786440 | tf_op jit(solution)/shard_map/ppermute | solution.py:290
  32.3 0.0 collective-permute-start.12
  32.3 0.0 collective-permute-done.6
  32.3 0.1 collective-permute-start.7
  32.4 3.7 %collective-permute-done.11.w_1 = f32[128,512]{1,0:T(8,128)S(1)} collective-permute-done((f32[128,512]{1,0:T(8,128)S(1)}, f32[128,512]{1,0:T(8,128)S(1)}, u32[]{:S(2)}, u32[]{:S(2)}) %collective-permute-start.11) | collective-permute-done | bytes 262176 | tf_op jit(solution)/shard_map/ppermute | solution.py:290
  36.1 2.8 %collective-permute-done.12.w_2 = f32[128,512]{1,0:T(8,128)S(1)} collective-permute-done((f32[128,512]{1,0:T(8,128)S(1)}, f32[128,512]{1,0:T(8,128)S(1)}, u32[]{:S(2)}, u32[]{:S(2)}) %collective-permute-start.12) | collective-permute-done | bytes 262176 | tf_op jit(solution)/shard_map/ppermute | solution.py:290
  39.0 0.0 collective-permute-start.13
  39.0 0.5 collective-permute-start.14
  39.5 0.1 collective-permute-start.15
  39.6 0.5 collective-permute-start.8
  40.0 0.0 collective-permute-done.7.refs_1_
  40.0 0.1 collective-permute-start.16
  40.1 0.5 collective-permute-done.13
  40.6 0.1 collective-permute-start.9
  40.7 0.2 collective-permute-done.14
  40.9 0.4 collective-permute-done.15
  41.3 0.1 select_select_fusion.refs_5_
  41.4 0.2 collective-permute-start.17
  41.6 0.1 collective-permute-done.8.refs_2_
  41.7 0.4 collective-permute-done.16.refs_6_
  42.1 0.4 collective-permute-done.9.refs_3_
  42.4 0.5 collective-permute-done.17.refs_7_
  43.0 3.3 %update_first.1 = (f32[832,128]{1,0:T(8,128)S(1)}, f32[840,128]{1,0:T(8,128)S(1)}, f32[64,128]{1,0:T(8,128)S(1)}) custom-call(f32[128,512]{1,0:T(8,128)S(1)} %broadcast_select_fusion.refs_0_, f32[128,512]{1,0:T(8,128)S(1)} %collective-permute-done.7.refs_1_, f32[128,512]{1,0:T(8,128)S(1)} %collective-permute-done.8.refs_2_, ...), custom_call_target="tpu_custom_call" | custom-call | flops 1000 | bytes 1000 | tf_op jit(solution)/shard_map/update_first/pallas_call | solution.py:434
  46.2 0.0 copy-start
  46.3 0.1 collective-permute-start.18
  46.3 9.4 %collective-permute-start.19 = (f32[840,128]{1,0:T(8,128)S(1)}, f32[840,128]{1,0:T(8,128)S(1)}, u32[]{:S(2)}, u32[]{:S(2)}) collective-permute-start(f32[840,128]{1,0:T(8,128)S(1)} %get-tuple-element.25), channel_id=1, source_target_pairs={{0,4},{1,5},{2,0},{3,1},{4,6},{5,7},{6,2},{7,3},{8,12},{9,13},{10,... | collective-permute-start | bytes 1290248 | tf_op jit(solution)/shard_map/ppermute | solution.py:290
  55.8 0.0 collective-permute-start.21
  55.8 3.3 %update_second.1 = (f32[832,128]{1,0:T(8,128)S(1)}, f32[840,128]{1,0:T(8,128)S(1)}) custom-call(f32[128,512]{1,0:T(8,128)S(1)} %broadcast_select_fusion.refs_0_, f32[128,512]{1,0:T(8,128)S(1)} %collective-permute-done.7.refs_1_, f32[128,512]{1,0:T(8,128)S(1)} %collective-permute-done.8.refs_2_, f32[128,512]{1,0:T(8,128)S(1)} %collective-permute-done.9.refs_3_, ...), custom_call_target="tpu_custom_call" | custom-call | flops 1000 | bytes 1000 | tf_op jit(solution)/shard_map/update_second/pallas_call | solution.py:434
  59.1 4.5 %collective-permute-start.20 = (f32[840,128]{1,0:T(8,128)S(1)}, f32[840,128]{1,0:T(8,128)S(1)}, u32[]{:S(2)}, u32[]{:S(2)}) collective-permute-start(f32[840,128]{1,0:T(8,128)S(1)} %get-tuple-element.26.mine), channel_id=1, source_target_pairs={{6,4},{7,5},{14,12},{15,13},{22,20},{23,21},{30,28},{31,29},{0,2},... | collective-permute-start | bytes 1290248 | tf_op jit(solution)/shard_map/ppermute | solution.py:293
  63.5 0.0 collective-permute-done.18.theirs.got_1
  63.6 1.3 %collective-permute-start.22 = (f32[832,128]{1,0:T(8,128)S(1)}, f32[832,128]{1,0:T(8,128)S(1)}, u32[]{:S(2)}, u32[]{:S(2)}) collective-permute-start(f32[832,128]{1,0:T(8,128)S(1)} %join.1), channel_id=1, source_target_pairs={{4,0},{5,1},{12,8},{13,9},{20,16},{21,17},{28,24},{29,25},{2,6},{3... | collective-permute-start | bytes 1277960 | tf_op jit(solution)/shard_map/ppermute | solution.py:293
  64.9 4.3 %collective-permute-start.23 = (f32[64,128]{1,0:T(8,128)S(1)}, f32[64,128]{1,0:T(8,128)S(1)}, u32[]{:S(2)}, u32[]{:S(2)}) collective-permute-start(f32[64,128]{1,0:T(8,128)S(1)} %get-tuple-element.27), channel_id=1, source_target_pairs={{0,6},{1,7},{2,4},{3,5},{4,2},{5,3},{6,0},{7,1},{8,14},{9,15},{10,... | collective-permute-start | bytes 98312 | tf_op jit(solution)/shard_map/ppermute | solution.py:290
  69.1 17.1 %collective-permute-done.23.far = f32[64,128]{1,0:T(8,128)S(1)} collective-permute-done((f32[64,128]{1,0:T(8,128)S(1)}, f32[64,128]{1,0:T(8,128)S(1)}, u32[]{:S(2)}, u32[]{:S(2)}) %collective-permute-start.23) | collective-permute-done | bytes 32800 | tf_op jit(solution)/shard_map/ppermute | solution.py:290
  86.3 0.0 collective-permute-done.19.got_2
  86.3 0.0 collective-permute-done.21.got_4
  86.3 0.0 collective-permute-done.20.got_3
  86.3 0.3 collective-permute-done.22.joined
  86.6 0.0 copy-done
  86.7 1.0 %add_up.1 = (f32[4,64,128]{2,1,0:T(8,128)}, f32[6,128,128]{2,1,0:T(8,128)}) custom-call(f32[6,128,128]{2,1,0:T(8,128)S(1)} %bitcast.4, f32[832,128]{1,0:T(8,128)S(1)} %get-tuple-element.23.own, f32[832,128]{1,0:T(8,128)S(1)} %collective-permute-done.18.theirs.got_1, f32[840,128]{1,0:T(8,128)S(1)} %collective-permute-done.19.got_2, ...), custom_call_target="tpu_custom_call" | custom-call | flops 1000 | bytes 1000 | tf_op jit(solution)/shard_map/add_up/pallas_call | solution.py:475
  (3 shorter events, 0.1 us)
Async XLA Ops:
  1.9 19.9 %collective-permute-start.5 = (f32[512,512]{1,0:T(8,128)S(1)}, f32[512,512]{1,0:T(8,128)S(1)}, u32[]{:S(2)}, u32[]{:S(2)}) collective-permute-start(f32[512,512]{1,0:T(8,128)S(1)} %get-tuple-element.22.near), channel_id=1, source_target_pairs={{10,0},{11,1},{13,15}} | collective-permute-start | bytes 3145736 | tf_op jit(solution)/shard_map/ppermute | solution.py:293
  3.2 18.6 %collective-permute-start.4 = (f32[512,512]{1,0:T(8,128)S(1)}, f32[512,512]{1,0:T(8,128)S(1)}, u32[]{:S(2)}, u32[]{:S(2)}) collective-permute-start(f32[512,512]{1,0:T(8,128)S(1)} %get-tuple-element.22.near), channel_id=1, source_target_pairs={{0,8},{1,0},{2,10},{3,11},{4,12},{5,13},{6,14},{7,15},{8,9},{9,1},... | collective-permute-start | bytes 3145736 | tf_op jit(solution)/shard_map/ppermute | solution.py:290
  3.3 6.7 %collective-permute-start = (f32[128,128]{1,0:T(8,128)S(1)}, f32[128,128]{1,0:T(8,128)S(1)}, u32[]{:S(2)}, u32[]{:S(2)}) collective-permute-start(f32[128,128]{1,0:T(8,128)S(1)} %get-tuple-element.16.own), channel_id=1, source_target_pairs={{0,2},{1,9},{2,0},{3,1},{4,28},{5,13},{6,14},{7,5},{8,24},{9,11},{... | collective-permute-start | bytes 196616 | tf_op jit(solution)/shard_map/ppermute | solution.py:290
  6.2 5.3 %collective-permute-start.1 = (f32[128,128]{1,0:T(8,128)S(1)}, f32[128,128]{1,0:T(8,128)S(1)}, u32[]{:S(2)}, u32[]{:S(2)}) collective-permute-start(f32[128,128]{1,0:T(8,128)S(1)} %get-tuple-element.16.own), channel_id=1, source_target_pairs={{0,4},{1,9},{2,10},{3,11},{4,0},{5,1},{6,14},{7,3},{8,12},{9,13},{... | collective-permute-start | bytes 196616 | tf_op jit(solution)/shard_map/ppermute | solution.py:290
  8.3 6.2 %collective-permute-start.2 = (f32[128,128]{1,0:T(8,128)S(1)}, f32[128,128]{1,0:T(8,128)S(1)}, u32[]{:S(2)}, u32[]{:S(2)}) collective-permute-start(f32[128,128]{1,0:T(8,128)S(1)} %get-tuple-element.16.own), channel_id=1, source_target_pairs={{0,6},{1,7},{2,10},{3,11},{4,28},{5,13},{6,0},{7,1},{8,24},{9,15},... | collective-permute-start | bytes 196616 | tf_op jit(solution)/shard_map/ppermute | solution.py:290
  15.0 7.7 %collective-permute-start.10 = (f32[512,512]{1,0:T(8,128)S(1)}, f32[512,512]{1,0:T(8,128)S(1)}, u32[]{:S(2)}, u32[]{:S(2)}) collective-permute-start(f32[512,512]{1,0:T(8,128)S(1)} %get-tuple-element.22.near), channel_id=1, source_target_pairs={{0,8},{1,9},{2,10},{3,11},{4,12},{5,13},{6,14},{7,15},{8,0},{9,1},... | collective-permute-start | bytes 3145736 | tf_op jit(solution)/shard_map/ppermute | solution.py:290
  15.1 6.8 %collective-permute-start.3 = (f32[128,512]{1,0:T(8,128)S(1)}, f32[128,512]{1,0:T(8,128)S(1)}, u32[]{:S(2)}, u32[]{:S(2)}) collective-permute-start(f32[128,512]{1,0:T(8,128)S(1)} %turn.1.out.own), channel_id=1, source_target_pairs={{0,1},{1,0},{2,10},{3,11},{4,12},{5,13},{6,14},{7,4},{8,24},{9,25}... | collective-permute-start | bytes 786440 | tf_op jit(solution)/shard_map/ppermute | solution.py:290
  22.6 9.6 %collective-permute-start.6 = (f32[128,512]{1,0:T(8,128)S(1)}, f32[128,512]{1,0:T(8,128)S(1)}, u32[]{:S(2)}, u32[]{:S(2)}) collective-permute-start(f32[128,512]{1,0:T(8,128)S(1)} %get-tuple-element.21.s_b), channel_id=1, source_target_pairs={{0,2},{1,3},{2,10},{3,11},{4,12},{5,13},{6,14},{7,15},{8,0},{9,1},... | collective-permute-start | bytes 786440 | tf_op jit(solution)/shard_map/ppermute | solution.py:290
  23.3 12.8 %collective-permute-start.11 = (f32[128,512]{1,0:T(8,128)S(1)}, f32[128,512]{1,0:T(8,128)S(1)}, u32[]{:S(2)}, u32[]{:S(2)}) collective-permute-start(f32[128,512]{1,0:T(8,128)S(1)} %reduce_low.1), channel_id=1, source_target_pairs={{0,15},{1,9},{2,10},{3,11},{4,12},{5,13},{6,14},{7,8},{8,0},{9,1},... | collective-permute-start | bytes 786440 | tf_op jit(solution)/shard_map/ppermute | solution.py:290
  32.3 6.7 %collective-permute-start.12 = (f32[128,512]{1,0:T(8,128)S(1)}, f32[128,512]{1,0:T(8,128)S(1)}, u32[]{:S(2)}, u32[]{:S(2)}) collective-permute-start(f32[128,512]{1,0:T(8,128)S(1)} %reduce_low.1), channel_id=1, source_target_pairs={{0,12},{1,15},{2,10},{3,11},{4,8},{5,13},{6,14},{7,9},{8,0},{9,1},... | collective-permute-start | bytes 786440 | tf_op jit(solution)/shard_map/ppermute | solution.py:290
  32.3 7.7 %collective-permute-start.7 = (f32[128,512]{1,0:T(8,128)S(1)}, f32[128,512]{1,0:T(8,128)S(1)}, u32[]{:S(2)}, u32[]{:S(2)}) collective-permute-start(f32[128,512]{1,0:T(8,128)S(1)} %broadcast_select_fusion.refs_0_), channel_id=1, source_target_pairs={{0,16},{1,17},{2,18},{3,19},{4,12},{5,13},{6,14},{7,15},{8,0},{9,1... | collective-permute-start | bytes 786440 | tf_op jit(solution)/shard_map/ppermute | solution.py:290
  39.0 1.6 %collective-permute-start.13 = (f32[128,512]{1,0:T(8,128)S(1)}, f32[128,512]{1,0:T(8,128)S(1)}, u32[]{:S(2)}, u32[]{:S(2)}) collective-permute-start(f32[128,512]{1,0:T(8,128)S(1)} %solve_high.1.refs_4_), channel_id=1, source_target_pairs={{0,8},{1,9},{2,10},{3,11},{4,12},{5,13},{6,14},{7,15},{8,0},{9,1},... | collective-permute-start | bytes 786440 | tf_op jit(solution)/shard_map/ppermute | solution.py:290
  39.0 1.9 %collective-permute-start.14 = (f32[128,512]{1,0:T(8,128)S(1)}, f32[128,512]{1,0:T(8,128)S(1)}, u32[]{:S(2)}, u32[]{:S(2)}) collective-permute-start(f32[128,512]{1,0:T(8,128)S(1)} %solve_high.1.refs_4_), channel_id=1, source_target_pairs={{0,8},{1,9},{2,10},{3,11},{4,12},{5,4},{6,7},{7,15},{8,0},{9,1},{1... | collective-permute-start | bytes 786440 | tf_op jit(solution)/shard_map/ppermute | solution.py:290
  39.5 1.8 %collective-permute-start.15 = (f32[128,512]{1,0:T(8,128)S(1)}, f32[128,512]{1,0:T(8,128)S(1)}, u32[]{:S(2)}, u32[]{:S(2)}) collective-permute-start(f32[128,512]{1,0:T(8,128)S(1)} %solve_high.1.refs_4_), channel_id=1, source_target_pairs={{0,8},{1,9},{2,10},{3,11},{4,12},{5,13},{6,14},{7,15},{8,0},{9,1},... | collective-permute-start | bytes 786440 | tf_op jit(solution)/shard_map/ppermute | solution.py:290
  39.6 2.1 %collective-permute-start.8 = (f32[128,512]{1,0:T(8,128)S(1)}, f32[128,512]{1,0:T(8,128)S(1)}, u32[]{:S(2)}, u32[]{:S(2)}) collective-permute-start(f32[128,512]{1,0:T(8,128)S(1)} %broadcast_select_fusion.refs_0_), channel_id=1, source_target_pairs={{0,8},{1,9},{2,10},{3,11},{4,12},{5,13},{6,14},{7,15},{8,0},{9,1},... | collective-permute-start | bytes 786440 | tf_op jit(solution)/shard_map/ppermute | solution.py:290
  40.0 2.0 %collective-permute-start.16 = (f32[128,512]{1,0:T(8,128)S(1)}, f32[128,512]{1,0:T(8,128)S(1)}, u32[]{:S(2)}, u32[]{:S(2)}) collective-permute-start(f32[128,512]{1,0:T(8,128)S(1)} %solve_high.1.refs_4_), channel_id=1, source_target_pairs={{0,8},{1,9},{2,10},{3,11},{4,12},{5,13},{6,14},{7,15},{8,0},{9,1},... | collective-permute-start | bytes 786440 | tf_op jit(solution)/shard_map/ppermute | solution.py:290
  40.6 1.9 %collective-permute-start.9 = (f32[128,512]{1,0:T(8,128)S(1)}, f32[128,512]{1,0:T(8,128)S(1)}, u32[]{:S(2)}, u32[]{:S(2)}) collective-permute-start(f32[128,512]{1,0:T(8,128)S(1)} %collective-permute-done.7.refs_1_), channel_id=1, source_target_pairs={{0,8},{1,9},{2,10},{3,11},{4,12},{5,13},{6,14},{7,15},{8,0},{9,1},... | collective-permute-start | bytes 786440 | tf_op jit(solution)/shard_map/ppermute | solution.py:290
  41.4 1.6 %collective-permute-start.17 = (f32[128,512]{1,0:T(8,128)S(1)}, f32[128,512]{1,0:T(8,128)S(1)}, u32[]{:S(2)}, u32[]{:S(2)}) collective-permute-start(f32[128,512]{1,0:T(8,128)S(1)} %select_select_fusion.refs_5_), channel_id=1, source_target_pairs={{0,8},{1,9},{2,10},{3,11},{4,12},{5,13},{6,14},{7,15},{8,0},{9,1},... | collective-permute-start | bytes 786440 | tf_op jit(solution)/shard_map/ppermute | solution.py:290
  46.2 40.4 %copy-start = (f32[6,1,1,128,128]{4,3,2,1,0:T(8,128)S(1)}, f32[6,1,1,128,128]{4,3,2,1,0:T(8,128)}, u32[]{:S(2)}) copy-start(f32[6,1,1,128,128]{4,3,2,1,0:T(8,128)} %rhs.1) | copy-start | bytes 1179652
  46.3 17.3 %collective-permute-start.18 = (f32[832,128]{1,0:T(8,128)S(1)}, f32[832,128]{1,0:T(8,128)S(1)}, u32[]{:S(2)}, u32[]{:S(2)}) collective-permute-start(f32[832,128]{1,0:T(8,128)S(1)} %get-tuple-element.24), channel_id=1, source_target_pairs={{0,2},{1,3},{2,0},{3,1},{4,6},{5,7},{6,4},{7,5},{8,10},{9,11},{10,... | collective-permute-start | bytes 1277960 | tf_op jit(solution)/shard_map/ppermute | solution.py:290
  46.3 40.0 %collective-permute-start.19 = (f32[840,128]{1,0:T(8,128)S(1)}, f32[840,128]{1,0:T(8,128)S(1)}, u32[]{:S(2)}, u32[]{:S(2)}) collective-permute-start(f32[840,128]{1,0:T(8,128)S(1)} %get-tuple-element.25), channel_id=1, source_target_pairs={{0,4},{1,5},{2,0},{3,1},{4,6},{5,7},{6,2},{7,3},{8,12},{9,13},{10,... | collective-permute-start | bytes 1290248 | tf_op jit(solution)/shard_map/ppermute | solution.py:290
  55.8 30.5 %collective-permute-start.21 = (f32[840,128]{1,0:T(8,128)S(1)}, f32[840,128]{1,0:T(8,128)S(1)}, u32[]{:S(2)}, u32[]{:S(2)}) collective-permute-start(f32[840,128]{1,0:T(8,128)S(1)} %get-tuple-element.25), channel_id=1, source_target_pairs={{0,8},{1,9},{2,4},{3,5},{4,2},{5,3},{6,14},{7,15},{8,0},{9,1},{10,... | collective-permute-start | bytes 1290248 | tf_op jit(solution)/shard_map/ppermute | solution.py:290
  59.1 27.2 %collective-permute-start.20 = (f32[840,128]{1,0:T(8,128)S(1)}, f32[840,128]{1,0:T(8,128)S(1)}, u32[]{:S(2)}, u32[]{:S(2)}) collective-permute-start(f32[840,128]{1,0:T(8,128)S(1)} %get-tuple-element.26.mine), channel_id=1, source_target_pairs={{6,4},{7,5},{14,12},{15,13},{22,20},{23,21},{30,28},{31,29},{0,2},... | collective-permute-start | bytes 1290248 | tf_op jit(solution)/shard_map/ppermute | solution.py:293
  63.6 23.1 %collective-permute-start.22 = (f32[832,128]{1,0:T(8,128)S(1)}, f32[832,128]{1,0:T(8,128)S(1)}, u32[]{:S(2)}, u32[]{:S(2)}) collective-permute-start(f32[832,128]{1,0:T(8,128)S(1)} %join.1), channel_id=1, source_target_pairs={{4,0},{5,1},{12,8},{13,9},{20,16},{21,17},{28,24},{29,25},{2,6},{3... | collective-permute-start | bytes 1277960 | tf_op jit(solution)/shard_map/ppermute | solution.py:293
  64.9 21.4 %collective-permute-start.23 = (f32[64,128]{1,0:T(8,128)S(1)}, f32[64,128]{1,0:T(8,128)S(1)}, u32[]{:S(2)}, u32[]{:S(2)}) collective-permute-start(f32[64,128]{1,0:T(8,128)S(1)} %get-tuple-element.27), channel_id=1, source_target_pairs={{0,6},{1,7},{2,4},{3,5},{4,2},{5,3},{6,0},{7,1},{8,14},{9,15},{10,... | collective-permute-start | bytes 98312 | tf_op jit(solution)/shard_map/ppermute | solution.py:290

commit v13 on v12

--- a/solution.py
+++ b/solution.py
@@ -334,7 +334,7 @@
         for j in range(1, steps)
     ]
     la = send(near, [(line(1, 0), low_homes[0])])
-    ly = send_some(near, [(line(2, 1), low_homes[0]), (line(3, 1), low_homes[1]), (line(3, 2), high_homes[1])])
+    ly = send_some(near, [(line(2, 1), low_homes[0]), (line(3, 1), low_homes[1])])
 
     vector = jax.ShapeDtypeStruct((nrhs, width), F32)
     order = ((low_homes[1], (0, 1, 2, 3)), (high_homes[0], (2, 1, 0, 3)), (high_homes[1], (3, 2, 1, 0)))
@@ -349,6 +349,7 @@
     )(mine, *gathered, *ready)
     swapped = send(turned, [low_homes, low_homes[::-1], high_homes])
     later = lax.optimization_barrier((near, turned))[0]
+    last_block = send_some(later, [(line(3, 2), high_homes[1])])
     lx = send(later, [(line(2, 0), low_homes[0]), (line(3, 0), low_homes[1])])
     s_0, s_1 = pl.pallas_call(
         functools.partial(low_kernel, low_homes, col_count),
@@ -380,7 +381,7 @@
         compiler_params=PARAMS,
         cost_estimate=CHEAP,
         name="solve_high",
-    )(turned, swapped, ly, w_1, w_2, held_inverses)
+    )(turned, swapped, last_block, w_1, w_2, held_inverses)
 
     def spread(s, homes):
         have = {k: list(homes[k]) for k in homes}

time: 87.9 us -> 82.4 us (0.937)
  starting transfers between devices: 38.3 us -> 31.1 us
  Pallas kernels: 12.4 us -> 14.1 us
    ppermute x21, starting transfers between devices: 31.3 us -> 23.5 us  [send(): return lax.ppermute(x, AXES, sorted(onward.items()))]
    pallas_call x1, Pallas kernels: 0.02 us -> 1.05 us  [on_device(): pl.pallas_call(functools.partial(high_kernel, high_homes, col_count), in_...]
    ppermute x3 -> x4, starting transfers between devices: 7.04 us -> 7.51 us  [send_some(): return lax.ppermute(x, AXES, pairs)]
  transfers between devices with their start and end apart: 24 -> 25, of which waited for: 14 -> 13; matrix products, arithmetic and copies ran while one was open for 0% -> 0% of each run, Pallas kernels for 8% -> 10%
where the time goes in v13:
time: 82.4 us; the launch traced here: 82.1 us
  waiting for transfers between devices  36 us (44%)
  starting transfers between devices  31.1 us (38%)
  Pallas kernels  14.1 us (17%)
  between operations  0.83 us (1%)
    ppermute x21, waiting for transfers between devices, send(): return lax.ppermute(x, AXES, sorted(onward.items()))  35.7 us
    ppermute x21, starting transfers between devices, send(): return lax.ppermute(x, AXES, sorted(onward.items()))  23.5 us
    ppermute x4, starting transfers between devices, send_some(): return lax.ppermute(x, AXES, pairs)  7.51 us
    pallas_call x2, Pallas kernels, update(): pl.pallas_call(functools.partial(update_kernel, (groups, row_count, share...  6.55 us
    pallas_call x1, Pallas kernels, on_device(): pl.pallas_call(functools.partial(ready_kernel, low_homes, col_count), in_...  1.69 us
  transfers between devices with their start and end apart: 25, of which 13 were waited for; matrix products, arithmetic and copies ran while one was open for 0% of the time, Pallas kernels for 10%

profile of v13, /device:TPU:0, one launch (start us, length us, event | category | flops | bytes accessed | tf_op | source)
XLA Modules:
  0.0 82.1 jit_solution(16258093625402911808)
XLA Ops:
  0.6 1.3 %fetch.1 = (f32[512,512]{1,0:T(8,128)S(1)}, f32[128,128]{1,0:T(8,128)S(1)}) custom-call(f32[6,1,1,512,512]{4,3,2,1,0:T(8,128)} %refs_8_.3, f32[6,1,1,128,128]{4,3,2,1,0:T(8,128)} %rhs.1), custom_call_target="tpu_custom_call" | custom-call | flops 1000 | bytes 1000 | tf_op jit(solution)/shard_map/fetch/pallas_call | solution.py:306
  1.9 1.3 %collective-permute-start.5 = (f32[512,512]{1,0:T(8,128)S(1)}, f32[512,512]{1,0:T(8,128)S(1)}, u32[]{:S(2)}, u32[]{:S(2)}) collective-permute-start(f32[512,512]{1,0:T(8,128)S(1)} %get-tuple-element.22.near), channel_id=1, source_target_pairs={{10,0},{11,1}} | collective-permute-start | bytes 3145736 | tf_op jit(solution)/shard_map/ppermute | solution.py:293
  3.2 0.1 collective-permute-start.4
  3.3 2.9 %collective-permute-start = (f32[128,128]{1,0:T(8,128)S(1)}, f32[128,128]{1,0:T(8,128)S(1)}, u32[]{:S(2)}, u32[]{:S(2)}) collective-permute-start(f32[128,128]{1,0:T(8,128)S(1)} %get-tuple-element.16.own), channel_id=1, source_target_pairs={{0,2},{1,9},{2,0},{3,1},{4,28},{5,13},{6,14},{7,5},{8,24},{9,11},{... | collective-permute-start | bytes 196616 | tf_op jit(solution)/shard_map/ppermute | solution.py:290
  6.2 2.1 %collective-permute-start.1 = (f32[128,128]{1,0:T(8,128)S(1)}, f32[128,128]{1,0:T(8,128)S(1)}, u32[]{:S(2)}, u32[]{:S(2)}) collective-permute-start(f32[128,128]{1,0:T(8,128)S(1)} %get-tuple-element.16.own), channel_id=1, source_target_pairs={{0,4},{1,9},{2,10},{3,11},{4,0},{5,1},{6,14},{7,3},{8,12},{9,13},{... | collective-permute-start | bytes 196616 | tf_op jit(solution)/shard_map/ppermute | solution.py:290
  8.3 0.0 collective-permute-start.2
  8.3 1.7 %ready.1 = (bf16[2,512,512]{2,1,0:T(8,128)(2,1)S(1)}, bf16[2,512,512]{2,1,0:T(8,128)(2,1)S(1)}) custom-call(f32[4,512,512]{2,1,0:T(8,128)} %inverses.3), custom_call_target="tpu_custom_call" | custom-call | flops 1000 | bytes 1000 | tf_op jit(solution)/shard_map/ready/pallas_call | solution.py:318
  10.0 0.0 collective-permute-done.g1
  10.1 1.4 %collective-permute-done.1.g2 = f32[128,128]{1,0:T(8,128)S(1)} collective-permute-done((f32[128,128]{1,0:T(8,128)S(1)}, f32[128,128]{1,0:T(8,128)S(1)}, u32[]{:S(2)}, u32[]{:S(2)}) %collective-permute-start.1) | collective-permute-done | bytes 65568 | tf_op jit(solution)/shard_map/ppermute | solution.py:290
  11.5 3.0 %collective-permute-done.2.g3 = f32[128,128]{1,0:T(8,128)S(1)} collective-permute-done((f32[128,128]{1,0:T(8,128)S(1)}, f32[128,128]{1,0:T(8,128)S(1)}, u32[]{:S(2)}, u32[]{:S(2)}) %collective-permute-start.2) | collective-permute-done | bytes 65568 | tf_op jit(solution)/shard_map/ppermute | solution.py:290
  14.5 0.5 turn.1.out.own
  15.0 0.1 collective-permute-start.11
  15.1 0.7 collective-permute-start.10
  15.8 0.9 %collective-permute-start.3 = (f32[128,512]{1,0:T(8,128)S(1)}, f32[128,512]{1,0:T(8,128)S(1)}, u32[]{:S(2)}, u32[]{:S(2)}) collective-permute-start(f32[128,512]{1,0:T(8,128)S(1)} %turn.1.out.own), channel_id=1, source_target_pairs={{0,1},{1,0},{2,10},{3,11},{4,12},{5,13},{6,14},{7,4},{8,24},{9,25}... | collective-permute-start | bytes 786440 | tf_op jit(solution)/shard_map/ppermute | solution.py:290
  16.7 5.5 %collective-permute-done.3.swapped = f32[128,512]{1,0:T(8,128)S(1)} collective-permute-done((f32[128,512]{1,0:T(8,128)S(1)}, f32[128,512]{1,0:T(8,128)S(1)}, u32[]{:S(2)}, u32[]{:S(2)}) %collective-permute-start.3) | collective-permute-done | bytes 262176 | tf_op jit(solution)/shard_map/ppermute | solution.py:290
  22.2 0.0 collective-permute-done.5.ly
  22.2 0.0 collective-permute-done.4.la
  22.2 0.7 solve_low.1
  23.0 0.1 collective-permute-start.6
  23.1 0.0 collective-permute-done.11.lx
  23.1 1.3 %reduce_low.1 = f32[128,512]{1,0:T(8,128)} custom-call(f32[128,512]{1,0:T(8,128)S(1)} %get-tuple-element.20.s_a, f32[128,512]{1,0:T(8,128)S(1)} %get-tuple-element.21.s_b, f32[512,512]{1,0:T(8,128)S(1)} %collective-permute-done.11.lx, f32[512,512]{1,0:T(8,128)S(1)} %collective-permute-done.5.ly), custom_call_target="tpu_custom_call" | custom-call | flops 1000 | bytes 1000 | tf_op jit(solution)/shard_map/reduce_low/pallas_call | solution.py:363
  24.4 0.9 %collective-permute-start.12 = (f32[128,512]{1,0:T(8,128)}, f32[128,512]{1,0:T(8,128)}, u32[]{:S(2)}, u32[]{:S(2)}) collective-permute-start(f32[128,512]{1,0:T(8,128)} %reduce_low.1), channel_id=1, source_target_pairs={{0,15},{1,9},{2,10},{3,11},{4,12},{5,13},{6,14},{7,8},{8,0},{9,1},... | collective-permute-start | bytes 786440 | tf_op jit(solution)/shard_map/ppermute | solution.py:290
  25.3 0.0 collective-permute-start.13
  25.3 1.6 %collective-permute-done.6 = f32[128,512]{1,0:T(8,128)S(1)} collective-permute-done((f32[128,512]{1,0:T(8,128)S(1)}, f32[128,512]{1,0:T(8,128)S(1)}, u32[]{:S(2)}, u32[]{:S(2)}) %collective-permute-start.6) | collective-permute-done | bytes 262176 | tf_op jit(solution)/shard_map/ppermute | solution.py:290
  27.0 0.1 collective-permute-start.7
  27.1 0.0 collective-permute-done.10.block
  27.1 2.8 %collective-permute-done.12.w_1 = f32[128,512]{1,0:T(8,128)} collective-permute-done((f32[128,512]{1,0:T(8,128)}, f32[128,512]{1,0:T(8,128)}, u32[]{:S(2)}, u32[]{:S(2)}) %collective-permute-start.12) | collective-permute-done | bytes 262176 | tf_op jit(solution)/shard_map/ppermute | solution.py:290
  29.9 2.8 %collective-permute-done.13.w_2 = f32[128,512]{1,0:T(8,128)} collective-permute-done((f32[128,512]{1,0:T(8,128)}, f32[128,512]{1,0:T(8,128)}, u32[]{:S(2)}, u32[]{:S(2)}) %collective-permute-start.13) | collective-permute-done | bytes 262176 | tf_op jit(solution)/shard_map/ppermute | solution.py:290
  32.7 1.0 %solve_high.1.refs_4_ = f32[128,512]{1,0:T(8,128)S(1)} custom-call(f32[128,512]{1,0:T(8,128)S(1)} %turn.1.out.own, f32[128,512]{1,0:T(8,128)S(1)} %collective-permute-done.3.swapped, f32[512,512]{1,0:T(8,128)S(1)} %collective-permute-done.10.block, f32[128,512]{1,0:T(8,128)} %collective-permute-done.12.w_1, f32[128,512]{1,0:T(8,128)} %collective-permute-done.13.w_2, ...), custom_call_target="tpu_custom_call" | custom-call | flops 1000 | bytes 1000 | tf_op jit(solution)/shard_map/solve_high/pallas_call | solution.py:375
  33.7 0.4 collective-permute-start.14
  34.2 0.1 collective-permute-start.15
  34.3 0.4 collective-permute-start.16
  34.7 0.1 collective-permute-start.8
  34.8 0.0 collective-permute-done.7.refs_1_
  34.8 0.4 collective-permute-start.17
  35.2 0.1 collective-permute-done.14
  35.4 0.4 collective-permute-start.9
  35.7 0.0 collective-permute-done.15
  35.7 0.4 collective-permute-done.16
  36.1 0.1 select_select_fusion.refs_5_
  36.2 0.4 collective-permute-start.18
  36.6 0.0 collective-permute-done.8.refs_2_
  36.6 0.2 collective-permute-done.17.refs_6_
  36.9 0.4 collective-permute-done.9.refs_3_
  37.2 0.5 collective-permute-done.18.refs_7_
  37.8 3.3 %update_first.1 = (f32[832,128]{1,0:T(8,128)S(1)}, f32[840,128]{1,0:T(8,128)S(1)}, f32[64,128]{1,0:T(8,128)S(1)}) custom-call(f32[128,512]{1,0:T(8,128)S(1)} %broadcast_select_fusion.refs_0_, f32[128,512]{1,0:T(8,128)S(1)} %collective-permute-done.7.refs_1_, f32[128,512]{1,0:T(8,128)S(1)} %collective-permute-done.8.refs_2_, ...), custom_call_target="tpu_custom_call" | custom-call | flops 1000 | bytes 1000 | tf_op jit(solution)/shard_map/update_first/pallas_call | solution.py:435
  41.1 0.0 copy-start
  41.1 0.1 collective-permute-start.19
  41.1 9.4 %collective-permute-start.20 = (f32[840,128]{1,0:T(8,128)S(1)}, f32[840,128]{1,0:T(8,128)S(1)}, u32[]{:S(2)}, u32[]{:S(2)}) collective-permute-start(f32[840,128]{1,0:T(8,128)S(1)} %get-tuple-element.25), channel_id=1, source_target_pairs={{0,4},{1,5},{2,0},{3,1},{4,6},{5,7},{6,2},{7,3},{8,12},{9,13},{10,... | collective-permute-start | bytes 1290248 | tf_op jit(solution)/shard_map/ppermute | solution.py:290
  50.5 0.0 collective-permute-start.22
  50.5 3.3 %update_second.1 = (f32[832,128]{1,0:T(8,128)S(1)}, f32[840,128]{1,0:T(8,128)S(1)}) custom-call(f32[128,512]{1,0:T(8,128)S(1)} %broadcast_select_fusion.refs_0_, f32[128,512]{1,0:T(8,128)S(1)} %collective-permute-done.7.refs_1_, f32[128,512]{1,0:T(8,128)S(1)} %collective-permute-done.8.refs_2_, f32[128,512]{1,0:T(8,128)S(1)} %collective-permute-done.9.refs_3_, ...), custom_call_target="tpu_custom_call" | custom-call | flops 1000 | bytes 1000 | tf_op jit(solution)/shard_map/update_second/pallas_call | solution.py:435
  53.8 4.2 %collective-permute-start.21 = (f32[840,128]{1,0:T(8,128)S(1)}, f32[840,128]{1,0:T(8,128)S(1)}, u32[]{:S(2)}, u32[]{:S(2)}) collective-permute-start(f32[840,128]{1,0:T(8,128)S(1)} %get-tuple-element.26.mine), channel_id=1, source_target_pairs={{6,4},{7,5},{14,12},{15,13},{22,20},{23,21},{30,28},{31,29},{0,2},... | collective-permute-start | bytes 1290248 | tf_op jit(solution)/shard_map/ppermute | solution.py:293
  58.0 0.0 collective-permute-done.19.theirs.got_1
  58.0 1.3 %collective-permute-start.23 = (f32[832,128]{1,0:T(8,128)S(1)}, f32[832,128]{1,0:T(8,128)S(1)}, u32[]{:S(2)}, u32[]{:S(2)}) collective-permute-start(f32[832,128]{1,0:T(8,128)S(1)} %join.1), channel_id=1, source_target_pairs={{4,0},{5,1},{12,8},{13,9},{20,16},{21,17},{28,24},{29,25},{2,6},{3... | collective-permute-start | bytes 1277960 | tf_op jit(solution)/shard_map/ppermute | solution.py:293
  59.3 4.6 %collective-permute-start.24 = (f32[64,128]{1,0:T(8,128)S(1)}, f32[64,128]{1,0:T(8,128)S(1)}, u32[]{:S(2)}, u32[]{:S(2)}) collective-permute-start(f32[64,128]{1,0:T(8,128)S(1)} %get-tuple-element.27), channel_id=1, source_target_pairs={{0,6},{1,7},{2,4},{3,5},{4,2},{5,3},{6,0},{7,1},{8,14},{9,15},{10,... | collective-permute-start | bytes 98312 | tf_op jit(solution)/shard_map/ppermute | solution.py:290
  64.0 16.8 %collective-permute-done.24.far = f32[64,128]{1,0:T(8,128)S(1)} collective-permute-done((f32[64,128]{1,0:T(8,128)S(1)}, f32[64,128]{1,0:T(8,128)S(1)}, u32[]{:S(2)}, u32[]{:S(2)}) %collective-permute-start.24) | collective-permute-done | bytes 32800 | tf_op jit(solution)/shard_map/ppermute | solution.py:290
  80.8 0.0 collective-permute-done.20.got_2
  80.8 0.0 collective-permute-done.22.got_4
  80.8 0.0 collective-permute-done.21.got_3
  80.8 0.3 collective-permute-done.23.joined
  81.1 0.0 copy-done
  81.1 1.0 %add_up.1 = (f32[4,64,128]{2,1,0:T(8,128)}, f32[6,128,128]{2,1,0:T(8,128)}) custom-call(f32[6,128,128]{2,1,0:T(8,128)S(1)} %bitcast.4, f32[832,128]{1,0:T(8,128)S(1)} %get-tuple-element.23.own, f32[832,128]{1,0:T(8,128)S(1)} %collective-permute-done.19.theirs.got_1, f32[840,128]{1,0:T(8,128)S(1)} %collective-permute-done.20.got_2, ...), custom_call_target="tpu_custom_call" | custom-call | flops 1000 | bytes 1000 | tf_op jit(solution)/shard_map/add_up/pallas_call | solution.py:476
  (2 shorter events, 0.1 us)
Async XLA Ops:
  1.9 20.3 %collective-permute-start.5 = (f32[512,512]{1,0:T(8,128)S(1)}, f32[512,512]{1,0:T(8,128)S(1)}, u32[]{:S(2)}, u32[]{:S(2)}) collective-permute-start(f32[512,512]{1,0:T(8,128)S(1)} %get-tuple-element.22.near), channel_id=1, source_target_pairs={{10,0},{11,1}} | collective-permute-start | bytes 3145736 | tf_op jit(solution)/shard_map/ppermute | solution.py:293
  3.2 19.0 %collective-permute-start.4 = (f32[512,512]{1,0:T(8,128)S(1)}, f32[512,512]{1,0:T(8,128)S(1)}, u32[]{:S(2)}, u32[]{:S(2)}) collective-permute-start(f32[512,512]{1,0:T(8,128)S(1)} %get-tuple-element.22.near), channel_id=1, source_target_pairs={{0,8},{1,0},{2,10},{3,11},{4,12},{5,13},{6,14},{7,15},{8,9},{9,1},... | collective-permute-start | bytes 3145736 | tf_op jit(solution)/shard_map/ppermute | solution.py:290
  3.3 6.7 %collective-permute-start = (f32[128,128]{1,0:T(8,128)S(1)}, f32[128,128]{1,0:T(8,128)S(1)}, u32[]{:S(2)}, u32[]{:S(2)}) collective-permute-start(f32[128,128]{1,0:T(8,128)S(1)} %get-tuple-element.16.own), channel_id=1, source_target_pairs={{0,2},{1,9},{2,0},{3,1},{4,28},{5,13},{6,14},{7,5},{8,24},{9,11},{... | collective-permute-start | bytes 196616 | tf_op jit(solution)/shard_map/ppermute | solution.py:290
  6.2 5.3 %collective-permute-start.1 = (f32[128,128]{1,0:T(8,128)S(1)}, f32[128,128]{1,0:T(8,128)S(1)}, u32[]{:S(2)}, u32[]{:S(2)}) collective-permute-start(f32[128,128]{1,0:T(8,128)S(1)} %get-tuple-element.16.own), channel_id=1, source_target_pairs={{0,4},{1,9},{2,10},{3,11},{4,0},{5,1},{6,14},{7,3},{8,12},{9,13},{... | collective-permute-start | bytes 196616 | tf_op jit(solution)/shard_map/ppermute | solution.py:290
  8.3 6.2 %collective-permute-start.2 = (f32[128,128]{1,0:T(8,128)S(1)}, f32[128,128]{1,0:T(8,128)S(1)}, u32[]{:S(2)}, u32[]{:S(2)}) collective-permute-start(f32[128,128]{1,0:T(8,128)S(1)} %get-tuple-element.16.own), channel_id=1, source_target_pairs={{0,6},{1,7},{2,10},{3,11},{4,28},{5,13},{6,0},{7,1},{8,24},{9,15},... | collective-permute-start | bytes 196616 | tf_op jit(solution)/shard_map/ppermute | solution.py:290
  15.0 8.1 %collective-permute-start.11 = (f32[512,512]{1,0:T(8,128)S(1)}, f32[512,512]{1,0:T(8,128)S(1)}, u32[]{:S(2)}, u32[]{:S(2)}) collective-permute-start(f32[512,512]{1,0:T(8,128)S(1)} %get-tuple-element.22.near), channel_id=1, source_target_pairs={{0,8},{1,9},{2,10},{3,11},{4,12},{5,13},{6,14},{7,15},{8,0},{9,1},... | collective-permute-start | bytes 3145736 | tf_op jit(solution)/shard_map/ppermute | solution.py:290
  15.1 12.0 %collective-permute-start.10 = (f32[512,512]{1,0:T(8,128)S(1)}, f32[512,512]{1,0:T(8,128)S(1)}, u32[]{:S(2)}, u32[]{:S(2)}) collective-permute-start(f32[512,512]{1,0:T(8,128)S(1)} %get-tuple-element.22.near), channel_id=1, source_target_pairs={{13,15}} | collective-permute-start | bytes 3145736 | tf_op jit(solution)/shard_map/ppermute | solution.py:293
  15.8 6.4 %collective-permute-start.3 = (f32[128,512]{1,0:T(8,128)S(1)}, f32[128,512]{1,0:T(8,128)S(1)}, u32[]{:S(2)}, u32[]{:S(2)}) collective-permute-start(f32[128,512]{1,0:T(8,128)S(1)} %turn.1.out.own), channel_id=1, source_target_pairs={{0,1},{1,0},{2,10},{3,11},{4,12},{5,13},{6,14},{7,4},{8,24},{9,25}... | collective-permute-start | bytes 786440 | tf_op jit(solution)/shard_map/ppermute | solution.py:290
  23.0 4.0 %collective-permute-start.6 = (f32[128,512]{1,0:T(8,128)S(1)}, f32[128,512]{1,0:T(8,128)S(1)}, u32[]{:S(2)}, u32[]{:S(2)}) collective-permute-start(f32[128,512]{1,0:T(8,128)S(1)} %get-tuple-element.21.s_b), channel_id=1, source_target_pairs={{0,2},{1,3},{2,10},{3,11},{4,12},{5,13},{6,14},{7,15},{8,0},{9,1},... | collective-permute-start | bytes 786440 | tf_op jit(solution)/shard_map/ppermute | solution.py:290
  24.4 5.5 %collective-permute-start.12 = (f32[128,512]{1,0:T(8,128)}, f32[128,512]{1,0:T(8,128)}, u32[]{:S(2)}, u32[]{:S(2)}) collective-permute-start(f32[128,512]{1,0:T(8,128)} %reduce_low.1), channel_id=1, source_target_pairs={{0,15},{1,9},{2,10},{3,11},{4,12},{5,13},{6,14},{7,8},{8,0},{9,1},... | collective-permute-start | bytes 786440 | tf_op jit(solution)/shard_map/ppermute | solution.py:290
  25.3 7.4 %collective-permute-start.13 = (f32[128,512]{1,0:T(8,128)}, f32[128,512]{1,0:T(8,128)}, u32[]{:S(2)}, u32[]{:S(2)}) collective-permute-start(f32[128,512]{1,0:T(8,128)} %reduce_low.1), channel_id=1, source_target_pairs={{0,12},{1,15},{2,10},{3,11},{4,8},{5,13},{6,14},{7,9},{8,0},{9,1},... | collective-permute-start | bytes 786440 | tf_op jit(solution)/shard_map/ppermute | solution.py:290
  27.0 7.8 %collective-permute-start.7 = (f32[128,512]{1,0:T(8,128)S(1)}, f32[128,512]{1,0:T(8,128)S(1)}, u32[]{:S(2)}, u32[]{:S(2)}) collective-permute-start(f32[128,512]{1,0:T(8,128)S(1)} %broadcast_select_fusion.refs_0_), channel_id=1, source_target_pairs={{0,16},{1,17},{2,18},{3,19},{4,12},{5,13},{6,14},{7,15},{8,0},{9,1... | collective-permute-start | bytes 786440 | tf_op jit(solution)/shard_map/ppermute | solution.py:290
  33.7 1.6 %collective-permute-start.14 = (f32[128,512]{1,0:T(8,128)S(1)}, f32[128,512]{1,0:T(8,128)S(1)}, u32[]{:S(2)}, u32[]{:S(2)}) collective-permute-start(f32[128,512]{1,0:T(8,128)S(1)} %solve_high.1.refs_4_), channel_id=1, source_target_pairs={{0,8},{1,9},{2,10},{3,11},{4,12},{5,13},{6,14},{7,15},{8,0},{9,1},... | collective-permute-start | bytes 786440 | tf_op jit(solution)/shard_map/ppermute | solution.py:290
  34.2 1.5 %collective-permute-start.15 = (f32[128,512]{1,0:T(8,128)S(1)}, f32[128,512]{1,0:T(8,128)S(1)}, u32[]{:S(2)}, u32[]{:S(2)}) collective-permute-start(f32[128,512]{1,0:T(8,128)S(1)} %solve_high.1.refs_4_), channel_id=1, source_target_pairs={{0,8},{1,9},{2,10},{3,11},{4,12},{5,4},{6,7},{7,15},{8,0},{9,1},{1... | collective-permute-start | bytes 786440 | tf_op jit(solution)/shard_map/ppermute | solution.py:290
  34.3 1.8 %collective-permute-start.16 = (f32[128,512]{1,0:T(8,128)S(1)}, f32[128,512]{1,0:T(8,128)S(1)}, u32[]{:S(2)}, u32[]{:S(2)}) collective-permute-start(f32[128,512]{1,0:T(8,128)S(1)} %solve_high.1.refs_4_), channel_id=1, source_target_pairs={{0,8},{1,9},{2,10},{3,11},{4,12},{5,13},{6,14},{7,15},{8,0},{9,1},... | collective-permute-start | bytes 786440 | tf_op jit(solution)/shard_map/ppermute | solution.py:290
  34.7 1.9 %collective-permute-start.8 = (f32[128,512]{1,0:T(8,128)S(1)}, f32[128,512]{1,0:T(8,128)S(1)}, u32[]{:S(2)}, u32[]{:S(2)}) collective-permute-start(f32[128,512]{1,0:T(8,128)S(1)} %broadcast_select_fusion.refs_0_), channel_id=1, source_target_pairs={{0,8},{1,9},{2,10},{3,11},{4,12},{5,13},{6,14},{7,15},{8,0},{9,1},... | collective-permute-start | bytes 786440 | tf_op jit(solution)/shard_map/ppermute | solution.py:290
  34.8 2.0 %collective-permute-start.17 = (f32[128,512]{1,0:T(8,128)S(1)}, f32[128,512]{1,0:T(8,128)S(1)}, u32[]{:S(2)}, u32[]{:S(2)}) collective-permute-start(f32[128,512]{1,0:T(8,128)S(1)} %solve_high.1.refs_4_), channel_id=1, source_target_pairs={{0,8},{1,9},{2,10},{3,11},{4,12},{5,13},{6,14},{7,15},{8,0},{9,1},... | collective-permute-start | bytes 786440 | tf_op jit(solution)/shard_map/ppermute | solution.py:290
  35.4 1.9 %collective-permute-start.9 = (f32[128,512]{1,0:T(8,128)S(1)}, f32[128,512]{1,0:T(8,128)S(1)}, u32[]{:S(2)}, u32[]{:S(2)}) collective-permute-start(f32[128,512]{1,0:T(8,128)S(1)} %collective-permute-done.7.refs_1_), channel_id=1, source_target_pairs={{0,8},{1,9},{2,10},{3,11},{4,12},{5,13},{6,14},{7,15},{8,0},{9,1},... | collective-permute-start | bytes 786440 | tf_op jit(solution)/shard_map/ppermute | solution.py:290
  36.2 1.6 %collective-permute-start.18 = (f32[128,512]{1,0:T(8,128)S(1)}, f32[128,512]{1,0:T(8,128)S(1)}, u32[]{:S(2)}, u32[]{:S(2)}) collective-permute-start(f32[128,512]{1,0:T(8,128)S(1)} %select_select_fusion.refs_5_), channel_id=1, source_target_pairs={{0,8},{1,9},{2,10},{3,11},{4,12},{5,13},{6,14},{7,15},{8,0},{9,1},... | collective-permute-start | bytes 786440 | tf_op jit(solution)/shard_map/ppermute | solution.py:290
  41.1 40.1 %copy-start = (f32[6,1,1,128,128]{4,3,2,1,0:T(8,128)S(1)}, f32[6,1,1,128,128]{4,3,2,1,0:T(8,128)}, u32[]{:S(2)}) copy-start(f32[6,1,1,128,128]{4,3,2,1,0:T(8,128)} %rhs.1) | copy-start | bytes 1179652
  41.1 16.9 %collective-permute-start.19 = (f32[832,128]{1,0:T(8,128)S(1)}, f32[832,128]{1,0:T(8,128)S(1)}, u32[]{:S(2)}, u32[]{:S(2)}) collective-permute-start(f32[832,128]{1,0:T(8,128)S(1)} %get-tuple-element.24), channel_id=1, source_target_pairs={{0,2},{1,3},{2,0},{3,1},{4,6},{5,7},{6,4},{7,5},{8,10},{9,11},{10,... | collective-permute-start | bytes 1277960 | tf_op jit(solution)/shard_map/ppermute | solution.py:290
  41.1 39.6 %collective-permute-start.20 = (f32[840,128]{1,0:T(8,128)S(1)}, f32[840,128]{1,0:T(8,128)S(1)}, u32[]{:S(2)}, u32[]{:S(2)}) collective-permute-start(f32[840,128]{1,0:T(8,128)S(1)} %get-tuple-element.25), channel_id=1, source_target_pairs={{0,4},{1,5},{2,0},{3,1},{4,6},{5,7},{6,2},{7,3},{8,12},{9,13},{10,... | collective-permute-start | bytes 1290248 | tf_op jit(solution)/shard_map/ppermute | solution.py:290
  50.5 30.3 %collective-permute-start.22 = (f32[840,128]{1,0:T(8,128)S(1)}, f32[840,128]{1,0:T(8,128)S(1)}, u32[]{:S(2)}, u32[]{:S(2)}) collective-permute-start(f32[840,128]{1,0:T(8,128)S(1)} %get-tuple-element.25), channel_id=1, source_target_pairs={{0,8},{1,9},{2,4},{3,5},{4,2},{5,3},{6,14},{7,15},{8,0},{9,1},{10,... | collective-permute-start | bytes 1290248 | tf_op jit(solution)/shard_map/ppermute | solution.py:290
  53.8 27.0 %collective-permute-start.21 = (f32[840,128]{1,0:T(8,128)S(1)}, f32[840,128]{1,0:T(8,128)S(1)}, u32[]{:S(2)}, u32[]{:S(2)}) collective-permute-start(f32[840,128]{1,0:T(8,128)S(1)} %get-tuple-element.26.mine), channel_id=1, source_target_pairs={{6,4},{7,5},{14,12},{15,13},{22,20},{23,21},{30,28},{31,29},{0,2},... | collective-permute-start | bytes 1290248 | tf_op jit(solution)/shard_map/ppermute | solution.py:293
  58.0 23.1 %collective-permute-start.23 = (f32[832,128]{1,0:T(8,128)S(1)}, f32[832,128]{1,0:T(8,128)S(1)}, u32[]{:S(2)}, u32[]{:S(2)}) collective-permute-start(f32[832,128]{1,0:T(8,128)S(1)} %join.1), channel_id=1, source_target_pairs={{4,0},{5,1},{12,8},{13,9},{20,16},{21,17},{28,24},{29,25},{2,6},{3... | collective-permute-start | bytes 1277960 | tf_op jit(solution)/shard_map/ppermute | solution.py:293
  59.3 21.4 %collective-permute-start.24 = (f32[64,128]{1,0:T(8,128)S(1)}, f32[64,128]{1,0:T(8,128)S(1)}, u32[]{:S(2)}, u32[]{:S(2)}) collective-permute-start(f32[64,128]{1,0:T(8,128)S(1)} %get-tuple-element.27), channel_id=1, source_target_pairs={{0,6},{1,7},{2,4},{3,5},{4,2},{5,3},{6,0},{7,1},{8,14},{9,15},{10,... | collective-permute-start | bytes 98312 | tf_op jit(solution)/shard_map/ppermute | solution.py:290

commit v14 on v13

--- a/solution.py
+++ b/solution.py
@@ -10,7 +10,7 @@
 AXES = ("row", "col")
 F32 = jnp.float32
 VMEM = pltpu.VMEM
-PARAMS = pltpu.CompilerParams(vmem_limit_bytes=20 * 2**20)
+PARAMS = pltpu.CompilerParams(vmem_limit_bytes=12 * 2**20)
 CHEAP = pl.CostEstimate(flops=1000, bytes_accessed=1000, transcendentals=0)
 
 
@@ -115,17 +115,24 @@
         work(swapped, out, near)
 
 
-def reduce_kernel(homes, col_count, s_a, s_b, lx, ly, w):
+def reduce_kernel(homes, col_count, s_a, s_b, lx, ly, w, block, sem):
     me = position(col_count)
 
     @pl.when((me == homes[0]) | (me == homes[1]))
     def _():
-        w[...] = product(s_a[...], lx[...]) + product(s_b[...], ly[...])
-
-
-def high_kernel(homes, col_count, own, swapped, block, w_1, w_2, inverses, s, inv, sem):
+        copies = [pltpu.make_async_copy(ref, block.at[i], sem.at[i]) for i, ref in enumerate((ly, lx))]
+        for copy in copies:
+            copy.start()
+        copies[0].wait()
+        later = product(s_b[...], block[0])
+        copies[1].wait()
+        w[...] = product(s_a[...], block[1]) + later
+
+
+def high_kernel(homes, col_count, own, swapped, w_1, w_2, inverses, last_block, s, inv, block, sem):
     me = position(col_count)
     copies = [pltpu.make_async_copy(inverses.at[2 + i], inv.at[i], sem.at[i]) for i in range(2)]
+    copies.append(pltpu.make_async_copy(last_block, block, sem.at[2]))
 
     @pl.when(me == homes[0])
     def _():
@@ -141,6 +148,7 @@
         right = swapped[...] - w_1[...]
         copies[0].wait()
         first = product(right, inv[0], True)
+        copies[2].wait()
         right = own[...] - w_2[...] - product(first, block[...])
         copies[1].wait()
         s[...] = product(right, inv[1], True)
@@ -362,9 +370,10 @@
     )(turned, swapped, near, la, *ready, ly)
     w = pl.pallas_call(
         functools.partial(reduce_kernel, low_homes, col_count),
-        in_specs=[vmem] * 4,
+        in_specs=[vmem] * 2 + [pl.BlockSpec(memory_space=pl.ANY)] * 2,
         out_specs=vmem,
         out_shape=vector,
+        scratch_shapes=[VMEM((2, width, width), F32), pltpu.SemaphoreType.DMA((2,))],
         compiler_params=PARAMS,
         cost_estimate=CHEAP,
         name="reduce_low",
@@ -374,14 +383,16 @@
     first_slots, second_slots = ((3, 0, 3, 0), (2, 2, 1, 1)), ((0, 1, 2, 3), (1, 3, 0, 2))
     s_high = pl.pallas_call(
         functools.partial(high_kernel, high_homes, col_count),
-        in_specs=[vmem] * 5 + [hbm],
+        in_specs=[vmem] * 4 + [hbm, pl.BlockSpec(memory_space=pl.ANY)],
         out_specs=vmem,
         out_shape=vector,
-        scratch_shapes=[VMEM((2, width, width), F32), pltpu.SemaphoreType.DMA((2,))],
+        scratch_shapes=[
+            VMEM((2, width, width), F32), VMEM((width, width), F32), pltpu.SemaphoreType.DMA((3,))
+        ],
         compiler_params=PARAMS,
         cost_estimate=CHEAP,
         name="solve_high",
-    )(turned, swapped, last_block, w_1, w_2, held_inverses)
+    )(turned, swapped, w_1, w_2, held_inverses, last_block)
 
     def spread(s, homes):
         have = {k: list(homes[k]) for k in homes}

time: 82.4 us -> 82.4 us (level)
  transfers between devices with their start and end apart: 25 -> 25, of which waited for: 13 -> 13; matrix products, arithmetic and copies ran while one was open for 0% -> 0% of each run, Pallas kernels for 10% -> 11%
where the time goes in v14:
time: 82.4 us; the launch traced here: 82.1 us
  waiting for transfers between devices  35.9 us (44%)
  starting transfers between devices  31 us (38%)
  Pallas kernels  14.3 us (17%)
  between operations  0.84 us (1%)
    ppermute x21, waiting for transfers between devices, send(): return lax.ppermute(x, AXES, sorted(onward.items()))  35.6 us
    ppermute x21, starting transfers between devices, send(): return lax.ppermute(x, AXES, sorted(onward.items()))  23.5 us
    ppermute x4, starting transfers between devices, send_some(): return lax.ppermute(x, AXES, pairs)  7.44 us
    pallas_call x2, Pallas kernels, update(): pl.pallas_call(functools.partial(update_kernel, (groups, row_count, share...  6.55 us
    pallas_call x1, Pallas kernels, on_device(): pl.pallas_call(functools.partial(ready_kernel, low_homes, col_count), in_...  1.69 us
  transfers between devices with their start and end apart: 25, of which 13 were waited for; matrix products, arithmetic and copies ran while one was open for 0% of the time, Pallas kernels for 11%

profile of v14, /device:TPU:0, one launch (start us, length us, event | category | flops | bytes accessed | tf_op | source)
XLA Modules:
  0.0 82.1 jit_solution(5784749158654175489)
XLA Ops:
  0.6 1.3 %fetch.1 = (f32[512,512]{1,0:T(8,128)S(1)}, f32[128,128]{1,0:T(8,128)S(1)}) custom-call(f32[6,1,1,512,512]{4,3,2,1,0:T(8,128)} %refs_8_.3, f32[6,1,1,128,128]{4,3,2,1,0:T(8,128)} %rhs.1), custom_call_target="tpu_custom_call" | custom-call | flops 1000 | bytes 1000 | tf_op jit(solution)/shard_map/fetch/pallas_call | solution.py:314
  1.9 1.3 %collective-permute-start.5 = (f32[512,512]{1,0:T(8,128)S(1)}, f32[512,512]{1,0:T(8,128)S(1)}, u32[]{:S(2)}, u32[]{:S(2)}) collective-permute-start(f32[512,512]{1,0:T(8,128)S(1)} %get-tuple-element.22.near), channel_id=1, source_target_pairs={{10,0},{11,1}} | collective-permute-start | bytes 3145736 | tf_op jit(solution)/shard_map/ppermute | solution.py:301
  3.2 0.1 collective-permute-start.4
  3.3 2.9 %collective-permute-start = (f32[128,128]{1,0:T(8,128)S(1)}, f32[128,128]{1,0:T(8,128)S(1)}, u32[]{:S(2)}, u32[]{:S(2)}) collective-permute-start(f32[128,128]{1,0:T(8,128)S(1)} %get-tuple-element.16.own), channel_id=1, source_target_pairs={{0,2},{1,9},{2,0},{3,1},{4,28},{5,13},{6,14},{7,5},{8,24},{9,11},{... | collective-permute-start | bytes 196616 | tf_op jit(solution)/shard_map/ppermute | solution.py:298
  6.2 2.1 %collective-permute-start.1 = (f32[128,128]{1,0:T(8,128)S(1)}, f32[128,128]{1,0:T(8,128)S(1)}, u32[]{:S(2)}, u32[]{:S(2)}) collective-permute-start(f32[128,128]{1,0:T(8,128)S(1)} %get-tuple-element.16.own), channel_id=1, source_target_pairs={{0,4},{1,9},{2,10},{3,11},{4,0},{5,1},{6,14},{7,3},{8,12},{9,13},{... | collective-permute-start | bytes 196616 | tf_op jit(solution)/shard_map/ppermute | solution.py:298
  8.3 0.0 collective-permute-start.2
  8.3 1.7 %ready.1 = (bf16[2,512,512]{2,1,0:T(8,128)(2,1)S(1)}, bf16[2,512,512]{2,1,0:T(8,128)(2,1)S(1)}) custom-call(f32[4,512,512]{2,1,0:T(8,128)} %inverses.3), custom_call_target="tpu_custom_call" | custom-call | flops 1000 | bytes 1000 | tf_op jit(solution)/shard_map/ready/pallas_call | solution.py:326
  10.0 0.0 collective-permute-done.g1
  10.1 1.4 %collective-permute-done.1.g2 = f32[128,128]{1,0:T(8,128)S(1)} collective-permute-done((f32[128,128]{1,0:T(8,128)S(1)}, f32[128,128]{1,0:T(8,128)S(1)}, u32[]{:S(2)}, u32[]{:S(2)}) %collective-permute-start.1) | collective-permute-done | bytes 65568 | tf_op jit(solution)/shard_map/ppermute | solution.py:298
  11.5 3.0 %collective-permute-done.2.g3 = f32[128,128]{1,0:T(8,128)S(1)} collective-permute-done((f32[128,128]{1,0:T(8,128)S(1)}, f32[128,128]{1,0:T(8,128)S(1)}, u32[]{:S(2)}, u32[]{:S(2)}) %collective-permute-start.2) | collective-permute-done | bytes 65568 | tf_op jit(solution)/shard_map/ppermute | solution.py:298
  14.5 0.5 turn.1.out.own
  15.0 0.1 collective-permute-start.10
  15.1 0.7 collective-permute-start.13
  15.8 0.9 %collective-permute-start.3 = (f32[128,512]{1,0:T(8,128)S(1)}, f32[128,512]{1,0:T(8,128)S(1)}, u32[]{:S(2)}, u32[]{:S(2)}) collective-permute-start(f32[128,512]{1,0:T(8,128)S(1)} %turn.1.out.own), channel_id=1, source_target_pairs={{0,1},{1,0},{2,10},{3,11},{4,12},{5,13},{6,14},{7,4},{8,24},{9,25}... | collective-permute-start | bytes 786440 | tf_op jit(solution)/shard_map/ppermute | solution.py:298
  16.7 5.5 %collective-permute-done.3.swapped = f32[128,512]{1,0:T(8,128)S(1)} collective-permute-done((f32[128,512]{1,0:T(8,128)S(1)}, f32[128,512]{1,0:T(8,128)S(1)}, u32[]{:S(2)}, u32[]{:S(2)}) %collective-permute-start.3) | collective-permute-done | bytes 262176 | tf_op jit(solution)/shard_map/ppermute | solution.py:298
  22.2 0.0 collective-permute-done.5.ly
  22.2 0.0 collective-permute-done.4.la
  22.2 0.7 solve_low.1
  23.0 0.1 collective-permute-start.6
  23.1 0.0 collective-permute-done.10.lx
  23.1 1.5 %reduce_low.1 = f32[128,512]{1,0:T(8,128)} custom-call(f32[128,512]{1,0:T(8,128)S(1)} %get-tuple-element.20.s_a, f32[128,512]{1,0:T(8,128)S(1)} %get-tuple-element.21.s_b, f32[512,512]{1,0:T(8,128)S(1)} %collective-permute-done.10.lx, f32[512,512]{1,0:T(8,128)S(1)} %collective-permute-done.5.ly), custom_call_target="tpu_custom_call" | custom-call | flops 1000 | bytes 1000 | tf_op jit(solution)/shard_map/reduce_low/pallas_call | solution.py:371
  24.6 0.8 collective-permute-start.11
  25.4 0.0 collective-permute-start.12
  25.4 1.6 %collective-permute-done.6 = f32[128,512]{1,0:T(8,128)S(1)} collective-permute-done((f32[128,512]{1,0:T(8,128)S(1)}, f32[128,512]{1,0:T(8,128)S(1)}, u32[]{:S(2)}, u32[]{:S(2)}) %collective-permute-start.6) | collective-permute-done | bytes 262176 | tf_op jit(solution)/shard_map/ppermute | solution.py:298
  27.0 0.1 collective-permute-start.7
  27.1 0.0 collective-permute-done.13.last_block
  27.1 2.8 %collective-permute-done.11.w_1 = f32[128,512]{1,0:T(8,128)} collective-permute-done((f32[128,512]{1,0:T(8,128)}, f32[128,512]{1,0:T(8,128)}, u32[]{:S(2)}, u32[]{:S(2)}) %collective-permute-start.11) | collective-permute-done | bytes 262176 | tf_op jit(solution)/shard_map/ppermute | solution.py:298
  29.9 2.8 %collective-permute-done.12.w_2 = f32[128,512]{1,0:T(8,128)} collective-permute-done((f32[128,512]{1,0:T(8,128)}, f32[128,512]{1,0:T(8,128)}, u32[]{:S(2)}, u32[]{:S(2)}) %collective-permute-start.12) | collective-permute-done | bytes 262176 | tf_op jit(solution)/shard_map/ppermute | solution.py:298
  32.7 1.1 %solve_high.1.refs_4_ = f32[128,512]{1,0:T(8,128)S(1)} custom-call(f32[128,512]{1,0:T(8,128)S(1)} %turn.1.out.own, f32[128,512]{1,0:T(8,128)S(1)} %collective-permute-done.3.swapped, f32[128,512]{1,0:T(8,128)} %collective-permute-done.11.w_1, f32[128,512]{1,0:T(8,128)} %collective-permute-done.12.w_2, f32[4,512,512]{2,1,0:T(8,128)} %inverses.3, ...), custom_call_target="tpu_custom_call" | custom-call | flops 1000 | bytes 1000 | tf_op jit(solution)/shard_map/solve_high/pallas_call | solution.py:384
  33.8 0.5 collective-permute-start.14
  34.3 0.1 collective-permute-start.15
  34.3 0.5 collective-permute-start.16
  34.8 0.1 collective-permute-start.8
  34.8 0.0 collective-permute-done.7.refs_1_
  34.8 0.5 collective-permute-start.17
  35.3 0.1 collective-permute-done.14
  35.4 0.4 collective-permute-start.9
  35.8 0.0 collective-permute-done.15
  35.8 0.4 collective-permute-done.16
  36.2 0.1 select_select_fusion.refs_5_
  36.2 0.4 collective-permute-start.18
  36.7 0.0 collective-permute-done.8.refs_2_
  36.7 0.2 collective-permute-done.17.refs_6_
  36.9 0.4 collective-permute-done.9.refs_3_
  37.3 0.5 collective-permute-done.18.refs_7_
  37.9 3.3 %update_first.1 = (f32[832,128]{1,0:T(8,128)S(1)}, f32[840,128]{1,0:T(8,128)S(1)}, f32[64,128]{1,0:T(8,128)S(1)}) custom-call(f32[128,512]{1,0:T(8,128)S(1)} %broadcast_select_fusion.refs_0_, f32[128,512]{1,0:T(8,128)S(1)} %collective-permute-done.7.refs_1_, f32[128,512]{1,0:T(8,128)S(1)} %collective-permute-done.8.refs_2_, ...), custom_call_target="tpu_custom_call" | custom-call | flops 1000 | bytes 1000 | tf_op jit(solution)/shard_map/update_first/pallas_call | solution.py:446
  41.1 0.0 copy-start
  41.1 0.1 collective-permute-start.19
  41.2 9.4 %collective-permute-start.20 = (f32[840,128]{1,0:T(8,128)S(1)}, f32[840,128]{1,0:T(8,128)S(1)}, u32[]{:S(2)}, u32[]{:S(2)}) collective-permute-start(f32[840,128]{1,0:T(8,128)S(1)} %get-tuple-element.25), channel_id=1, source_target_pairs={{0,4},{1,5},{2,0},{3,1},{4,6},{5,7},{6,2},{7,3},{8,12},{9,13},{10,... | collective-permute-start | bytes 1290248 | tf_op jit(solution)/shard_map/ppermute | solution.py:298
  50.6 0.0 collective-permute-start.22
  50.6 3.3 %update_second.1 = (f32[832,128]{1,0:T(8,128)S(1)}, f32[840,128]{1,0:T(8,128)S(1)}) custom-call(f32[128,512]{1,0:T(8,128)S(1)} %broadcast_select_fusion.refs_0_, f32[128,512]{1,0:T(8,128)S(1)} %collective-permute-done.7.refs_1_, f32[128,512]{1,0:T(8,128)S(1)} %collective-permute-done.8.refs_2_, f32[128,512]{1,0:T(8,128)S(1)} %collective-permute-done.9.refs_3_, ...), custom_call_target="tpu_custom_call" | custom-call | flops 1000 | bytes 1000 | tf_op jit(solution)/shard_map/update_second/pallas_call | solution.py:446
  53.9 4.1 %collective-permute-start.21 = (f32[840,128]{1,0:T(8,128)S(1)}, f32[840,128]{1,0:T(8,128)S(1)}, u32[]{:S(2)}, u32[]{:S(2)}) collective-permute-start(f32[840,128]{1,0:T(8,128)S(1)} %get-tuple-element.26.mine), channel_id=1, source_target_pairs={{6,4},{7,5},{14,12},{15,13},{22,20},{23,21},{30,28},{31,29},{0,2},... | collective-permute-start | bytes 1290248 | tf_op jit(solution)/shard_map/ppermute | solution.py:301
  58.0 0.0 collective-permute-done.19.theirs.got_1
  58.1 1.3 %collective-permute-start.23 = (f32[832,128]{1,0:T(8,128)S(1)}, f32[832,128]{1,0:T(8,128)S(1)}, u32[]{:S(2)}, u32[]{:S(2)}) collective-permute-start(f32[832,128]{1,0:T(8,128)S(1)} %join.1), channel_id=1, source_target_pairs={{4,0},{5,1},{12,8},{13,9},{20,16},{21,17},{28,24},{29,25},{2,6},{3... | collective-permute-start | bytes 1277960 | tf_op jit(solution)/shard_map/ppermute | solution.py:301
  59.4 4.7 %collective-permute-start.24 = (f32[64,128]{1,0:T(8,128)S(1)}, f32[64,128]{1,0:T(8,128)S(1)}, u32[]{:S(2)}, u32[]{:S(2)}) collective-permute-start(f32[64,128]{1,0:T(8,128)S(1)} %get-tuple-element.27), channel_id=1, source_target_pairs={{0,6},{1,7},{2,4},{3,5},{4,2},{5,3},{6,0},{7,1},{8,14},{9,15},{10,... | collective-permute-start | bytes 98312 | tf_op jit(solution)/shard_map/ppermute | solution.py:298
  64.0 16.7 %collective-permute-done.24.far = f32[64,128]{1,0:T(8,128)S(1)} collective-permute-done((f32[64,128]{1,0:T(8,128)S(1)}, f32[64,128]{1,0:T(8,128)S(1)}, u32[]{:S(2)}, u32[]{:S(2)}) %collective-permute-start.24) | collective-permute-done | bytes 32800 | tf_op jit(solution)/shard_map/ppermute | solution.py:298
  80.8 0.0 collective-permute-done.20.got_2
  80.8 0.0 collective-permute-done.22.got_4
  80.8 0.0 collective-permute-done.21.got_3
  80.8 0.3 collective-permute-done.23.joined
  81.1 0.0 copy-done
  81.1 1.0 %add_up.1 = (f32[4,64,128]{2,1,0:T(8,128)}, f32[6,128,128]{2,1,0:T(8,128)}) custom-call(f32[6,128,128]{2,1,0:T(8,128)S(1)} %bitcast.4, f32[832,128]{1,0:T(8,128)S(1)} %get-tuple-element.23.own, f32[832,128]{1,0:T(8,128)S(1)} %collective-permute-done.19.theirs.got_1, f32[840,128]{1,0:T(8,128)S(1)} %collective-permute-done.20.got_2, ...), custom_call_target="tpu_custom_call" | custom-call | flops 1000 | bytes 1000 | tf_op jit(solution)/shard_map/add_up/pallas_call | solution.py:487
  (2 shorter events, 0.1 us)
Async XLA Ops:
  1.9 20.3 %collective-permute-start.5 = (f32[512,512]{1,0:T(8,128)S(1)}, f32[512,512]{1,0:T(8,128)S(1)}, u32[]{:S(2)}, u32[]{:S(2)}) collective-permute-start(f32[512,512]{1,0:T(8,128)S(1)} %get-tuple-element.22.near), channel_id=1, source_target_pairs={{10,0},{11,1}} | collective-permute-start | bytes 3145736 | tf_op jit(solution)/shard_map/ppermute | solution.py:301
  3.2 19.0 %collective-permute-start.4 = (f32[512,512]{1,0:T(8,128)S(1)}, f32[512,512]{1,0:T(8,128)S(1)}, u32[]{:S(2)}, u32[]{:S(2)}) collective-permute-start(f32[512,512]{1,0:T(8,128)S(1)} %get-tuple-element.22.near), channel_id=1, source_target_pairs={{0,8},{1,0},{2,10},{3,11},{4,12},{5,13},{6,14},{7,15},{8,9},{9,1},... | collective-permute-start | bytes 3145736 | tf_op jit(solution)/shard_map/ppermute | solution.py:298
  3.3 6.7 %collective-permute-start = (f32[128,128]{1,0:T(8,128)S(1)}, f32[128,128]{1,0:T(8,128)S(1)}, u32[]{:S(2)}, u32[]{:S(2)}) collective-permute-start(f32[128,128]{1,0:T(8,128)S(1)} %get-tuple-element.16.own), channel_id=1, source_target_pairs={{0,2},{1,9},{2,0},{3,1},{4,28},{5,13},{6,14},{7,5},{8,24},{9,11},{... | collective-permute-start | bytes 196616 | tf_op jit(solution)/shard_map/ppermute | solution.py:298
  6.2 5.3 %collective-permute-start.1 = (f32[128,128]{1,0:T(8,128)S(1)}, f32[128,128]{1,0:T(8,128)S(1)}, u32[]{:S(2)}, u32[]{:S(2)}) collective-permute-start(f32[128,128]{1,0:T(8,128)S(1)} %get-tuple-element.16.own), channel_id=1, source_target_pairs={{0,4},{1,9},{2,10},{3,11},{4,0},{5,1},{6,14},{7,3},{8,12},{9,13},{... | collective-permute-start | bytes 196616 | tf_op jit(solution)/shard_map/ppermute | solution.py:298
  8.3 6.2 %collective-permute-start.2 = (f32[128,128]{1,0:T(8,128)S(1)}, f32[128,128]{1,0:T(8,128)S(1)}, u32[]{:S(2)}, u32[]{:S(2)}) collective-permute-start(f32[128,128]{1,0:T(8,128)S(1)} %get-tuple-element.16.own), channel_id=1, source_target_pairs={{0,6},{1,7},{2,10},{3,11},{4,28},{5,13},{6,0},{7,1},{8,24},{9,15},... | collective-permute-start | bytes 196616 | tf_op jit(solution)/shard_map/ppermute | solution.py:298
  15.0 8.1 %collective-permute-start.10 = (f32[512,512]{1,0:T(8,128)S(1)}, f32[512,512]{1,0:T(8,128)S(1)}, u32[]{:S(2)}, u32[]{:S(2)}) collective-permute-start(f32[512,512]{1,0:T(8,128)S(1)} %get-tuple-element.22.near), channel_id=1, source_target_pairs={{0,8},{1,9},{2,10},{3,11},{4,12},{5,13},{6,14},{7,15},{8,0},{9,1},... | collective-permute-start | bytes 3145736 | tf_op jit(solution)/shard_map/ppermute | solution.py:298
  15.1 12.0 %collective-permute-start.13 = (f32[512,512]{1,0:T(8,128)S(1)}, f32[512,512]{1,0:T(8,128)S(1)}, u32[]{:S(2)}, u32[]{:S(2)}) collective-permute-start(f32[512,512]{1,0:T(8,128)S(1)} %get-tuple-element.22.near), channel_id=1, source_target_pairs={{13,15}} | collective-permute-start | bytes 3145736 | tf_op jit(solution)/shard_map/ppermute | solution.py:301
  15.8 6.4 %collective-permute-start.3 = (f32[128,512]{1,0:T(8,128)S(1)}, f32[128,512]{1,0:T(8,128)S(1)}, u32[]{:S(2)}, u32[]{:S(2)}) collective-permute-start(f32[128,512]{1,0:T(8,128)S(1)} %turn.1.out.own), channel_id=1, source_target_pairs={{0,1},{1,0},{2,10},{3,11},{4,12},{5,13},{6,14},{7,4},{8,24},{9,25}... | collective-permute-start | bytes 786440 | tf_op jit(solution)/shard_map/ppermute | solution.py:298
  23.0 4.0 %collective-permute-start.6 = (f32[128,512]{1,0:T(8,128)S(1)}, f32[128,512]{1,0:T(8,128)S(1)}, u32[]{:S(2)}, u32[]{:S(2)}) collective-permute-start(f32[128,512]{1,0:T(8,128)S(1)} %get-tuple-element.21.s_b), channel_id=1, source_target_pairs={{0,2},{1,3},{2,10},{3,11},{4,12},{5,13},{6,14},{7,15},{8,0},{9,1},... | collective-permute-start | bytes 786440 | tf_op jit(solution)/shard_map/ppermute | solution.py:298
  24.6 5.3 %collective-permute-start.11 = (f32[128,512]{1,0:T(8,128)}, f32[128,512]{1,0:T(8,128)}, u32[]{:S(2)}, u32[]{:S(2)}) collective-permute-start(f32[128,512]{1,0:T(8,128)} %reduce_low.1), channel_id=1, source_target_pairs={{0,15},{1,9},{2,10},{3,11},{4,12},{5,13},{6,14},{7,8},{8,0},{9,1},... | collective-permute-start | bytes 786440 | tf_op jit(solution)/shard_map/ppermute | solution.py:298
  25.4 7.3 %collective-permute-start.12 = (f32[128,512]{1,0:T(8,128)}, f32[128,512]{1,0:T(8,128)}, u32[]{:S(2)}, u32[]{:S(2)}) collective-permute-start(f32[128,512]{1,0:T(8,128)} %reduce_low.1), channel_id=1, source_target_pairs={{0,12},{1,15},{2,10},{3,11},{4,8},{5,13},{6,14},{7,9},{8,0},{9,1},... | collective-permute-start | bytes 786440 | tf_op jit(solution)/shard_map/ppermute | solution.py:298
  27.0 7.8 %collective-permute-start.7 = (f32[128,512]{1,0:T(8,128)S(1)}, f32[128,512]{1,0:T(8,128)S(1)}, u32[]{:S(2)}, u32[]{:S(2)}) collective-permute-start(f32[128,512]{1,0:T(8,128)S(1)} %broadcast_select_fusion.refs_0_), channel_id=1, source_target_pairs={{0,16},{1,17},{2,18},{3,19},{4,12},{5,13},{6,14},{7,15},{8,0},{9,1... | collective-permute-start | bytes 786440 | tf_op jit(solution)/shard_map/ppermute | solution.py:298
  33.8 1.7 %collective-permute-start.14 = (f32[128,512]{1,0:T(8,128)S(1)}, f32[128,512]{1,0:T(8,128)S(1)}, u32[]{:S(2)}, u32[]{:S(2)}) collective-permute-start(f32[128,512]{1,0:T(8,128)S(1)} %solve_high.1.refs_4_), channel_id=1, source_target_pairs={{0,8},{1,9},{2,10},{3,11},{4,12},{5,13},{6,14},{7,15},{8,0},{9,1},... | collective-permute-start | bytes 786440 | tf_op jit(solution)/shard_map/ppermute | solution.py:298
  34.3 1.5 %collective-permute-start.15 = (f32[128,512]{1,0:T(8,128)S(1)}, f32[128,512]{1,0:T(8,128)S(1)}, u32[]{:S(2)}, u32[]{:S(2)}) collective-permute-start(f32[128,512]{1,0:T(8,128)S(1)} %solve_high.1.refs_4_), channel_id=1, source_target_pairs={{0,8},{1,9},{2,10},{3,11},{4,12},{5,4},{6,7},{7,15},{8,0},{9,1},{1... | collective-permute-start | bytes 786440 | tf_op jit(solution)/shard_map/ppermute | solution.py:298
  34.3 1.9 %collective-permute-start.16 = (f32[128,512]{1,0:T(8,128)S(1)}, f32[128,512]{1,0:T(8,128)S(1)}, u32[]{:S(2)}, u32[]{:S(2)}) collective-permute-start(f32[128,512]{1,0:T(8,128)S(1)} %solve_high.1.refs_4_), channel_id=1, source_target_pairs={{0,8},{1,9},{2,10},{3,11},{4,12},{5,13},{6,14},{7,15},{8,0},{9,1},... | collective-permute-start | bytes 786440 | tf_op jit(solution)/shard_map/ppermute | solution.py:298
  34.8 1.9 %collective-permute-start.8 = (f32[128,512]{1,0:T(8,128)S(1)}, f32[128,512]{1,0:T(8,128)S(1)}, u32[]{:S(2)}, u32[]{:S(2)}) collective-permute-start(f32[128,512]{1,0:T(8,128)S(1)} %broadcast_select_fusion.refs_0_), channel_id=1, source_target_pairs={{0,8},{1,9},{2,10},{3,11},{4,12},{5,13},{6,14},{7,15},{8,0},{9,1},... | collective-permute-start | bytes 786440 | tf_op jit(solution)/shard_map/ppermute | solution.py:298
  34.8 2.1 %collective-permute-start.17 = (f32[128,512]{1,0:T(8,128)S(1)}, f32[128,512]{1,0:T(8,128)S(1)}, u32[]{:S(2)}, u32[]{:S(2)}) collective-permute-start(f32[128,512]{1,0:T(8,128)S(1)} %solve_high.1.refs_4_), channel_id=1, source_target_pairs={{0,8},{1,9},{2,10},{3,11},{4,12},{5,13},{6,14},{7,15},{8,0},{9,1},... | collective-permute-start | bytes 786440 | tf_op jit(solution)/shard_map/ppermute | solution.py:298
  35.4 1.9 %collective-permute-start.9 = (f32[128,512]{1,0:T(8,128)S(1)}, f32[128,512]{1,0:T(8,128)S(1)}, u32[]{:S(2)}, u32[]{:S(2)}) collective-permute-start(f32[128,512]{1,0:T(8,128)S(1)} %collective-permute-done.7.refs_1_), channel_id=1, source_target_pairs={{0,8},{1,9},{2,10},{3,11},{4,12},{5,13},{6,14},{7,15},{8,0},{9,1},... | collective-permute-start | bytes 786440 | tf_op jit(solution)/shard_map/ppermute | solution.py:298
  36.2 1.6 %collective-permute-start.18 = (f32[128,512]{1,0:T(8,128)S(1)}, f32[128,512]{1,0:T(8,128)S(1)}, u32[]{:S(2)}, u32[]{:S(2)}) collective-permute-start(f32[128,512]{1,0:T(8,128)S(1)} %select_select_fusion.refs_5_), channel_id=1, source_target_pairs={{0,8},{1,9},{2,10},{3,11},{4,12},{5,13},{6,14},{7,15},{8,0},{9,1},... | collective-permute-start | bytes 786440 | tf_op jit(solution)/shard_map/ppermute | solution.py:298
  41.1 40.0 %copy-start = (f32[6,1,1,128,128]{4,3,2,1,0:T(8,128)S(1)}, f32[6,1,1,128,128]{4,3,2,1,0:T(8,128)}, u32[]{:S(2)}) copy-start(f32[6,1,1,128,128]{4,3,2,1,0:T(8,128)} %rhs.1) | copy-start | bytes 1179652
  41.1 16.9 %collective-permute-start.19 = (f32[832,128]{1,0:T(8,128)S(1)}, f32[832,128]{1,0:T(8,128)S(1)}, u32[]{:S(2)}, u32[]{:S(2)}) collective-permute-start(f32[832,128]{1,0:T(8,128)S(1)} %get-tuple-element.24), channel_id=1, source_target_pairs={{0,2},{1,3},{2,0},{3,1},{4,6},{5,7},{6,4},{7,5},{8,10},{9,11},{10,... | collective-permute-start | bytes 1277960 | tf_op jit(solution)/shard_map/ppermute | solution.py:298
  41.2 39.6 %collective-permute-start.20 = (f32[840,128]{1,0:T(8,128)S(1)}, f32[840,128]{1,0:T(8,128)S(1)}, u32[]{:S(2)}, u32[]{:S(2)}) collective-permute-start(f32[840,128]{1,0:T(8,128)S(1)} %get-tuple-element.25), channel_id=1, source_target_pairs={{0,4},{1,5},{2,0},{3,1},{4,6},{5,7},{6,2},{7,3},{8,12},{9,13},{10,... | collective-permute-start | bytes 1290248 | tf_op jit(solution)/shard_map/ppermute | solution.py:298
  50.6 30.2 %collective-permute-start.22 = (f32[840,128]{1,0:T(8,128)S(1)}, f32[840,128]{1,0:T(8,128)S(1)}, u32[]{:S(2)}, u32[]{:S(2)}) collective-permute-start(f32[840,128]{1,0:T(8,128)S(1)} %get-tuple-element.25), channel_id=1, source_target_pairs={{0,8},{1,9},{2,4},{3,5},{4,2},{5,3},{6,14},{7,15},{8,0},{9,1},{10,... | collective-permute-start | bytes 1290248 | tf_op jit(solution)/shard_map/ppermute | solution.py:298
  53.9 26.9 %collective-permute-start.21 = (f32[840,128]{1,0:T(8,128)S(1)}, f32[840,128]{1,0:T(8,128)S(1)}, u32[]{:S(2)}, u32[]{:S(2)}) collective-permute-start(f32[840,128]{1,0:T(8,128)S(1)} %get-tuple-element.26.mine), channel_id=1, source_target_pairs={{6,4},{7,5},{14,12},{15,13},{22,20},{23,21},{30,28},{31,29},{0,2},... | collective-permute-start | bytes 1290248 | tf_op jit(solution)/shard_map/ppermute | solution.py:301
  58.1 23.1 %collective-permute-start.23 = (f32[832,128]{1,0:T(8,128)S(1)}, f32[832,128]{1,0:T(8,128)S(1)}, u32[]{:S(2)}, u32[]{:S(2)}) collective-permute-start(f32[832,128]{1,0:T(8,128)S(1)} %join.1), channel_id=1, source_target_pairs={{4,0},{5,1},{12,8},{13,9},{20,16},{21,17},{28,24},{29,25},{2,6},{3... | collective-permute-start | bytes 1277960 | tf_op jit(solution)/shard_map/ppermute | solution.py:301
  59.4 21.4 %collective-permute-start.24 = (f32[64,128]{1,0:T(8,128)S(1)}, f32[64,128]{1,0:T(8,128)S(1)}, u32[]{:S(2)}, u32[]{:S(2)}) collective-permute-start(f32[64,128]{1,0:T(8,128)S(1)} %get-tuple-element.27), channel_id=1, source_target_pairs={{0,6},{1,7},{2,4},{3,5},{4,2},{5,3},{6,0},{7,1},{8,14},{9,15},{10,... | collective-permute-start | bytes 98312 | tf_op jit(solution)/shard_map/ppermute | solution.py:298

commit v15 on v14

--- a/solution.py
+++ b/solution.py
@@ -344,7 +344,7 @@
     la = send(near, [(line(1, 0), low_homes[0])])
     ly = send_some(near, [(line(2, 1), low_homes[0]), (line(3, 1), low_homes[1])])
 
-    vector = jax.ShapeDtypeStruct((nrhs, width), F32)
+    vector = VMEM((nrhs, width), F32)
     order = ((low_homes[1], (0, 1, 2, 3)), (high_homes[0], (2, 1, 0, 3)), (high_homes[1], (3, 2, 1, 0)))
     turned = pl.pallas_call(
         functools.partial(turn_kernel, order, low_homes[0], col_count),

time: 82.4 us -> 82.4 us (level)
  no operation moved by 1% of the time
where the time goes in v15:
time: 82.4 us; the launch traced here: 82.1 us
  waiting for transfers between devices  35.9 us (44%)
  starting transfers between devices  31 us (38%)
  Pallas kernels  14.3 us (17%)
  between operations  0.84 us (1%)
    ppermute x21, waiting for transfers between devices, send(): return lax.ppermute(x, AXES, sorted(onward.items()))  35.6 us
    ppermute x21, starting transfers between devices, send(): return lax.ppermute(x, AXES, sorted(onward.items()))  23.5 us
    ppermute x4, starting transfers between devices, send_some(): return lax.ppermute(x, AXES, pairs)  7.44 us
    pallas_call x2, Pallas kernels, update(): pl.pallas_call(functools.partial(update_kernel, (groups, row_count, share...  6.55 us
    pallas_call x1, Pallas kernels, on_device(): pl.pallas_call(functools.partial(ready_kernel, low_homes, col_count), in_...  1.69 us
  transfers between devices with their start and end apart: 25, of which 13 were waited for; matrix products, arithmetic and copies ran while one was open for 0% of the time, Pallas kernels for 11%

profile of v15, /device:TPU:0, one launch (start us, length us, event | category | flops | bytes accessed | tf_op | source)
XLA Modules:
  0.0 82.1 jit_solution(5784749158654175489)
XLA Ops:
  0.6 1.3 %fetch.1 = (f32[512,512]{1,0:T(8,128)S(1)}, f32[128,128]{1,0:T(8,128)S(1)}) custom-call(f32[6,1,1,512,512]{4,3,2,1,0:T(8,128)} %refs_8_.3, f32[6,1,1,128,128]{4,3,2,1,0:T(8,128)} %rhs.1), custom_call_target="tpu_custom_call" | custom-call | flops 1000 | bytes 1000 | tf_op jit(solution)/shard_map/fetch/pallas_call | solution.py:314
  1.9 1.3 %collective-permute-start.5 = (f32[512,512]{1,0:T(8,128)S(1)}, f32[512,512]{1,0:T(8,128)S(1)}, u32[]{:S(2)}, u32[]{:S(2)}) collective-permute-start(f32[512,512]{1,0:T(8,128)S(1)} %get-tuple-element.22.near), channel_id=1, source_target_pairs={{10,0},{11,1}} | collective-permute-start | bytes 3145736 | tf_op jit(solution)/shard_map/ppermute | solution.py:301
  3.2 0.1 collective-permute-start.4
  3.3 2.9 %collective-permute-start = (f32[128,128]{1,0:T(8,128)S(1)}, f32[128,128]{1,0:T(8,128)S(1)}, u32[]{:S(2)}, u32[]{:S(2)}) collective-permute-start(f32[128,128]{1,0:T(8,128)S(1)} %get-tuple-element.16.own), channel_id=1, source_target_pairs={{0,2},{1,9},{2,0},{3,1},{4,28},{5,13},{6,14},{7,5},{8,24},{9,11},{... | collective-permute-start | bytes 196616 | tf_op jit(solution)/shard_map/ppermute | solution.py:298
  6.2 2.1 %collective-permute-start.1 = (f32[128,128]{1,0:T(8,128)S(1)}, f32[128,128]{1,0:T(8,128)S(1)}, u32[]{:S(2)}, u32[]{:S(2)}) collective-permute-start(f32[128,128]{1,0:T(8,128)S(1)} %get-tuple-element.16.own), channel_id=1, source_target_pairs={{0,4},{1,9},{2,10},{3,11},{4,0},{5,1},{6,14},{7,3},{8,12},{9,13},{... | collective-permute-start | bytes 196616 | tf_op jit(solution)/shard_map/ppermute | solution.py:298
  8.3 0.0 collective-permute-start.2
  8.3 1.7 %ready.1 = (bf16[2,512,512]{2,1,0:T(8,128)(2,1)S(1)}, bf16[2,512,512]{2,1,0:T(8,128)(2,1)S(1)}) custom-call(f32[4,512,512]{2,1,0:T(8,128)} %inverses.3), custom_call_target="tpu_custom_call" | custom-call | flops 1000 | bytes 1000 | tf_op jit(solution)/shard_map/ready/pallas_call | solution.py:326
  10.0 0.0 collective-permute-done.g1
  10.1 1.4 %collective-permute-done.1.g2 = f32[128,128]{1,0:T(8,128)S(1)} collective-permute-done((f32[128,128]{1,0:T(8,128)S(1)}, f32[128,128]{1,0:T(8,128)S(1)}, u32[]{:S(2)}, u32[]{:S(2)}) %collective-permute-start.1) | collective-permute-done | bytes 65568 | tf_op jit(solution)/shard_map/ppermute | solution.py:298
  11.5 3.0 %collective-permute-done.2.g3 = f32[128,128]{1,0:T(8,128)S(1)} collective-permute-done((f32[128,128]{1,0:T(8,128)S(1)}, f32[128,128]{1,0:T(8,128)S(1)}, u32[]{:S(2)}, u32[]{:S(2)}) %collective-permute-start.2) | collective-permute-done | bytes 65568 | tf_op jit(solution)/shard_map/ppermute | solution.py:298
  14.5 0.5 turn.1.out.own
  15.0 0.1 collective-permute-start.10
  15.1 0.7 collective-permute-start.13
  15.8 0.9 %collective-permute-start.3 = (f32[128,512]{1,0:T(8,128)S(1)}, f32[128,512]{1,0:T(8,128)S(1)}, u32[]{:S(2)}, u32[]{:S(2)}) collective-permute-start(f32[128,512]{1,0:T(8,128)S(1)} %turn.1.out.own), channel_id=1, source_target_pairs={{0,1},{1,0},{2,10},{3,11},{4,12},{5,13},{6,14},{7,4},{8,24},{9,25}... | collective-permute-start | bytes 786440 | tf_op jit(solution)/shard_map/ppermute | solution.py:298
  16.7 5.5 %collective-permute-done.3.swapped = f32[128,512]{1,0:T(8,128)S(1)} collective-permute-done((f32[128,512]{1,0:T(8,128)S(1)}, f32[128,512]{1,0:T(8,128)S(1)}, u32[]{:S(2)}, u32[]{:S(2)}) %collective-permute-start.3) | collective-permute-done | bytes 262176 | tf_op jit(solution)/shard_map/ppermute | solution.py:298
  22.2 0.0 collective-permute-done.5.ly
  22.2 0.0 collective-permute-done.4.la
  22.2 0.7 solve_low.1
  23.0 0.1 collective-permute-start.6
  23.1 0.0 collective-permute-done.10.lx
  23.1 1.5 %reduce_low.1 = f32[128,512]{1,0:T(8,128)} custom-call(f32[128,512]{1,0:T(8,128)S(1)} %get-tuple-element.20.s_a, f32[128,512]{1,0:T(8,128)S(1)} %get-tuple-element.21.s_b, f32[512,512]{1,0:T(8,128)S(1)} %collective-permute-done.10.lx, f32[512,512]{1,0:T(8,128)S(1)} %collective-permute-done.5.ly), custom_call_target="tpu_custom_call" | custom-call | flops 1000 | bytes 1000 | tf_op jit(solution)/shard_map/reduce_low/pallas_call | solution.py:371
  24.6 0.8 collective-permute-start.11
  25.4 0.0 collective-permute-start.12
  25.4 1.6 %collective-permute-done.6 = f32[128,512]{1,0:T(8,128)S(1)} collective-permute-done((f32[128,512]{1,0:T(8,128)S(1)}, f32[128,512]{1,0:T(8,128)S(1)}, u32[]{:S(2)}, u32[]{:S(2)}) %collective-permute-start.6) | collective-permute-done | bytes 262176 | tf_op jit(solution)/shard_map/ppermute | solution.py:298
  27.0 0.1 collective-permute-start.7
  27.1 0.0 collective-permute-done.13.last_block
  27.1 2.8 %collective-permute-done.11.w_1 = f32[128,512]{1,0:T(8,128)} collective-permute-done((f32[128,512]{1,0:T(8,128)}, f32[128,512]{1,0:T(8,128)}, u32[]{:S(2)}, u32[]{:S(2)}) %collective-permute-start.11) | collective-permute-done | bytes 262176 | tf_op jit(solution)/shard_map/ppermute | solution.py:298
  29.9 2.8 %collective-permute-done.12.w_2 = f32[128,512]{1,0:T(8,128)} collective-permute-done((f32[128,512]{1,0:T(8,128)}, f32[128,512]{1,0:T(8,128)}, u32[]{:S(2)}, u32[]{:S(2)}) %collective-permute-start.12) | collective-permute-done | bytes 262176 | tf_op jit(solution)/shard_map/ppermute | solution.py:298
  32.7 1.1 %solve_high.1.refs_4_ = f32[128,512]{1,0:T(8,128)S(1)} custom-call(f32[128,512]{1,0:T(8,128)S(1)} %turn.1.out.own, f32[128,512]{1,0:T(8,128)S(1)} %collective-permute-done.3.swapped, f32[128,512]{1,0:T(8,128)} %collective-permute-done.11.w_1, f32[128,512]{1,0:T(8,128)} %collective-permute-done.12.w_2, f32[4,512,512]{2,1,0:T(8,128)} %inverses.3, ...), custom_call_target="tpu_custom_call" | custom-call | flops 1000 | bytes 1000 | tf_op jit(solution)/shard_map/solve_high/pallas_call | solution.py:384
  33.8 0.5 collective-permute-start.14
  34.3 0.1 collective-permute-start.15
  34.3 0.5 collective-permute-start.16
  34.8 0.1 collective-permute-start.8
  34.8 0.0 collective-permute-done.7.refs_1_
  34.8 0.5 collective-permute-start.17
  35.3 0.1 collective-permute-done.14
  35.4 0.4 collective-permute-start.9
  35.8 0.0 collective-permute-done.15
  35.8 0.4 collective-permute-done.16
  36.2 0.1 select_select_fusion.refs_5_
  36.2 0.4 collective-permute-start.18
  36.7 0.0 collective-permute-done.8.refs_2_
  36.7 0.2 collective-permute-done.17.refs_6_
  36.9 0.4 collective-permute-done.9.refs_3_
  37.3 0.5 collective-permute-done.18.refs_7_
  37.9 3.3 %update_first.1 = (f32[832,128]{1,0:T(8,128)S(1)}, f32[840,128]{1,0:T(8,128)S(1)}, f32[64,128]{1,0:T(8,128)S(1)}) custom-call(f32[128,512]{1,0:T(8,128)S(1)} %broadcast_select_fusion.refs_0_, f32[128,512]{1,0:T(8,128)S(1)} %collective-permute-done.7.refs_1_, f32[128,512]{1,0:T(8,128)S(1)} %collective-permute-done.8.refs_2_, ...), custom_call_target="tpu_custom_call" | custom-call | flops 1000 | bytes 1000 | tf_op jit(solution)/shard_map/update_first/pallas_call | solution.py:446
  41.1 0.0 copy-start
  41.1 0.1 collective-permute-start.19
  41.2 9.4 %collective-permute-start.20 = (f32[840,128]{1,0:T(8,128)S(1)}, f32[840,128]{1,0:T(8,128)S(1)}, u32[]{:S(2)}, u32[]{:S(2)}) collective-permute-start(f32[840,128]{1,0:T(8,128)S(1)} %get-tuple-element.25), channel_id=1, source_target_pairs={{0,4},{1,5},{2,0},{3,1},{4,6},{5,7},{6,2},{7,3},{8,12},{9,13},{10,... | collective-permute-start | bytes 1290248 | tf_op jit(solution)/shard_map/ppermute | solution.py:298
  50.6 0.0 collective-permute-start.22
  50.6 3.3 %update_second.1 = (f32[832,128]{1,0:T(8,128)S(1)}, f32[840,128]{1,0:T(8,128)S(1)}) custom-call(f32[128,512]{1,0:T(8,128)S(1)} %broadcast_select_fusion.refs_0_, f32[128,512]{1,0:T(8,128)S(1)} %collective-permute-done.7.refs_1_, f32[128,512]{1,0:T(8,128)S(1)} %collective-permute-done.8.refs_2_, f32[128,512]{1,0:T(8,128)S(1)} %collective-permute-done.9.refs_3_, ...), custom_call_target="tpu_custom_call" | custom-call | flops 1000 | bytes 1000 | tf_op jit(solution)/shard_map/update_second/pallas_call | solution.py:446
  53.9 4.1 %collective-permute-start.21 = (f32[840,128]{1,0:T(8,128)S(1)}, f32[840,128]{1,0:T(8,128)S(1)}, u32[]{:S(2)}, u32[]{:S(2)}) collective-permute-start(f32[840,128]{1,0:T(8,128)S(1)} %get-tuple-element.26.mine), channel_id=1, source_target_pairs={{6,4},{7,5},{14,12},{15,13},{22,20},{23,21},{30,28},{31,29},{0,2},... | collective-permute-start | bytes 1290248 | tf_op jit(solution)/shard_map/ppermute | solution.py:301
  58.0 0.0 collective-permute-done.19.theirs.got_1
  58.1 1.3 %collective-permute-start.23 = (f32[832,128]{1,0:T(8,128)S(1)}, f32[832,128]{1,0:T(8,128)S(1)}, u32[]{:S(2)}, u32[]{:S(2)}) collective-permute-start(f32[832,128]{1,0:T(8,128)S(1)} %join.1), channel_id=1, source_target_pairs={{4,0},{5,1},{12,8},{13,9},{20,16},{21,17},{28,24},{29,25},{2,6},{3... | collective-permute-start | bytes 1277960 | tf_op jit(solution)/shard_map/ppermute | solution.py:301
  59.4 4.7 %collective-permute-start.24 = (f32[64,128]{1,0:T(8,128)S(1)}, f32[64,128]{1,0:T(8,128)S(1)}, u32[]{:S(2)}, u32[]{:S(2)}) collective-permute-start(f32[64,128]{1,0:T(8,128)S(1)} %get-tuple-element.27), channel_id=1, source_target_pairs={{0,6},{1,7},{2,4},{3,5},{4,2},{5,3},{6,0},{7,1},{8,14},{9,15},{10,... | collective-permute-start | bytes 98312 | tf_op jit(solution)/shard_map/ppermute | solution.py:298
  64.0 16.7 %collective-permute-done.24.far = f32[64,128]{1,0:T(8,128)S(1)} collective-permute-done((f32[64,128]{1,0:T(8,128)S(1)}, f32[64,128]{1,0:T(8,128)S(1)}, u32[]{:S(2)}, u32[]{:S(2)}) %collective-permute-start.24) | collective-permute-done | bytes 32800 | tf_op jit(solution)/shard_map/ppermute | solution.py:298
  80.8 0.0 collective-permute-done.20.got_2
  80.8 0.0 collective-permute-done.22.got_4
  80.8 0.0 collective-permute-done.21.got_3
  80.8 0.3 collective-permute-done.23.joined
  81.1 0.0 copy-done
  81.1 1.0 %add_up.1 = (f32[4,64,128]{2,1,0:T(8,128)}, f32[6,128,128]{2,1,0:T(8,128)}) custom-call(f32[6,128,128]{2,1,0:T(8,128)S(1)} %bitcast.4, f32[832,128]{1,0:T(8,128)S(1)} %get-tuple-element.23.own, f32[832,128]{1,0:T(8,128)S(1)} %collective-permute-done.19.theirs.got_1, f32[840,128]{1,0:T(8,128)S(1)} %collective-permute-done.20.got_2, ...), custom_call_target="tpu_custom_call" | custom-call | flops 1000 | bytes 1000 | tf_op jit(solution)/shard_map/add_up/pallas_call | solution.py:487
  (2 shorter events, 0.1 us)
Async XLA Ops:
  1.9 20.3 %collective-permute-start.5 = (f32[512,512]{1,0:T(8,128)S(1)}, f32[512,512]{1,0:T(8,128)S(1)}, u32[]{:S(2)}, u32[]{:S(2)}) collective-permute-start(f32[512,512]{1,0:T(8,128)S(1)} %get-tuple-element.22.near), channel_id=1, source_target_pairs={{10,0},{11,1}} | collective-permute-start | bytes 3145736 | tf_op jit(solution)/shard_map/ppermute | solution.py:301
  3.2 19.0 %collective-permute-start.4 = (f32[512,512]{1,0:T(8,128)S(1)}, f32[512,512]{1,0:T(8,128)S(1)}, u32[]{:S(2)}, u32[]{:S(2)}) collective-permute-start(f32[512,512]{1,0:T(8,128)S(1)} %get-tuple-element.22.near), channel_id=1, source_target_pairs={{0,8},{1,0},{2,10},{3,11},{4,12},{5,13},{6,14},{7,15},{8,9},{9,1},... | collective-permute-start | bytes 3145736 | tf_op jit(solution)/shard_map/ppermute | solution.py:298
  3.3 6.7 %collective-permute-start = (f32[128,128]{1,0:T(8,128)S(1)}, f32[128,128]{1,0:T(8,128)S(1)}, u32[]{:S(2)}, u32[]{:S(2)}) collective-permute-start(f32[128,128]{1,0:T(8,128)S(1)} %get-tuple-element.16.own), channel_id=1, source_target_pairs={{0,2},{1,9},{2,0},{3,1},{4,28},{5,13},{6,14},{7,5},{8,24},{9,11},{... | collective-permute-start | bytes 196616 | tf_op jit(solution)/shard_map/ppermute | solution.py:298
  6.2 5.3 %collective-permute-start.1 = (f32[128,128]{1,0:T(8,128)S(1)}, f32[128,128]{1,0:T(8,128)S(1)}, u32[]{:S(2)}, u32[]{:S(2)}) collective-permute-start(f32[128,128]{1,0:T(8,128)S(1)} %get-tuple-element.16.own), channel_id=1, source_target_pairs={{0,4},{1,9},{2,10},{3,11},{4,0},{5,1},{6,14},{7,3},{8,12},{9,13},{... | collective-permute-start | bytes 196616 | tf_op jit(solution)/shard_map/ppermute | solution.py:298
  8.3 6.2 %collective-permute-start.2 = (f32[128,128]{1,0:T(8,128)S(1)}, f32[128,128]{1,0:T(8,128)S(1)}, u32[]{:S(2)}, u32[]{:S(2)}) collective-permute-start(f32[128,128]{1,0:T(8,128)S(1)} %get-tuple-element.16.own), channel_id=1, source_target_pairs={{0,6},{1,7},{2,10},{3,11},{4,28},{5,13},{6,0},{7,1},{8,24},{9,15},... | collective-permute-start | bytes 196616 | tf_op jit(solution)/shard_map/ppermute | solution.py:298
  15.0 8.1 %collective-permute-start.10 = (f32[512,512]{1,0:T(8,128)S(1)}, f32[512,512]{1,0:T(8,128)S(1)}, u32[]{:S(2)}, u32[]{:S(2)}) collective-permute-start(f32[512,512]{1,0:T(8,128)S(1)} %get-tuple-element.22.near), channel_id=1, source_target_pairs={{0,8},{1,9},{2,10},{3,11},{4,12},{5,13},{6,14},{7,15},{8,0},{9,1},... | collective-permute-start | bytes 3145736 | tf_op jit(solution)/shard_map/ppermute | solution.py:298
  15.1 12.0 %collective-permute-start.13 = (f32[512,512]{1,0:T(8,128)S(1)}, f32[512,512]{1,0:T(8,128)S(1)}, u32[]{:S(2)}, u32[]{:S(2)}) collective-permute-start(f32[512,512]{1,0:T(8,128)S(1)} %get-tuple-element.22.near), channel_id=1, source_target_pairs={{13,15}} | collective-permute-start | bytes 3145736 | tf_op jit(solution)/shard_map/ppermute | solution.py:301
  15.8 6.4 %collective-permute-start.3 = (f32[128,512]{1,0:T(8,128)S(1)}, f32[128,512]{1,0:T(8,128)S(1)}, u32[]{:S(2)}, u32[]{:S(2)}) collective-permute-start(f32[128,512]{1,0:T(8,128)S(1)} %turn.1.out.own), channel_id=1, source_target_pairs={{0,1},{1,0},{2,10},{3,11},{4,12},{5,13},{6,14},{7,4},{8,24},{9,25}... | collective-permute-start | bytes 786440 | tf_op jit(solution)/shard_map/ppermute | solution.py:298
  23.0 4.0 %collective-permute-start.6 = (f32[128,512]{1,0:T(8,128)S(1)}, f32[128,512]{1,0:T(8,128)S(1)}, u32[]{:S(2)}, u32[]{:S(2)}) collective-permute-start(f32[128,512]{1,0:T(8,128)S(1)} %get-tuple-element.21.s_b), channel_id=1, source_target_pairs={{0,2},{1,3},{2,10},{3,11},{4,12},{5,13},{6,14},{7,15},{8,0},{9,1},... | collective-permute-start | bytes 786440 | tf_op jit(solution)/shard_map/ppermute | solution.py:298
  24.6 5.3 %collective-permute-start.11 = (f32[128,512]{1,0:T(8,128)}, f32[128,512]{1,0:T(8,128)}, u32[]{:S(2)}, u32[]{:S(2)}) collective-permute-start(f32[128,512]{1,0:T(8,128)} %reduce_low.1), channel_id=1, source_target_pairs={{0,15},{1,9},{2,10},{3,11},{4,12},{5,13},{6,14},{7,8},{8,0},{9,1},... | collective-permute-start | bytes 786440 | tf_op jit(solution)/shard_map/ppermute | solution.py:298
  25.4 7.3 %collective-permute-start.12 = (f32[128,512]{1,0:T(8,128)}, f32[128,512]{1,0:T(8,128)}, u32[]{:S(2)}, u32[]{:S(2)}) collective-permute-start(f32[128,512]{1,0:T(8,128)} %reduce_low.1), channel_id=1, source_target_pairs={{0,12},{1,15},{2,10},{3,11},{4,8},{5,13},{6,14},{7,9},{8,0},{9,1},... | collective-permute-start | bytes 786440 | tf_op jit(solution)/shard_map/ppermute | solution.py:298
  27.0 7.8 %collective-permute-start.7 = (f32[128,512]{1,0:T(8,128)S(1)}, f32[128,512]{1,0:T(8,128)S(1)}, u32[]{:S(2)}, u32[]{:S(2)}) collective-permute-start(f32[128,512]{1,0:T(8,128)S(1)} %broadcast_select_fusion.refs_0_), channel_id=1, source_target_pairs={{0,16},{1,17},{2,18},{3,19},{4,12},{5,13},{6,14},{7,15},{8,0},{9,1... | collective-permute-start | bytes 786440 | tf_op jit(solution)/shard_map/ppermute | solution.py:298
  33.8 1.7 %collective-permute-start.14 = (f32[128,512]{1,0:T(8,128)S(1)}, f32[128,512]{1,0:T(8,128)S(1)}, u32[]{:S(2)}, u32[]{:S(2)}) collective-permute-start(f32[128,512]{1,0:T(8,128)S(1)} %solve_high.1.refs_4_), channel_id=1, source_target_pairs={{0,8},{1,9},{2,10},{3,11},{4,12},{5,13},{6,14},{7,15},{8,0},{9,1},... | collective-permute-start | bytes 786440 | tf_op jit(solution)/shard_map/ppermute | solution.py:298
  34.3 1.5 %collective-permute-start.15 = (f32[128,512]{1,0:T(8,128)S(1)}, f32[128,512]{1,0:T(8,128)S(1)}, u32[]{:S(2)}, u32[]{:S(2)}) collective-permute-start(f32[128,512]{1,0:T(8,128)S(1)} %solve_high.1.refs_4_), channel_id=1, source_target_pairs={{0,8},{1,9},{2,10},{3,11},{4,12},{5,4},{6,7},{7,15},{8,0},{9,1},{1... | collective-permute-start | bytes 786440 | tf_op jit(solution)/shard_map/ppermute | solution.py:298
  34.3 1.9 %collective-permute-start.16 = (f32[128,512]{1,0:T(8,128)S(1)}, f32[128,512]{1,0:T(8,128)S(1)}, u32[]{:S(2)}, u32[]{:S(2)}) collective-permute-start(f32[128,512]{1,0:T(8,128)S(1)} %solve_high.1.refs_4_), channel_id=1, source_target_pairs={{0,8},{1,9},{2,10},{3,11},{4,12},{5,13},{6,14},{7,15},{8,0},{9,1},... | collective-permute-start | bytes 786440 | tf_op jit(solution)/shard_map/ppermute | solution.py:298
  34.8 1.9 %collective-permute-start.8 = (f32[128,512]{1,0:T(8,128)S(1)}, f32[128,512]{1,0:T(8,128)S(1)}, u32[]{:S(2)}, u32[]{:S(2)}) collective-permute-start(f32[128,512]{1,0:T(8,128)S(1)} %broadcast_select_fusion.refs_0_), channel_id=1, source_target_pairs={{0,8},{1,9},{2,10},{3,11},{4,12},{5,13},{6,14},{7,15},{8,0},{9,1},... | collective-permute-start | bytes 786440 | tf_op jit(solution)/shard_map/ppermute | solution.py:298
  34.8 2.1 %collective-permute-start.17 = (f32[128,512]{1,0:T(8,128)S(1)}, f32[128,512]{1,0:T(8,128)S(1)}, u32[]{:S(2)}, u32[]{:S(2)}) collective-permute-start(f32[128,512]{1,0:T(8,128)S(1)} %solve_high.1.refs_4_), channel_id=1, source_target_pairs={{0,8},{1,9},{2,10},{3,11},{4,12},{5,13},{6,14},{7,15},{8,0},{9,1},... | collective-permute-start | bytes 786440 | tf_op jit(solution)/shard_map/ppermute | solution.py:298
  35.4 1.9 %collective-permute-start.9 = (f32[128,512]{1,0:T(8,128)S(1)}, f32[128,512]{1,0:T(8,128)S(1)}, u32[]{:S(2)}, u32[]{:S(2)}) collective-permute-start(f32[128,512]{1,0:T(8,128)S(1)} %collective-permute-done.7.refs_1_), channel_id=1, source_target_pairs={{0,8},{1,9},{2,10},{3,11},{4,12},{5,13},{6,14},{7,15},{8,0},{9,1},... | collective-permute-start | bytes 786440 | tf_op jit(solution)/shard_map/ppermute | solution.py:298
  36.2 1.6 %collective-permute-start.18 = (f32[128,512]{1,0:T(8,128)S(1)}, f32[128,512]{1,0:T(8,128)S(1)}, u32[]{:S(2)}, u32[]{:S(2)}) collective-permute-start(f32[128,512]{1,0:T(8,128)S(1)} %select_select_fusion.refs_5_), channel_id=1, source_target_pairs={{0,8},{1,9},{2,10},{3,11},{4,12},{5,13},{6,14},{7,15},{8,0},{9,1},... | collective-permute-start | bytes 786440 | tf_op jit(solution)/shard_map/ppermute | solution.py:298
  41.1 40.0 %copy-start = (f32[6,1,1,128,128]{4,3,2,1,0:T(8,128)S(1)}, f32[6,1,1,128,128]{4,3,2,1,0:T(8,128)}, u32[]{:S(2)}) copy-start(f32[6,1,1,128,128]{4,3,2,1,0:T(8,128)} %rhs.1) | copy-start | bytes 1179652
  41.1 16.9 %collective-permute-start.19 = (f32[832,128]{1,0:T(8,128)S(1)}, f32[832,128]{1,0:T(8,128)S(1)}, u32[]{:S(2)}, u32[]{:S(2)}) collective-permute-start(f32[832,128]{1,0:T(8,128)S(1)} %get-tuple-element.24), channel_id=1, source_target_pairs={{0,2},{1,3},{2,0},{3,1},{4,6},{5,7},{6,4},{7,5},{8,10},{9,11},{10,... | collective-permute-start | bytes 1277960 | tf_op jit(solution)/shard_map/ppermute | solution.py:298
  41.2 39.6 %collective-permute-start.20 = (f32[840,128]{1,0:T(8,128)S(1)}, f32[840,128]{1,0:T(8,128)S(1)}, u32[]{:S(2)}, u32[]{:S(2)}) collective-permute-start(f32[840,128]{1,0:T(8,128)S(1)} %get-tuple-element.25), channel_id=1, source_target_pairs={{0,4},{1,5},{2,0},{3,1},{4,6},{5,7},{6,2},{7,3},{8,12},{9,13},{10,... | collective-permute-start | bytes 1290248 | tf_op jit(solution)/shard_map/ppermute | solution.py:298
  50.6 30.2 %collective-permute-start.22 = (f32[840,128]{1,0:T(8,128)S(1)}, f32[840,128]{1,0:T(8,128)S(1)}, u32[]{:S(2)}, u32[]{:S(2)}) collective-permute-start(f32[840,128]{1,0:T(8,128)S(1)} %get-tuple-element.25), channel_id=1, source_target_pairs={{0,8},{1,9},{2,4},{3,5},{4,2},{5,3},{6,14},{7,15},{8,0},{9,1},{10,... | collective-permute-start | bytes 1290248 | tf_op jit(solution)/shard_map/ppermute | solution.py:298
  53.9 26.9 %collective-permute-start.21 = (f32[840,128]{1,0:T(8,128)S(1)}, f32[840,128]{1,0:T(8,128)S(1)}, u32[]{:S(2)}, u32[]{:S(2)}) collective-permute-start(f32[840,128]{1,0:T(8,128)S(1)} %get-tuple-element.26.mine), channel_id=1, source_target_pairs={{6,4},{7,5},{14,12},{15,13},{22,20},{23,21},{30,28},{31,29},{0,2},... | collective-permute-start | bytes 1290248 | tf_op jit(solution)/shard_map/ppermute | solution.py:301
  58.1 23.1 %collective-permute-start.23 = (f32[832,128]{1,0:T(8,128)S(1)}, f32[832,128]{1,0:T(8,128)S(1)}, u32[]{:S(2)}, u32[]{:S(2)}) collective-permute-start(f32[832,128]{1,0:T(8,128)S(1)} %join.1), channel_id=1, source_target_pairs={{4,0},{5,1},{12,8},{13,9},{20,16},{21,17},{28,24},{29,25},{2,6},{3... | collective-permute-start | bytes 1277960 | tf_op jit(solution)/shard_map/ppermute | solution.py:301
  59.4 21.4 %collective-permute-start.24 = (f32[64,128]{1,0:T(8,128)S(1)}, f32[64,128]{1,0:T(8,128)S(1)}, u32[]{:S(2)}, u32[]{:S(2)}) collective-permute-start(f32[64,128]{1,0:T(8,128)S(1)} %get-tuple-element.27), channel_id=1, source_target_pairs={{0,6},{1,7},{2,4},{3,5},{4,2},{5,3},{6,0},{7,1},{8,14},{9,15},{10,... | collective-permute-start | bytes 98312 | tf_op jit(solution)/shard_map/ppermute | solution.py:298

commit v16 on v15

--- a/solution.py
+++ b/solution.py
@@ -358,6 +358,7 @@
     swapped = send(turned, [low_homes, low_homes[::-1], high_homes])
     later = lax.optimization_barrier((near, turned))[0]
     last_block = send_some(later, [(line(3, 2), high_homes[1])])
+    last_block = pltpu.with_memory_space_constraint(last_block, pltpu.HBM)
     lx = send(later, [(line(2, 0), low_homes[0]), (line(3, 0), low_homes[1])])
     s_0, s_1 = pl.pallas_call(
         functools.partial(low_kernel, low_homes, col_count),

time: 82.4 us -> 82.4 us (level)
  waiting for transfers between devices: 35.9 us -> 38.3 us
  Pallas kernels: 14.3 us -> 12.6 us
    ppermute x21, waiting for transfers between devices: 35.6 us -> 38 us  [send(): return lax.ppermute(x, AXES, sorted(onward.items()))]
    ppermute x21, starting transfers between devices: 23.5 us -> 21.6 us  [send(): return lax.ppermute(x, AXES, sorted(onward.items()))]
    ppermute x4, starting transfers between devices: 7.44 us -> 8.69 us  [send_some(): return lax.ppermute(x, AXES, pairs)]
    pallas_call x1, Pallas kernels: 1.06 us -> 0.03 us  [on_device(): pl.pallas_call(functools.partial(high_kernel, high_homes, col_count), in_...]
  transfers between devices with their start and end apart: 25 -> 25, of which waited for: 13 -> 15; matrix products, arithmetic and copies ran while one was open for 0% -> 0% of each run, Pallas kernels for 11% -> 9%
where the time goes in v16:
time: 82.4 us; the launch traced here: 82.1 us
  waiting for transfers between devices  38.3 us (46%)
  starting transfers between devices  30.2 us (37%)
  Pallas kernels  12.6 us (15%)
  between operations  0.87 us (1%)
    ppermute x21, waiting for transfers between devices, send(): return lax.ppermute(x, AXES, sorted(onward.items()))  38 us
    ppermute x21, starting transfers between devices, send(): return lax.ppermute(x, AXES, sorted(onward.items()))  21.6 us
    ppermute x4, starting transfers between devices, send_some(): return lax.ppermute(x, AXES, pairs)  8.69 us
    pallas_call x2, Pallas kernels, update(): pl.pallas_call(functools.partial(update_kernel, (groups, row_count, share...  6.55 us
    pallas_call x1, Pallas kernels, on_device(): pl.pallas_call(functools.partial(ready_kernel, low_homes, col_count), in_...  1.69 us
  transfers between devices with their start and end apart: 25, of which 15 were waited for; matrix products, arithmetic and copies ran while one was open for 0% of the time, Pallas kernels for 9%

profile of v16, /device:TPU:0, one launch (start us, length us, event | category | flops | bytes accessed | tf_op | source)
XLA Modules:
  0.0 82.1 jit_solution(5020615546088391648)
XLA Ops:
  0.6 1.3 %fetch.1 = (f32[512,512]{1,0:T(8,128)S(1)}, f32[128,128]{1,0:T(8,128)S(1)}) custom-call(f32[6,1,1,512,512]{4,3,2,1,0:T(8,128)} %refs_8_.3, f32[6,1,1,128,128]{4,3,2,1,0:T(8,128)} %rhs.1), custom_call_target="tpu_custom_call" | custom-call | flops 1000 | bytes 1000 | tf_op jit(solution)/shard_map/fetch/pallas_call | solution.py:314
  1.9 1.3 %collective-permute-start.5 = (f32[512,512]{1,0:T(8,128)S(1)}, f32[512,512]{1,0:T(8,128)S(1)}, u32[]{:S(2)}, u32[]{:S(2)}) collective-permute-start(f32[512,512]{1,0:T(8,128)S(1)} %get-tuple-element.22.near), channel_id=1, source_target_pairs={{10,0},{11,1}} | collective-permute-start | bytes 3145736 | tf_op jit(solution)/shard_map/ppermute | solution.py:301
  3.2 0.1 collective-permute-start.4
  3.3 2.9 %collective-permute-start = (f32[128,128]{1,0:T(8,128)S(1)}, f32[128,128]{1,0:T(8,128)S(1)}, u32[]{:S(2)}, u32[]{:S(2)}) collective-permute-start(f32[128,128]{1,0:T(8,128)S(1)} %get-tuple-element.16.own), channel_id=1, source_target_pairs={{0,2},{1,9},{2,0},{3,1},{4,28},{5,13},{6,14},{7,5},{8,24},{9,11},{... | collective-permute-start | bytes 196616 | tf_op jit(solution)/shard_map/ppermute | solution.py:298
  6.2 2.1 %collective-permute-start.1 = (f32[128,128]{1,0:T(8,128)S(1)}, f32[128,128]{1,0:T(8,128)S(1)}, u32[]{:S(2)}, u32[]{:S(2)}) collective-permute-start(f32[128,128]{1,0:T(8,128)S(1)} %get-tuple-element.16.own), channel_id=1, source_target_pairs={{0,4},{1,9},{2,10},{3,11},{4,0},{5,1},{6,14},{7,3},{8,12},{9,13},{... | collective-permute-start | bytes 196616 | tf_op jit(solution)/shard_map/ppermute | solution.py:298
  8.3 0.0 collective-permute-start.2
  8.3 1.7 %ready.1 = (bf16[2,512,512]{2,1,0:T(8,128)(2,1)S(1)}, bf16[2,512,512]{2,1,0:T(8,128)(2,1)S(1)}) custom-call(f32[4,512,512]{2,1,0:T(8,128)} %inverses.3), custom_call_target="tpu_custom_call" | custom-call | flops 1000 | bytes 1000 | tf_op jit(solution)/shard_map/ready/pallas_call | solution.py:326
  10.0 0.0 collective-permute-done.g1
  10.1 1.4 %collective-permute-done.1.g2 = f32[128,128]{1,0:T(8,128)S(1)} collective-permute-done((f32[128,128]{1,0:T(8,128)S(1)}, f32[128,128]{1,0:T(8,128)S(1)}, u32[]{:S(2)}, u32[]{:S(2)}) %collective-permute-start.1) | collective-permute-done | bytes 65568 | tf_op jit(solution)/shard_map/ppermute | solution.py:298
  11.5 3.0 %collective-permute-done.2.g3 = f32[128,128]{1,0:T(8,128)S(1)} collective-permute-done((f32[128,128]{1,0:T(8,128)S(1)}, f32[128,128]{1,0:T(8,128)S(1)}, u32[]{:S(2)}, u32[]{:S(2)}) %collective-permute-start.2) | collective-permute-done | bytes 65568 | tf_op jit(solution)/shard_map/ppermute | solution.py:298
  14.5 0.5 turn.1.out.own
  15.0 0.1 collective-permute-start.10
  15.1 1.7 %collective-permute-start.13 = (f32[512,512]{1,0:T(8,128)S(1)}, f32[512,512]{1,0:T(8,128)}, u32[]{:S(2)}, u32[]{:S(2)}) collective-permute-start(f32[512,512]{1,0:T(8,128)S(1)} %get-tuple-element.22.near), channel_id=1, source_target_pairs={{13,15}} | collective-permute-start | bytes 3145736 | tf_op jit(solution)/shard_map/ppermute | solution.py:301
  16.7 0.8 %collective-permute-start.3 = (f32[128,512]{1,0:T(8,128)S(1)}, f32[128,512]{1,0:T(8,128)S(1)}, u32[]{:S(2)}, u32[]{:S(2)}) collective-permute-start(f32[128,512]{1,0:T(8,128)S(1)} %turn.1.out.own), channel_id=1, source_target_pairs={{0,1},{1,0},{2,10},{3,11},{4,12},{5,13},{6,14},{7,4},{8,24},{9,25}... | collective-permute-start | bytes 786440 | tf_op jit(solution)/shard_map/ppermute | solution.py:298
  17.6 5.5 %collective-permute-done.3.swapped = f32[128,512]{1,0:T(8,128)S(1)} collective-permute-done((f32[128,512]{1,0:T(8,128)S(1)}, f32[128,512]{1,0:T(8,128)S(1)}, u32[]{:S(2)}, u32[]{:S(2)}) %collective-permute-start.3) | collective-permute-done | bytes 262176 | tf_op jit(solution)/shard_map/ppermute | solution.py:298
  23.1 0.0 collective-permute-done.5.ly
  23.1 0.0 collective-permute-done.4.la
  23.1 0.8 solve_low.1
  23.9 0.1 collective-permute-start.6
  24.0 0.0 collective-permute-done.10.lx
  24.0 0.8 reduce_low.1
  24.8 0.1 collective-permute-start.11
  24.9 0.1 collective-permute-start.12
  24.9 2.9 %collective-permute-done.6 = f32[128,512]{1,0:T(8,128)S(1)} collective-permute-done((f32[128,512]{1,0:T(8,128)S(1)}, f32[128,512]{1,0:T(8,128)S(1)}, u32[]{:S(2)}, u32[]{:S(2)}) %collective-permute-start.6) | collective-permute-done | bytes 262176 | tf_op jit(solution)/shard_map/ppermute | solution.py:298
  27.9 0.1 collective-permute-start.7
  28.0 0.0 collective-permute-done.13.last_block
  28.0 2.7 %collective-permute-done.11.w_1 = f32[128,512]{1,0:T(8,128)S(1)} collective-permute-done((f32[128,512]{1,0:T(8,128)S(1)}, f32[128,512]{1,0:T(8,128)S(1)}, u32[]{:S(2)}, u32[]{:S(2)}) %collective-permute-start.11) | collective-permute-done | bytes 262176 | tf_op jit(solution)/shard_map/ppermute | solution.py:298
  30.7 2.8 %collective-permute-done.12.w_2 = f32[128,512]{1,0:T(8,128)S(1)} collective-permute-done((f32[128,512]{1,0:T(8,128)S(1)}, f32[128,512]{1,0:T(8,128)S(1)}, u32[]{:S(2)}, u32[]{:S(2)}) %collective-permute-start.12) | collective-permute-done | bytes 262176 | tf_op jit(solution)/shard_map/ppermute | solution.py:298
  33.5 0.0 collective-permute-start.14
  33.6 0.5 collective-permute-start.15
  34.0 0.1 collective-permute-start.16
  34.1 0.5 collective-permute-start.8
  34.6 0.0 collective-permute-done.7.refs_1_
  34.6 0.1 collective-permute-start.17
  34.6 0.5 collective-permute-done.14
  35.1 0.1 collective-permute-start.9
  35.2 0.2 collective-permute-done.15
  35.4 0.4 collective-permute-done.16
  35.8 0.1 select_select_fusion.refs_5_
  35.9 0.2 collective-permute-start.18
  36.1 0.1 collective-permute-done.8.refs_2_
  36.2 0.4 collective-permute-done.17.refs_6_
  36.6 0.4 collective-permute-done.9.refs_3_
  36.9 0.5 collective-permute-done.18.refs_7_
  37.5 3.3 %update_first.1 = (f32[832,128]{1,0:T(8,128)S(1)}, f32[840,128]{1,0:T(8,128)S(1)}, f32[64,128]{1,0:T(8,128)S(1)}) custom-call(f32[128,512]{1,0:T(8,128)S(1)} %broadcast_select_fusion.refs_0_, f32[128,512]{1,0:T(8,128)S(1)} %collective-permute-done.7.refs_1_, f32[128,512]{1,0:T(8,128)S(1)} %collective-permute-done.8.refs_2_, ...), custom_call_target="tpu_custom_call" | custom-call | flops 1000 | bytes 1000 | tf_op jit(solution)/shard_map/update_first/pallas_call | solution.py:447
  40.8 0.0 copy-start
  40.8 0.1 collective-permute-start.19
  40.9 9.5 %collective-permute-start.20 = (f32[840,128]{1,0:T(8,128)S(1)}, f32[840,128]{1,0:T(8,128)S(1)}, u32[]{:S(2)}, u32[]{:S(2)}) collective-permute-start(f32[840,128]{1,0:T(8,128)S(1)} %get-tuple-element.25), channel_id=1, source_target_pairs={{0,4},{1,5},{2,0},{3,1},{4,6},{5,7},{6,2},{7,3},{8,12},{9,13},{10,... | collective-permute-start | bytes 1290248 | tf_op jit(solution)/shard_map/ppermute | solution.py:298
  50.3 0.0 collective-permute-start.22
  50.3 3.3 %update_second.1 = (f32[832,128]{1,0:T(8,128)S(1)}, f32[840,128]{1,0:T(8,128)S(1)}) custom-call(f32[128,512]{1,0:T(8,128)S(1)} %broadcast_select_fusion.refs_0_, f32[128,512]{1,0:T(8,128)S(1)} %collective-permute-done.7.refs_1_, f32[128,512]{1,0:T(8,128)S(1)} %collective-permute-done.8.refs_2_, f32[128,512]{1,0:T(8,128)S(1)} %collective-permute-done.9.refs_3_, ...), custom_call_target="tpu_custom_call" | custom-call | flops 1000 | bytes 1000 | tf_op jit(solution)/shard_map/update_second/pallas_call | solution.py:447
  53.6 4.5 %collective-permute-start.21 = (f32[840,128]{1,0:T(8,128)S(1)}, f32[840,128]{1,0:T(8,128)S(1)}, u32[]{:S(2)}, u32[]{:S(2)}) collective-permute-start(f32[840,128]{1,0:T(8,128)S(1)} %get-tuple-element.26.mine), channel_id=1, source_target_pairs={{6,4},{7,5},{14,12},{15,13},{22,20},{23,21},{30,28},{31,29},{0,2},... | collective-permute-start | bytes 1290248 | tf_op jit(solution)/shard_map/ppermute | solution.py:301
  58.1 0.0 collective-permute-done.19.theirs.got_1
  58.1 1.3 %collective-permute-start.23 = (f32[832,128]{1,0:T(8,128)S(1)}, f32[832,128]{1,0:T(8,128)S(1)}, u32[]{:S(2)}, u32[]{:S(2)}) collective-permute-start(f32[832,128]{1,0:T(8,128)S(1)} %join.1), channel_id=1, source_target_pairs={{4,0},{5,1},{12,8},{13,9},{20,16},{21,17},{28,24},{29,25},{2,6},{3... | collective-permute-start | bytes 1277960 | tf_op jit(solution)/shard_map/ppermute | solution.py:301
  59.4 4.3 %collective-permute-start.24 = (f32[64,128]{1,0:T(8,128)S(1)}, f32[64,128]{1,0:T(8,128)S(1)}, u32[]{:S(2)}, u32[]{:S(2)}) collective-permute-start(f32[64,128]{1,0:T(8,128)S(1)} %get-tuple-element.27), channel_id=1, source_target_pairs={{0,6},{1,7},{2,4},{3,5},{4,2},{5,3},{6,0},{7,1},{8,14},{9,15},{10,... | collective-permute-start | bytes 98312 | tf_op jit(solution)/shard_map/ppermute | solution.py:298
  63.7 17.2 %collective-permute-done.24.far = f32[64,128]{1,0:T(8,128)S(1)} collective-permute-done((f32[64,128]{1,0:T(8,128)S(1)}, f32[64,128]{1,0:T(8,128)S(1)}, u32[]{:S(2)}, u32[]{:S(2)}) %collective-permute-start.24) | collective-permute-done | bytes 32800 | tf_op jit(solution)/shard_map/ppermute | solution.py:298
  80.8 0.0 collective-permute-done.20.got_2
  80.8 0.0 collective-permute-done.22.got_4
  80.8 0.0 collective-permute-done.21.got_3
  80.8 0.3 collective-permute-done.23.joined
  81.2 0.0 copy-done
  81.2 1.0 %add_up.1 = (f32[4,64,128]{2,1,0:T(8,128)}, f32[6,128,128]{2,1,0:T(8,128)}) custom-call(f32[6,128,128]{2,1,0:T(8,128)S(1)} %bitcast.4, f32[832,128]{1,0:T(8,128)S(1)} %get-tuple-element.23.own, f32[832,128]{1,0:T(8,128)S(1)} %collective-permute-done.19.theirs.got_1, f32[840,128]{1,0:T(8,128)S(1)} %collective-permute-done.20.got_2, ...), custom_call_target="tpu_custom_call" | custom-call | flops 1000 | bytes 1000 | tf_op jit(solution)/shard_map/add_up/pallas_call | solution.py:488
  (3 shorter events, 0.1 us)
Async XLA Ops:
  1.9 21.2 %collective-permute-start.5 = (f32[512,512]{1,0:T(8,128)S(1)}, f32[512,512]{1,0:T(8,128)S(1)}, u32[]{:S(2)}, u32[]{:S(2)}) collective-permute-start(f32[512,512]{1,0:T(8,128)S(1)} %get-tuple-element.22.near), channel_id=1, source_target_pairs={{10,0},{11,1}} | collective-permute-start | bytes 3145736 | tf_op jit(solution)/shard_map/ppermute | solution.py:301
  3.2 19.9 %collective-permute-start.4 = (f32[512,512]{1,0:T(8,128)S(1)}, f32[512,512]{1,0:T(8,128)S(1)}, u32[]{:S(2)}, u32[]{:S(2)}) collective-permute-start(f32[512,512]{1,0:T(8,128)S(1)} %get-tuple-element.22.near), channel_id=1, source_target_pairs={{0,8},{1,0},{2,10},{3,11},{4,12},{5,13},{6,14},{7,15},{8,9},{9,1},... | collective-permute-start | bytes 3145736 | tf_op jit(solution)/shard_map/ppermute | solution.py:298
  3.3 6.7 %collective-permute-start = (f32[128,128]{1,0:T(8,128)S(1)}, f32[128,128]{1,0:T(8,128)S(1)}, u32[]{:S(2)}, u32[]{:S(2)}) collective-permute-start(f32[128,128]{1,0:T(8,128)S(1)} %get-tuple-element.16.own), channel_id=1, source_target_pairs={{0,2},{1,9},{2,0},{3,1},{4,28},{5,13},{6,14},{7,5},{8,24},{9,11},{... | collective-permute-start | bytes 196616 | tf_op jit(solution)/shard_map/ppermute | solution.py:298
  6.2 5.3 %collective-permute-start.1 = (f32[128,128]{1,0:T(8,128)S(1)}, f32[128,128]{1,0:T(8,128)S(1)}, u32[]{:S(2)}, u32[]{:S(2)}) collective-permute-start(f32[128,128]{1,0:T(8,128)S(1)} %get-tuple-element.16.own), channel_id=1, source_target_pairs={{0,4},{1,9},{2,10},{3,11},{4,0},{5,1},{6,14},{7,3},{8,12},{9,13},{... | collective-permute-start | bytes 196616 | tf_op jit(solution)/shard_map/ppermute | solution.py:298
  8.3 6.2 %collective-permute-start.2 = (f32[128,128]{1,0:T(8,128)S(1)}, f32[128,128]{1,0:T(8,128)S(1)}, u32[]{:S(2)}, u32[]{:S(2)}) collective-permute-start(f32[128,128]{1,0:T(8,128)S(1)} %get-tuple-element.16.own), channel_id=1, source_target_pairs={{0,6},{1,7},{2,10},{3,11},{4,28},{5,13},{6,0},{7,1},{8,24},{9,15},... | collective-permute-start | bytes 196616 | tf_op jit(solution)/shard_map/ppermute | solution.py:298
  15.0 9.0 %collective-permute-start.10 = (f32[512,512]{1,0:T(8,128)S(1)}, f32[512,512]{1,0:T(8,128)S(1)}, u32[]{:S(2)}, u32[]{:S(2)}) collective-permute-start(f32[512,512]{1,0:T(8,128)S(1)} %get-tuple-element.22.near), channel_id=1, source_target_pairs={{0,8},{1,9},{2,10},{3,11},{4,12},{5,13},{6,14},{7,15},{8,0},{9,1},... | collective-permute-start | bytes 3145736 | tf_op jit(solution)/shard_map/ppermute | solution.py:298
  15.1 12.9 %collective-permute-start.13 = (f32[512,512]{1,0:T(8,128)S(1)}, f32[512,512]{1,0:T(8,128)}, u32[]{:S(2)}, u32[]{:S(2)}) collective-permute-start(f32[512,512]{1,0:T(8,128)S(1)} %get-tuple-element.22.near), channel_id=1, source_target_pairs={{13,15}} | collective-permute-start | bytes 3145736 | tf_op jit(solution)/shard_map/ppermute | solution.py:301
  16.7 6.4 %collective-permute-start.3 = (f32[128,512]{1,0:T(8,128)S(1)}, f32[128,512]{1,0:T(8,128)S(1)}, u32[]{:S(2)}, u32[]{:S(2)}) collective-permute-start(f32[128,512]{1,0:T(8,128)S(1)} %turn.1.out.own), channel_id=1, source_target_pairs={{0,1},{1,0},{2,10},{3,11},{4,12},{5,13},{6,14},{7,4},{8,24},{9,25}... | collective-permute-start | bytes 786440 | tf_op jit(solution)/shard_map/ppermute | solution.py:298
  23.9 4.0 %collective-permute-start.6 = (f32[128,512]{1,0:T(8,128)S(1)}, f32[128,512]{1,0:T(8,128)S(1)}, u32[]{:S(2)}, u32[]{:S(2)}) collective-permute-start(f32[128,512]{1,0:T(8,128)S(1)} %get-tuple-element.21.s_b), channel_id=1, source_target_pairs={{0,2},{1,3},{2,10},{3,11},{4,12},{5,13},{6,14},{7,15},{8,0},{9,1},... | collective-permute-start | bytes 786440 | tf_op jit(solution)/shard_map/ppermute | solution.py:298
  24.8 5.9 %collective-permute-start.11 = (f32[128,512]{1,0:T(8,128)S(1)}, f32[128,512]{1,0:T(8,128)S(1)}, u32[]{:S(2)}, u32[]{:S(2)}) collective-permute-start(f32[128,512]{1,0:T(8,128)S(1)} %reduce_low.1), channel_id=1, source_target_pairs={{0,15},{1,9},{2,10},{3,11},{4,12},{5,13},{6,14},{7,8},{8,0},{9,1},... | collective-permute-start | bytes 786440 | tf_op jit(solution)/shard_map/ppermute | solution.py:298
  24.9 8.6 %collective-permute-start.12 = (f32[128,512]{1,0:T(8,128)S(1)}, f32[128,512]{1,0:T(8,128)S(1)}, u32[]{:S(2)}, u32[]{:S(2)}) collective-permute-start(f32[128,512]{1,0:T(8,128)S(1)} %reduce_low.1), channel_id=1, source_target_pairs={{0,12},{1,15},{2,10},{3,11},{4,8},{5,13},{6,14},{7,9},{8,0},{9,1},... | collective-permute-start | bytes 786440 | tf_op jit(solution)/shard_map/ppermute | solution.py:298
  27.9 6.7 %collective-permute-start.7 = (f32[128,512]{1,0:T(8,128)S(1)}, f32[128,512]{1,0:T(8,128)S(1)}, u32[]{:S(2)}, u32[]{:S(2)}) collective-permute-start(f32[128,512]{1,0:T(8,128)S(1)} %broadcast_select_fusion.refs_0_), channel_id=1, source_target_pairs={{0,16},{1,17},{2,18},{3,19},{4,12},{5,13},{6,14},{7,15},{8,0},{9,1... | collective-permute-start | bytes 786440 | tf_op jit(solution)/shard_map/ppermute | solution.py:298
  33.5 1.6 %collective-permute-start.14 = (f32[128,512]{1,0:T(8,128)S(1)}, f32[128,512]{1,0:T(8,128)S(1)}, u32[]{:S(2)}, u32[]{:S(2)}) collective-permute-start(f32[128,512]{1,0:T(8,128)S(1)} %solve_high.1.refs_4_), channel_id=1, source_target_pairs={{0,8},{1,9},{2,10},{3,11},{4,12},{5,13},{6,14},{7,15},{8,0},{9,1},... | collective-permute-start | bytes 786440 | tf_op jit(solution)/shard_map/ppermute | solution.py:298
  33.6 1.9 %collective-permute-start.15 = (f32[128,512]{1,0:T(8,128)S(1)}, f32[128,512]{1,0:T(8,128)S(1)}, u32[]{:S(2)}, u32[]{:S(2)}) collective-permute-start(f32[128,512]{1,0:T(8,128)S(1)} %solve_high.1.refs_4_), channel_id=1, source_target_pairs={{0,8},{1,9},{2,10},{3,11},{4,12},{5,4},{6,7},{7,15},{8,0},{9,1},{1... | collective-permute-start | bytes 786440 | tf_op jit(solution)/shard_map/ppermute | solution.py:298
  34.0 1.8 %collective-permute-start.16 = (f32[128,512]{1,0:T(8,128)S(1)}, f32[128,512]{1,0:T(8,128)S(1)}, u32[]{:S(2)}, u32[]{:S(2)}) collective-permute-start(f32[128,512]{1,0:T(8,128)S(1)} %solve_high.1.refs_4_), channel_id=1, source_target_pairs={{0,8},{1,9},{2,10},{3,11},{4,12},{5,13},{6,14},{7,15},{8,0},{9,1},... | collective-permute-start | bytes 786440 | tf_op jit(solution)/shard_map/ppermute | solution.py:298
  34.1 2.1 %collective-permute-start.8 = (f32[128,512]{1,0:T(8,128)S(1)}, f32[128,512]{1,0:T(8,128)S(1)}, u32[]{:S(2)}, u32[]{:S(2)}) collective-permute-start(f32[128,512]{1,0:T(8,128)S(1)} %broadcast_select_fusion.refs_0_), channel_id=1, source_target_pairs={{0,8},{1,9},{2,10},{3,11},{4,12},{5,13},{6,14},{7,15},{8,0},{9,1},... | collective-permute-start | bytes 786440 | tf_op jit(solution)/shard_map/ppermute | solution.py:298
  34.6 2.0 %collective-permute-start.17 = (f32[128,512]{1,0:T(8,128)S(1)}, f32[128,512]{1,0:T(8,128)S(1)}, u32[]{:S(2)}, u32[]{:S(2)}) collective-permute-start(f32[128,512]{1,0:T(8,128)S(1)} %solve_high.1.refs_4_), channel_id=1, source_target_pairs={{0,8},{1,9},{2,10},{3,11},{4,12},{5,13},{6,14},{7,15},{8,0},{9,1},... | collective-permute-start | bytes 786440 | tf_op jit(solution)/shard_map/ppermute | solution.py:298
  35.1 1.9 %collective-permute-start.9 = (f32[128,512]{1,0:T(8,128)S(1)}, f32[128,512]{1,0:T(8,128)S(1)}, u32[]{:S(2)}, u32[]{:S(2)}) collective-permute-start(f32[128,512]{1,0:T(8,128)S(1)} %collective-permute-done.7.refs_1_), channel_id=1, source_target_pairs={{0,8},{1,9},{2,10},{3,11},{4,12},{5,13},{6,14},{7,15},{8,0},{9,1},... | collective-permute-start | bytes 786440 | tf_op jit(solution)/shard_map/ppermute | solution.py:298
  35.9 1.6 %collective-permute-start.18 = (f32[128,512]{1,0:T(8,128)S(1)}, f32[128,512]{1,0:T(8,128)S(1)}, u32[]{:S(2)}, u32[]{:S(2)}) collective-permute-start(f32[128,512]{1,0:T(8,128)S(1)} %select_select_fusion.refs_5_), channel_id=1, source_target_pairs={{0,8},{1,9},{2,10},{3,11},{4,12},{5,13},{6,14},{7,15},{8,0},{9,1},... | collective-permute-start | bytes 786440 | tf_op jit(solution)/shard_map/ppermute | solution.py:298
  40.8 40.4 %copy-start = (f32[6,1,1,128,128]{4,3,2,1,0:T(8,128)S(1)}, f32[6,1,1,128,128]{4,3,2,1,0:T(8,128)}, u32[]{:S(2)}) copy-start(f32[6,1,1,128,128]{4,3,2,1,0:T(8,128)} %rhs.1) | copy-start | bytes 1179652
  40.8 17.3 %collective-permute-start.19 = (f32[832,128]{1,0:T(8,128)S(1)}, f32[832,128]{1,0:T(8,128)S(1)}, u32[]{:S(2)}, u32[]{:S(2)}) collective-permute-start(f32[832,128]{1,0:T(8,128)S(1)} %get-tuple-element.24), channel_id=1, source_target_pairs={{0,2},{1,3},{2,0},{3,1},{4,6},{5,7},{6,4},{7,5},{8,10},{9,11},{10,... | collective-permute-start | bytes 1277960 | tf_op jit(solution)/shard_map/ppermute | solution.py:298
  40.9 40.0 %collective-permute-start.20 = (f32[840,128]{1,0:T(8,128)S(1)}, f32[840,128]{1,0:T(8,128)S(1)}, u32[]{:S(2)}, u32[]{:S(2)}) collective-permute-start(f32[840,128]{1,0:T(8,128)S(1)} %get-tuple-element.25), channel_id=1, source_target_pairs={{0,4},{1,5},{2,0},{3,1},{4,6},{5,7},{6,2},{7,3},{8,12},{9,13},{10,... | collective-permute-start | bytes 1290248 | tf_op jit(solution)/shard_map/ppermute | solution.py:298
  50.3 30.5 %collective-permute-start.22 = (f32[840,128]{1,0:T(8,128)S(1)}, f32[840,128]{1,0:T(8,128)S(1)}, u32[]{:S(2)}, u32[]{:S(2)}) collective-permute-start(f32[840,128]{1,0:T(8,128)S(1)} %get-tuple-element.25), channel_id=1, source_target_pairs={{0,8},{1,9},{2,4},{3,5},{4,2},{5,3},{6,14},{7,15},{8,0},{9,1},{10,... | collective-permute-start | bytes 1290248 | tf_op jit(solution)/shard_map/ppermute | solution.py:298
  53.6 27.2 %collective-permute-start.21 = (f32[840,128]{1,0:T(8,128)S(1)}, f32[840,128]{1,0:T(8,128)S(1)}, u32[]{:S(2)}, u32[]{:S(2)}) collective-permute-start(f32[840,128]{1,0:T(8,128)S(1)} %get-tuple-element.26.mine), channel_id=1, source_target_pairs={{6,4},{7,5},{14,12},{15,13},{22,20},{23,21},{30,28},{31,29},{0,2},... | collective-permute-start | bytes 1290248 | tf_op jit(solution)/shard_map/ppermute | solution.py:301
  58.1 23.1 %collective-permute-start.23 = (f32[832,128]{1,0:T(8,128)S(1)}, f32[832,128]{1,0:T(8,128)S(1)}, u32[]{:S(2)}, u32[]{:S(2)}) collective-permute-start(f32[832,128]{1,0:T(8,128)S(1)} %join.1), channel_id=1, source_target_pairs={{4,0},{5,1},{12,8},{13,9},{20,16},{21,17},{28,24},{29,25},{2,6},{3... | collective-permute-start | bytes 1277960 | tf_op jit(solution)/shard_map/ppermute | solution.py:301
  59.4 21.4 %collective-permute-start.24 = (f32[64,128]{1,0:T(8,128)S(1)}, f32[64,128]{1,0:T(8,128)S(1)}, u32[]{:S(2)}, u32[]{:S(2)}) collective-permute-start(f32[64,128]{1,0:T(8,128)S(1)} %get-tuple-element.27), channel_id=1, source_target_pairs={{0,6},{1,7},{2,4},{3,5},{4,2},{5,3},{6,0},{7,1},{8,14},{9,15},{10,... | collective-permute-start | bytes 98312 | tf_op jit(solution)/shard_map/ppermute | solution.py:298

commit v17 on v16

--- a/solution.py
+++ b/solution.py
@@ -434,7 +434,7 @@
 
     spots = [(g // groups, g % groups) for g in range(4)]
     homes = (tuple(spots[:2]), tuple(spots[:2]), (spots[2],), (spots[3],))
-    moved = send(s_1, [(line(g, 0), line(g, 1)) for g in (0, 1)])
+    moved = send(lax.optimization_barrier((s_1, w))[0], [(line(g, 0), line(g, 1)) for g in (0, 1)])
     s_low = jnp.where(member == 0, s_0, moved)
     ways = spread(s_low, {0: homes[0], 1: homes[1]}) + spread(s_high, {2: homes[2], 3: homes[3]})
 

time: 82.4 us -> 83.9 us (1.018)
  waiting for transfers between devices: 38.3 us -> 44.2 us
  starting transfers between devices: 30.2 us -> 25.9 us
    ppermute x21, waiting for transfers between devices: 38 us -> 43.8 us  [send(): return lax.ppermute(x, AXES, sorted(onward.items()))]
    ppermute x21, starting transfers between devices: 21.6 us -> 18.2 us  [send(): return lax.ppermute(x, AXES, sorted(onward.items()))]
    ppermute x4, starting transfers between devices: 8.69 us -> 7.74 us  [send_some(): return lax.ppermute(x, AXES, pairs)]
  transfers between devices with their start and end apart: 25 -> 25, of which waited for: 15 -> 10; matrix products, arithmetic and copies ran while one was open for 0% -> 0% of each run, Pallas kernels for 9% -> 8%
where the time goes in v17:
time: 83.9 us; the launch traced here: 83.7 us
  waiting for transfers between devices  44.2 us (53%)
  starting transfers between devices  25.9 us (31%)
  Pallas kernels  12.6 us (15%)
  between operations  0.88 us (1%)
    ppermute x21, waiting for transfers between devices, send(): return lax.ppermute(x, AXES, sorted(onward.items()))  43.8 us
    ppermute x21, starting transfers between devices, send(): return lax.ppermute(x, AXES, sorted(onward.items()))  18.2 us
    ppermute x4, starting transfers between devices, send_some(): return lax.ppermute(x, AXES, pairs)  7.74 us
    pallas_call x2, Pallas kernels, update(): pl.pallas_call(functools.partial(update_kernel, (groups, row_count, share...  6.55 us
    pallas_call x1, Pallas kernels, on_device(): pl.pallas_call(functools.partial(ready_kernel, low_homes, col_count), in_...  1.71 us
  transfers between devices with their start and end apart: 25, of which 10 were waited for; matrix products, arithmetic and copies ran while one was open for 0% of the time, Pallas kernels for 8%

profile of v17, /device:TPU:0, one launch (start us, length us, event | category | flops | bytes accessed | tf_op | source)
XLA Modules:
  0.0 83.7 jit_solution(8274486047898130969)
XLA Ops:
  0.6 1.3 %fetch.1 = (f32[512,512]{1,0:T(8,128)S(1)}, f32[128,128]{1,0:T(8,128)S(1)}) custom-call(f32[6,1,1,512,512]{4,3,2,1,0:T(8,128)} %refs_8_.3, f32[6,1,1,128,128]{4,3,2,1,0:T(8,128)} %rhs.1), custom_call_target="tpu_custom_call" | custom-call | flops 1000 | bytes 1000 | tf_op jit(solution)/shard_map/fetch/pallas_call | solution.py:314
  1.9 3.1 %collective-permute-start = (f32[128,128]{1,0:T(8,128)S(1)}, f32[128,128]{1,0:T(8,128)S(1)}, u32[]{:S(2)}, u32[]{:S(2)}) collective-permute-start(f32[128,128]{1,0:T(8,128)S(1)} %get-tuple-element.17.own), channel_id=1, source_target_pairs={{0,2},{1,9},{2,0},{3,1},{4,28},{5,13},{6,14},{7,5},{8,24},{9,11},{... | collective-permute-start | bytes 196616 | tf_op jit(solution)/shard_map/ppermute | solution.py:298
  5.0 1.9 %collective-permute-start.1 = (f32[128,128]{1,0:T(8,128)S(1)}, f32[128,128]{1,0:T(8,128)S(1)}, u32[]{:S(2)}, u32[]{:S(2)}) collective-permute-start(f32[128,128]{1,0:T(8,128)S(1)} %get-tuple-element.17.own), channel_id=1, source_target_pairs={{0,4},{1,9},{2,10},{3,11},{4,0},{5,1},{6,14},{7,3},{8,12},{9,13},{... | collective-permute-start | bytes 196616 | tf_op jit(solution)/shard_map/ppermute | solution.py:298
  6.9 0.6 collective-permute-start.2
  7.5 1.3 %collective-permute-start.5 = (f32[512,512]{1,0:T(8,128)S(1)}, f32[512,512]{1,0:T(8,128)S(1)}, u32[]{:S(2)}, u32[]{:S(2)}) collective-permute-start(f32[512,512]{1,0:T(8,128)S(1)} %get-tuple-element.23.near), channel_id=1, source_target_pairs={{10,0},{11,1}} | collective-permute-start | bytes 3145736 | tf_op jit(solution)/shard_map/ppermute | solution.py:301
  8.8 0.1 collective-permute-start.4
  8.9 1.7 %ready.1 = (bf16[2,512,512]{2,1,0:T(8,128)(2,1)S(1)}, bf16[2,512,512]{2,1,0:T(8,128)(2,1)S(1)}) custom-call(f32[4,512,512]{2,1,0:T(8,128)} %inverses.3), custom_call_target="tpu_custom_call" | custom-call | flops 1000 | bytes 1000 | tf_op jit(solution)/shard_map/ready/pallas_call | solution.py:326
  10.6 0.0 collective-permute-done.g1
  10.6 0.0 collective-permute-done.1.g2
  10.7 2.4 %collective-permute-done.2.g3 = f32[128,128]{1,0:T(8,128)S(1)} collective-permute-done((f32[128,128]{1,0:T(8,128)S(1)}, f32[128,128]{1,0:T(8,128)S(1)}, u32[]{:S(2)}, u32[]{:S(2)}) %collective-permute-start.2) | collective-permute-done | bytes 65568 | tf_op jit(solution)/shard_map/ppermute | solution.py:298
  13.1 0.5 turn.1.out.own
  13.5 0.1 collective-permute-start.6
  13.6 0.7 collective-permute-start.13
  14.4 0.1 collective-permute-start.3
  14.4 12.1 %collective-permute-done.3.swapped = f32[128,512]{1,0:T(8,128)S(1)} collective-permute-done((f32[128,512]{1,0:T(8,128)S(1)}, f32[128,512]{1,0:T(8,128)S(1)}, u32[]{:S(2)}, u32[]{:S(2)}) %collective-permute-start.3) | collective-permute-done | bytes 262176 | tf_op jit(solution)/shard_map/ppermute | solution.py:298
  26.5 0.0 collective-permute-done.5.ly
  26.5 0.0 collective-permute-done.4.la
  26.5 0.8 solve_low.1
  27.3 0.0 collective-permute-done.6.lx
  27.3 0.8 reduce_low.1
  28.1 0.1 collective-permute-start.11
  28.2 0.1 collective-permute-start.12
  28.2 0.1 collective-permute-start.7
  28.3 0.0 collective-permute-done.13.last_block
  28.4 0.0 copy-start.1
  28.4 3.7 %collective-permute-done.11.w_1 = f32[128,512]{1,0:T(8,128)S(1)} collective-permute-done((f32[128,512]{1,0:T(8,128)S(1)}, f32[128,512]{1,0:T(8,128)S(1)}, u32[]{:S(2)}, u32[]{:S(2)}) %collective-permute-start.11) | collective-permute-done | bytes 262176 | tf_op jit(solution)/shard_map/ppermute | solution.py:298
  32.1 2.8 %collective-permute-done.12.w_2 = f32[128,512]{1,0:T(8,128)S(1)} collective-permute-done((f32[128,512]{1,0:T(8,128)S(1)}, f32[128,512]{1,0:T(8,128)S(1)}, u32[]{:S(2)}, u32[]{:S(2)}) %collective-permute-start.12) | collective-permute-done | bytes 262176 | tf_op jit(solution)/shard_map/ppermute | solution.py:298
  34.9 0.0 copy-done.1
  34.9 0.6 collective-permute-start.14
  35.6 0.1 collective-permute-start.15
  35.6 0.5 collective-permute-start.16
  36.1 1.6 %collective-permute-done.7 = f32[128,512]{1,0:T(8,128)S(1)} collective-permute-done((f32[128,512]{1,0:T(8,128)S(1)}, f32[128,512]{1,0:T(8,128)S(1)}, u32[]{:S(2)}, u32[]{:S(2)}) %collective-permute-start.7) | collective-permute-done | bytes 262176 | tf_op jit(solution)/shard_map/ppermute | solution.py:298
  37.7 0.1 collective-permute-start.8
  37.8 0.5 collective-permute-start.17
  38.3 0.0 collective-permute-done.14
  38.3 0.1 collective-permute-start.9
  38.4 0.0 collective-permute-done.15
  38.4 0.0 collective-permute-done.16
  38.4 0.1 select_select_fusion.refs_5_
  38.5 0.5 collective-permute-start.18
  39.0 2.7 %collective-permute-done.8.refs_1_ = f32[128,512]{1,0:T(8,128)S(1)} collective-permute-done((f32[128,512]{1,0:T(8,128)S(1)}, f32[128,512]{1,0:T(8,128)S(1)}, u32[]{:S(2)}, u32[]{:S(2)}) %collective-permute-start.8) | collective-permute-done | bytes 262176 | tf_op jit(solution)/shard_map/ppermute | solution.py:298
  41.7 0.4 collective-permute-start.10
  42.1 0.0 collective-permute-done.17.refs_6_
  42.1 0.0 collective-permute-done.9.refs_2_
  42.1 0.0 collective-permute-done.18.refs_7_
  42.1 1.1 %collective-permute-done.10.refs_3_ = f32[128,512]{1,0:T(8,128)S(1)} collective-permute-done((f32[128,512]{1,0:T(8,128)S(1)}, f32[128,512]{1,0:T(8,128)S(1)}, u32[]{:S(2)}, u32[]{:S(2)}) %collective-permute-start.10) | collective-permute-done | bytes 262176 | tf_op jit(solution)/shard_map/ppermute | solution.py:298
  43.3 3.3 %update_first.1 = (f32[832,128]{1,0:T(8,128)S(1)}, f32[840,128]{1,0:T(8,128)S(1)}, f32[64,128]{1,0:T(8,128)S(1)}) custom-call(f32[128,512]{1,0:T(8,128)S(1)} %broadcast_select_fusion.refs_0_, f32[128,512]{1,0:T(8,128)S(1)} %collective-permute-done.8.refs_1_, f32[128,512]{1,0:T(8,128)S(1)} %collective-permute-done.9.refs_2_, ...), custom_call_target="tpu_custom_call" | custom-call | flops 1000 | bytes 1000 | tf_op jit(solution)/shard_map/update_first/pallas_call | solution.py:447
  46.6 0.0 copy-start
  46.6 2.5 %collective-permute-start.19 = (f32[832,128]{1,0:T(8,128)S(1)}, f32[832,128]{1,0:T(8,128)S(1)}, u32[]{:S(2)}, u32[]{:S(2)}) collective-permute-start(f32[832,128]{1,0:T(8,128)S(1)} %get-tuple-element.26), channel_id=1, source_target_pairs={{0,2},{1,3},{2,0},{3,1},{4,6},{5,7},{6,4},{7,5},{8,10},{9,11},{10,... | collective-permute-start | bytes 1277960 | tf_op jit(solution)/shard_map/ppermute | solution.py:298
  49.1 2.7 %collective-permute-start.20 = (f32[840,128]{1,0:T(8,128)S(1)}, f32[840,128]{1,0:T(8,128)S(1)}, u32[]{:S(2)}, u32[]{:S(2)}) collective-permute-start(f32[840,128]{1,0:T(8,128)S(1)} %get-tuple-element.27), channel_id=1, source_target_pairs={{0,4},{1,5},{2,0},{3,1},{4,6},{5,7},{6,2},{7,3},{8,12},{9,13},{10,... | collective-permute-start | bytes 1290248 | tf_op jit(solution)/shard_map/ppermute | solution.py:298
  51.8 0.0 collective-permute-start.22
  51.8 3.3 %update_second.1 = (f32[832,128]{1,0:T(8,128)S(1)}, f32[840,128]{1,0:T(8,128)S(1)}) custom-call(f32[128,512]{1,0:T(8,128)S(1)} %broadcast_select_fusion.refs_0_, f32[128,512]{1,0:T(8,128)S(1)} %collective-permute-done.8.refs_1_, f32[128,512]{1,0:T(8,128)S(1)} %collective-permute-done.9.refs_2_, f32[128,512]{1,0:T(8,128)S(1)} %collective-permute-done.10.refs_3_, ...), custom_call_target="tpu_custom_call" | custom-call | flops 1000 | bytes 1000 | tf_op jit(solution)/shard_map/update_second/pallas_call | solution.py:447
  55.1 4.5 %collective-permute-start.21 = (f32[840,128]{1,0:T(8,128)S(1)}, f32[840,128]{1,0:T(8,128)S(1)}, u32[]{:S(2)}, u32[]{:S(2)}) collective-permute-start(f32[840,128]{1,0:T(8,128)S(1)} %get-tuple-element.28.mine), channel_id=1, source_target_pairs={{6,4},{7,5},{14,12},{15,13},{22,20},{23,21},{30,28},{31,29},{0,2},... | collective-permute-start | bytes 1290248 | tf_op jit(solution)/shard_map/ppermute | solution.py:301
  59.6 0.1 collective-permute-done.19.theirs.got_1
  59.7 1.3 %collective-permute-start.23 = (f32[832,128]{1,0:T(8,128)S(1)}, f32[832,128]{1,0:T(8,128)S(1)}, u32[]{:S(2)}, u32[]{:S(2)}) collective-permute-start(f32[832,128]{1,0:T(8,128)S(1)} %join.1), channel_id=1, source_target_pairs={{4,0},{5,1},{12,8},{13,9},{20,16},{21,17},{28,24},{29,25},{2,6},{3... | collective-permute-start | bytes 1277960 | tf_op jit(solution)/shard_map/ppermute | solution.py:301
  61.0 4.2 %collective-permute-start.24 = (f32[64,128]{1,0:T(8,128)S(1)}, f32[64,128]{1,0:T(8,128)S(1)}, u32[]{:S(2)}, u32[]{:S(2)}) collective-permute-start(f32[64,128]{1,0:T(8,128)S(1)} %get-tuple-element.29), channel_id=1, source_target_pairs={{0,6},{1,7},{2,4},{3,5},{4,2},{5,3},{6,0},{7,1},{8,14},{9,15},{10,... | collective-permute-start | bytes 98312 | tf_op jit(solution)/shard_map/ppermute | solution.py:298
  65.2 17.2 %collective-permute-done.24.far = f32[64,128]{1,0:T(8,128)S(1)} collective-permute-done((f32[64,128]{1,0:T(8,128)S(1)}, f32[64,128]{1,0:T(8,128)S(1)}, u32[]{:S(2)}, u32[]{:S(2)}) %collective-permute-start.24) | collective-permute-done | bytes 32800 | tf_op jit(solution)/shard_map/ppermute | solution.py:298
  82.3 0.0 collective-permute-done.20.got_2
  82.3 0.0 collective-permute-done.22.got_4
  82.3 0.0 collective-permute-done.21.got_3
  82.3 0.3 collective-permute-done.23.joined
  82.7 0.0 copy-done
  82.7 1.0 %add_up.1 = (f32[4,64,128]{2,1,0:T(8,128)}, f32[6,128,128]{2,1,0:T(8,128)}) custom-call(f32[6,128,128]{2,1,0:T(8,128)S(1)} %bitcast.4, f32[832,128]{1,0:T(8,128)S(1)} %get-tuple-element.25.own, f32[832,128]{1,0:T(8,128)S(1)} %collective-permute-done.19.theirs.got_1, f32[840,128]{1,0:T(8,128)S(1)} %collective-permute-done.20.got_2, ...), custom_call_target="tpu_custom_call" | custom-call | flops 1000 | bytes 1000 | tf_op jit(solution)/shard_map/add_up/pallas_call | solution.py:488
  (3 shorter events, 0.1 us)
Async XLA Ops:
  1.9 8.7 %collective-permute-start = (f32[128,128]{1,0:T(8,128)S(1)}, f32[128,128]{1,0:T(8,128)S(1)}, u32[]{:S(2)}, u32[]{:S(2)}) collective-permute-start(f32[128,128]{1,0:T(8,128)S(1)} %get-tuple-element.17.own), channel_id=1, source_target_pairs={{0,2},{1,9},{2,0},{3,1},{4,28},{5,13},{6,14},{7,5},{8,24},{9,11},{... | collective-permute-start | bytes 196616 | tf_op jit(solution)/shard_map/ppermute | solution.py:298
  5.0 5.6 %collective-permute-start.1 = (f32[128,128]{1,0:T(8,128)S(1)}, f32[128,128]{1,0:T(8,128)S(1)}, u32[]{:S(2)}, u32[]{:S(2)}) collective-permute-start(f32[128,128]{1,0:T(8,128)S(1)} %get-tuple-element.17.own), channel_id=1, source_target_pairs={{0,4},{1,9},{2,10},{3,11},{4,0},{5,1},{6,14},{7,3},{8,12},{9,13},{... | collective-permute-start | bytes 196616 | tf_op jit(solution)/shard_map/ppermute | solution.py:298
  6.9 6.1 %collective-permute-start.2 = (f32[128,128]{1,0:T(8,128)S(1)}, f32[128,128]{1,0:T(8,128)S(1)}, u32[]{:S(2)}, u32[]{:S(2)}) collective-permute-start(f32[128,128]{1,0:T(8,128)S(1)} %get-tuple-element.17.own), channel_id=1, source_target_pairs={{0,6},{1,7},{2,10},{3,11},{4,28},{5,13},{6,0},{7,1},{8,24},{9,15},... | collective-permute-start | bytes 196616 | tf_op jit(solution)/shard_map/ppermute | solution.py:298
  7.5 19.0 %collective-permute-start.5 = (f32[512,512]{1,0:T(8,128)S(1)}, f32[512,512]{1,0:T(8,128)S(1)}, u32[]{:S(2)}, u32[]{:S(2)}) collective-permute-start(f32[512,512]{1,0:T(8,128)S(1)} %get-tuple-element.23.near), channel_id=1, source_target_pairs={{10,0},{11,1}} | collective-permute-start | bytes 3145736 | tf_op jit(solution)/shard_map/ppermute | solution.py:301
  8.8 17.7 %collective-permute-start.4 = (f32[512,512]{1,0:T(8,128)S(1)}, f32[512,512]{1,0:T(8,128)S(1)}, u32[]{:S(2)}, u32[]{:S(2)}) collective-permute-start(f32[512,512]{1,0:T(8,128)S(1)} %get-tuple-element.23.near), channel_id=1, source_target_pairs={{0,8},{1,0},{2,10},{3,11},{4,12},{5,13},{6,14},{7,15},{8,9},{9,1},... | collective-permute-start | bytes 3145736 | tf_op jit(solution)/shard_map/ppermute | solution.py:298
  13.5 13.7 %collective-permute-start.6 = (f32[512,512]{1,0:T(8,128)S(1)}, f32[512,512]{1,0:T(8,128)S(1)}, u32[]{:S(2)}, u32[]{:S(2)}) collective-permute-start(f32[512,512]{1,0:T(8,128)S(1)} %get-tuple-element.23.near), channel_id=1, source_target_pairs={{0,8},{1,9},{2,10},{3,11},{4,12},{5,13},{6,14},{7,15},{8,0},{9,1},... | collective-permute-start | bytes 3145736 | tf_op jit(solution)/shard_map/ppermute | solution.py:298
  13.6 14.7 %collective-permute-start.13 = (f32[512,512]{1,0:T(8,128)S(1)}, f32[512,512]{1,0:T(8,128)S(1)}, u32[]{:S(2)}, u32[]{:S(2)}) collective-permute-start(f32[512,512]{1,0:T(8,128)S(1)} %get-tuple-element.23.near), channel_id=1, source_target_pairs={{13,15}} | collective-permute-start | bytes 3145736 | tf_op jit(solution)/shard_map/ppermute | solution.py:301
  14.4 12.2 %collective-permute-start.3 = (f32[128,512]{1,0:T(8,128)S(1)}, f32[128,512]{1,0:T(8,128)S(1)}, u32[]{:S(2)}, u32[]{:S(2)}) collective-permute-start(f32[128,512]{1,0:T(8,128)S(1)} %turn.1.out.own), channel_id=1, source_target_pairs={{0,1},{1,0},{2,10},{3,11},{4,12},{5,13},{6,14},{7,4},{8,24},{9,25}... | collective-permute-start | bytes 786440 | tf_op jit(solution)/shard_map/ppermute | solution.py:298
  28.1 3.9 %collective-permute-start.11 = (f32[128,512]{1,0:T(8,128)S(1)}, f32[128,512]{1,0:T(8,128)S(1)}, u32[]{:S(2)}, u32[]{:S(2)}) collective-permute-start(f32[128,512]{1,0:T(8,128)S(1)} %reduce_low.1), channel_id=1, source_target_pairs={{0,15},{1,9},{2,10},{3,11},{4,12},{5,13},{6,14},{7,8},{8,0},{9,1},... | collective-permute-start | bytes 786440 | tf_op jit(solution)/shard_map/ppermute | solution.py:298
  28.2 6.7 %collective-permute-start.12 = (f32[128,512]{1,0:T(8,128)S(1)}, f32[128,512]{1,0:T(8,128)S(1)}, u32[]{:S(2)}, u32[]{:S(2)}) collective-permute-start(f32[128,512]{1,0:T(8,128)S(1)} %reduce_low.1), channel_id=1, source_target_pairs={{0,12},{1,15},{2,10},{3,11},{4,8},{5,13},{6,14},{7,9},{8,0},{9,1},... | collective-permute-start | bytes 786440 | tf_op jit(solution)/shard_map/ppermute | solution.py:298
  28.2 9.4 %collective-permute-start.7 = (f32[128,512]{1,0:T(8,128)S(1)}, f32[128,512]{1,0:T(8,128)S(1)}, u32[]{:S(2)}, u32[]{:S(2)}) collective-permute-start(f32[128,512]{1,0:T(8,128)S(1)} %get-tuple-element.24.s_b), channel_id=1, source_target_pairs={{0,2},{1,3},{2,10},{3,11},{4,12},{5,13},{6,14},{7,15},{8,0},{9,1},... | collective-permute-start | bytes 786440 | tf_op jit(solution)/shard_map/ppermute | solution.py:298
  28.4 6.5 %copy-start.1 = (f32[512,512]{1,0:T(8,128)}, f32[512,512]{1,0:T(8,128)S(1)}, u32[]{:S(2)}) copy-start(f32[512,512]{1,0:T(8,128)S(1)} %collective-permute-done.13.last_block) | copy-start | bytes 3145732
  34.9 3.4 %collective-permute-start.14 = (f32[128,512]{1,0:T(8,128)S(1)}, f32[128,512]{1,0:T(8,128)S(1)}, u32[]{:S(2)}, u32[]{:S(2)}) collective-permute-start(f32[128,512]{1,0:T(8,128)S(1)} %solve_high.1.refs_4_), channel_id=1, source_target_pairs={{0,8},{1,9},{2,10},{3,11},{4,12},{5,13},{6,14},{7,15},{8,0},{9,1},... | collective-permute-start | bytes 786440 | tf_op jit(solution)/shard_map/ppermute | solution.py:298
  35.6 2.9 %collective-permute-start.15 = (f32[128,512]{1,0:T(8,128)S(1)}, f32[128,512]{1,0:T(8,128)S(1)}, u32[]{:S(2)}, u32[]{:S(2)}) collective-permute-start(f32[128,512]{1,0:T(8,128)S(1)} %solve_high.1.refs_4_), channel_id=1, source_target_pairs={{0,8},{1,9},{2,10},{3,11},{4,12},{5,4},{6,7},{7,15},{8,0},{9,1},{1... | collective-permute-start | bytes 786440 | tf_op jit(solution)/shard_map/ppermute | solution.py:298
  35.6 2.8 %collective-permute-start.16 = (f32[128,512]{1,0:T(8,128)S(1)}, f32[128,512]{1,0:T(8,128)S(1)}, u32[]{:S(2)}, u32[]{:S(2)}) collective-permute-start(f32[128,512]{1,0:T(8,128)S(1)} %solve_high.1.refs_4_), channel_id=1, source_target_pairs={{0,8},{1,9},{2,10},{3,11},{4,12},{5,13},{6,14},{7,15},{8,0},{9,1},... | collective-permute-start | bytes 786440 | tf_op jit(solution)/shard_map/ppermute | solution.py:298
  37.7 4.0 %collective-permute-start.8 = (f32[128,512]{1,0:T(8,128)S(1)}, f32[128,512]{1,0:T(8,128)S(1)}, u32[]{:S(2)}, u32[]{:S(2)}) collective-permute-start(f32[128,512]{1,0:T(8,128)S(1)} %broadcast_select_fusion.refs_0_), channel_id=1, source_target_pairs={{0,16},{1,17},{2,18},{3,19},{4,12},{5,13},{6,14},{7,15},{8,0},{9,1... | collective-permute-start | bytes 786440 | tf_op jit(solution)/shard_map/ppermute | solution.py:298
  37.8 4.3 %collective-permute-start.17 = (f32[128,512]{1,0:T(8,128)S(1)}, f32[128,512]{1,0:T(8,128)S(1)}, u32[]{:S(2)}, u32[]{:S(2)}) collective-permute-start(f32[128,512]{1,0:T(8,128)S(1)} %solve_high.1.refs_4_), channel_id=1, source_target_pairs={{0,8},{1,9},{2,10},{3,11},{4,12},{5,13},{6,14},{7,15},{8,0},{9,1},... | collective-permute-start | bytes 786440 | tf_op jit(solution)/shard_map/ppermute | solution.py:298
  38.3 3.8 %collective-permute-start.9 = (f32[128,512]{1,0:T(8,128)S(1)}, f32[128,512]{1,0:T(8,128)S(1)}, u32[]{:S(2)}, u32[]{:S(2)}) collective-permute-start(f32[128,512]{1,0:T(8,128)S(1)} %broadcast_select_fusion.refs_0_), channel_id=1, source_target_pairs={{0,8},{1,9},{2,10},{3,11},{4,12},{5,13},{6,14},{7,15},{8,0},{9,1},... | collective-permute-start | bytes 786440 | tf_op jit(solution)/shard_map/ppermute | solution.py:298
  38.5 3.6 %collective-permute-start.18 = (f32[128,512]{1,0:T(8,128)S(1)}, f32[128,512]{1,0:T(8,128)S(1)}, u32[]{:S(2)}, u32[]{:S(2)}) collective-permute-start(f32[128,512]{1,0:T(8,128)S(1)} %select_select_fusion.refs_5_), channel_id=1, source_target_pairs={{0,8},{1,9},{2,10},{3,11},{4,12},{5,13},{6,14},{7,15},{8,0},{9,1},... | collective-permute-start | bytes 786440 | tf_op jit(solution)/shard_map/ppermute | solution.py:298
  41.7 1.6 %collective-permute-start.10 = (f32[128,512]{1,0:T(8,128)S(1)}, f32[128,512]{1,0:T(8,128)S(1)}, u32[]{:S(2)}, u32[]{:S(2)}) collective-permute-start(f32[128,512]{1,0:T(8,128)S(1)} %collective-permute-done.8.refs_1_), channel_id=1, source_target_pairs={{0,8},{1,9},{2,10},{3,11},{4,12},{5,13},{6,14},{7,15},{8,0},{9,1},... | collective-permute-start | bytes 786440 | tf_op jit(solution)/shard_map/ppermute | solution.py:298
  46.6 36.1 %copy-start = (f32[6,1,1,128,128]{4,3,2,1,0:T(8,128)S(1)}, f32[6,1,1,128,128]{4,3,2,1,0:T(8,128)}, u32[]{:S(2)}) copy-start(f32[6,1,1,128,128]{4,3,2,1,0:T(8,128)} %rhs.1) | copy-start | bytes 1179652
  46.6 13.1 %collective-permute-start.19 = (f32[832,128]{1,0:T(8,128)S(1)}, f32[832,128]{1,0:T(8,128)S(1)}, u32[]{:S(2)}, u32[]{:S(2)}) collective-permute-start(f32[832,128]{1,0:T(8,128)S(1)} %get-tuple-element.26), channel_id=1, source_target_pairs={{0,2},{1,3},{2,0},{3,1},{4,6},{5,7},{6,4},{7,5},{8,10},{9,11},{10,... | collective-permute-start | bytes 1277960 | tf_op jit(solution)/shard_map/ppermute | solution.py:298
  49.1 33.2 %collective-permute-start.20 = (f32[840,128]{1,0:T(8,128)S(1)}, f32[840,128]{1,0:T(8,128)S(1)}, u32[]{:S(2)}, u32[]{:S(2)}) collective-permute-start(f32[840,128]{1,0:T(8,128)S(1)} %get-tuple-element.27), channel_id=1, source_target_pairs={{0,4},{1,5},{2,0},{3,1},{4,6},{5,7},{6,2},{7,3},{8,12},{9,13},{10,... | collective-permute-start | bytes 1290248 | tf_op jit(solution)/shard_map/ppermute | solution.py:298
  51.8 30.5 %collective-permute-start.22 = (f32[840,128]{1,0:T(8,128)S(1)}, f32[840,128]{1,0:T(8,128)S(1)}, u32[]{:S(2)}, u32[]{:S(2)}) collective-permute-start(f32[840,128]{1,0:T(8,128)S(1)} %get-tuple-element.27), channel_id=1, source_target_pairs={{0,8},{1,9},{2,4},{3,5},{4,2},{5,3},{6,14},{7,15},{8,0},{9,1},{10,... | collective-permute-start | bytes 1290248 | tf_op jit(solution)/shard_map/ppermute | solution.py:298
  55.1 27.2 %collective-permute-start.21 = (f32[840,128]{1,0:T(8,128)S(1)}, f32[840,128]{1,0:T(8,128)S(1)}, u32[]{:S(2)}, u32[]{:S(2)}) collective-permute-start(f32[840,128]{1,0:T(8,128)S(1)} %get-tuple-element.28.mine), channel_id=1, source_target_pairs={{6,4},{7,5},{14,12},{15,13},{22,20},{23,21},{30,28},{31,29},{0,2},... | collective-permute-start | bytes 1290248 | tf_op jit(solution)/shard_map/ppermute | solution.py:301
  59.7 23.0 %collective-permute-start.23 = (f32[832,128]{1,0:T(8,128)S(1)}, f32[832,128]{1,0:T(8,128)S(1)}, u32[]{:S(2)}, u32[]{:S(2)}) collective-permute-start(f32[832,128]{1,0:T(8,128)S(1)} %join.1), channel_id=1, source_target_pairs={{4,0},{5,1},{12,8},{13,9},{20,16},{21,17},{28,24},{29,25},{2,6},{3... | collective-permute-start | bytes 1277960 | tf_op jit(solution)/shard_map/ppermute | solution.py:301
  61.0 21.3 %collective-permute-start.24 = (f32[64,128]{1,0:T(8,128)S(1)}, f32[64,128]{1,0:T(8,128)S(1)}, u32[]{:S(2)}, u32[]{:S(2)}) collective-permute-start(f32[64,128]{1,0:T(8,128)S(1)} %get-tuple-element.29), channel_id=1, source_target_pairs={{0,6},{1,7},{2,4},{3,5},{4,2},{5,3},{6,0},{7,1},{8,14},{9,15},{10,... | collective-permute-start | bytes 98312 | tf_op jit(solution)/shard_map/ppermute | solution.py:298

commit v18 on v17

--- a/solution.py
+++ b/solution.py
@@ -433,8 +433,8 @@
         return s, far, send(s, near_twins), send(far, far_twins)
 
     spots = [(g // groups, g % groups) for g in range(4)]
-    homes = (tuple(spots[:2]), tuple(spots[:2]), (spots[2],), (spots[3],))
-    moved = send(lax.optimization_barrier((s_1, w))[0], [(line(g, 0), line(g, 1)) for g in (0, 1)])
+    homes = (tuple(spots[:2]), (spots[1],), (spots[2],), (spots[3],))
+    moved = send(s_1, [(line(1, 0), line(1, 1))])
     s_low = jnp.where(member == 0, s_0, moved)
     ways = spread(s_low, {0: homes[0], 1: homes[1]}) + spread(s_high, {2: homes[2], 3: homes[3]})
 

time: 83.9 us -> 81.1 us (0.967)
  waiting for transfers between devices: 44.2 us -> 34.2 us
  starting transfers between devices: 25.9 us -> 32.2 us
  Pallas kernels: 12.6 us -> 13.5 us
    ppermute x21 -> x23, waiting for transfers between devices: 43.8 us -> 33.8 us  [send(): return lax.ppermute(x, AXES, sorted(onward.items()))]
    ppermute x21 -> x23, starting transfers between devices: 18.2 us -> 24.3 us  [send(): return lax.ppermute(x, AXES, sorted(onward.items()))]
    pallas_call x1, Pallas kernels: 0.82 us -> 1.71 us  [on_device(): pl.pallas_call(functools.partial(reduce_kernel, low_homes, col_count), in...]
  transfers between devices with their start and end apart: 25 -> 27, of which waited for: 10 -> 12; matrix products, arithmetic and copies ran while one was open for 0% -> 0% of each run, Pallas kernels for 8% -> 10%
where the time goes in v18:
time: 81.1 us; the launch traced here: 80.9 us
  waiting for transfers between devices  34.2 us (42%)
  starting transfers between devices  32.2 us (40%)
  Pallas kernels  13.5 us (17%)
  between operations  0.86 us (1%)
    ppermute x23, waiting for transfers between devices, send(): return lax.ppermute(x, AXES, sorted(onward.items()))  33.8 us
    ppermute x23, starting transfers between devices, send(): return lax.ppermute(x, AXES, sorted(onward.items()))  24.3 us
    ppermute x4, starting transfers between devices, send_some(): return lax.ppermute(x, AXES, pairs)  7.9 us
    pallas_call x2, Pallas kernels, update(): pl.pallas_call(functools.partial(update_kernel, (groups, row_count, share...  6.55 us
    pallas_call x1, Pallas kernels, on_device(): pl.pallas_call(functools.partial(reduce_kernel, low_homes, col_count), in...  1.71 us
    pallas_call x1, Pallas kernels, on_device(): pl.pallas_call(functools.partial(ready_kernel, low_homes, col_count), in_...  1.69 us
  transfers between devices with their start and end apart: 27, of which 12 were waited for; matrix products, arithmetic and copies ran while one was open for 0% of the time, Pallas kernels for 10%

profile of v18, /device:TPU:0, one launch (start us, length us, event | category | flops | bytes accessed | tf_op | source)
XLA Modules:
  0.0 80.9 jit_solution(17171338560811015660)
XLA Ops:
  0.6 1.3 %fetch.1 = (f32[512,512]{1,0:T(8,128)S(1)}, f32[128,128]{1,0:T(8,128)S(1)}) custom-call(f32[6,1,1,512,512]{4,3,2,1,0:T(8,128)} %refs_8_.3, f32[6,1,1,128,128]{4,3,2,1,0:T(8,128)} %rhs.1), custom_call_target="tpu_custom_call" | custom-call | flops 1000 | bytes 1000 | tf_op jit(solution)/shard_map/fetch/pallas_call | solution.py:314
  1.9 1.3 %collective-permute-start.5 = (f32[512,512]{1,0:T(8,128)S(1)}, f32[512,512]{1,0:T(8,128)S(1)}, u32[]{:S(2)}, u32[]{:S(2)}) collective-permute-start(f32[512,512]{1,0:T(8,128)S(1)} %get-tuple-element.22.near), channel_id=1, source_target_pairs={{10,0},{11,1}} | collective-permute-start | bytes 3145736 | tf_op jit(solution)/shard_map/ppermute | solution.py:301
  3.2 0.1 collective-permute-start.4
  3.3 2.9 %collective-permute-start = (f32[128,128]{1,0:T(8,128)S(1)}, f32[128,128]{1,0:T(8,128)S(1)}, u32[]{:S(2)}, u32[]{:S(2)}) collective-permute-start(f32[128,128]{1,0:T(8,128)S(1)} %get-tuple-element.16.own), channel_id=1, source_target_pairs={{0,2},{1,9},{2,0},{3,1},{4,28},{5,13},{6,14},{7,5},{8,24},{9,11},{... | collective-permute-start | bytes 196616 | tf_op jit(solution)/shard_map/ppermute | solution.py:298
  6.2 2.1 %collective-permute-start.1 = (f32[128,128]{1,0:T(8,128)S(1)}, f32[128,128]{1,0:T(8,128)S(1)}, u32[]{:S(2)}, u32[]{:S(2)}) collective-permute-start(f32[128,128]{1,0:T(8,128)S(1)} %get-tuple-element.16.own), channel_id=1, source_target_pairs={{0,4},{1,9},{2,10},{3,11},{4,0},{5,1},{6,14},{7,3},{8,12},{9,13},{... | collective-permute-start | bytes 196616 | tf_op jit(solution)/shard_map/ppermute | solution.py:298
  8.3 0.0 collective-permute-start.2
  8.3 1.7 %ready.1 = (bf16[2,512,512]{2,1,0:T(8,128)(2,1)S(1)}, bf16[2,512,512]{2,1,0:T(8,128)(2,1)S(1)}) custom-call(f32[4,512,512]{2,1,0:T(8,128)} %inverses.3), custom_call_target="tpu_custom_call" | custom-call | flops 1000 | bytes 1000 | tf_op jit(solution)/shard_map/ready/pallas_call | solution.py:326
  10.0 0.0 collective-permute-done.g1
  10.1 1.4 %collective-permute-done.1.g2 = f32[128,128]{1,0:T(8,128)S(1)} collective-permute-done((f32[128,128]{1,0:T(8,128)S(1)}, f32[128,128]{1,0:T(8,128)S(1)}, u32[]{:S(2)}, u32[]{:S(2)}) %collective-permute-start.1) | collective-permute-done | bytes 65568 | tf_op jit(solution)/shard_map/ppermute | solution.py:298
  11.5 3.0 %collective-permute-done.2.g3 = f32[128,128]{1,0:T(8,128)S(1)} collective-permute-done((f32[128,128]{1,0:T(8,128)S(1)}, f32[128,128]{1,0:T(8,128)S(1)}, u32[]{:S(2)}, u32[]{:S(2)}) %collective-permute-start.2) | collective-permute-done | bytes 65568 | tf_op jit(solution)/shard_map/ppermute | solution.py:298
  14.5 0.5 turn.1.out.own
  15.0 0.1 collective-permute-start.12
  15.1 1.6 %collective-permute-start.15 = (f32[512,512]{1,0:T(8,128)S(1)}, f32[512,512]{1,0:T(8,128)}, u32[]{:S(2)}, u32[]{:S(2)}) collective-permute-start(f32[512,512]{1,0:T(8,128)S(1)} %get-tuple-element.22.near), channel_id=1, source_target_pairs={{13,15}} | collective-permute-start | bytes 3145736 | tf_op jit(solution)/shard_map/ppermute | solution.py:301
  16.7 0.8 %collective-permute-start.3 = (f32[128,512]{1,0:T(8,128)S(1)}, f32[128,512]{1,0:T(8,128)S(1)}, u32[]{:S(2)}, u32[]{:S(2)}) collective-permute-start(f32[128,512]{1,0:T(8,128)S(1)} %turn.1.out.own), channel_id=1, source_target_pairs={{0,1},{1,0},{2,10},{3,11},{4,12},{5,13},{6,14},{7,4},{8,24},{9,25}... | collective-permute-start | bytes 786440 | tf_op jit(solution)/shard_map/ppermute | solution.py:298
  17.6 5.5 %collective-permute-done.3.swapped = f32[128,512]{1,0:T(8,128)S(1)} collective-permute-done((f32[128,512]{1,0:T(8,128)S(1)}, f32[128,512]{1,0:T(8,128)S(1)}, u32[]{:S(2)}, u32[]{:S(2)}) %collective-permute-start.3) | collective-permute-done | bytes 262176 | tf_op jit(solution)/shard_map/ppermute | solution.py:298
  23.1 0.0 collective-permute-done.5.ly
  23.1 0.0 collective-permute-done.4.la
  23.1 0.8 solve_low.1
  23.9 0.1 collective-permute-start.6
  24.0 0.0 collective-permute-done.12.lx
  24.0 1.7 %reduce_low.1 = f32[128,512]{1,0:T(8,128)S(1)} custom-call(f32[128,512]{1,0:T(8,128)S(1)} %get-tuple-element.20.s_a, f32[128,512]{1,0:T(8,128)S(1)} %get-tuple-element.21.s_b, f32[512,512]{1,0:T(8,128)} %collective-permute-done.12.lx, f32[512,512]{1,0:T(8,128)S(1)} %collective-permute-done.5.ly), custom_call_target="tpu_custom_call" | custom-call | flops 1000 | bytes 1000 | tf_op jit(solution)/shard_map/reduce_low/pallas_call | solution.py:372
  25.7 0.1 collective-permute-start.13
  25.8 0.1 collective-permute-start.14
  25.8 0.0 collective-permute-done.6
  25.9 0.6 collective-permute-start.7
  26.4 0.1 collective-permute-start.8
  26.5 0.0 collective-permute-done.15.last_block
  26.5 0.0 collective-permute-start.9
  26.5 3.1 %collective-permute-done.13.w_1 = f32[128,512]{1,0:T(8,128)S(1)} collective-permute-done((f32[128,512]{1,0:T(8,128)S(1)}, f32[128,512]{1,0:T(8,128)S(1)}, u32[]{:S(2)}, u32[]{:S(2)}) %collective-permute-start.13) | collective-permute-done | bytes 262176 | tf_op jit(solution)/shard_map/ppermute | solution.py:298
  29.6 2.8 %collective-permute-done.14.w_2 = f32[128,512]{1,0:T(8,128)S(1)} collective-permute-done((f32[128,512]{1,0:T(8,128)S(1)}, f32[128,512]{1,0:T(8,128)S(1)}, u32[]{:S(2)}, u32[]{:S(2)}) %collective-permute-start.14) | collective-permute-done | bytes 262176 | tf_op jit(solution)/shard_map/ppermute | solution.py:298
  32.5 0.6 collective-permute-start.16
  33.1 0.1 collective-permute-start.17
  33.1 0.0 collective-permute-done.7
  33.1 0.5 collective-permute-start.18
  33.6 0.0 collective-permute-done.8
  33.6 0.1 collective-permute-start.10
  33.7 0.0 collective-permute-done.9
  33.7 0.4 collective-permute-start.19
  34.1 0.1 select_select_fusion.1.refs_1_
  34.2 0.1 collective-permute-done.16
  34.3 0.4 collective-permute-start.11
  34.6 0.0 collective-permute-done.17
  34.6 0.4 collective-permute-done.18
  35.0 0.1 select_select_fusion.refs_5_
  35.1 0.4 collective-permute-start.20
  35.5 0.0 collective-permute-done.10.refs_2_
  35.5 0.2 collective-permute-done.19.refs_6_
  35.8 0.4 collective-permute-done.11.refs_3_
  36.1 0.5 collective-permute-done.20.refs_7_
  36.7 3.3 %update_first.1 = (f32[832,128]{1,0:T(8,128)S(1)}, f32[840,128]{1,0:T(8,128)S(1)}, f32[64,128]{1,0:T(8,128)S(1)}) custom-call(f32[128,512]{1,0:T(8,128)S(1)} %broadcast_select_fusion.refs_0_, f32[128,512]{1,0:T(8,128)S(1)} %select_select_fusion.1.refs_1_, f32[128,512]{1,0:T(8,128)S(1)} %collective-permute-done.10.refs_2_, ...), custom_call_target="tpu_custom_call" | custom-call | flops 1000 | bytes 1000 | tf_op jit(solution)/shard_map/update_first/pallas_call | solution.py:447
  39.9 0.0 copy-start
  40.0 1.8 %collective-permute-start.21 = (f32[832,128]{1,0:T(8,128)S(1)}, f32[832,128]{1,0:T(8,128)S(1)}, u32[]{:S(2)}, u32[]{:S(2)}) collective-permute-start(f32[832,128]{1,0:T(8,128)S(1)} %get-tuple-element.24), channel_id=1, source_target_pairs={{0,2},{1,3},{2,0},{3,1},{4,6},{5,7},{6,4},{7,5},{8,10},{9,11},{10,... | collective-permute-start | bytes 1277960 | tf_op jit(solution)/shard_map/ppermute | solution.py:298
  41.7 8.1 %collective-permute-start.22 = (f32[840,128]{1,0:T(8,128)S(1)}, f32[840,128]{1,0:T(8,128)S(1)}, u32[]{:S(2)}, u32[]{:S(2)}) collective-permute-start(f32[840,128]{1,0:T(8,128)S(1)} %get-tuple-element.25), channel_id=1, source_target_pairs={{0,4},{1,5},{2,0},{3,1},{4,6},{5,7},{6,2},{7,3},{8,12},{9,13},{10,... | collective-permute-start | bytes 1290248 | tf_op jit(solution)/shard_map/ppermute | solution.py:298
  49.8 0.0 collective-permute-start.24
  49.8 3.3 %update_second.1 = (f32[832,128]{1,0:T(8,128)S(1)}, f32[840,128]{1,0:T(8,128)S(1)}) custom-call(f32[128,512]{1,0:T(8,128)S(1)} %broadcast_select_fusion.refs_0_, f32[128,512]{1,0:T(8,128)S(1)} %select_select_fusion.1.refs_1_, f32[128,512]{1,0:T(8,128)S(1)} %collective-permute-done.10.refs_2_, f32[128,512]{1,0:T(8,128)S(1)} %collective-permute-done.11.refs_3_, ...), custom_call_target="tpu_custom_call" | custom-call | flops 1000 | bytes 1000 | tf_op jit(solution)/shard_map/update_second/pallas_call | solution.py:447
  53.1 3.7 %collective-permute-start.23 = (f32[840,128]{1,0:T(8,128)S(1)}, f32[840,128]{1,0:T(8,128)S(1)}, u32[]{:S(2)}, u32[]{:S(2)}) collective-permute-start(f32[840,128]{1,0:T(8,128)S(1)} %get-tuple-element.26.mine), channel_id=1, source_target_pairs={{6,4},{7,5},{14,12},{15,13},{22,20},{23,21},{30,28},{31,29},{0,2},... | collective-permute-start | bytes 1290248 | tf_op jit(solution)/shard_map/ppermute | solution.py:301
  56.7 0.0 collective-permute-done.21.theirs.got_1
  56.8 1.3 %collective-permute-start.25 = (f32[832,128]{1,0:T(8,128)S(1)}, f32[832,128]{1,0:T(8,128)S(1)}, u32[]{:S(2)}, u32[]{:S(2)}) collective-permute-start(f32[832,128]{1,0:T(8,128)S(1)} %join.1), channel_id=1, source_target_pairs={{4,0},{5,1},{12,8},{13,9},{20,16},{21,17},{28,24},{29,25},{2,6},{3... | collective-permute-start | bytes 1277960 | tf_op jit(solution)/shard_map/ppermute | solution.py:301
  58.1 5.2 %collective-permute-start.26 = (f32[64,128]{1,0:T(8,128)S(1)}, f32[64,128]{1,0:T(8,128)S(1)}, u32[]{:S(2)}, u32[]{:S(2)}) collective-permute-start(f32[64,128]{1,0:T(8,128)S(1)} %get-tuple-element.27), channel_id=1, source_target_pairs={{0,6},{1,7},{2,4},{3,5},{4,2},{5,3},{6,0},{7,1},{8,14},{9,15},{10,... | collective-permute-start | bytes 98312 | tf_op jit(solution)/shard_map/ppermute | solution.py:298
  63.2 16.3 %collective-permute-done.26.far = f32[64,128]{1,0:T(8,128)S(1)} collective-permute-done((f32[64,128]{1,0:T(8,128)S(1)}, f32[64,128]{1,0:T(8,128)S(1)}, u32[]{:S(2)}, u32[]{:S(2)}) %collective-permute-start.26) | collective-permute-done | bytes 32800 | tf_op jit(solution)/shard_map/ppermute | solution.py:298
  79.5 0.0 collective-permute-done.22.got_2
  79.5 0.0 collective-permute-done.23.got_3
  79.5 0.3 collective-permute-done.25.joined
  79.9 1.0 %add_up.1 = (f32[4,64,128]{2,1,0:T(8,128)}, f32[6,128,128]{2,1,0:T(8,128)}) custom-call(f32[6,128,128]{2,1,0:T(8,128)S(1)} %bitcast.4, f32[832,128]{1,0:T(8,128)S(1)} %get-tuple-element.23.own, f32[832,128]{1,0:T(8,128)S(1)} %collective-permute-done.21.theirs.got_1, f32[840,128]{1,0:T(8,128)S(1)} %collective-permute-done.22.got_2, ...), custom_call_target="tpu_custom_call" | custom-call | flops 1000 | bytes 1000 | tf_op jit(solution)/shard_map/add_up/pallas_call | solution.py:488
  (5 shorter events, 0.1 us)
Async XLA Ops:
  1.9 21.2 %collective-permute-start.5 = (f32[512,512]{1,0:T(8,128)S(1)}, f32[512,512]{1,0:T(8,128)S(1)}, u32[]{:S(2)}, u32[]{:S(2)}) collective-permute-start(f32[512,512]{1,0:T(8,128)S(1)} %get-tuple-element.22.near), channel_id=1, source_target_pairs={{10,0},{11,1}} | collective-permute-start | bytes 3145736 | tf_op jit(solution)/shard_map/ppermute | solution.py:301
  3.2 19.9 %collective-permute-start.4 = (f32[512,512]{1,0:T(8,128)S(1)}, f32[512,512]{1,0:T(8,128)S(1)}, u32[]{:S(2)}, u32[]{:S(2)}) collective-permute-start(f32[512,512]{1,0:T(8,128)S(1)} %get-tuple-element.22.near), channel_id=1, source_target_pairs={{0,8},{1,0},{2,10},{3,11},{4,12},{5,13},{6,14},{7,15},{8,9},{9,1},... | collective-permute-start | bytes 3145736 | tf_op jit(solution)/shard_map/ppermute | solution.py:298
  3.3 6.7 %collective-permute-start = (f32[128,128]{1,0:T(8,128)S(1)}, f32[128,128]{1,0:T(8,128)S(1)}, u32[]{:S(2)}, u32[]{:S(2)}) collective-permute-start(f32[128,128]{1,0:T(8,128)S(1)} %get-tuple-element.16.own), channel_id=1, source_target_pairs={{0,2},{1,9},{2,0},{3,1},{4,28},{5,13},{6,14},{7,5},{8,24},{9,11},{... | collective-permute-start | bytes 196616 | tf_op jit(solution)/shard_map/ppermute | solution.py:298
  6.2 5.3 %collective-permute-start.1 = (f32[128,128]{1,0:T(8,128)S(1)}, f32[128,128]{1,0:T(8,128)S(1)}, u32[]{:S(2)}, u32[]{:S(2)}) collective-permute-start(f32[128,128]{1,0:T(8,128)S(1)} %get-tuple-element.16.own), channel_id=1, source_target_pairs={{0,4},{1,9},{2,10},{3,11},{4,0},{5,1},{6,14},{7,3},{8,12},{9,13},{... | collective-permute-start | bytes 196616 | tf_op jit(solution)/shard_map/ppermute | solution.py:298
  8.3 6.2 %collective-permute-start.2 = (f32[128,128]{1,0:T(8,128)S(1)}, f32[128,128]{1,0:T(8,128)S(1)}, u32[]{:S(2)}, u32[]{:S(2)}) collective-permute-start(f32[128,128]{1,0:T(8,128)S(1)} %get-tuple-element.16.own), channel_id=1, source_target_pairs={{0,6},{1,7},{2,10},{3,11},{4,28},{5,13},{6,0},{7,1},{8,24},{9,15},... | collective-permute-start | bytes 196616 | tf_op jit(solution)/shard_map/ppermute | solution.py:298
  15.0 9.0 %collective-permute-start.12 = (f32[512,512]{1,0:T(8,128)S(1)}, f32[512,512]{1,0:T(8,128)}, u32[]{:S(2)}, u32[]{:S(2)}) collective-permute-start(f32[512,512]{1,0:T(8,128)S(1)} %get-tuple-element.22.near), channel_id=1, source_target_pairs={{0,8},{1,9},{2,10},{3,11},{4,12},{5,13},{6,14},{7,15},{8,0},{9,1},... | collective-permute-start | bytes 3145736 | tf_op jit(solution)/shard_map/ppermute | solution.py:298
  15.1 11.5 %collective-permute-start.15 = (f32[512,512]{1,0:T(8,128)S(1)}, f32[512,512]{1,0:T(8,128)}, u32[]{:S(2)}, u32[]{:S(2)}) collective-permute-start(f32[512,512]{1,0:T(8,128)S(1)} %get-tuple-element.22.near), channel_id=1, source_target_pairs={{13,15}} | collective-permute-start | bytes 3145736 | tf_op jit(solution)/shard_map/ppermute | solution.py:301
  16.7 6.4 %collective-permute-start.3 = (f32[128,512]{1,0:T(8,128)S(1)}, f32[128,512]{1,0:T(8,128)S(1)}, u32[]{:S(2)}, u32[]{:S(2)}) collective-permute-start(f32[128,512]{1,0:T(8,128)S(1)} %turn.1.out.own), channel_id=1, source_target_pairs={{0,1},{1,0},{2,10},{3,11},{4,12},{5,13},{6,14},{7,4},{8,24},{9,25}... | collective-permute-start | bytes 786440 | tf_op jit(solution)/shard_map/ppermute | solution.py:298
  23.9 2.0 %collective-permute-start.6 = (f32[128,512]{1,0:T(8,128)S(1)}, f32[128,512]{1,0:T(8,128)S(1)}, u32[]{:S(2)}, u32[]{:S(2)}) collective-permute-start(f32[128,512]{1,0:T(8,128)S(1)} %get-tuple-element.21.s_b), channel_id=1, source_target_pairs={{0,8},{1,3},{2,10},{3,11},{4,12},{5,13},{6,14},{7,15},{8,0},{9,1},... | collective-permute-start | bytes 786440 | tf_op jit(solution)/shard_map/ppermute | solution.py:298
  25.7 3.9 %collective-permute-start.13 = (f32[128,512]{1,0:T(8,128)S(1)}, f32[128,512]{1,0:T(8,128)S(1)}, u32[]{:S(2)}, u32[]{:S(2)}) collective-permute-start(f32[128,512]{1,0:T(8,128)S(1)} %reduce_low.1), channel_id=1, source_target_pairs={{0,15},{1,9},{2,10},{3,11},{4,12},{5,13},{6,14},{7,8},{8,0},{9,1},... | collective-permute-start | bytes 786440 | tf_op jit(solution)/shard_map/ppermute | solution.py:298
  25.8 6.7 %collective-permute-start.14 = (f32[128,512]{1,0:T(8,128)S(1)}, f32[128,512]{1,0:T(8,128)S(1)}, u32[]{:S(2)}, u32[]{:S(2)}) collective-permute-start(f32[128,512]{1,0:T(8,128)S(1)} %reduce_low.1), channel_id=1, source_target_pairs={{0,12},{1,15},{2,10},{3,11},{4,8},{5,13},{6,14},{7,9},{8,0},{9,1},... | collective-permute-start | bytes 786440 | tf_op jit(solution)/shard_map/ppermute | solution.py:298
  25.9 7.3 %collective-permute-start.7 = (f32[128,512]{1,0:T(8,128)S(1)}, f32[128,512]{1,0:T(8,128)S(1)}, u32[]{:S(2)}, u32[]{:S(2)}) collective-permute-start(f32[128,512]{1,0:T(8,128)S(1)} %broadcast_select_fusion.refs_0_), channel_id=1, source_target_pairs={{0,8},{1,9},{2,10},{3,18},{4,12},{5,13},{6,14},{7,15},{8,0},{9,1},... | collective-permute-start | bytes 786440 | tf_op jit(solution)/shard_map/ppermute | solution.py:298
  26.4 7.2 %collective-permute-start.8 = (f32[128,512]{1,0:T(8,128)S(1)}, f32[128,512]{1,0:T(8,128)S(1)}, u32[]{:S(2)}, u32[]{:S(2)}) collective-permute-start(f32[128,512]{1,0:T(8,128)S(1)} %broadcast_select_fusion.refs_0_), channel_id=1, source_target_pairs={{0,8},{1,9},{2,10},{3,2},{4,12},{5,13},{6,14},{7,15},{8,0},{9,1},{... | collective-permute-start | bytes 786440 | tf_op jit(solution)/shard_map/ppermute | solution.py:298
  26.5 7.2 %collective-permute-start.9 = (f32[128,512]{1,0:T(8,128)S(1)}, f32[128,512]{1,0:T(8,128)S(1)}, u32[]{:S(2)}, u32[]{:S(2)}) collective-permute-start(f32[128,512]{1,0:T(8,128)S(1)} %broadcast_select_fusion.refs_0_), channel_id=1, source_target_pairs={{0,16},{1,17},{2,10},{3,19},{4,12},{5,13},{6,14},{7,15},{8,0},{9,1... | collective-permute-start | bytes 786440 | tf_op jit(solution)/shard_map/ppermute | solution.py:298
  32.5 1.8 %collective-permute-start.16 = (f32[128,512]{1,0:T(8,128)S(1)}, f32[128,512]{1,0:T(8,128)S(1)}, u32[]{:S(2)}, u32[]{:S(2)}) collective-permute-start(f32[128,512]{1,0:T(8,128)S(1)} %solve_high.1.refs_4_), channel_id=1, source_target_pairs={{0,8},{1,9},{2,10},{3,11},{4,12},{5,13},{6,14},{7,15},{8,0},{9,1},... | collective-permute-start | bytes 786440 | tf_op jit(solution)/shard_map/ppermute | solution.py:298
  33.1 1.5 %collective-permute-start.17 = (f32[128,512]{1,0:T(8,128)S(1)}, f32[128,512]{1,0:T(8,128)S(1)}, u32[]{:S(2)}, u32[]{:S(2)}) collective-permute-start(f32[128,512]{1,0:T(8,128)S(1)} %solve_high.1.refs_4_), channel_id=1, source_target_pairs={{0,8},{1,9},{2,10},{3,11},{4,12},{5,4},{6,7},{7,15},{8,0},{9,1},{1... | collective-permute-start | bytes 786440 | tf_op jit(solution)/shard_map/ppermute | solution.py:298
  33.1 1.9 %collective-permute-start.18 = (f32[128,512]{1,0:T(8,128)S(1)}, f32[128,512]{1,0:T(8,128)S(1)}, u32[]{:S(2)}, u32[]{:S(2)}) collective-permute-start(f32[128,512]{1,0:T(8,128)S(1)} %solve_high.1.refs_4_), channel_id=1, source_target_pairs={{0,8},{1,9},{2,10},{3,11},{4,12},{5,13},{6,14},{7,15},{8,0},{9,1},... | collective-permute-start | bytes 786440 | tf_op jit(solution)/shard_map/ppermute | solution.py:298
  33.6 1.9 %collective-permute-start.10 = (f32[128,512]{1,0:T(8,128)S(1)}, f32[128,512]{1,0:T(8,128)S(1)}, u32[]{:S(2)}, u32[]{:S(2)}) collective-permute-start(f32[128,512]{1,0:T(8,128)S(1)} %broadcast_select_fusion.refs_0_), channel_id=1, source_target_pairs={{0,8},{1,9},{2,10},{3,11},{4,12},{5,13},{6,14},{7,15},{8,0},{9,1},... | collective-permute-start | bytes 786440 | tf_op jit(solution)/shard_map/ppermute | solution.py:298
  33.7 2.1 %collective-permute-start.19 = (f32[128,512]{1,0:T(8,128)S(1)}, f32[128,512]{1,0:T(8,128)S(1)}, u32[]{:S(2)}, u32[]{:S(2)}) collective-permute-start(f32[128,512]{1,0:T(8,128)S(1)} %solve_high.1.refs_4_), channel_id=1, source_target_pairs={{0,8},{1,9},{2,10},{3,11},{4,12},{5,13},{6,14},{7,15},{8,0},{9,1},... | collective-permute-start | bytes 786440 | tf_op jit(solution)/shard_map/ppermute | solution.py:298
  34.3 1.9 %collective-permute-start.11 = (f32[128,512]{1,0:T(8,128)S(1)}, f32[128,512]{1,0:T(8,128)S(1)}, u32[]{:S(2)}, u32[]{:S(2)}) collective-permute-start(f32[128,512]{1,0:T(8,128)S(1)} %select_select_fusion.1.refs_1_), channel_id=1, source_target_pairs={{0,8},{1,9},{2,10},{3,11},{4,12},{5,13},{6,14},{7,15},{8,0},{9,1},... | collective-permute-start | bytes 786440 | tf_op jit(solution)/shard_map/ppermute | solution.py:298
  35.1 1.6 %collective-permute-start.20 = (f32[128,512]{1,0:T(8,128)S(1)}, f32[128,512]{1,0:T(8,128)S(1)}, u32[]{:S(2)}, u32[]{:S(2)}) collective-permute-start(f32[128,512]{1,0:T(8,128)S(1)} %select_select_fusion.refs_5_), channel_id=1, source_target_pairs={{0,8},{1,9},{2,10},{3,11},{4,12},{5,13},{6,14},{7,15},{8,0},{9,1},... | collective-permute-start | bytes 786440 | tf_op jit(solution)/shard_map/ppermute | solution.py:298
  39.9 39.9 %copy-start = (f32[6,1,1,128,128]{4,3,2,1,0:T(8,128)S(1)}, f32[6,1,1,128,128]{4,3,2,1,0:T(8,128)}, u32[]{:S(2)}) copy-start(f32[6,1,1,128,128]{4,3,2,1,0:T(8,128)} %rhs.1) | copy-start | bytes 1179652
  40.0 16.8 %collective-permute-start.21 = (f32[832,128]{1,0:T(8,128)S(1)}, f32[832,128]{1,0:T(8,128)S(1)}, u32[]{:S(2)}, u32[]{:S(2)}) collective-permute-start(f32[832,128]{1,0:T(8,128)S(1)} %get-tuple-element.24), channel_id=1, source_target_pairs={{0,2},{1,3},{2,0},{3,1},{4,6},{5,7},{6,4},{7,5},{8,10},{9,11},{10,... | collective-permute-start | bytes 1277960 | tf_op jit(solution)/shard_map/ppermute | solution.py:298
  41.7 37.8 %collective-permute-start.22 = (f32[840,128]{1,0:T(8,128)S(1)}, f32[840,128]{1,0:T(8,128)S(1)}, u32[]{:S(2)}, u32[]{:S(2)}) collective-permute-start(f32[840,128]{1,0:T(8,128)S(1)} %get-tuple-element.25), channel_id=1, source_target_pairs={{0,4},{1,5},{2,0},{3,1},{4,6},{5,7},{6,2},{7,3},{8,12},{9,13},{10,... | collective-permute-start | bytes 1290248 | tf_op jit(solution)/shard_map/ppermute | solution.py:298
  49.8 29.7 %collective-permute-start.24 = (f32[840,128]{1,0:T(8,128)S(1)}, f32[840,128]{1,0:T(8,128)S(1)}, u32[]{:S(2)}, u32[]{:S(2)}) collective-permute-start(f32[840,128]{1,0:T(8,128)S(1)} %get-tuple-element.25), channel_id=1, source_target_pairs={{0,8},{1,9},{2,4},{3,5},{4,2},{5,3},{6,14},{7,15},{8,0},{9,1},{10,... | collective-permute-start | bytes 1290248 | tf_op jit(solution)/shard_map/ppermute | solution.py:298
  53.1 26.5 %collective-permute-start.23 = (f32[840,128]{1,0:T(8,128)S(1)}, f32[840,128]{1,0:T(8,128)S(1)}, u32[]{:S(2)}, u32[]{:S(2)}) collective-permute-start(f32[840,128]{1,0:T(8,128)S(1)} %get-tuple-element.26.mine), channel_id=1, source_target_pairs={{6,4},{7,5},{14,12},{15,13},{22,20},{23,21},{30,28},{31,29},{0,2},... | collective-permute-start | bytes 1290248 | tf_op jit(solution)/shard_map/ppermute | solution.py:301
  56.8 23.1 %collective-permute-start.25 = (f32[832,128]{1,0:T(8,128)S(1)}, f32[832,128]{1,0:T(8,128)S(1)}, u32[]{:S(2)}, u32[]{:S(2)}) collective-permute-start(f32[832,128]{1,0:T(8,128)S(1)} %join.1), channel_id=1, source_target_pairs={{4,0},{5,1},{12,8},{13,9},{20,16},{21,17},{28,24},{29,25},{2,6},{3... | collective-permute-start | bytes 1277960 | tf_op jit(solution)/shard_map/ppermute | solution.py:301
  58.1 21.4 %collective-permute-start.26 = (f32[64,128]{1,0:T(8,128)S(1)}, f32[64,128]{1,0:T(8,128)S(1)}, u32[]{:S(2)}, u32[]{:S(2)}) collective-permute-start(f32[64,128]{1,0:T(8,128)S(1)} %get-tuple-element.27), channel_id=1, source_target_pairs={{0,6},{1,7},{2,4},{3,5},{4,2},{5,3},{6,0},{7,1},{8,14},{9,15},{10,... | collective-permute-start | bytes 98312 | tf_op jit(solution)/shard_map/ppermute | solution.py:298

commit v19 on v18

--- a/solution.py
+++ b/solution.py
@@ -360,6 +360,7 @@
     last_block = send_some(later, [(line(3, 2), high_homes[1])])
     last_block = pltpu.with_memory_space_constraint(last_block, pltpu.HBM)
     lx = send(later, [(line(2, 0), low_homes[0]), (line(3, 0), low_homes[1])])
+    lx = pltpu.with_memory_space_constraint(lx, pltpu.HBM)
     s_0, s_1 = pl.pallas_call(
         functools.partial(low_kernel, low_homes, col_count),
         in_specs=[vmem] * 6 + [pl.BlockSpec(memory_space=pl.ANY)],

time: 81.1 us -> 81.1 us (level)
  no operation moved by 1% of the time
where the time goes in v19:
time: 81.1 us; the launch traced here: 80.9 us
  waiting for transfers between devices  34.2 us (42%)
  starting transfers between devices  32.2 us (40%)
  Pallas kernels  13.5 us (17%)
  between operations  0.86 us (1%)
    ppermute x23, waiting for transfers between devices, send(): return lax.ppermute(x, AXES, sorted(onward.items()))  33.8 us
    ppermute x23, starting transfers between devices, send(): return lax.ppermute(x, AXES, sorted(onward.items()))  24.3 us
    ppermute x4, starting transfers between devices, send_some(): return lax.ppermute(x, AXES, pairs)  7.9 us
    pallas_call x2, Pallas kernels, update(): pl.pallas_call(functools.partial(update_kernel, (groups, row_count, share...  6.55 us
    pallas_call x1, Pallas kernels, on_device(): pl.pallas_call(functools.partial(reduce_kernel, low_homes, col_count), in...  1.71 us
    pallas_call x1, Pallas kernels, on_device(): pl.pallas_call(functools.partial(ready_kernel, low_homes, col_count), in_...  1.69 us
  transfers between devices with their start and end apart: 27, of which 12 were waited for; matrix products, arithmetic and copies ran while one was open for 0% of the time, Pallas kernels for 10%

profile of v19, /device:TPU:0, one launch (start us, length us, event | category | flops | bytes accessed | tf_op | source)
XLA Modules:
  0.0 80.9 jit_solution(17171338560811015660)
XLA Ops:
  0.6 1.3 %fetch.1 = (f32[512,512]{1,0:T(8,128)S(1)}, f32[128,128]{1,0:T(8,128)S(1)}) custom-call(f32[6,1,1,512,512]{4,3,2,1,0:T(8,128)} %refs_8_.3, f32[6,1,1,128,128]{4,3,2,1,0:T(8,128)} %rhs.1), custom_call_target="tpu_custom_call" | custom-call | flops 1000 | bytes 1000 | tf_op jit(solution)/shard_map/fetch/pallas_call | solution.py:314
  1.9 1.3 %collective-permute-start.5 = (f32[512,512]{1,0:T(8,128)S(1)}, f32[512,512]{1,0:T(8,128)S(1)}, u32[]{:S(2)}, u32[]{:S(2)}) collective-permute-start(f32[512,512]{1,0:T(8,128)S(1)} %get-tuple-element.22.near), channel_id=1, source_target_pairs={{10,0},{11,1}} | collective-permute-start | bytes 3145736 | tf_op jit(solution)/shard_map/ppermute | solution.py:301
  3.2 0.1 collective-permute-start.4
  3.3 2.9 %collective-permute-start = (f32[128,128]{1,0:T(8,128)S(1)}, f32[128,128]{1,0:T(8,128)S(1)}, u32[]{:S(2)}, u32[]{:S(2)}) collective-permute-start(f32[128,128]{1,0:T(8,128)S(1)} %get-tuple-element.16.own), channel_id=1, source_target_pairs={{0,2},{1,9},{2,0},{3,1},{4,28},{5,13},{6,14},{7,5},{8,24},{9,11},{... | collective-permute-start | bytes 196616 | tf_op jit(solution)/shard_map/ppermute | solution.py:298
  6.2 2.1 %collective-permute-start.1 = (f32[128,128]{1,0:T(8,128)S(1)}, f32[128,128]{1,0:T(8,128)S(1)}, u32[]{:S(2)}, u32[]{:S(2)}) collective-permute-start(f32[128,128]{1,0:T(8,128)S(1)} %get-tuple-element.16.own), channel_id=1, source_target_pairs={{0,4},{1,9},{2,10},{3,11},{4,0},{5,1},{6,14},{7,3},{8,12},{9,13},{... | collective-permute-start | bytes 196616 | tf_op jit(solution)/shard_map/ppermute | solution.py:298
  8.3 0.0 collective-permute-start.2
  8.3 1.7 %ready.1 = (bf16[2,512,512]{2,1,0:T(8,128)(2,1)S(1)}, bf16[2,512,512]{2,1,0:T(8,128)(2,1)S(1)}) custom-call(f32[4,512,512]{2,1,0:T(8,128)} %inverses.3), custom_call_target="tpu_custom_call" | custom-call | flops 1000 | bytes 1000 | tf_op jit(solution)/shard_map/ready/pallas_call | solution.py:326
  10.0 0.0 collective-permute-done.g1
  10.1 1.4 %collective-permute-done.1.g2 = f32[128,128]{1,0:T(8,128)S(1)} collective-permute-done((f32[128,128]{1,0:T(8,128)S(1)}, f32[128,128]{1,0:T(8,128)S(1)}, u32[]{:S(2)}, u32[]{:S(2)}) %collective-permute-start.1) | collective-permute-done | bytes 65568 | tf_op jit(solution)/shard_map/ppermute | solution.py:298
  11.5 3.0 %collective-permute-done.2.g3 = f32[128,128]{1,0:T(8,128)S(1)} collective-permute-done((f32[128,128]{1,0:T(8,128)S(1)}, f32[128,128]{1,0:T(8,128)S(1)}, u32[]{:S(2)}, u32[]{:S(2)}) %collective-permute-start.2) | collective-permute-done | bytes 65568 | tf_op jit(solution)/shard_map/ppermute | solution.py:298
  14.5 0.5 turn.1.out.own
  15.0 0.1 collective-permute-start.12
  15.1 1.6 %collective-permute-start.15 = (f32[512,512]{1,0:T(8,128)S(1)}, f32[512,512]{1,0:T(8,128)}, u32[]{:S(2)}, u32[]{:S(2)}) collective-permute-start(f32[512,512]{1,0:T(8,128)S(1)} %get-tuple-element.22.near), channel_id=1, source_target_pairs={{13,15}} | collective-permute-start | bytes 3145736 | tf_op jit(solution)/shard_map/ppermute | solution.py:301
  16.7 0.8 %collective-permute-start.3 = (f32[128,512]{1,0:T(8,128)S(1)}, f32[128,512]{1,0:T(8,128)S(1)}, u32[]{:S(2)}, u32[]{:S(2)}) collective-permute-start(f32[128,512]{1,0:T(8,128)S(1)} %turn.1.out.own), channel_id=1, source_target_pairs={{0,1},{1,0},{2,10},{3,11},{4,12},{5,13},{6,14},{7,4},{8,24},{9,25}... | collective-permute-start | bytes 786440 | tf_op jit(solution)/shard_map/ppermute | solution.py:298
  17.6 5.5 %collective-permute-done.3.swapped = f32[128,512]{1,0:T(8,128)S(1)} collective-permute-done((f32[128,512]{1,0:T(8,128)S(1)}, f32[128,512]{1,0:T(8,128)S(1)}, u32[]{:S(2)}, u32[]{:S(2)}) %collective-permute-start.3) | collective-permute-done | bytes 262176 | tf_op jit(solution)/shard_map/ppermute | solution.py:298
  23.1 0.0 collective-permute-done.5.ly
  23.1 0.0 collective-permute-done.4.la
  23.1 0.8 solve_low.1
  23.9 0.1 collective-permute-start.6
  24.0 0.0 collective-permute-done.12.lx
  24.0 1.7 %reduce_low.1 = f32[128,512]{1,0:T(8,128)S(1)} custom-call(f32[128,512]{1,0:T(8,128)S(1)} %get-tuple-element.20.s_a, f32[128,512]{1,0:T(8,128)S(1)} %get-tuple-element.21.s_b, f32[512,512]{1,0:T(8,128)} %collective-permute-done.12.lx, f32[512,512]{1,0:T(8,128)S(1)} %collective-permute-done.5.ly), custom_call_target="tpu_custom_call" | custom-call | flops 1000 | bytes 1000 | tf_op jit(solution)/shard_map/reduce_low/pallas_call | solution.py:373
  25.7 0.1 collective-permute-start.13
  25.8 0.1 collective-permute-start.14
  25.8 0.0 collective-permute-done.6
  25.9 0.6 collective-permute-start.7
  26.4 0.1 collective-permute-start.8
  26.5 0.0 collective-permute-done.15.last_block
  26.5 0.0 collective-permute-start.9
  26.5 3.1 %collective-permute-done.13.w_1 = f32[128,512]{1,0:T(8,128)S(1)} collective-permute-done((f32[128,512]{1,0:T(8,128)S(1)}, f32[128,512]{1,0:T(8,128)S(1)}, u32[]{:S(2)}, u32[]{:S(2)}) %collective-permute-start.13) | collective-permute-done | bytes 262176 | tf_op jit(solution)/shard_map/ppermute | solution.py:298
  29.6 2.8 %collective-permute-done.14.w_2 = f32[128,512]{1,0:T(8,128)S(1)} collective-permute-done((f32[128,512]{1,0:T(8,128)S(1)}, f32[128,512]{1,0:T(8,128)S(1)}, u32[]{:S(2)}, u32[]{:S(2)}) %collective-permute-start.14) | collective-permute-done | bytes 262176 | tf_op jit(solution)/shard_map/ppermute | solution.py:298
  32.5 0.6 collective-permute-start.16
  33.1 0.1 collective-permute-start.17
  33.1 0.0 collective-permute-done.7
  33.1 0.5 collective-permute-start.18
  33.6 0.0 collective-permute-done.8
  33.6 0.1 collective-permute-start.10
  33.7 0.0 collective-permute-done.9
  33.7 0.4 collective-permute-start.19
  34.1 0.1 select_select_fusion.1.refs_1_
  34.2 0.1 collective-permute-done.16
  34.3 0.4 collective-permute-start.11
  34.6 0.0 collective-permute-done.17
  34.6 0.4 collective-permute-done.18
  35.0 0.1 select_select_fusion.refs_5_
  35.1 0.4 collective-permute-start.20
  35.5 0.0 collective-permute-done.10.refs_2_
  35.5 0.2 collective-permute-done.19.refs_6_
  35.8 0.4 collective-permute-done.11.refs_3_
  36.1 0.5 collective-permute-done.20.refs_7_
  36.7 3.3 %update_first.1 = (f32[832,128]{1,0:T(8,128)S(1)}, f32[840,128]{1,0:T(8,128)S(1)}, f32[64,128]{1,0:T(8,128)S(1)}) custom-call(f32[128,512]{1,0:T(8,128)S(1)} %broadcast_select_fusion.refs_0_, f32[128,512]{1,0:T(8,128)S(1)} %select_select_fusion.1.refs_1_, f32[128,512]{1,0:T(8,128)S(1)} %collective-permute-done.10.refs_2_, ...), custom_call_target="tpu_custom_call" | custom-call | flops 1000 | bytes 1000 | tf_op jit(solution)/shard_map/update_first/pallas_call | solution.py:448
  39.9 0.0 copy-start
  40.0 1.8 %collective-permute-start.21 = (f32[832,128]{1,0:T(8,128)S(1)}, f32[832,128]{1,0:T(8,128)S(1)}, u32[]{:S(2)}, u32[]{:S(2)}) collective-permute-start(f32[832,128]{1,0:T(8,128)S(1)} %get-tuple-element.24), channel_id=1, source_target_pairs={{0,2},{1,3},{2,0},{3,1},{4,6},{5,7},{6,4},{7,5},{8,10},{9,11},{10,... | collective-permute-start | bytes 1277960 | tf_op jit(solution)/shard_map/ppermute | solution.py:298
  41.7 8.1 %collective-permute-start.22 = (f32[840,128]{1,0:T(8,128)S(1)}, f32[840,128]{1,0:T(8,128)S(1)}, u32[]{:S(2)}, u32[]{:S(2)}) collective-permute-start(f32[840,128]{1,0:T(8,128)S(1)} %get-tuple-element.25), channel_id=1, source_target_pairs={{0,4},{1,5},{2,0},{3,1},{4,6},{5,7},{6,2},{7,3},{8,12},{9,13},{10,... | collective-permute-start | bytes 1290248 | tf_op jit(solution)/shard_map/ppermute | solution.py:298
  49.8 0.0 collective-permute-start.24
  49.8 3.3 %update_second.1 = (f32[832,128]{1,0:T(8,128)S(1)}, f32[840,128]{1,0:T(8,128)S(1)}) custom-call(f32[128,512]{1,0:T(8,128)S(1)} %broadcast_select_fusion.refs_0_, f32[128,512]{1,0:T(8,128)S(1)} %select_select_fusion.1.refs_1_, f32[128,512]{1,0:T(8,128)S(1)} %collective-permute-done.10.refs_2_, f32[128,512]{1,0:T(8,128)S(1)} %collective-permute-done.11.refs_3_, ...), custom_call_target="tpu_custom_call" | custom-call | flops 1000 | bytes 1000 | tf_op jit(solution)/shard_map/update_second/pallas_call | solution.py:448
  53.1 3.7 %collective-permute-start.23 = (f32[840,128]{1,0:T(8,128)S(1)}, f32[840,128]{1,0:T(8,128)S(1)}, u32[]{:S(2)}, u32[]{:S(2)}) collective-permute-start(f32[840,128]{1,0:T(8,128)S(1)} %get-tuple-element.26.mine), channel_id=1, source_target_pairs={{6,4},{7,5},{14,12},{15,13},{22,20},{23,21},{30,28},{31,29},{0,2},... | collective-permute-start | bytes 1290248 | tf_op jit(solution)/shard_map/ppermute | solution.py:301
  56.7 0.0 collective-permute-done.21.theirs.got_1
  56.8 1.3 %collective-permute-start.25 = (f32[832,128]{1,0:T(8,128)S(1)}, f32[832,128]{1,0:T(8,128)S(1)}, u32[]{:S(2)}, u32[]{:S(2)}) collective-permute-start(f32[832,128]{1,0:T(8,128)S(1)} %join.1), channel_id=1, source_target_pairs={{4,0},{5,1},{12,8},{13,9},{20,16},{21,17},{28,24},{29,25},{2,6},{3... | collective-permute-start | bytes 1277960 | tf_op jit(solution)/shard_map/ppermute | solution.py:301
  58.1 5.2 %collective-permute-start.26 = (f32[64,128]{1,0:T(8,128)S(1)}, f32[64,128]{1,0:T(8,128)S(1)}, u32[]{:S(2)}, u32[]{:S(2)}) collective-permute-start(f32[64,128]{1,0:T(8,128)S(1)} %get-tuple-element.27), channel_id=1, source_target_pairs={{0,6},{1,7},{2,4},{3,5},{4,2},{5,3},{6,0},{7,1},{8,14},{9,15},{10,... | collective-permute-start | bytes 98312 | tf_op jit(solution)/shard_map/ppermute | solution.py:298
  63.2 16.3 %collective-permute-done.26.far = f32[64,128]{1,0:T(8,128)S(1)} collective-permute-done((f32[64,128]{1,0:T(8,128)S(1)}, f32[64,128]{1,0:T(8,128)S(1)}, u32[]{:S(2)}, u32[]{:S(2)}) %collective-permute-start.26) | collective-permute-done | bytes 32800 | tf_op jit(solution)/shard_map/ppermute | solution.py:298
  79.5 0.0 collective-permute-done.22.got_2
  79.5 0.0 collective-permute-done.23.got_3
  79.5 0.3 collective-permute-done.25.joined
  79.9 1.0 %add_up.1 = (f32[4,64,128]{2,1,0:T(8,128)}, f32[6,128,128]{2,1,0:T(8,128)}) custom-call(f32[6,128,128]{2,1,0:T(8,128)S(1)} %bitcast.4, f32[832,128]{1,0:T(8,128)S(1)} %get-tuple-element.23.own, f32[832,128]{1,0:T(8,128)S(1)} %collective-permute-done.21.theirs.got_1, f32[840,128]{1,0:T(8,128)S(1)} %collective-permute-done.22.got_2, ...), custom_call_target="tpu_custom_call" | custom-call | flops 1000 | bytes 1000 | tf_op jit(solution)/shard_map/add_up/pallas_call | solution.py:489
  (5 shorter events, 0.1 us)
Async XLA Ops:
  1.9 21.2 %collective-permute-start.5 = (f32[512,512]{1,0:T(8,128)S(1)}, f32[512,512]{1,0:T(8,128)S(1)}, u32[]{:S(2)}, u32[]{:S(2)}) collective-permute-start(f32[512,512]{1,0:T(8,128)S(1)} %get-tuple-element.22.near), channel_id=1, source_target_pairs={{10,0},{11,1}} | collective-permute-start | bytes 3145736 | tf_op jit(solution)/shard_map/ppermute | solution.py:301
  3.2 19.9 %collective-permute-start.4 = (f32[512,512]{1,0:T(8,128)S(1)}, f32[512,512]{1,0:T(8,128)S(1)}, u32[]{:S(2)}, u32[]{:S(2)}) collective-permute-start(f32[512,512]{1,0:T(8,128)S(1)} %get-tuple-element.22.near), channel_id=1, source_target_pairs={{0,8},{1,0},{2,10},{3,11},{4,12},{5,13},{6,14},{7,15},{8,9},{9,1},... | collective-permute-start | bytes 3145736 | tf_op jit(solution)/shard_map/ppermute | solution.py:298
  3.3 6.7 %collective-permute-start = (f32[128,128]{1,0:T(8,128)S(1)}, f32[128,128]{1,0:T(8,128)S(1)}, u32[]{:S(2)}, u32[]{:S(2)}) collective-permute-start(f32[128,128]{1,0:T(8,128)S(1)} %get-tuple-element.16.own), channel_id=1, source_target_pairs={{0,2},{1,9},{2,0},{3,1},{4,28},{5,13},{6,14},{7,5},{8,24},{9,11},{... | collective-permute-start | bytes 196616 | tf_op jit(solution)/shard_map/ppermute | solution.py:298
  6.2 5.3 %collective-permute-start.1 = (f32[128,128]{1,0:T(8,128)S(1)}, f32[128,128]{1,0:T(8,128)S(1)}, u32[]{:S(2)}, u32[]{:S(2)}) collective-permute-start(f32[128,128]{1,0:T(8,128)S(1)} %get-tuple-element.16.own), channel_id=1, source_target_pairs={{0,4},{1,9},{2,10},{3,11},{4,0},{5,1},{6,14},{7,3},{8,12},{9,13},{... | collective-permute-start | bytes 196616 | tf_op jit(solution)/shard_map/ppermute | solution.py:298
  8.3 6.2 %collective-permute-start.2 = (f32[128,128]{1,0:T(8,128)S(1)}, f32[128,128]{1,0:T(8,128)S(1)}, u32[]{:S(2)}, u32[]{:S(2)}) collective-permute-start(f32[128,128]{1,0:T(8,128)S(1)} %get-tuple-element.16.own), channel_id=1, source_target_pairs={{0,6},{1,7},{2,10},{3,11},{4,28},{5,13},{6,0},{7,1},{8,24},{9,15},... | collective-permute-start | bytes 196616 | tf_op jit(solution)/shard_map/ppermute | solution.py:298
  15.0 9.0 %collective-permute-start.12 = (f32[512,512]{1,0:T(8,128)S(1)}, f32[512,512]{1,0:T(8,128)}, u32[]{:S(2)}, u32[]{:S(2)}) collective-permute-start(f32[512,512]{1,0:T(8,128)S(1)} %get-tuple-element.22.near), channel_id=1, source_target_pairs={{0,8},{1,9},{2,10},{3,11},{4,12},{5,13},{6,14},{7,15},{8,0},{9,1},... | collective-permute-start | bytes 3145736 | tf_op jit(solution)/shard_map/ppermute | solution.py:298
  15.1 11.5 %collective-permute-start.15 = (f32[512,512]{1,0:T(8,128)S(1)}, f32[512,512]{1,0:T(8,128)}, u32[]{:S(2)}, u32[]{:S(2)}) collective-permute-start(f32[512,512]{1,0:T(8,128)S(1)} %get-tuple-element.22.near), channel_id=1, source_target_pairs={{13,15}} | collective-permute-start | bytes 3145736 | tf_op jit(solution)/shard_map/ppermute | solution.py:301
  16.7 6.4 %collective-permute-start.3 = (f32[128,512]{1,0:T(8,128)S(1)}, f32[128,512]{1,0:T(8,128)S(1)}, u32[]{:S(2)}, u32[]{:S(2)}) collective-permute-start(f32[128,512]{1,0:T(8,128)S(1)} %turn.1.out.own), channel_id=1, source_target_pairs={{0,1},{1,0},{2,10},{3,11},{4,12},{5,13},{6,14},{7,4},{8,24},{9,25}... | collective-permute-start | bytes 786440 | tf_op jit(solution)/shard_map/ppermute | solution.py:298
  23.9 2.0 %collective-permute-start.6 = (f32[128,512]{1,0:T(8,128)S(1)}, f32[128,512]{1,0:T(8,128)S(1)}, u32[]{:S(2)}, u32[]{:S(2)}) collective-permute-start(f32[128,512]{1,0:T(8,128)S(1)} %get-tuple-element.21.s_b), channel_id=1, source_target_pairs={{0,8},{1,3},{2,10},{3,11},{4,12},{5,13},{6,14},{7,15},{8,0},{9,1},... | collective-permute-start | bytes 786440 | tf_op jit(solution)/shard_map/ppermute | solution.py:298
  25.7 3.9 %collective-permute-start.13 = (f32[128,512]{1,0:T(8,128)S(1)}, f32[128,512]{1,0:T(8,128)S(1)}, u32[]{:S(2)}, u32[]{:S(2)}) collective-permute-start(f32[128,512]{1,0:T(8,128)S(1)} %reduce_low.1), channel_id=1, source_target_pairs={{0,15},{1,9},{2,10},{3,11},{4,12},{5,13},{6,14},{7,8},{8,0},{9,1},... | collective-permute-start | bytes 786440 | tf_op jit(solution)/shard_map/ppermute | solution.py:298
  25.8 6.7 %collective-permute-start.14 = (f32[128,512]{1,0:T(8,128)S(1)}, f32[128,512]{1,0:T(8,128)S(1)}, u32[]{:S(2)}, u32[]{:S(2)}) collective-permute-start(f32[128,512]{1,0:T(8,128)S(1)} %reduce_low.1), channel_id=1, source_target_pairs={{0,12},{1,15},{2,10},{3,11},{4,8},{5,13},{6,14},{7,9},{8,0},{9,1},... | collective-permute-start | bytes 786440 | tf_op jit(solution)/shard_map/ppermute | solution.py:298
  25.9 7.3 %collective-permute-start.7 = (f32[128,512]{1,0:T(8,128)S(1)}, f32[128,512]{1,0:T(8,128)S(1)}, u32[]{:S(2)}, u32[]{:S(2)}) collective-permute-start(f32[128,512]{1,0:T(8,128)S(1)} %broadcast_select_fusion.refs_0_), channel_id=1, source_target_pairs={{0,8},{1,9},{2,10},{3,18},{4,12},{5,13},{6,14},{7,15},{8,0},{9,1},... | collective-permute-start | bytes 786440 | tf_op jit(solution)/shard_map/ppermute | solution.py:298
  26.4 7.2 %collective-permute-start.8 = (f32[128,512]{1,0:T(8,128)S(1)}, f32[128,512]{1,0:T(8,128)S(1)}, u32[]{:S(2)}, u32[]{:S(2)}) collective-permute-start(f32[128,512]{1,0:T(8,128)S(1)} %broadcast_select_fusion.refs_0_), channel_id=1, source_target_pairs={{0,8},{1,9},{2,10},{3,2},{4,12},{5,13},{6,14},{7,15},{8,0},{9,1},{... | collective-permute-start | bytes 786440 | tf_op jit(solution)/shard_map/ppermute | solution.py:298
  26.5 7.2 %collective-permute-start.9 = (f32[128,512]{1,0:T(8,128)S(1)}, f32[128,512]{1,0:T(8,128)S(1)}, u32[]{:S(2)}, u32[]{:S(2)}) collective-permute-start(f32[128,512]{1,0:T(8,128)S(1)} %broadcast_select_fusion.refs_0_), channel_id=1, source_target_pairs={{0,16},{1,17},{2,10},{3,19},{4,12},{5,13},{6,14},{7,15},{8,0},{9,1... | collective-permute-start | bytes 786440 | tf_op jit(solution)/shard_map/ppermute | solution.py:298
  32.5 1.8 %collective-permute-start.16 = (f32[128,512]{1,0:T(8,128)S(1)}, f32[128,512]{1,0:T(8,128)S(1)}, u32[]{:S(2)}, u32[]{:S(2)}) collective-permute-start(f32[128,512]{1,0:T(8,128)S(1)} %solve_high.1.refs_4_), channel_id=1, source_target_pairs={{0,8},{1,9},{2,10},{3,11},{4,12},{5,13},{6,14},{7,15},{8,0},{9,1},... | collective-permute-start | bytes 786440 | tf_op jit(solution)/shard_map/ppermute | solution.py:298
  33.1 1.5 %collective-permute-start.17 = (f32[128,512]{1,0:T(8,128)S(1)}, f32[128,512]{1,0:T(8,128)S(1)}, u32[]{:S(2)}, u32[]{:S(2)}) collective-permute-start(f32[128,512]{1,0:T(8,128)S(1)} %solve_high.1.refs_4_), channel_id=1, source_target_pairs={{0,8},{1,9},{2,10},{3,11},{4,12},{5,4},{6,7},{7,15},{8,0},{9,1},{1... | collective-permute-start | bytes 786440 | tf_op jit(solution)/shard_map/ppermute | solution.py:298
  33.1 1.9 %collective-permute-start.18 = (f32[128,512]{1,0:T(8,128)S(1)}, f32[128,512]{1,0:T(8,128)S(1)}, u32[]{:S(2)}, u32[]{:S(2)}) collective-permute-start(f32[128,512]{1,0:T(8,128)S(1)} %solve_high.1.refs_4_), channel_id=1, source_target_pairs={{0,8},{1,9},{2,10},{3,11},{4,12},{5,13},{6,14},{7,15},{8,0},{9,1},... | collective-permute-start | bytes 786440 | tf_op jit(solution)/shard_map/ppermute | solution.py:298
  33.6 1.9 %collective-permute-start.10 = (f32[128,512]{1,0:T(8,128)S(1)}, f32[128,512]{1,0:T(8,128)S(1)}, u32[]{:S(2)}, u32[]{:S(2)}) collective-permute-start(f32[128,512]{1,0:T(8,128)S(1)} %broadcast_select_fusion.refs_0_), channel_id=1, source_target_pairs={{0,8},{1,9},{2,10},{3,11},{4,12},{5,13},{6,14},{7,15},{8,0},{9,1},... | collective-permute-start | bytes 786440 | tf_op jit(solution)/shard_map/ppermute | solution.py:298
  33.7 2.1 %collective-permute-start.19 = (f32[128,512]{1,0:T(8,128)S(1)}, f32[128,512]{1,0:T(8,128)S(1)}, u32[]{:S(2)}, u32[]{:S(2)}) collective-permute-start(f32[128,512]{1,0:T(8,128)S(1)} %solve_high.1.refs_4_), channel_id=1, source_target_pairs={{0,8},{1,9},{2,10},{3,11},{4,12},{5,13},{6,14},{7,15},{8,0},{9,1},... | collective-permute-start | bytes 786440 | tf_op jit(solution)/shard_map/ppermute | solution.py:298
  34.3 1.9 %collective-permute-start.11 = (f32[128,512]{1,0:T(8,128)S(1)}, f32[128,512]{1,0:T(8,128)S(1)}, u32[]{:S(2)}, u32[]{:S(2)}) collective-permute-start(f32[128,512]{1,0:T(8,128)S(1)} %select_select_fusion.1.refs_1_), channel_id=1, source_target_pairs={{0,8},{1,9},{2,10},{3,11},{4,12},{5,13},{6,14},{7,15},{8,0},{9,1},... | collective-permute-start | bytes 786440 | tf_op jit(solution)/shard_map/ppermute | solution.py:298
  35.1 1.6 %collective-permute-start.20 = (f32[128,512]{1,0:T(8,128)S(1)}, f32[128,512]{1,0:T(8,128)S(1)}, u32[]{:S(2)}, u32[]{:S(2)}) collective-permute-start(f32[128,512]{1,0:T(8,128)S(1)} %select_select_fusion.refs_5_), channel_id=1, source_target_pairs={{0,8},{1,9},{2,10},{3,11},{4,12},{5,13},{6,14},{7,15},{8,0},{9,1},... | collective-permute-start | bytes 786440 | tf_op jit(solution)/shard_map/ppermute | solution.py:298
  39.9 39.9 %copy-start = (f32[6,1,1,128,128]{4,3,2,1,0:T(8,128)S(1)}, f32[6,1,1,128,128]{4,3,2,1,0:T(8,128)}, u32[]{:S(2)}) copy-start(f32[6,1,1,128,128]{4,3,2,1,0:T(8,128)} %rhs.1) | copy-start | bytes 1179652
  40.0 16.8 %collective-permute-start.21 = (f32[832,128]{1,0:T(8,128)S(1)}, f32[832,128]{1,0:T(8,128)S(1)}, u32[]{:S(2)}, u32[]{:S(2)}) collective-permute-start(f32[832,128]{1,0:T(8,128)S(1)} %get-tuple-element.24), channel_id=1, source_target_pairs={{0,2},{1,3},{2,0},{3,1},{4,6},{5,7},{6,4},{7,5},{8,10},{9,11},{10,... | collective-permute-start | bytes 1277960 | tf_op jit(solution)/shard_map/ppermute | solution.py:298
  41.7 37.8 %collective-permute-start.22 = (f32[840,128]{1,0:T(8,128)S(1)}, f32[840,128]{1,0:T(8,128)S(1)}, u32[]{:S(2)}, u32[]{:S(2)}) collective-permute-start(f32[840,128]{1,0:T(8,128)S(1)} %get-tuple-element.25), channel_id=1, source_target_pairs={{0,4},{1,5},{2,0},{3,1},{4,6},{5,7},{6,2},{7,3},{8,12},{9,13},{10,... | collective-permute-start | bytes 1290248 | tf_op jit(solution)/shard_map/ppermute | solution.py:298
  49.8 29.7 %collective-permute-start.24 = (f32[840,128]{1,0:T(8,128)S(1)}, f32[840,128]{1,0:T(8,128)S(1)}, u32[]{:S(2)}, u32[]{:S(2)}) collective-permute-start(f32[840,128]{1,0:T(8,128)S(1)} %get-tuple-element.25), channel_id=1, source_target_pairs={{0,8},{1,9},{2,4},{3,5},{4,2},{5,3},{6,14},{7,15},{8,0},{9,1},{10,... | collective-permute-start | bytes 1290248 | tf_op jit(solution)/shard_map/ppermute | solution.py:298
  53.1 26.5 %collective-permute-start.23 = (f32[840,128]{1,0:T(8,128)S(1)}, f32[840,128]{1,0:T(8,128)S(1)}, u32[]{:S(2)}, u32[]{:S(2)}) collective-permute-start(f32[840,128]{1,0:T(8,128)S(1)} %get-tuple-element.26.mine), channel_id=1, source_target_pairs={{6,4},{7,5},{14,12},{15,13},{22,20},{23,21},{30,28},{31,29},{0,2},... | collective-permute-start | bytes 1290248 | tf_op jit(solution)/shard_map/ppermute | solution.py:301
  56.8 23.1 %collective-permute-start.25 = (f32[832,128]{1,0:T(8,128)S(1)}, f32[832,128]{1,0:T(8,128)S(1)}, u32[]{:S(2)}, u32[]{:S(2)}) collective-permute-start(f32[832,128]{1,0:T(8,128)S(1)} %join.1), channel_id=1, source_target_pairs={{4,0},{5,1},{12,8},{13,9},{20,16},{21,17},{28,24},{29,25},{2,6},{3... | collective-permute-start | bytes 1277960 | tf_op jit(solution)/shard_map/ppermute | solution.py:301
  58.1 21.4 %collective-permute-start.26 = (f32[64,128]{1,0:T(8,128)S(1)}, f32[64,128]{1,0:T(8,128)S(1)}, u32[]{:S(2)}, u32[]{:S(2)}) collective-permute-start(f32[64,128]{1,0:T(8,128)S(1)} %get-tuple-element.27), channel_id=1, source_target_pairs={{0,6},{1,7},{2,4},{3,5},{4,2},{5,3},{6,0},{7,1},{8,14},{9,15},{10,... | collective-permute-start | bytes 98312 | tf_op jit(solution)/shard_map/ppermute | solution.py:298

commit v20 on v18

--- a/solution.py
+++ b/solution.py
@@ -123,10 +123,10 @@
         copies = [pltpu.make_async_copy(ref, block.at[i], sem.at[i]) for i, ref in enumerate((ly, lx))]
         for copy in copies:
             copy.start()
+        copies[1].wait()
+        sooner = product(s_a[...], block[1])
         copies[0].wait()
-        later = product(s_b[...], block[0])
-        copies[1].wait()
-        w[...] = product(s_a[...], block[1]) + later
+        w[...] = sooner + product(s_b[...], block[0])
 
 
 def high_kernel(homes, col_count, own, swapped, w_1, w_2, inverses, last_block, s, inv, block, sem):
@@ -360,6 +360,7 @@
     last_block = send_some(later, [(line(3, 2), high_homes[1])])
     last_block = pltpu.with_memory_space_constraint(last_block, pltpu.HBM)
     lx = send(later, [(line(2, 0), low_homes[0]), (line(3, 0), low_homes[1])])
+    ly = pltpu.with_memory_space_constraint(ly, pltpu.HBM)
     s_0, s_1 = pl.pallas_call(
         functools.partial(low_kernel, low_homes, col_count),
         in_specs=[vmem] * 6 + [pl.BlockSpec(memory_space=pl.ANY)],

time: 81.1 us -> 82 us (1.011)
  local copies, waits for them, and re-layouts: 0.01 us -> 0.97 us
    unnamed x2 -> x4, local copies, waits for them, and re-layouts: 0.01 us -> 0.97 us
where the time goes in v20:
time: 82 us; the launch traced here: 81.8 us
  waiting for transfers between devices  34.5 us (42%)
  starting transfers between devices  31.9 us (39%)
  Pallas kernels  13.4 us (16%)
  local copies, waits for them, and re-layouts  0.97 us (1%)
  between operations  0.86 us (1%)
    ppermute x23, waiting for transfers between devices, send(): return lax.ppermute(x, AXES, sorted(onward.items()))  34.1 us
    ppermute x23, starting transfers between devices, send(): return lax.ppermute(x, AXES, sorted(onward.items()))  23.7 us
    ppermute x4, starting transfers between devices, send_some(): return lax.ppermute(x, AXES, pairs)  8.22 us
    pallas_call x2, Pallas kernels, update(): pl.pallas_call(functools.partial(update_kernel, (groups, row_count, share...  6.55 us
    pallas_call x1, Pallas kernels, on_device(): pl.pallas_call(functools.partial(ready_kernel, low_homes, col_count), in_...  1.69 us
  transfers between devices with their start and end apart: 27, of which 12 were waited for; matrix products, arithmetic and copies ran while one was open for 0% of the time, Pallas kernels for 10%

profile of v20, /device:TPU:0, one launch (start us, length us, event | category | flops | bytes accessed | tf_op | source)
XLA Modules:
  0.0 81.8 jit_solution(10471768451906414869)
XLA Ops:
  0.6 1.3 %fetch.1 = (f32[512,512]{1,0:T(8,128)S(1)}, f32[128,128]{1,0:T(8,128)S(1)}) custom-call(f32[6,1,1,512,512]{4,3,2,1,0:T(8,128)} %refs_8_.3, f32[6,1,1,128,128]{4,3,2,1,0:T(8,128)} %rhs.1), custom_call_target="tpu_custom_call" | custom-call | flops 1000 | bytes 1000 | tf_op jit(solution)/shard_map/fetch/pallas_call | solution.py:314
  1.9 1.3 %collective-permute-start.5 = (f32[512,512]{1,0:T(8,128)S(1)}, f32[512,512]{1,0:T(8,128)S(1)}, u32[]{:S(2)}, u32[]{:S(2)}) collective-permute-start(f32[512,512]{1,0:T(8,128)S(1)} %get-tuple-element.22.near), channel_id=1, source_target_pairs={{10,0},{11,1}} | collective-permute-start | bytes 3145736 | tf_op jit(solution)/shard_map/ppermute | solution.py:301
  3.2 0.1 collective-permute-start.4
  3.3 2.9 %collective-permute-start = (f32[128,128]{1,0:T(8,128)S(1)}, f32[128,128]{1,0:T(8,128)S(1)}, u32[]{:S(2)}, u32[]{:S(2)}) collective-permute-start(f32[128,128]{1,0:T(8,128)S(1)} %get-tuple-element.16.own), channel_id=1, source_target_pairs={{0,2},{1,9},{2,0},{3,1},{4,28},{5,13},{6,14},{7,5},{8,24},{9,11},{... | collective-permute-start | bytes 196616 | tf_op jit(solution)/shard_map/ppermute | solution.py:298
  6.2 2.1 %collective-permute-start.1 = (f32[128,128]{1,0:T(8,128)S(1)}, f32[128,128]{1,0:T(8,128)S(1)}, u32[]{:S(2)}, u32[]{:S(2)}) collective-permute-start(f32[128,128]{1,0:T(8,128)S(1)} %get-tuple-element.16.own), channel_id=1, source_target_pairs={{0,4},{1,9},{2,10},{3,11},{4,0},{5,1},{6,14},{7,3},{8,12},{9,13},{... | collective-permute-start | bytes 196616 | tf_op jit(solution)/shard_map/ppermute | solution.py:298
  8.3 0.0 collective-permute-start.2
  8.3 1.7 %ready.1 = (bf16[2,512,512]{2,1,0:T(8,128)(2,1)S(1)}, bf16[2,512,512]{2,1,0:T(8,128)(2,1)S(1)}) custom-call(f32[4,512,512]{2,1,0:T(8,128)} %inverses.3), custom_call_target="tpu_custom_call" | custom-call | flops 1000 | bytes 1000 | tf_op jit(solution)/shard_map/ready/pallas_call | solution.py:326
  10.0 0.0 collective-permute-done.g1
  10.1 1.4 %collective-permute-done.1.g2 = f32[128,128]{1,0:T(8,128)S(1)} collective-permute-done((f32[128,128]{1,0:T(8,128)S(1)}, f32[128,128]{1,0:T(8,128)S(1)}, u32[]{:S(2)}, u32[]{:S(2)}) %collective-permute-start.1) | collective-permute-done | bytes 65568 | tf_op jit(solution)/shard_map/ppermute | solution.py:298
  11.5 3.0 %collective-permute-done.2.g3 = f32[128,128]{1,0:T(8,128)S(1)} collective-permute-done((f32[128,128]{1,0:T(8,128)S(1)}, f32[128,128]{1,0:T(8,128)S(1)}, u32[]{:S(2)}, u32[]{:S(2)}) %collective-permute-start.2) | collective-permute-done | bytes 65568 | tf_op jit(solution)/shard_map/ppermute | solution.py:298
  14.5 0.5 turn.1.out.own
  15.0 0.1 collective-permute-start.12
  15.1 1.7 %collective-permute-start.15 = (f32[512,512]{1,0:T(8,128)S(1)}, f32[512,512]{1,0:T(8,128)}, u32[]{:S(2)}, u32[]{:S(2)}) collective-permute-start(f32[512,512]{1,0:T(8,128)S(1)} %get-tuple-element.22.near), channel_id=1, source_target_pairs={{13,15}} | collective-permute-start | bytes 3145736 | tf_op jit(solution)/shard_map/ppermute | solution.py:301
  16.7 0.8 %collective-permute-start.3 = (f32[128,512]{1,0:T(8,128)S(1)}, f32[128,512]{1,0:T(8,128)S(1)}, u32[]{:S(2)}, u32[]{:S(2)}) collective-permute-start(f32[128,512]{1,0:T(8,128)S(1)} %turn.1.out.own), channel_id=1, source_target_pairs={{0,1},{1,0},{2,10},{3,11},{4,12},{5,13},{6,14},{7,4},{8,24},{9,25}... | collective-permute-start | bytes 786440 | tf_op jit(solution)/shard_map/ppermute | solution.py:298
  17.6 5.5 %collective-permute-done.3.swapped = f32[128,512]{1,0:T(8,128)S(1)} collective-permute-done((f32[128,512]{1,0:T(8,128)S(1)}, f32[128,512]{1,0:T(8,128)S(1)}, u32[]{:S(2)}, u32[]{:S(2)}) %collective-permute-start.3) | collective-permute-done | bytes 262176 | tf_op jit(solution)/shard_map/ppermute | solution.py:298
  23.1 0.0 collective-permute-done.5.ly
  23.1 0.0 collective-permute-done.4.la
  23.1 1.0 %copy-done.1 = f32[512,512]{1,0:T(8,128)} copy-done((f32[512,512]{1,0:T(8,128)}, f32[512,512]{1,0:T(8,128)S(1)}, u32[]{:S(2)}) %copy-start.1) | copy-done | bytes 1048600
  24.1 0.8 solve_low.1
  24.8 0.1 collective-permute-start.6
  24.9 0.0 collective-permute-done.12.lx
  25.0 1.6 %reduce_low.1 = f32[128,512]{1,0:T(8,128)S(1)} custom-call(f32[128,512]{1,0:T(8,128)S(1)} %get-tuple-element.20.s_a, f32[128,512]{1,0:T(8,128)S(1)} %get-tuple-element.21.s_b, f32[512,512]{1,0:T(8,128)S(1)} %collective-permute-done.12.lx, f32[512,512]{1,0:T(8,128)} %copy-done.1), custom_call_target="tpu_custom_call" | custom-call | flops 1000 | bytes 1000 | tf_op jit(solution)/shard_map/reduce_low/pallas_call | solution.py:373
  26.6 0.1 collective-permute-start.13
  26.7 0.1 collective-permute-start.14
  26.7 0.0 collective-permute-done.6
  26.8 0.6 collective-permute-start.7
  27.3 0.1 collective-permute-start.8
  27.4 0.0 collective-permute-done.15.last_block
  27.4 0.0 collective-permute-start.9
  27.4 3.1 %collective-permute-done.13.w_1 = f32[128,512]{1,0:T(8,128)S(1)} collective-permute-done((f32[128,512]{1,0:T(8,128)S(1)}, f32[128,512]{1,0:T(8,128)S(1)}, u32[]{:S(2)}, u32[]{:S(2)}) %collective-permute-start.13) | collective-permute-done | bytes 262176 | tf_op jit(solution)/shard_map/ppermute | solution.py:298
  30.5 2.8 %collective-permute-done.14.w_2 = f32[128,512]{1,0:T(8,128)S(1)} collective-permute-done((f32[128,512]{1,0:T(8,128)S(1)}, f32[128,512]{1,0:T(8,128)S(1)}, u32[]{:S(2)}, u32[]{:S(2)}) %collective-permute-start.14) | collective-permute-done | bytes 262176 | tf_op jit(solution)/shard_map/ppermute | solution.py:298
  33.4 0.7 collective-permute-start.16
  34.1 0.1 collective-permute-start.17
  34.1 0.0 collective-permute-done.7
  34.1 0.5 collective-permute-start.18
  34.6 0.0 collective-permute-done.8
  34.6 0.1 collective-permute-start.10
  34.7 0.0 collective-permute-done.9
  34.7 0.4 collective-permute-start.19
  35.1 0.1 select_select_fusion.1.refs_1_
  35.2 0.1 collective-permute-done.16
  35.2 0.4 collective-permute-start.11
  35.6 0.4 collective-permute-done.18
  36.0 0.1 select_select_fusion.refs_5_
  36.0 0.4 collective-permute-start.20
  36.5 0.0 collective-permute-done.10.refs_2_
  36.5 0.2 collective-permute-done.19.refs_6_
  36.7 0.4 collective-permute-done.11.refs_3_
  37.1 0.5 collective-permute-done.20.refs_7_
  37.6 3.3 %update_first.1 = (f32[832,128]{1,0:T(8,128)S(1)}, f32[840,128]{1,0:T(8,128)S(1)}, f32[64,128]{1,0:T(8,128)S(1)}) custom-call(f32[128,512]{1,0:T(8,128)S(1)} %broadcast_select_fusion.refs_0_, f32[128,512]{1,0:T(8,128)S(1)} %select_select_fusion.1.refs_1_, f32[128,512]{1,0:T(8,128)S(1)} %collective-permute-done.10.refs_2_, ...), custom_call_target="tpu_custom_call" | custom-call | flops 1000 | bytes 1000 | tf_op jit(solution)/shard_map/update_first/pallas_call | solution.py:448
  40.9 0.0 copy-start
  40.9 1.8 %collective-permute-start.21 = (f32[832,128]{1,0:T(8,128)S(1)}, f32[832,128]{1,0:T(8,128)S(1)}, u32[]{:S(2)}, u32[]{:S(2)}) collective-permute-start(f32[832,128]{1,0:T(8,128)S(1)} %get-tuple-element.24), channel_id=1, source_target_pairs={{0,2},{1,3},{2,0},{3,1},{4,6},{5,7},{6,4},{7,5},{8,10},{9,11},{10,... | collective-permute-start | bytes 1277960 | tf_op jit(solution)/shard_map/ppermute | solution.py:298
  42.7 7.7 %collective-permute-start.22 = (f32[840,128]{1,0:T(8,128)S(1)}, f32[840,128]{1,0:T(8,128)S(1)}, u32[]{:S(2)}, u32[]{:S(2)}) collective-permute-start(f32[840,128]{1,0:T(8,128)S(1)} %get-tuple-element.25), channel_id=1, source_target_pairs={{0,4},{1,5},{2,0},{3,1},{4,6},{5,7},{6,2},{7,3},{8,12},{9,13},{10,... | collective-permute-start | bytes 1290248 | tf_op jit(solution)/shard_map/ppermute | solution.py:298
  50.4 3.3 %update_second.1 = (f32[832,128]{1,0:T(8,128)S(1)}, f32[840,128]{1,0:T(8,128)S(1)}) custom-call(f32[128,512]{1,0:T(8,128)S(1)} %broadcast_select_fusion.refs_0_, f32[128,512]{1,0:T(8,128)S(1)} %select_select_fusion.1.refs_1_, f32[128,512]{1,0:T(8,128)S(1)} %collective-permute-done.10.refs_2_, f32[128,512]{1,0:T(8,128)S(1)} %collective-permute-done.11.refs_3_, ...), custom_call_target="tpu_custom_call" | custom-call | flops 1000 | bytes 1000 | tf_op jit(solution)/shard_map/update_second/pallas_call | solution.py:448
  53.7 4.0 %collective-permute-start.23 = (f32[840,128]{1,0:T(8,128)S(1)}, f32[840,128]{1,0:T(8,128)S(1)}, u32[]{:S(2)}, u32[]{:S(2)}) collective-permute-start(f32[840,128]{1,0:T(8,128)S(1)} %get-tuple-element.26.mine), channel_id=1, source_target_pairs={{6,4},{7,5},{14,12},{15,13},{22,20},{23,21},{30,28},{31,29},{0,2},... | collective-permute-start | bytes 1290248 | tf_op jit(solution)/shard_map/ppermute | solution.py:301
  57.7 0.0 collective-permute-done.21.theirs.got_1
  57.7 1.3 %collective-permute-start.25 = (f32[832,128]{1,0:T(8,128)S(1)}, f32[832,128]{1,0:T(8,128)S(1)}, u32[]{:S(2)}, u32[]{:S(2)}) collective-permute-start(f32[832,128]{1,0:T(8,128)S(1)} %join.1), channel_id=1, source_target_pairs={{4,0},{5,1},{12,8},{13,9},{20,16},{21,17},{28,24},{29,25},{2,6},{3... | collective-permute-start | bytes 1277960 | tf_op jit(solution)/shard_map/ppermute | solution.py:301
  59.0 4.8 %collective-permute-start.26 = (f32[64,128]{1,0:T(8,128)S(1)}, f32[64,128]{1,0:T(8,128)S(1)}, u32[]{:S(2)}, u32[]{:S(2)}) collective-permute-start(f32[64,128]{1,0:T(8,128)S(1)} %get-tuple-element.27), channel_id=1, source_target_pairs={{0,6},{1,7},{2,4},{3,5},{4,2},{5,3},{6,0},{7,1},{8,14},{9,15},{10,... | collective-permute-start | bytes 98312 | tf_op jit(solution)/shard_map/ppermute | solution.py:298
  63.8 16.6 %collective-permute-done.26.far = f32[64,128]{1,0:T(8,128)S(1)} collective-permute-done((f32[64,128]{1,0:T(8,128)S(1)}, f32[64,128]{1,0:T(8,128)S(1)}, u32[]{:S(2)}, u32[]{:S(2)}) %collective-permute-start.26) | collective-permute-done | bytes 32800 | tf_op jit(solution)/shard_map/ppermute | solution.py:298
  80.4 0.0 collective-permute-done.22.got_2
  80.4 0.0 collective-permute-done.24.got_4
  80.4 0.0 collective-permute-done.23.got_3
  80.4 0.3 collective-permute-done.25.joined
  80.8 1.0 %add_up.1 = (f32[4,64,128]{2,1,0:T(8,128)}, f32[6,128,128]{2,1,0:T(8,128)}) custom-call(f32[6,128,128]{2,1,0:T(8,128)S(1)} %bitcast.4, f32[832,128]{1,0:T(8,128)S(1)} %get-tuple-element.23.own, f32[832,128]{1,0:T(8,128)S(1)} %collective-permute-done.21.theirs.got_1, f32[840,128]{1,0:T(8,128)S(1)} %collective-permute-done.22.got_2, ...), custom_call_target="tpu_custom_call" | custom-call | flops 1000 | bytes 1000 | tf_op jit(solution)/shard_map/add_up/pallas_call | solution.py:489
  (7 shorter events, 0.1 us)
Async XLA Ops:
  1.9 21.2 %collective-permute-start.5 = (f32[512,512]{1,0:T(8,128)S(1)}, f32[512,512]{1,0:T(8,128)S(1)}, u32[]{:S(2)}, u32[]{:S(2)}) collective-permute-start(f32[512,512]{1,0:T(8,128)S(1)} %get-tuple-element.22.near), channel_id=1, source_target_pairs={{10,0},{11,1}} | collective-permute-start | bytes 3145736 | tf_op jit(solution)/shard_map/ppermute | solution.py:301
  3.2 19.9 %collective-permute-start.4 = (f32[512,512]{1,0:T(8,128)S(1)}, f32[512,512]{1,0:T(8,128)S(1)}, u32[]{:S(2)}, u32[]{:S(2)}) collective-permute-start(f32[512,512]{1,0:T(8,128)S(1)} %get-tuple-element.22.near), channel_id=1, source_target_pairs={{0,8},{1,0},{2,10},{3,11},{4,12},{5,13},{6,14},{7,15},{8,9},{9,1},... | collective-permute-start | bytes 3145736 | tf_op jit(solution)/shard_map/ppermute | solution.py:298
  3.3 6.7 %collective-permute-start = (f32[128,128]{1,0:T(8,128)S(1)}, f32[128,128]{1,0:T(8,128)S(1)}, u32[]{:S(2)}, u32[]{:S(2)}) collective-permute-start(f32[128,128]{1,0:T(8,128)S(1)} %get-tuple-element.16.own), channel_id=1, source_target_pairs={{0,2},{1,9},{2,0},{3,1},{4,28},{5,13},{6,14},{7,5},{8,24},{9,11},{... | collective-permute-start | bytes 196616 | tf_op jit(solution)/shard_map/ppermute | solution.py:298
  6.2 5.3 %collective-permute-start.1 = (f32[128,128]{1,0:T(8,128)S(1)}, f32[128,128]{1,0:T(8,128)S(1)}, u32[]{:S(2)}, u32[]{:S(2)}) collective-permute-start(f32[128,128]{1,0:T(8,128)S(1)} %get-tuple-element.16.own), channel_id=1, source_target_pairs={{0,4},{1,9},{2,10},{3,11},{4,0},{5,1},{6,14},{7,3},{8,12},{9,13},{... | collective-permute-start | bytes 196616 | tf_op jit(solution)/shard_map/ppermute | solution.py:298
  8.3 6.2 %collective-permute-start.2 = (f32[128,128]{1,0:T(8,128)S(1)}, f32[128,128]{1,0:T(8,128)S(1)}, u32[]{:S(2)}, u32[]{:S(2)}) collective-permute-start(f32[128,128]{1,0:T(8,128)S(1)} %get-tuple-element.16.own), channel_id=1, source_target_pairs={{0,6},{1,7},{2,10},{3,11},{4,28},{5,13},{6,0},{7,1},{8,24},{9,15},... | collective-permute-start | bytes 196616 | tf_op jit(solution)/shard_map/ppermute | solution.py:298
  15.0 10.0 %collective-permute-start.12 = (f32[512,512]{1,0:T(8,128)S(1)}, f32[512,512]{1,0:T(8,128)S(1)}, u32[]{:S(2)}, u32[]{:S(2)}) collective-permute-start(f32[512,512]{1,0:T(8,128)S(1)} %get-tuple-element.22.near), channel_id=1, source_target_pairs={{0,8},{1,9},{2,10},{3,11},{4,12},{5,13},{6,14},{7,15},{8,0},{9,1},... | collective-permute-start | bytes 3145736 | tf_op jit(solution)/shard_map/ppermute | solution.py:298
  15.1 12.4 %collective-permute-start.15 = (f32[512,512]{1,0:T(8,128)S(1)}, f32[512,512]{1,0:T(8,128)}, u32[]{:S(2)}, u32[]{:S(2)}) collective-permute-start(f32[512,512]{1,0:T(8,128)S(1)} %get-tuple-element.22.near), channel_id=1, source_target_pairs={{13,15}} | collective-permute-start | bytes 3145736 | tf_op jit(solution)/shard_map/ppermute | solution.py:301
  16.7 6.4 %collective-permute-start.3 = (f32[128,512]{1,0:T(8,128)S(1)}, f32[128,512]{1,0:T(8,128)S(1)}, u32[]{:S(2)}, u32[]{:S(2)}) collective-permute-start(f32[128,512]{1,0:T(8,128)S(1)} %turn.1.out.own), channel_id=1, source_target_pairs={{0,1},{1,0},{2,10},{3,11},{4,12},{5,13},{6,14},{7,4},{8,24},{9,25}... | collective-permute-start | bytes 786440 | tf_op jit(solution)/shard_map/ppermute | solution.py:298
  23.1 1.0 %copy-start.1 = (f32[512,512]{1,0:T(8,128)}, f32[512,512]{1,0:T(8,128)S(1)}, u32[]{:S(2)}) copy-start(f32[512,512]{1,0:T(8,128)S(1)} %collective-permute-done.5.ly) | copy-start | bytes 3145732
  24.8 1.9 %collective-permute-start.6 = (f32[128,512]{1,0:T(8,128)S(1)}, f32[128,512]{1,0:T(8,128)S(1)}, u32[]{:S(2)}, u32[]{:S(2)}) collective-permute-start(f32[128,512]{1,0:T(8,128)S(1)} %get-tuple-element.21.s_b), channel_id=1, source_target_pairs={{0,8},{1,3},{2,10},{3,11},{4,12},{5,13},{6,14},{7,15},{8,0},{9,1},... | collective-permute-start | bytes 786440 | tf_op jit(solution)/shard_map/ppermute | solution.py:298
  26.6 3.9 %collective-permute-start.13 = (f32[128,512]{1,0:T(8,128)S(1)}, f32[128,512]{1,0:T(8,128)S(1)}, u32[]{:S(2)}, u32[]{:S(2)}) collective-permute-start(f32[128,512]{1,0:T(8,128)S(1)} %reduce_low.1), channel_id=1, source_target_pairs={{0,15},{1,9},{2,10},{3,11},{4,12},{5,13},{6,14},{7,8},{8,0},{9,1},... | collective-permute-start | bytes 786440 | tf_op jit(solution)/shard_map/ppermute | solution.py:298
  26.7 6.7 %collective-permute-start.14 = (f32[128,512]{1,0:T(8,128)S(1)}, f32[128,512]{1,0:T(8,128)S(1)}, u32[]{:S(2)}, u32[]{:S(2)}) collective-permute-start(f32[128,512]{1,0:T(8,128)S(1)} %reduce_low.1), channel_id=1, source_target_pairs={{0,12},{1,15},{2,10},{3,11},{4,8},{5,13},{6,14},{7,9},{8,0},{9,1},... | collective-permute-start | bytes 786440 | tf_op jit(solution)/shard_map/ppermute | solution.py:298
  26.8 7.3 %collective-permute-start.7 = (f32[128,512]{1,0:T(8,128)S(1)}, f32[128,512]{1,0:T(8,128)S(1)}, u32[]{:S(2)}, u32[]{:S(2)}) collective-permute-start(f32[128,512]{1,0:T(8,128)S(1)} %broadcast_select_fusion.refs_0_), channel_id=1, source_target_pairs={{0,8},{1,9},{2,10},{3,18},{4,12},{5,13},{6,14},{7,15},{8,0},{9,1},... | collective-permute-start | bytes 786440 | tf_op jit(solution)/shard_map/ppermute | solution.py:298
  27.3 7.2 %collective-permute-start.8 = (f32[128,512]{1,0:T(8,128)S(1)}, f32[128,512]{1,0:T(8,128)S(1)}, u32[]{:S(2)}, u32[]{:S(2)}) collective-permute-start(f32[128,512]{1,0:T(8,128)S(1)} %broadcast_select_fusion.refs_0_), channel_id=1, source_target_pairs={{0,8},{1,9},{2,10},{3,2},{4,12},{5,13},{6,14},{7,15},{8,0},{9,1},{... | collective-permute-start | bytes 786440 | tf_op jit(solution)/shard_map/ppermute | solution.py:298
  27.4 7.2 %collective-permute-start.9 = (f32[128,512]{1,0:T(8,128)S(1)}, f32[128,512]{1,0:T(8,128)S(1)}, u32[]{:S(2)}, u32[]{:S(2)}) collective-permute-start(f32[128,512]{1,0:T(8,128)S(1)} %broadcast_select_fusion.refs_0_), channel_id=1, source_target_pairs={{0,16},{1,17},{2,10},{3,19},{4,12},{5,13},{6,14},{7,15},{8,0},{9,1... | collective-permute-start | bytes 786440 | tf_op jit(solution)/shard_map/ppermute | solution.py:298
  33.4 1.8 %collective-permute-start.16 = (f32[128,512]{1,0:T(8,128)S(1)}, f32[128,512]{1,0:T(8,128)S(1)}, u32[]{:S(2)}, u32[]{:S(2)}) collective-permute-start(f32[128,512]{1,0:T(8,128)S(1)} %solve_high.1.refs_4_), channel_id=1, source_target_pairs={{0,8},{1,9},{2,10},{3,11},{4,12},{5,13},{6,14},{7,15},{8,0},{9,1},... | collective-permute-start | bytes 786440 | tf_op jit(solution)/shard_map/ppermute | solution.py:298
  34.1 1.5 %collective-permute-start.17 = (f32[128,512]{1,0:T(8,128)S(1)}, f32[128,512]{1,0:T(8,128)S(1)}, u32[]{:S(2)}, u32[]{:S(2)}) collective-permute-start(f32[128,512]{1,0:T(8,128)S(1)} %solve_high.1.refs_4_), channel_id=1, source_target_pairs={{0,8},{1,9},{2,10},{3,11},{4,12},{5,4},{6,7},{7,15},{8,0},{9,1},{1... | collective-permute-start | bytes 786440 | tf_op jit(solution)/shard_map/ppermute | solution.py:298
  34.1 1.9 %collective-permute-start.18 = (f32[128,512]{1,0:T(8,128)S(1)}, f32[128,512]{1,0:T(8,128)S(1)}, u32[]{:S(2)}, u32[]{:S(2)}) collective-permute-start(f32[128,512]{1,0:T(8,128)S(1)} %solve_high.1.refs_4_), channel_id=1, source_target_pairs={{0,8},{1,9},{2,10},{3,11},{4,12},{5,13},{6,14},{7,15},{8,0},{9,1},... | collective-permute-start | bytes 786440 | tf_op jit(solution)/shard_map/ppermute | solution.py:298
  34.6 1.9 %collective-permute-start.10 = (f32[128,512]{1,0:T(8,128)S(1)}, f32[128,512]{1,0:T(8,128)S(1)}, u32[]{:S(2)}, u32[]{:S(2)}) collective-permute-start(f32[128,512]{1,0:T(8,128)S(1)} %broadcast_select_fusion.refs_0_), channel_id=1, source_target_pairs={{0,8},{1,9},{2,10},{3,11},{4,12},{5,13},{6,14},{7,15},{8,0},{9,1},... | collective-permute-start | bytes 786440 | tf_op jit(solution)/shard_map/ppermute | solution.py:298
  34.7 2.1 %collective-permute-start.19 = (f32[128,512]{1,0:T(8,128)S(1)}, f32[128,512]{1,0:T(8,128)S(1)}, u32[]{:S(2)}, u32[]{:S(2)}) collective-permute-start(f32[128,512]{1,0:T(8,128)S(1)} %solve_high.1.refs_4_), channel_id=1, source_target_pairs={{0,8},{1,9},{2,10},{3,11},{4,12},{5,13},{6,14},{7,15},{8,0},{9,1},... | collective-permute-start | bytes 786440 | tf_op jit(solution)/shard_map/ppermute | solution.py:298
  35.2 1.9 %collective-permute-start.11 = (f32[128,512]{1,0:T(8,128)S(1)}, f32[128,512]{1,0:T(8,128)S(1)}, u32[]{:S(2)}, u32[]{:S(2)}) collective-permute-start(f32[128,512]{1,0:T(8,128)S(1)} %select_select_fusion.1.refs_1_), channel_id=1, source_target_pairs={{0,8},{1,9},{2,10},{3,11},{4,12},{5,13},{6,14},{7,15},{8,0},{9,1},... | collective-permute-start | bytes 786440 | tf_op jit(solution)/shard_map/ppermute | solution.py:298
  36.0 1.6 %collective-permute-start.20 = (f32[128,512]{1,0:T(8,128)S(1)}, f32[128,512]{1,0:T(8,128)S(1)}, u32[]{:S(2)}, u32[]{:S(2)}) collective-permute-start(f32[128,512]{1,0:T(8,128)S(1)} %select_select_fusion.refs_5_), channel_id=1, source_target_pairs={{0,8},{1,9},{2,10},{3,11},{4,12},{5,13},{6,14},{7,15},{8,0},{9,1},... | collective-permute-start | bytes 786440 | tf_op jit(solution)/shard_map/ppermute | solution.py:298
  40.9 39.8 %copy-start = (f32[6,1,1,128,128]{4,3,2,1,0:T(8,128)S(1)}, f32[6,1,1,128,128]{4,3,2,1,0:T(8,128)}, u32[]{:S(2)}) copy-start(f32[6,1,1,128,128]{4,3,2,1,0:T(8,128)} %rhs.1) | copy-start | bytes 1179652
  40.9 16.7 %collective-permute-start.21 = (f32[832,128]{1,0:T(8,128)S(1)}, f32[832,128]{1,0:T(8,128)S(1)}, u32[]{:S(2)}, u32[]{:S(2)}) collective-permute-start(f32[832,128]{1,0:T(8,128)S(1)} %get-tuple-element.24), channel_id=1, source_target_pairs={{0,2},{1,3},{2,0},{3,1},{4,6},{5,7},{6,4},{7,5},{8,10},{9,11},{10,... | collective-permute-start | bytes 1277960 | tf_op jit(solution)/shard_map/ppermute | solution.py:298
  42.7 37.7 %collective-permute-start.22 = (f32[840,128]{1,0:T(8,128)S(1)}, f32[840,128]{1,0:T(8,128)S(1)}, u32[]{:S(2)}, u32[]{:S(2)}) collective-permute-start(f32[840,128]{1,0:T(8,128)S(1)} %get-tuple-element.25), channel_id=1, source_target_pairs={{0,4},{1,5},{2,0},{3,1},{4,6},{5,7},{6,2},{7,3},{8,12},{9,13},{10,... | collective-permute-start | bytes 1290248 | tf_op jit(solution)/shard_map/ppermute | solution.py:298
  50.4 30.0 %collective-permute-start.24 = (f32[840,128]{1,0:T(8,128)S(1)}, f32[840,128]{1,0:T(8,128)S(1)}, u32[]{:S(2)}, u32[]{:S(2)}) collective-permute-start(f32[840,128]{1,0:T(8,128)S(1)} %get-tuple-element.25), channel_id=1, source_target_pairs={{0,8},{1,9},{2,4},{3,5},{4,2},{5,3},{6,14},{7,15},{8,0},{9,1},{10,... | collective-permute-start | bytes 1290248 | tf_op jit(solution)/shard_map/ppermute | solution.py:298
  53.7 26.8 %collective-permute-start.23 = (f32[840,128]{1,0:T(8,128)S(1)}, f32[840,128]{1,0:T(8,128)S(1)}, u32[]{:S(2)}, u32[]{:S(2)}) collective-permute-start(f32[840,128]{1,0:T(8,128)S(1)} %get-tuple-element.26.mine), channel_id=1, source_target_pairs={{6,4},{7,5},{14,12},{15,13},{22,20},{23,21},{30,28},{31,29},{0,2},... | collective-permute-start | bytes 1290248 | tf_op jit(solution)/shard_map/ppermute | solution.py:301
  57.7 23.1 %collective-permute-start.25 = (f32[832,128]{1,0:T(8,128)S(1)}, f32[832,128]{1,0:T(8,128)S(1)}, u32[]{:S(2)}, u32[]{:S(2)}) collective-permute-start(f32[832,128]{1,0:T(8,128)S(1)} %join.1), channel_id=1, source_target_pairs={{4,0},{5,1},{12,8},{13,9},{20,16},{21,17},{28,24},{29,25},{2,6},{3... | collective-permute-start | bytes 1277960 | tf_op jit(solution)/shard_map/ppermute | solution.py:301
  59.0 21.4 %collective-permute-start.26 = (f32[64,128]{1,0:T(8,128)S(1)}, f32[64,128]{1,0:T(8,128)S(1)}, u32[]{:S(2)}, u32[]{:S(2)}) collective-permute-start(f32[64,128]{1,0:T(8,128)S(1)} %get-tuple-element.27), channel_id=1, source_target_pairs={{0,6},{1,7},{2,4},{3,5},{4,2},{5,3},{6,0},{7,1},{8,14},{9,15},{10,... | collective-permute-start | bytes 98312 | tf_op jit(solution)/shard_map/ppermute | solution.py:298
